TPU v7x, 32 devices: a whole 2x2x4 slice. The times are simulated.
32 devices in a mesh: dp: 8 (over z, x), seq: 4 (over y, core).
Axes of the slice: x: 2, y: 2, z: 4, core: 2. Of those that a mesh axis runs over, the one named last changes fastest.
Arguments:
- frames: bfloat16 [12288, 768], P(('dp', 'seq')), may hold values from -6 to 6
- cotangent: bfloat16 [12288, 768], P(('dp', 'seq')), may hold values from -6 to 6
- lengths: int32 [8, 3], P('dp'), may hold values from 48 to 1440, as said below
- input_weight: bfloat16 [768, 2304], replicated, may hold values from -0.21875 to 0.21875
- output_weight: bfloat16 [768, 768], replicated, may hold values from -0.21875 to 0.21875
- expand_weight: bfloat16 [768, 3072], replicated, may hold values from -0.21875 to 0.21875
- reduce_weight: bfloat16 [3072, 768], replicated, may hold values from -0.109375 to 0.109375
- vector_copy: bfloat16 [12, 768], replicated, may hold values from -0.6 to 2.6
- input_master: float32 [768, 2304], P('dp', 'seq'), may hold values from -0.21875 to 0.21875
- output_master: float32 [768, 768], P('seq', 'dp'), may hold values from -0.21875 to 0.21875
- expand_master: float32 [768, 3072], P('seq', 'dp'), may hold values from -0.21875 to 0.21875
- reduce_master: float32 [3072, 768], P('seq', 'dp'), may hold values from -0.109375 to 0.109375
- vector_master: float32 [12, 768], P('seq', 'dp'), may hold values from -0.6 to 2.6
- input_first: float32 [768, 2304], P('dp', 'seq'), may hold values from -0.00024414062 to 0.00024414062
- output_first: float32 [768, 768], P('seq', 'dp'), may hold values from -0.00024414062 to 0.00024414062
- expand_first: float32 [768, 3072], P('seq', 'dp'), may hold values from -0.00024414062 to 0.00024414062
- reduce_first: float32 [3072, 768], P('seq', 'dp'), may hold values from -0.00024414062 to 0.00024414062
- vector_first: float32 [12, 768], P('seq', 'dp'), may hold values from -0.00024414062 to 0.00024414062
- input_second: float32 [768, 2304], P('dp', 'seq'), may hold values from 1.4110135e-10 to 5.644054e-10
- output_second: float32 [768, 768], P('seq', 'dp'), may hold values from 1.4110135e-10 to 5.644054e-10
- expand_second: float32 [768, 3072], P('seq', 'dp'), may hold values from 1.4110135e-10 to 5.644054e-10
- reduce_second: float32 [3072, 768], P('seq', 'dp'), may hold values from 1.4110135e-10 to 5.644054e-10
- vector_second: float32 [12, 768], P('seq', 'dp'), may hold values from 1.4110135e-10 to 5.644054e-10
Outputs:
- layer_output: bfloat16 [12288, 768], P(('dp', 'seq'))
- frames_gradient: float32 [12288, 768], P(('dp', 'seq'))
- gradient_norm: float32 [], replicated
- input_mean: float32 [768, 2304], P('dp', 'seq')
- input_square: float32 [768, 2304], P('dp', 'seq')
- input_new: float32 [768, 2304], P('dp', 'seq')
- input_rounded: bfloat16 [768, 2304], P('dp', 'seq')
- output_mean: float32 [768, 768], P('seq', 'dp')
- output_square: float32 [768, 768], P('seq', 'dp')
- output_new: float32 [768, 768], P('seq', 'dp')
- output_rounded: bfloat16 [768, 768], P('seq', 'dp')
- expand_mean: float32 [768, 3072], P('seq', 'dp')
- expand_square: float32 [768, 3072], P('seq', 'dp')
- expand_new: float32 [768, 3072], P('seq', 'dp')
- expand_rounded: bfloat16 [768, 3072], P('seq', 'dp')
- reduce_mean: float32 [3072, 768], P('seq', 'dp')
- reduce_square: float32 [3072, 768], P('seq', 'dp')
- reduce_new: float32 [3072, 768], P('seq', 'dp')
- reduce_rounded: bfloat16 [3072, 768], P('seq', 'dp')
- vector_mean: float32 [12, 768], P('seq', 'dp')
- vector_square: float32 [12, 768], P('seq', 'dp')
- vector_new: float32 [12, 768], P('seq', 'dp')
- vector_rounded: bfloat16 [12, 768], P('seq', 'dp')
Inputs may be any that keep to these rules, and one draw needn't show every extreme that they name: `lengths`: the utterances of a group stand end to end from the group's first frame; the group's frames after the last one are padding.
All inputs are finite; a program needn't handle non-finite values.
Results may differ from a plain program's by a relative error of at most 0.012.
Values may be sent and summed in bfloat16 or wider, within the bound.
No kernel may reach another device: no remote copies, remote signals or barrier semaphores. Data moves between devices by JAX's collectives and lax.ppermute only.
A program may use at most 128 MiB of HBM per device.

v0:
```python
import jax
import jax.numpy as jnp
from jax import lax
from jax.sharding import PartitionSpec as P

HD = 64
STEP = 10


layer_eps = 1e-05
masked_score = -1000000000.0
clip_limit = 1.0


def layer_norm(values, gain_row, shift_row):
    center = values - jnp.mean(values, axis=-1, keepdims=True)
    inverse = lax.rsqrt(jnp.mean(center * center, axis=-1, keepdims=True) + layer_eps)
    normed = center * inverse
    return (normed * gain_row + shift_row, normed, inverse)


def norm_back(grad_output, normed, inverse, gain_row):
    grad_normed = grad_output * gain_row
    centered = grad_normed - jnp.mean(grad_normed, axis=-1, keepdims=True)
    centered = centered - normed * jnp.mean(grad_normed * normed, axis=-1, keepdims=True)
    return (inverse * centered, jnp.sum(grad_output * normed, axis=0), jnp.sum(grad_output, axis=0))


def gelu_both(values):
    normal_cdf = 0.5 * (1.0 + jax.scipy.special.erf(values * 0.7071067811865476))
    density = jnp.exp(-0.5 * values * values) * 0.3989422804014327
    return (values * normal_cdf, normal_cdf + values * density)


def block_weights(query_block, key_rows, segment_block, segments, score_scale):
    scores = (
        jnp.einsum("qhd,khd->hqk", query_block, key_rows, preferred_element_type=jnp.float32)
        * score_scale
    )
    allowed = segment_block[:, None] == segments[None, :]
    scores = jnp.where(allowed[None], scores, masked_score)
    row_top = jnp.max(scores, axis=-1, keepdims=True)
    row_total = jnp.sum(jnp.exp(scores - row_top), axis=-1, keepdims=True)
    return jnp.exp(scores - (row_top + jnp.log(row_total)))


def attend_forward(queries, key_rows, value_rows, segments):
    slab_rows, head_local, head_size = queries.shape
    block_rows = min(512, slab_rows)
    score_scale = head_size ** (-0.5)

    def one_block(block_index):
        block_start = block_index * block_rows
        query_block = lax.dynamic_slice_in_dim(queries, block_start, block_rows, 0)
        segment_block = lax.dynamic_slice_in_dim(segments, block_start, block_rows, 0)
        weights_low = block_weights(
            query_block, key_rows, segment_block, segments, score_scale
        ).astype(jnp.bfloat16)
        return jnp.einsum(
            "hqk,khd->qhd", weights_low, value_rows, preferred_element_type=jnp.float32
        )

    mixed_blocks = lax.map(one_block, jnp.arange(slab_rows // block_rows))
    return mixed_blocks.reshape(slab_rows, head_local, head_size)


def attend_backward(queries, key_rows, value_rows, segments, grad_mixed):
    slab_rows, head_local, head_size = queries.shape
    block_rows = min(512, slab_rows)
    score_scale = head_size ** (-0.5)

    def one_block(running, block_index):
        grad_keys, grad_values = running
        block_start = block_index * block_rows
        query_block = lax.dynamic_slice_in_dim(queries, block_start, block_rows, 0)
        grad_block = lax.dynamic_slice_in_dim(grad_mixed, block_start, block_rows, 0)
        segment_block = lax.dynamic_slice_in_dim(segments, block_start, block_rows, 0)
        weights_exact = block_weights(query_block, key_rows, segment_block, segments, score_scale)
        weights_low = weights_exact.astype(jnp.bfloat16)
        grad_values = grad_values + jnp.einsum(
            "hqk,qhd->khd", weights_low, grad_block, preferred_element_type=jnp.float32
        )
        grad_weights = jnp.einsum(
            "qhd,khd->hqk", grad_block, value_rows, preferred_element_type=jnp.float32
        )
        grad_scores = weights_exact * (
            grad_weights - jnp.sum(weights_exact * grad_weights, axis=-1, keepdims=True)
        )
        grad_low = grad_scores.astype(jnp.bfloat16)
        grad_queries = (
            jnp.einsum("hqk,khd->qhd", grad_low, key_rows, preferred_element_type=jnp.float32)
            * score_scale
        )
        grad_keys = (
            grad_keys
            + jnp.einsum("hqk,qhd->khd", grad_low, query_block, preferred_element_type=jnp.float32)
            * score_scale
        )
        return ((grad_keys, grad_values), grad_queries.astype(jnp.bfloat16))

    zero_block = jnp.zeros((slab_rows, head_local, head_size), jnp.float32)
    finals, grad_queries = lax.scan(
        one_block, (zero_block, zero_block), jnp.arange(slab_rows // block_rows)
    )
    grad_queries = grad_queries.reshape(slab_rows, head_local, head_size)
    return (grad_queries, finals[0].astype(jnp.bfloat16), finals[1].astype(jnp.bfloat16))


def forward_pass(
    frames, input_weight, output_weight, expand_weight, reduce_weight, vectors, segments, own_valid
):
    row_count, model_width = frames.shape
    groups = lax.axis_size("seq")
    slab_rows = row_count * groups
    part_width = model_width // groups
    head_local = part_width // HD
    bias_row = jnp.concatenate([vectors[0], jnp.zeros_like(vectors[0]), vectors[1]])
    projected = jnp.dot(frames, input_weight, preferred_element_type=jnp.float32) + bias_row
    projected = projected.astype(jnp.bfloat16).reshape(row_count, 3, groups, part_width)
    by_heads = lax.all_to_all(projected, "seq", split_axis=2, concat_axis=0, tiled=True)
    by_heads = by_heads.reshape(slab_rows, 3, head_local, HD)
    mixed_heads = attend_forward(by_heads[:, 0], by_heads[:, 1], by_heads[:, 2], segments)
    mixed_low = mixed_heads.astype(jnp.bfloat16).reshape(slab_rows, 1, part_width)
    mixed_time = lax.all_to_all(mixed_low, "seq", split_axis=0, concat_axis=1, tiled=True).reshape(
        row_count, model_width
    )
    attended = jnp.dot(mixed_time, output_weight, preferred_element_type=jnp.float32) + vectors[2]
    hidden, normed_first, inverse_first = layer_norm(
        frames.astype(jnp.float32) + attended, vectors[3], vectors[4]
    )
    hidden_low = hidden.astype(jnp.bfloat16)
    expanded = jnp.dot(hidden_low, expand_weight, preferred_element_type=jnp.float32) + vectors[
        8:12
    ].reshape(-1)
    activated, gate_slope = gelu_both(expanded)
    activated_low = activated.astype(jnp.bfloat16)
    branch = jnp.dot(activated_low, reduce_weight, preferred_element_type=jnp.float32) + vectors[5]
    result, normed_second, inverse_second = layer_norm(hidden + branch, vectors[6], vectors[7])
    return (
        result * own_valid[:, None],
        by_heads,
        mixed_time,
        normed_first,
        inverse_first,
        hidden_low,
        gate_slope,
        activated_low,
        normed_second,
        inverse_second,
    )


def adam_step(master, moment_one, moment_two, gradient, step_rate, decay_weight):
    new_one = 0.9 * moment_one + 0.1 * gradient
    new_two = 0.999 * moment_two + 0.001 * gradient * gradient
    corrected_one = new_one / (1.0 - 0.9**STEP)
    corrected_two = new_two / (1.0 - 0.999**STEP)
    new_master = master - step_rate * (
        corrected_one / (jnp.sqrt(corrected_two) + 1e-08) + decay_weight * master
    )
    return (new_one, new_two, new_master, new_master.astype(jnp.bfloat16))


def local(
    frames,
    cotangent,
    lengths,
    input_weight,
    output_weight,
    expand_weight,
    reduce_weight,
    vector_copy,
    input_master,
    output_master,
    expand_master,
    reduce_master,
    vector_master,
    input_first,
    output_first,
    expand_first,
    reduce_first,
    vector_first,
    input_second,
    output_second,
    expand_second,
    reduce_second,
    vector_second,
):
    row_count, model_width = frames.shape
    groups = lax.axis_size("seq")
    slab_rows = row_count * groups
    part_width = model_width // groups
    head_local = part_width // HD
    vectors = vector_copy.astype(jnp.float32)
    utterance_ends = jnp.cumsum(lengths[0])
    positions = jnp.arange(slab_rows, dtype=jnp.int32)
    segments = jnp.sum((positions[:, None] >= utterance_ends[None, :]).astype(jnp.int32), axis=1)
    own_segments = lax.dynamic_slice_in_dim(
        segments, lax.axis_index("seq") * row_count, row_count, 0
    )
    own_valid = (own_segments < lengths.shape[1]).astype(jnp.float32)
    kept_values = forward_pass(
        frames,
        input_weight,
        output_weight,
        expand_weight,
        reduce_weight,
        vectors,
        segments,
        own_valid,
    )
    layer_output = kept_values[0].astype(jnp.bfloat16)
    grad_result = cotangent.astype(jnp.float32) * own_valid[:, None]
    frames_again, grad_result = lax.optimization_barrier((frames, grad_result))
    kept_values = forward_pass(
        frames_again,
        input_weight,
        output_weight,
        expand_weight,
        reduce_weight,
        vectors,
        segments,
        own_valid,
    )
    by_heads = kept_values[1]
    mixed_time = kept_values[2]
    normed_first = kept_values[3]
    inverse_first = kept_values[4]
    hidden_low = kept_values[5]
    gate_slope = kept_values[6]
    activated_low = kept_values[7]
    normed_second = kept_values[8]
    inverse_second = kept_values[9]
    grad_second, grad_gain_two, grad_shift_two = norm_back(
        grad_result, normed_second, inverse_second, vectors[6]
    )
    grad_branch = grad_second.astype(jnp.bfloat16)
    grad_bias_two = jnp.sum(grad_branch, axis=0, dtype=jnp.float32)
    reduce_gradient = jnp.einsum(
        "tf,td->fd", activated_low, grad_branch, preferred_element_type=jnp.float32
    )
    grad_activated = jnp.einsum(
        "td,fd->tf", grad_branch, reduce_weight, preferred_element_type=jnp.float32
    )
    grad_expanded = (grad_activated * gate_slope).astype(jnp.bfloat16)
    grad_bias_one = jnp.sum(grad_expanded, axis=0, dtype=jnp.float32)
    expand_gradient = jnp.einsum(
        "td,tf->df", hidden_low, grad_expanded, preferred_element_type=jnp.float32
    )
    grad_hidden = grad_second + jnp.einsum(
        "tf,df->td", grad_expanded, expand_weight, preferred_element_type=jnp.float32
    )
    grad_first, grad_gain_one, grad_shift_one = norm_back(
        grad_hidden, normed_first, inverse_first, vectors[3]
    )
    grad_attended = grad_first.astype(jnp.bfloat16)
    grad_bias_out = jnp.sum(grad_attended, axis=0, dtype=jnp.float32)
    output_gradient = jnp.einsum(
        "tc,td->cd", mixed_time, grad_attended, preferred_element_type=jnp.float32
    )
    grad_mixed = jnp.einsum(
        "td,cd->tc", grad_attended, output_weight, preferred_element_type=jnp.float32
    ).astype(jnp.bfloat16)
    grad_mixed = grad_mixed.reshape(row_count, groups, part_width)
    grad_mixed = lax.all_to_all(grad_mixed, "seq", split_axis=1, concat_axis=0, tiled=True).reshape(
        slab_rows, head_local, HD
    )
    grad_queries, grad_keys, grad_values = attend_backward(
        by_heads[:, 0], by_heads[:, 1], by_heads[:, 2], segments, grad_mixed
    )
    grad_stacked = jnp.stack([grad_queries, grad_keys, grad_values], axis=1).reshape(
        slab_rows, 3, 1, part_width
    )
    grad_projected = lax.all_to_all(
        grad_stacked, "seq", split_axis=0, concat_axis=2, tiled=True
    ).reshape(row_count, 3 * model_width)
    grad_bias_query = jnp.sum(grad_projected[:, :model_width], axis=0, dtype=jnp.float32)
    grad_bias_value = jnp.sum(grad_projected[:, 2 * model_width :], axis=0, dtype=jnp.float32)
    input_gradient = jnp.einsum(
        "td,tc->dc", frames, grad_projected, preferred_element_type=jnp.float32
    )
    frames_gradient = grad_first + jnp.einsum(
        "tc,dc->td", grad_projected, input_weight, preferred_element_type=jnp.float32
    )
    vector_rows = jnp.stack(
        [
            grad_bias_query,
            grad_bias_value,
            grad_bias_out,
            grad_gain_one,
            grad_shift_one,
            grad_bias_two,
            grad_gain_two,
            grad_shift_two,
        ],
        axis=0,
    )
    vector_gradient = jnp.concatenate([vector_rows, grad_bias_one.reshape(-1, model_width)], axis=0)
    partial_sums = (
        lax.psum_scatter(
            input_gradient.astype(jnp.bfloat16), "seq", scatter_dimension=1, tiled=True
        ).astype(jnp.float32),
        lax.psum_scatter(
            output_gradient.astype(jnp.bfloat16), "seq", scatter_dimension=0, tiled=True
        ).astype(jnp.float32),
        lax.psum_scatter(
            expand_gradient.astype(jnp.bfloat16), "seq", scatter_dimension=0, tiled=True
        ).astype(jnp.float32),
        lax.psum_scatter(
            reduce_gradient.astype(jnp.bfloat16), "seq", scatter_dimension=0, tiled=True
        ).astype(jnp.float32),
        lax.psum_scatter(
            vector_gradient.astype(jnp.bfloat16), "seq", scatter_dimension=0, tiled=True
        ).astype(jnp.float32),
    )
    shards = (
        lax.psum_scatter(partial_sums[0], "dp", scatter_dimension=0, tiled=True),
        lax.psum_scatter(partial_sums[1], "dp", scatter_dimension=1, tiled=True),
        lax.psum_scatter(partial_sums[2], "dp", scatter_dimension=1, tiled=True),
        lax.psum_scatter(partial_sums[3], "dp", scatter_dimension=1, tiled=True),
        lax.psum_scatter(partial_sums[4], "dp", scatter_dimension=1, tiled=True),
    )
    local_squares = jnp.float32(0.0)
    for shard_piece in shards:
        local_squares = local_squares + jnp.sum(shard_piece * shard_piece)
    squares_total = lax.psum(local_squares, ("dp", "seq"))
    gradient_norm = jnp.sqrt(squares_total)
    factor = clip_limit / jnp.maximum(gradient_norm, clip_limit)
    ffn_width = expand_weight.shape[1]
    input_parts = adam_step(
        input_master,
        input_first,
        input_second,
        shards[0] * factor,
        2.0 * model_width ** (-0.5),
        0.01,
    )
    output_parts = adam_step(
        output_master,
        output_first,
        output_second,
        shards[1] * factor,
        2.0 * model_width ** (-0.5),
        0.01,
    )
    expand_parts = adam_step(
        expand_master,
        expand_first,
        expand_second,
        shards[2] * factor,
        2.0 * model_width ** (-0.5),
        0.01,
    )
    reduce_parts = adam_step(
        reduce_master,
        reduce_first,
        reduce_second,
        shards[3] * factor,
        2.0 * ffn_width ** (-0.5),
        0.01,
    )
    vector_parts = adam_step(
        vector_master, vector_first, vector_second, shards[4] * factor, 0.5, 0.0
    )
    return (
        layer_output,
        frames_gradient,
        gradient_norm,
        input_parts[0],
        input_parts[1],
        input_parts[2],
        input_parts[3],
        output_parts[0],
        output_parts[1],
        output_parts[2],
        output_parts[3],
        expand_parts[0],
        expand_parts[1],
        expand_parts[2],
        expand_parts[3],
        reduce_parts[0],
        reduce_parts[1],
        reduce_parts[2],
        reduce_parts[3],
        vector_parts[0],
        vector_parts[1],
        vector_parts[2],
        vector_parts[3],
    )


def solution(mesh):
    placed = (
        P(("dp", "seq"), None),
        P(("dp", "seq"), None),
        P("dp", None),
        P(),
        P(),
        P(),
        P(),
        P(),
        P("dp", "seq"),
        P("seq", "dp"),
        P("seq", "dp"),
        P("seq", "dp"),
        P("seq", "dp"),
        P("dp", "seq"),
        P("seq", "dp"),
        P("seq", "dp"),
        P("seq", "dp"),
        P("seq", "dp"),
        P("dp", "seq"),
        P("seq", "dp"),
        P("seq", "dp"),
        P("seq", "dp"),
        P("seq", "dp"),
    )
    return jax.shard_map(
        local,
        mesh=mesh,
        in_specs=placed,
        out_specs=(
            P(("dp", "seq"), None),
            P(("dp", "seq"), None),
            P(),
            P("dp", "seq"),
            P("dp", "seq"),
            P("dp", "seq"),
            P("dp", "seq"),
            P("seq", "dp"),
            P("seq", "dp"),
            P("seq", "dp"),
            P("seq", "dp"),
            P("seq", "dp"),
            P("seq", "dp"),
            P("seq", "dp"),
            P("seq", "dp"),
            P("seq", "dp"),
            P("seq", "dp"),
            P("seq", "dp"),
            P("seq", "dp"),
            P("seq", "dp"),
            P("seq", "dp"),
            P("seq", "dp"),
            P("seq", "dp"),
        ),
        check_vma=False,
    )
```

profile of v0, /device:TPU:0, one launch (start us, length us, event | category | flops | bytes accessed | tf_op | source)
XLA Modules:
  0.0 1015.5 jit_solution(8897608420811538903)
XLA Ops:
  9.4 3.8 fusion.55
  13.2 3.9 copy.260
  19.9 4.4 all-to-all-start
  33.5 3.9 copy.267
  40.2 7.0 all-to-all-done
  47.2 4.6 all-to-all-start.2
  51.8 4.1 copy.262
  55.9 4.0 reshape.325
  63.5 33.7 %while.35 = (s32[]{:T(128)}, bf16[3,512,3,64]{1,3,2,0:T(8,128)(2,1)}, s32[3]{0:T(128)S(1)}, s32[1536]{0:T(1024)S(1)}, bf16[1536,3,64]{0,2,1:T(8,128)(2,1)}, /*in...) while((s32[]{:T(128)}, ...), condition=%wide.region_5.6_spmd, body=%wide.region_2.5_spmd.sunk | while | flops 630716928 | bytes 35642056 | solution.py:63
  100.6 7.1 reshape.334
  108.3 10.8 %reduce.27 = bf16[1536,192]{1,0:T(8,128)(2,1)} reduce(bf16[1536,1,192]{2,1,0:T(2,128)(2,1)} %reshape.334, bf16[]{:T(256)} %broadcast.309), dimensions={1}, to_apply=%reshape.334.reduce_sub_computation | reduce | bytes 1179650 | tf_op jit(solution)/shard_map/convert_element_type | solution.py:123
  119.1 3.5 reshape.355
  122.6 4.2 all-to-all-start.1
  126.8 4.0 copy.269
  130.8 4.0 reshape.328
  138.4 33.7 %while.36 = (s32[]{:T(128)}, bf16[3,512,3,64]{1,3,2,0:T(8,128)(2,1)}, s32[3]{0:T(128)S(1)}, s32[1536]{0:T(1024)S(1)}, bf16[1536,3,64]{0,2,1:T(8,128)(2,1)}, /*in...) while((s32[]{:T(128)}, ...), condition=%wide.region_13.14_spmd, body=%wide.region_10.13_spmd.sunk | while | flops 630716928 | bytes 35642056 | solution.py:63
  175.5 7.1 reshape.335
  182.6 10.8 %reduce.26 = bf16[1536,192]{1,0:T(8,128)(2,1)} reduce(bf16[1536,1,192]{2,1,0:T(2,128)(2,1)} %reshape.335, bf16[]{:T(256)} %broadcast.309), dimensions={1}, to_apply=%reshape.335.reduce_sub_computation | reduce | bytes 1179650 | tf_op jit(solution)/shard_map/convert_element_type | solution.py:123
  196.7 4.2 all-to-all-start.3
  200.9 3.9 reshape.356
  204.7 4.6 copy.265
  216.9 10.1 fusion.101
  229.8 3.9 reshape.354
  233.6 4.6 copy.272
  244.5 4.5 multiply_convert_fusion.1
  249.1 5.4 fusion.99
  258.9 4.5 fusion.104
  272.1 4.1 all-to-all-start.4
  279.7 6.2 all-to-all-done.4
  291.0 98.0 %while.37 = (s32[]{:T(128)}, f32[1536,3,64]{0,2,1:T(8,128)}, f32[1536,3,64]{0,2,1:T(8,128)}, bf16[3,512,3,64]{1,3,2,0:T(8,128)(2,1)}, s32[3]{0:T(128)}, /*index=...) while((s32[]{:T(128)}, f32[1536,3,64]{0,2,1:T(8,128)}, ...), condition=%wide.region_26.27_spmd.clone, body=%wide.region_22.26_spmd.clone.sunk | while | flops 1564308480 | bytes 176634752 | solution.py:102
  293.5 3.5 fusion.174
  299.9 4.7 multiply_reduce_fusion.17
  304.6 4.3 multiply_convert_fusion.5
  309.0 4.5 fusion.175
  313.5 4.8 fusion.177
  318.3 4.8 fusion.176
  325.6 3.5 fusion.174
  332.0 4.8 multiply_reduce_fusion.17
  336.8 4.3 multiply_convert_fusion.5
  341.1 4.9 fusion.175
  346.0 4.8 fusion.177
  350.8 5.3 fusion.176
  358.6 3.5 fusion.174
  365.0 4.8 multiply_reduce_fusion.17
  369.7 4.3 multiply_convert_fusion.5
  374.1 4.9 fusion.175
  379.0 4.8 fusion.177
  383.7 5.3 fusion.176
  398.3 5.5 copy.277
  403.8 42.2 %all_to_all.90 = bf16[1536,3,1,192]{3,1,2,0:T(4,128)(2,1)} all-to-all(bf16[1536,3,1,192]{3,1,2,0:T(4,128)(2,1)} %copy.277), channel_id=1, replica_groups=mesh['dp'=8,'seq'=4] {'seq'}, dimensions={0} | all-to-all | bytes 3538944 | tf_op jit(solution)/shard_map/all_to_all | solution.py:274
  446.1 5.8 copy.291
  455.0 3.8 fusion.54
  458.9 6.8 convolution_convert_fusion
  466.4 7.5 convolution_convert_fusion.1
  486.3 12.7 %all-reduce = bf16[12,768]{1,0:T(8,128)(2,1)} all-reduce(bf16[12,768]{1,0:T(8,128)(2,1)} %concatenate.10), channel_id=10, replica_groups=mesh['dp'=8,'seq'=4] {'seq'}, use_global_device_ids=true, to_apply=%region_48.49.clone | all-reduce | flops 9216 | bytes 36864
  505.5 46.0 %reduce-scatter.26.cloned.1.call-done = bf16[768,768]{1,0:T(8,128)(2,1)} async-done(((bf16[3072,768]{1,0:T(8,128)(2,1)}), bf16[768,768]{1,0:T(8,128)(2,1)}) %reduce-scatter.26.cloned.1.call-update) | async-done | bytes 1179664 | tf_op jit(solution)/shard_map/reduce_scatter | solution.py:309
  554.5 47.4 %reduce-scatter.22.cloned.1.call-done = bf16[192,3072]{1,0:T(8,128)(2,1)} async-done(((bf16[768,3072]{1,0:T(8,128)(2,1)}), bf16[192,3072]{1,0:T(8,128)(2,1)}) %reduce-scatter.22.cloned.1.call-update) | async-done | bytes 1179664 | tf_op jit(solution)/shard_map/reduce_scatter | solution.py:306
  610.3 56.1 %reduce-scatter.34.cloned.1.call-done = f32[96,3]{1,0:T(8,128)} async-done(((f32[768,3]{1,0:T(8,128)}), f32[96,3]{1,0:T(8,128)}) %reduce-scatter.34.cloned.1.call-update) | async-done | bytes 1168
  667.9 63.2 %reduce-scatter.30.cloned.1.call-done = f32[96,192]{1,0:T(8,128)} async-done(((f32[768,192]{1,0:T(8,128)}), f32[96,192]{1,0:T(8,128)}) %reduce-scatter.30.cloned.1.call-update) | async-done | bytes 73744
  734.2 66.4 %reduce-scatter.28.cloned.1.call-done = f32[96,576]{1,0:T(8,128)} async-done(((f32[768,576]{1,0:T(8,128)}), f32[96,576]{1,0:T(8,128)}) %reduce-scatter.28.cloned.1.call-update) | async-done | bytes 221200
  805.4 66.6 %reduce-scatter.32.cloned.1.call-done = f32[96,768]{1,0:T(8,128)} async-done(((f32[768,768]{1,0:T(8,128)}), f32[96,768]{1,0:T(8,128)}) %reduce-scatter.32.cloned.1.call-update) | async-done | bytes 294928
  875.6 68.4 %reduce-scatter.24.cloned.1.call-done = f32[192,384]{1,0:T(8,128)} async-done(((f32[192,3072]{1,0:T(8,128)}), f32[192,384]{1,0:T(8,128)}) %reduce-scatter.24.cloned.1.call-update) | async-done | bytes 294928 | tf_op jit(solution)/shard_map/reduce_scatter | solution.py:319
  947.6 4.4 convolution_add_fusion.8
  952.0 39.5 %psum.7 = f32[]{:T(128)} all-reduce(f32[]{:T(128)S(6)} %add.350), channel_id=1, replica_groups=mesh['dp'=8,'seq'=4] {'dp','seq'}, use_global_device_ids=true, to_apply=%region_51.52 | all-reduce | flops 1 | bytes 8 | tf_op jit(solution)/shard_map/psum | solution.py:326
  (320 shorter events, 221.4 us)
Async XLA Ops:
  8.8 257.7 %copy-start.28 = (f32[768]{0:T(1024)}, f32[768]{0:T(1024)S(1)}, u32[]{:S(2)}) copy-start(f32[768]{0:T(1024)S(1)} %get-tuple-element.391) | copy-start | bytes 9220
  19.9 27.3 %all-to-all-start = ((bf16[384,3,4,192]{0,3,1,2:T(8,128)(2,1)}), bf16[384,3,4,192]{0,3,1,2:T(8,128)(2,1)}, u32[]{:S(2)}, u32[]{:S(2)}) async-start(bf16[384,3,4,192]{0,3,1,2:T(8,128)(2,1)} %copy.261), calls=%async_computation | async-start | bytes 3538944 | tf_op jit(solution)/shard_map/all_to_all | solution.py:120
  27.0 3.7 copy-start.32
  27.0 3.7 copy-start.45
  47.2 75.4 %all-to-all-start.2 = ((bf16[384,3,4,192]{0,3,1,2:T(8,128)(2,1)}), bf16[384,3,4,192]{0,3,1,2:T(8,128)(2,1)}, u32[]{:S(2)}, u32[]{:S(2)}) async-start(bf16[384,3,4,192]{0,3,1,2:T(8,128)(2,1)} %copy.268), calls=%async_computation.2 | async-start | bytes 3538944 | tf_op jit(solution)/shard_map/all_to_all | solution.py:120
  68.5 2.9 copy-start.18
  79.8 2.9 copy-start.18
  91.0 2.9 copy-start.18
  122.6 74.1 %all-to-all-start.1 = ((bf16[4,2,36864]{2,1,0:T(2,128)(2,1)}), bf16[4,2,36864]{2,1,0:T(2,128)(2,1)}, u32[]{:S(2)}, u32[]{:S(2)}) async-start(bf16[4,2,36864]{2,1,0:T(2,128)(2,1)} %reshape.355), calls=%async_computation.1 | async-start | bytes 1179648 | tf_op jit(solution)/shard_map/all_to_all | solution.py:124
  143.4 2.9 copy-start.5
  154.6 2.9 copy-start.5
  165.9 2.9 copy-start.5
  196.7 33.1 %all-to-all-start.3 = ((bf16[4,2,36864]{2,1,0:T(2,128)(2,1)}), bf16[4,2,36864]{2,1,0:T(2,128)(2,1)}, u32[]{:S(2)}, u32[]{:S(2)}) async-start(bf16[4,2,36864]{2,1,0:T(2,128)(2,1)} %reshape.353), calls=%async_computation.3 | async-start | bytes 1179648 | tf_op jit(solution)/shard_map/all_to_all | solution.py:124
  204.7 8.1 copy-start.40
  241.7 2.8 copy-start.30
  244.2 22.3 %copy-start.11 = (f32[384,768]{1,0:T(8,128)}, f32[384,768]{1,0:T(8,128)S(1)}, u32[]{:S(2)}) copy-start(f32[384,768]{1,0:T(8,128)S(1)} %get-tuple-element.483) | copy-start | bytes 3538948
  244.2 22.3 %copy-start.25 = (f32[384]{0:T(512)}, f32[384]{0:T(512)S(1)}, u32[]{:S(2)}) copy-start(f32[384]{0:T(512)S(1)} %broadcast_multiply_fusion.5) | copy-start | bytes 4612
  244.5 22.0 %copy-start.34 = (f32[384]{0:T(512)}, f32[384]{0:T(512)S(1)}, u32[]{:S(2)}) copy-start(f32[384]{0:T(512)S(1)} %add_rsqrt_fusion.1) | copy-start | bytes 4612
  244.5 4.5 copy-start.39
  244.5 14.4 %slice-start = ((s8[4718592]{0:T(1024)(128)(4,1)}), s8[4194304]{0:T(1024)(128)(4,1)S(1)}, s32[]{:S(2)}) async-start(s8[4718592]{0:T(1024)(128)(4,1)} %bitcast.179), calls=%async_computation.24 | async-start | bytes 8388608
  249.0 5.5 copy-start.48
  249.0 5.8 copy-start.10
  249.0 5.8 copy-start.22
  249.0 5.7 copy-start.24
  249.0 5.7 copy-start.27
  249.1 5.7 copy-start.33
  249.1 9.9 slice-start.1
  255.7 7.8 slice-start.2
  258.9 4.6 copy-start.17
  258.9 4.6 slice-start.3
  263.5 2.9 copy-start.49
  272.1 13.8 %all-to-all-start.4 = ((bf16[384,4,192]{0,2,1:T(8,128)(2,1)}), bf16[384,4,192]{0,2,1:T(8,128)(2,1)}, u32[]{:S(2)}, u32[]{:S(2)}) async-start(bf16[384,4,192]{0,2,1:T(8,128)(2,1)} %bitcast.168), calls=%async_computation.4 | async-start | bytes 1179648 | tf_op jit(solution)/shard_map/all_to_all | solution.py:265
  276.2 224.5 %reduce-scatter.20.cloned.1.call-start = ((), (), s32[]{:S(2)}) async-start(), calls=%async_computation.16 | async-start | bytes 1474560 | tf_op jit(solution)/shard_map/reduce_scatter | solution.py:303
  279.6 223.3 %reduce-scatter.18.cloned.1.call-start = ((), (), s32[]{:S(2)}) async-start(), calls=%async_computation.15 | async-start | bytes 4423680 | tf_op jit(solution)/shard_map/reduce_scatter | solution.py:300
  293.5 11.1 %copy-start.3 = (pred[512,1536]{1,0:T(8,128)(4,1)}, pred[512,1536]{1,0:T(8,128)(4,1)S(1)}, u32[]{:S(2)}) copy-start(pred[512,1536]{1,0:T(8,128)(4,1)S(1)} %broadcast_compare_fusion.8) | copy-start | bytes 2359300 | tf_op jit(solution)/shard_map/while
  297.0 7.7 copy-start.1
  297.0 2.9 copy-start.6
  309.0 9.3 copy-start.2
  313.5 4.8 copy-start.4
  325.6 11.1 %copy-start.3 = (pred[512,1536]{1,0:T(8,128)(4,1)}, pred[512,1536]{1,0:T(8,128)(4,1)S(1)}, u32[]{:S(2)}) copy-start(pred[512,1536]{1,0:T(8,128)(4,1)S(1)} %broadcast_compare_fusion.8) | copy-start | bytes 2359300 | tf_op jit(solution)/shard_map/while
  329.1 7.7 copy-start.1
  329.1 2.9 copy-start.6
  341.1 9.7 copy-start.2
  346.0 4.8 copy-start.4
  358.6 11.1 %copy-start.3 = (pred[512,1536]{1,0:T(8,128)(4,1)}, pred[512,1536]{1,0:T(8,128)(4,1)S(1)}, u32[]{:S(2)}) copy-start(pred[512,1536]{1,0:T(8,128)(4,1)S(1)} %broadcast_compare_fusion.8) | copy-start | bytes 2359300 | tf_op jit(solution)/shard_map/while
  362.1 7.7 copy-start.1
  362.1 2.9 copy-start.6
  374.1 9.7 copy-start.2
  379.0 4.8 copy-start.4
  451.9 3.1 copy-start.46
  458.8 92.7 %reduce-scatter.26.cloned.1.call-start = ((), (), s32[]{:S(2)}) async-start(), calls=%async_computation.19 | async-start | bytes 5898240 | tf_op jit(solution)/shard_map/reduce_scatter | solution.py:309
  465.7 136.2 %reduce-scatter.22.cloned.1.call-start = ((), (), s32[]{:S(2)}) async-start(), calls=%async_computation.17 | async-start | bytes 5898240 | tf_op jit(solution)/shard_map/reduce_scatter | solution.py:306
  473.9 192.5 %reduce-scatter.34.cloned.1.call-start = ((), (), s32[]{:S(2)}) async-start(), calls=%async_computation.23 | async-start | bytes 442368
  500.7 230.4 %reduce-scatter.30.cloned.1.call-start = ((), (), s32[]{:S(2)}) async-start(), calls=%async_computation.21 | async-start | bytes 884736
  502.9 297.8 %reduce-scatter.28.cloned.1.call-start = ((), (), s32[]{:S(2)}) async-start(), calls=%async_computation.20 | async-start | bytes 2211840
  505.4 366.6 %reduce-scatter.32.cloned.1.call-start = ((), (), s32[]{:S(2)}) async-start(), calls=%async_computation.22 | async-start | bytes 2654208
  554.3 389.7 %reduce-scatter.24.cloned.1.call-start = ((), (), s32[]{:S(2)}) async-start(), calls=%async_computation.18 | async-start | bytes 2654208 | tf_op jit(solution)/shard_map/reduce_scatter | solution.py:319
  992.2 9.5 copy-start.42
  992.2 9.5 copy-start.43
  992.2 9.5 copy-start.44
  1001.7 4.8 copy-start.14
  1001.7 4.8 copy-start.19
  1001.7 4.8 copy-start.20
  1001.7 4.8 copy-start.21
  (18 other events, 25.8 us)
Sparse Core Ops, SparseCore 0:
  279.7 28.2 reduce-scatter.19
  458.9 42.0 reduce-scatter.17
  503.6 47.8 reduce-scatter.25
  554.0 47.8 reduce-scatter.21
  605.0 61.3 reduce-scatter.33
  669.6 61.4 reduce-scatter.29
  735.0 65.6 reduce-scatter.27
  804.1 67.8 reduce-scatter.31
  875.5 68.4 reduce-scatter.23
where the time goes:
time: 1020 us
  waiting for transfers between devices  428 us (42%)
  matrix products  174 us (17%)
  local copies, waits for them, and re-layouts  168 us (16%)
  other arithmetic  103 us (10%)
  blocking collectives  94.4 us (9%)
  starting transfers between devices  22 us (2%)
  between operations  20.5 us (2%)
    unnamed x13, waiting for transfers between devices  252 us
    reduce_scatter x1, waiting for transfers between devices, local(): lax.psum_scatter(partial_sums[2], 'dp', scatter_dimension=1, tiled=True)  68.4 us
    unnamed x114, local copies, waits for them, and re-layouts  48.8 us
    reduce_scatter x1, waiting for transfers between devices, local(): lax.psum_scatter(expand_gradient.astype(jnp.bfloat16), 'seq', scatter_dim...  47.4 us
    reduce_scatter x1, waiting for transfers between devices, local(): lax.psum_scatter(reduce_gradient.astype(jnp.bfloat16), 'seq', scatter_dim...  46 us
    all_to_all x1, blocking collectives, local(): lax.all_to_all(grad_stacked, 'seq', split_axis=0, concat_axis=2, tiled=True)  42.2 us
    psum x1, blocking collectives, local(): squares_total = lax.psum(local_squares, ('dp', 'seq'))  39.5 us
    dot_general x9, matrix products, block_weights(): jnp.einsum('qhd,khd->hqk', query_block, key_rows, preferred_element_type=...  29.6 us
  transfers between devices with their start and end apart: 14, of which 9 were waited for; matrix products, arithmetic and copies ran while one was open for 36% of the time, Pallas kernels for 0%

commit v1 on v0

v1 whole, which is shorter than its diff:
```python
import functools

import jax
import jax.numpy as jnp
from jax import lax
from jax.experimental import pallas as pl
from jax.experimental.pallas import tpu as pltpu
from jax.sharding import PartitionSpec as P

HD = 64
STEP = 10
LANES = 128
NORM_EPS = 1e-05
MASK = -float(2**30)
BF = jnp.bfloat16
F32 = jnp.float32
AXES = ("dp", "seq")

GROUPS = (
    (0, 2, 3, 5),
    (1, 4),
)
PLACES = (
    {
        0: ((0, 0, 0), (1, 1, 1), (2, 2, 2)),
        2: ((0, 0, 1), (1, 1, 2), (2, 3, 0)),
        3: ((0, 0, 2), (1, 2, 0), (2, 3, 1)),
        5: ((0, 1, 0), (1, 2, 1), (2, 3, 2)),
    },
    {
        1: ((0, 0, 0), (1, 1, 1), (2, 2, 1), (2, 3, 0)),
        4: ((0, 0, 1), (0, 1, 0), (1, 2, 0), (2, 3, 1)),
    },
)
WIDTHS = (3 * LANES, 2 * LANES)


def params(**more):
    return pltpu.CompilerParams(vmem_limit_bytes=60 * 2**20, **more)


def dot(a, b):
    return lax.dot_general(a, b, (((1,), (0,)), ((), ())), preferred_element_type=F32)


def dot_t(a, b):
    return lax.dot_general(a, b, (((1,), (1,)), ((), ())), preferred_element_type=F32)


def attend_kernel(
    x_ref, xp_ref, wq_ref, wk_ref, wv_ref, vec_ref, kmask_ref, qhot_ref,
    mixed_ref, e_ref, rinv_ref, q_ref, k_ref, v_ref, xt_ref,
):
    rows = q_ref.shape[0]
    xt_ref[...] = xp_ref[...].T
    wkv = jnp.concatenate([wk_ref[...], wv_ref[...]], axis=1)
    kv = dot(x_ref[...], wkv)
    k = kv[:, :LANES].astype(BF)
    v = (kv[:, LANES:] + vec_ref[1:2, :]).astype(BF)
    q = (dot(x_ref[:rows, :], wq_ref[...]) + vec_ref[0:1, :]).astype(BF)
    q = q * jnp.asarray(HD**-0.5, BF)
    q_ref[...] = q
    k_ref[...] = k
    v_ref[...] = v
    keys = jnp.concatenate([k, kmask_ref[...]], axis=1)
    low = lax.broadcasted_iota(jnp.int32, (rows, LANES), 1) < HD
    outs, inverses = [], []
    for head in range(2):
        own = low if head == 0 else jnp.logical_not(low)
        qh = jnp.where(own, q, jnp.zeros_like(q))
        scores = dot_t(jnp.concatenate([qh, qhot_ref[...]], axis=1), keys)
        top = jnp.max(scores, axis=1, keepdims=True)
        e = jnp.exp(scores - top)
        total = jnp.sum(e, axis=1, keepdims=True)
        e_low = e.astype(BF)
        e_ref[head] = e_low
        outs.append(dot(e_low, v))
        inverses.append(1.0 / total)
    rinv = jnp.where(low, inverses[0], inverses[1])
    rinv_ref[...] = rinv
    mixed_ref[...] = (jnp.where(low, outs[0], outs[1]) * rinv).astype(BF)


def attend(x_all, input_weight, vectors, kmask, qhot):
    slab, width = x_all.shape
    rows = qhot.shape[0]
    pairs = width // LANES
    full = lambda a: pl.BlockSpec(a.shape, lambda p: (0,) * a.ndim)
    cols = lambda r, off=0: pl.BlockSpec((r, LANES), lambda p: (0, p + off))
    return pl.pallas_call(
        attend_kernel,
        grid=(pairs,),
        in_specs=[
            full(x_all), cols(slab), cols(width), cols(width, pairs), cols(width, 2 * pairs),
            cols(vectors.shape[0]), full(kmask), full(qhot),
        ],
        out_specs=[
            cols(rows), pl.BlockSpec((2, rows, slab), lambda p: (p, 0, 0)), cols(rows), cols(rows),
            cols(slab), cols(slab), pl.BlockSpec((LANES, slab), lambda p: (p, 0)),
        ],
        out_shape=[
            jax.ShapeDtypeStruct((rows, width), BF),
            jax.ShapeDtypeStruct((2 * pairs, rows, slab), BF),
            jax.ShapeDtypeStruct((rows, width), F32),
            jax.ShapeDtypeStruct((rows, width), BF),
            jax.ShapeDtypeStruct((slab, width), BF),
            jax.ShapeDtypeStruct((slab, width), BF),
            jax.ShapeDtypeStruct((width, slab), BF),
        ],
        compiler_params=params(),
        name="attend",
    )(x_all, x_all, input_weight, input_weight, input_weight, vectors, kmask, qhot)


def spot(d, own_d):
    rel = d ^ own_d
    return (rel & 1) * 4 + (rel >> 1)


def mid_kernel(
    own_ref, mixed_ref, x_ref, cot_ref, qhot_ref, wo_ref, we_ref, wr_ref, vec_ref,
    layer_ref, gf_ref, gm_ref, rs_ref, rk_ref, es_ref, ek_ref, os_ref, ok_ref, vg_ref,
    act, slope, hid, norm1, inv1, hl, hlt, acc, gb, gbt, tmp,
):
    step = pl.program_id(0)
    own_s, own_d = own_ref[0], own_ref[1]
    rows, width = x_ref.shape
    chunks = act.shape[0]
    j = lax.rem(step, chunks)
    rel = jnp.where(j < 2, 2 * j + 1, 2 * (j - 2))
    shard = rel ^ own_s
    row = lambda i: vec_ref[i : i + 1, :]

    @pl.when(step == 0)
    def _():
        z = x_ref[...].astype(F32) + dot(mixed_ref[...], wo_ref[...]) + row(2)
        center = z - jnp.mean(z, axis=1, keepdims=True)
        inverse = lax.rsqrt(jnp.mean(center * center, axis=1, keepdims=True) + NORM_EPS)
        normed = center * inverse
        hidden = normed * row(3) + row(4)
        hid[...] = hidden
        norm1[...] = normed
        inv1[...] = jnp.broadcast_to(inverse, inv1.shape)
        low = hidden.astype(BF)
        hl[...] = low
        hlt[...] = low.T

    @pl.when(step < chunks)
    def _():
        pre = dot(hl[...], we_ref[...]) + vec_ref[pl.ds(8 + shard, 1), :]
        cdf = 0.5 * (1.0 + lax.erf(pre * 0.7071067811865476))
        density = jnp.exp(-0.5 * pre * pre) * 0.3989422804014327
        low = (pre * cdf).astype(BF)
        act[j] = low
        slope[j] = cdf + pre * density
        part = dot(low, wr_ref[...])

        @pl.when(step == 0)
        def _():
            acc[...] = part

        @pl.when(step > 0)
        def _():
            acc[...] += part

    @pl.when(step == chunks - 1)
    def _():
        z = hid[...] + acc[...] + row(5)
        center = z - jnp.mean(z, axis=1, keepdims=True)
        inverse = lax.rsqrt(jnp.mean(center * center, axis=1, keepdims=True) + NORM_EPS)
        normed = center * inverse
        valid = 1.0 - qhot_ref[:, 3:4].astype(F32)
        layer_ref[...] = ((normed * row(6) + row(7)) * valid).astype(BF)
        gy = cot_ref[...].astype(F32) * valid
        vg_ref[6:7, :] = jnp.sum(gy * normed, axis=0, keepdims=True)
        vg_ref[7:8, :] = jnp.sum(gy, axis=0, keepdims=True)
        e = gy * row(6)
        grad = e - jnp.mean(e, axis=1, keepdims=True)
        grad = (grad - normed * jnp.mean(e * normed, axis=1, keepdims=True)) * inverse
        low = grad.astype(BF)
        vg_ref[5:6, :] = jnp.sum(low.astype(F32), axis=0, keepdims=True)
        gb[...] = low
        gbt[...] = low.T
        acc[...] = grad

    @pl.when(step >= chunks)
    def _():
        grad_act = dot_t(gb[...], wr_ref[...])
        low = (grad_act * slope[j]).astype(BF)
        vg_ref[pl.ds(8 + shard, 1), :] = jnp.sum(low.astype(F32), axis=0, keepdims=True)
        acc[...] += dot_t(low, we_ref[...])
        piece = width // 8
        reduce_t = dot(gbt[...], act[j]).astype(BF)
        for ref, ours in ((rs_ref, j < 2), (rk_ref, j >= 2)):

            @pl.when(ours)
            def _():
                for d in range(8):
                    ref[0, spot(d, own_d)] = reduce_t[d * piece : (d + 1) * piece, :]

        grad_e = dot(hlt[...], low).astype(BF)
        tmp[...] = grad_e.reshape(tmp.shape)
        half = grad_e.shape[1] // 2
        for part, ref in ((1, es_ref), (0, ek_ref)):
            for ry in range(2):
                for t in range(2):
                    ref[t ^ (own_d & 1), ry, 0] = tmp[own_s ^ (2 * ry + part), :, t * half : (t + 1) * half]

    @pl.when(step == 2 * chunks - 1)
    def _():
        gy = acc[...]
        normed = norm1[...]
        vg_ref[3:4, :] = jnp.sum(gy * normed, axis=0, keepdims=True)
        vg_ref[4:5, :] = jnp.sum(gy, axis=0, keepdims=True)
        e = gy * row(3)
        grad = e - jnp.mean(e, axis=1, keepdims=True)
        grad = (grad - normed * jnp.mean(e * normed, axis=1, keepdims=True)) * inv1[:, :1]
        gf_ref[...] = grad
        low = grad.astype(BF)
        vg_ref[2:3, :] = jnp.sum(low.astype(F32), axis=0, keepdims=True)
        vg_ref[0:2, :] = jnp.zeros((2, width), F32)
        vg_ref[12:16, :] = jnp.zeros((4, width), F32)
        gm_ref[...] = dot_t(low, wo_ref[...]).astype(BF)
        gat = low.T
        tmp2 = mixed_ref[...].T
        hlt[...] = tmp2
        piece, fourth = width // 8, width // 4
        for ref, part in ((os_ref, 1), (ok_ref, 0)):
            for ry in range(2):
                start = pl.multiple_of((own_s ^ (2 * ry + part)) * fourth, fourth)
                out = dot_t(gat, hlt[pl.ds(start, fourth), :]).astype(BF)
                for d in range(8):
                    ref[ry, spot(d, own_d)] = out[d * piece : (d + 1) * piece, :]


def middle(own, mixed, frames, cotangent, qhot, output_weight, expand_weight, reduce_weight, vectors):
    rows, width = frames.shape
    hidden = expand_weight.shape[1]
    chunks = 4
    cut = hidden // chunks
    piece, fourth, eighth = width // 8, width // 4, hidden // 8

    def shard_of(step, own):
        j = lax.rem(step, chunks)
        return jnp.where(j < 2, 2 * j + 1, 2 * (j - 2)) ^ own[0]

    def deep(step, own):
        return (0, 0, shard_of(jnp.maximum(step, chunks), own) ^ (own[1] >> 1), 0, 0)

    full = lambda shape: pl.BlockSpec(shape, lambda s, own: (0,) * len(shape))
    spread = pl.BlockSpec((2, 2, 1, fourth, eighth), deep)
    return pl.pallas_call(
        mid_kernel,
        grid_spec=pltpu.PrefetchScalarGridSpec(
            num_scalar_prefetch=1,
            grid=(2 * chunks,),
            in_specs=[
                full(mixed.shape), full(frames.shape), full(cotangent.shape), full(qhot.shape),
                full(output_weight.shape),
                pl.BlockSpec((width, cut), lambda s, own: (0, shard_of(s, own))),
                pl.BlockSpec((cut, width), lambda s, own: (shard_of(s, own), 0)),
                full(vectors.shape),
            ],
            out_specs=[
                full((rows, width)), full((rows, width)), full((rows, width)),
                pl.BlockSpec((1, 8, piece, cut), lambda s, own: (jnp.clip(s - chunks, 0, 1), 0, 0, 0)),
                pl.BlockSpec((1, 8, piece, cut), lambda s, own: (jnp.clip(s - chunks - 2, 0, 1), 0, 0, 0)),
                spread, spread,
                full((2, 8, piece, fourth)), full((2, 8, piece, fourth)), full((16, width)),
            ],
            scratch_shapes=[
                pltpu.VMEM((chunks, rows, cut), BF),
                pltpu.VMEM((chunks, rows, cut), F32),
                pltpu.VMEM((rows, width), F32),
                pltpu.VMEM((rows, width), F32),
                pltpu.VMEM((rows, LANES), F32),
                pltpu.VMEM((rows, width), BF),
                pltpu.VMEM((width, rows), BF),
                pltpu.VMEM((rows, width), F32),
                pltpu.VMEM((rows, width), BF),
                pltpu.VMEM((width, rows), BF),
                pltpu.VMEM((4, fourth, cut), BF),
            ],
        ),
        out_shape=[
            jax.ShapeDtypeStruct((rows, width), BF),
            jax.ShapeDtypeStruct((rows, width), F32),
            jax.ShapeDtypeStruct((rows, width), BF),
            jax.ShapeDtypeStruct((2, 8, piece, cut), BF),
            jax.ShapeDtypeStruct((2, 8, piece, cut), BF),
            jax.ShapeDtypeStruct((2, 2, 4, fourth, eighth), BF),
            jax.ShapeDtypeStruct((2, 2, 4, fourth, eighth), BF),
            jax.ShapeDtypeStruct((2, 8, piece, fourth), BF),
            jax.ShapeDtypeStruct((2, 8, piece, fourth), BF),
            jax.ShapeDtypeStruct((16, width), F32),
        ],
        compiler_params=params(),
        name="middle",
    )(own, mixed, frames, cotangent, qhot, output_weight, expand_weight, reduce_weight, vectors)


def back_kernel(group, own_ref, e_ref, q_ref, k_ref, v_ref, gm_ref, mixed_ref, rinv_ref, wq_ref, wk_ref, wv_ref,
                xt_ref, gx_in_ref, *rest):
    first, last = group == 0, group == len(GROUPS) - 1
    rest = list(rest)
    dx_in_ref = None if first else rest.pop(0)
    gs_ref, gk_ref, gx_ref, vb_ref = rest[:4]
    rest = rest[4:]
    dxs_ref = dxk_ref = None
    if last:
        dxs_ref, dxk_ref, gw, dx = rest
    else:
        dx, gw = rest
    i = pl.program_id(0)
    own_s, own_d = own_ref[0], own_ref[1]
    rows = q_ref.shape[0]
    q, k, v = q_ref[...], k_ref[...], v_ref[...]
    rinv = rinv_ref[...]
    gm = gm_ref[...].astype(F32) * rinv
    both = gm * mixed_ref[...].astype(F32)
    gm_low = gm.astype(BF)
    gm_t = gm_low.T
    q_t = q.T
    low = lax.broadcasted_iota(jnp.int32, (rows, LANES), 1) < HD
    dqs, dks, dvs = [], [], []
    for head in range(2):
        own = low if head == 0 else jnp.logical_not(low)
        span = slice(head * HD, (head + 1) * HD)
        e = e_ref[head]
        inner = jnp.sum(jnp.where(own, both, 0.0), axis=1, keepdims=True)
        grad_e = dot_t(jnp.where(own, gm_low, jnp.zeros_like(gm_low)), v)
        ds = (e.astype(F32) * (grad_e - inner)).astype(BF)
        dqs.append(dot(ds, k))
        dks.append(dot(q_t[span, :], ds))
        dvs.append(dot(gm_t[span, :], e))
    dq = (jnp.where(low, dqs[0], dqs[1]) * HD**-0.5).astype(BF)
    dkv_t = jnp.concatenate([*dks, *dvs], axis=0).astype(BF)
    ones = jnp.ones((8, dkv_t.shape[1]), BF)
    vb_ref[0:1, :] = jnp.sum(dq.astype(F32), axis=0, keepdims=True)
    vb_ref[1:2, :] = dot_t(ones, dkv_t[LANES:, :])[0:1, :]

    @pl.when(i == 0)
    def _():
        gx_ref[...] = gx_in_ref[...]
        dx[...] = jnp.zeros_like(dx) if first else dx_in_ref[...]

    gx_ref[...] += dot_t(dq, wq_ref[...])
    dx[...] += dot(jnp.concatenate([wk_ref[...], wv_ref[...]], axis=1), dkv_t)
    grad_q = dot(xt_ref[:, :rows], dq).astype(BF)
    grad_kv = dot_t(xt_ref[...], dkv_t).astype(BF)
    piece = grad_q.shape[0] // 8
    blocks = [b.reshape(8, piece, LANES) for b in (grad_q, grad_kv[:, :LANES], grad_kv[:, LANES:])]
    for n, pair in enumerate(GROUPS[group]):

        @pl.when(i == n)
        def _():
            for which, shard, place in PLACES[group][pair]:
                gw[shard, :, :, place * LANES : (place + 1) * LANES] = blocks[which]

    @pl.when(i == len(GROUPS[group]) - 1)
    def _():
        for ref, part in ((gs_ref, 1), (gk_ref, 0)):
            for ry in range(2):
                for d in range(8):
                    ref[ry, spot(d, own_d)] = gw[own_s ^ (2 * ry + part), d]
        if last:
            for ry in range(2):
                dxk_ref[ry] = dx[:, ry * rows : (ry + 1) * rows]
                dxs_ref[ry] = dx[:, (2 + ry) * rows : (3 + ry) * rows].astype(BF)


def attend_back(group, own, e, q, k, v, grad_mixed, mixed, rinv, input_weight, x_t, gx, dx):
    pairs = GROUPS[group]
    first, last = group == 0, group == len(GROUPS) - 1
    rows, width = q.shape
    slab = k.shape[0]
    count = width // LANES
    piece = width // 8
    span = WIDTHS[group]
    own = jnp.concatenate([own, jnp.array(pairs, jnp.int32)])
    full = lambda shape: pl.BlockSpec(shape, lambda i, own: (0,) * len(shape))
    cols = lambda r, off=0: pl.BlockSpec((r, LANES), lambda i, own: (0, own[2 + i] + off))
    inputs = [e, q, k, v, grad_mixed, mixed, rinv, input_weight, input_weight, input_weight, x_t, gx]
    in_specs = [
        pl.BlockSpec((2, rows, slab), lambda i, own: (own[2 + i], 0, 0)),
        cols(rows), cols(slab), cols(slab), cols(rows), cols(rows), cols(rows),
        cols(width), cols(width, count), cols(width, 2 * count), full(x_t.shape), full(gx.shape),
    ]
    out_shape = [
        jax.ShapeDtypeStruct((2, 8, piece, span), BF),
        jax.ShapeDtypeStruct((2, 8, piece, span), BF),
        jax.ShapeDtypeStruct((rows, width), F32),
        jax.ShapeDtypeStruct((8, len(pairs) * LANES), F32),
    ]
    out_specs = [
        full((2, 8, piece, span)), full((2, 8, piece, span)), full((rows, width)),
        pl.BlockSpec((8, LANES), lambda i, own: (0, i)),
    ]
    scratch = [pltpu.VMEM((4, 8, piece, span), BF)]
    if not first:
        inputs.append(dx)
        in_specs.append(full((width, slab)))
    if last:
        out_shape += [jax.ShapeDtypeStruct((2, width, rows), BF), jax.ShapeDtypeStruct((2, width, rows), F32)]
        out_specs += [full((2, width, rows)), full((2, width, rows))]
        scratch.append(pltpu.VMEM((width, slab), F32))
    else:
        out_shape.append(jax.ShapeDtypeStruct((width, slab), F32))
        out_specs.append(full((width, slab)))
    return pl.pallas_call(
        functools.partial(back_kernel, group),
        grid_spec=pltpu.PrefetchScalarGridSpec(
            num_scalar_prefetch=1, grid=(len(pairs),), in_specs=in_specs, out_specs=out_specs, scratch_shapes=scratch
        ),
        out_shape=out_shape,
        compiler_params=params(),
        name=f"attend_back_{group}",
    )(own, *inputs)


def split_kernel(count, *refs):
    n = len(refs) // (2 + count)
    for a in range(n):
        keep, came = refs[2 * a], refs[2 * a + 1]
        for part in range(count):
            out = refs[2 * n + a * count + part]
            out[...] = (keep[part].astype(F32) + came[part].astype(F32)).astype(out.dtype)


def split_sum(pairs, count, kinds=None):
    kinds = kinds or (BF,) * count
    inputs, in_specs, out_shape, out_specs = [], [], [], []
    steps = 4 if count == 2 else 2
    for keep, came in pairs:
        rows, cols = keep.size // keep.shape[-1] // count, keep.shape[-1]
        for a in (keep, came):
            inputs.append(a.reshape(count, rows, cols))
            in_specs.append(pl.BlockSpec((count, rows // steps, cols), lambda i: (0, i, 0)))
        for kind in kinds:
            out_shape.append(jax.ShapeDtypeStruct((rows, cols), kind))
            out_specs.append(pl.BlockSpec((rows // steps, cols), lambda i: (i, 0)))
    outs = pl.pallas_call(
        functools.partial(split_kernel, count),
        grid=(steps,), in_specs=in_specs, out_specs=out_specs, out_shape=out_shape,
        compiler_params=params(), name="split_sum",
    )(*inputs)
    return [outs[count * a : count * (a + 1)] for a in range(len(pairs))]


def frames_kernel(gx_ref, keep_ref, came_ref, out_ref):
    out_ref[...] = gx_ref[...] + (keep_ref[...] + came_ref[...].astype(F32)).T


def frames_end(gx, keep, came):
    rows, width = gx.shape
    across = pl.BlockSpec((rows, LANES), lambda p: (0, p))
    down = pl.BlockSpec((LANES, rows), lambda p: (p, 0))
    return pl.pallas_call(
        frames_kernel,
        grid=(width // LANES,), in_specs=[across, down, down], out_specs=across,
        out_shape=jax.ShapeDtypeStruct((rows, width), F32), compiler_params=params(), name="frames_end",
    )(gx, keep, came)


def adam_step(master, moment_one, moment_two, gradient, step_rate, decay_weight):
    new_one = 0.9 * moment_one + 0.1 * gradient
    new_two = 0.999 * moment_two + 0.001 * gradient * gradient
    corrected_one = new_one / (1.0 - 0.9**STEP)
    corrected_two = new_two / (1.0 - 0.999**STEP)
    new_master = master - step_rate * (
        corrected_one / (jnp.sqrt(corrected_two) + 1e-08) + decay_weight * master
    )
    return (new_one, new_two, new_master, new_master.astype(BF))


def adam_kernel(rates, turned, squares_ref, *refs):
    n = len(rates)
    ins, outs = refs[: 4 * n], refs[4 * n :]
    norm = jnp.sqrt(squares_ref[0:1, 0:1])
    outs[0][...] = norm
    factor = 1.0 / jnp.maximum(norm, 1.0)
    for a in range(n):
        master, one, two, grad = (r[...] for r in ins[4 * a : 4 * a + 4])
        if turned[a]:
            grad = grad.T
        made = adam_step(master, one, two, grad * factor, rates[a][0], rates[a][1])
        for b in range(4):
            outs[1 + 4 * a + b][...] = made[b]


def adam_all(squares, states, grads, rates, turned):
    inputs, out_shape = [squares], [jax.ShapeDtypeStruct((1, 1), F32)]
    for state, grad in zip(states, grads):
        inputs += [*state, grad]
        shape = state[0].shape
        out_shape += [jax.ShapeDtypeStruct(shape, F32)] * 3 + [jax.ShapeDtypeStruct(shape, BF)]
    vmem = pl.BlockSpec(memory_space=pltpu.VMEM)
    return pl.pallas_call(
        functools.partial(adam_kernel, rates, turned),
        in_specs=[vmem] * len(inputs), out_specs=[vmem] * len(out_shape), out_shape=out_shape,
        compiler_params=params(), name="adam",
    )(*inputs)


def mover(dp, seq):
    def move(value, bits_d, bits_s):
        pairs = [(d * seq + s, (d ^ bits_d) * seq + (s ^ bits_s)) for d in range(dp) for s in range(seq)]
        return lax.ppermute(value, AXES, pairs)

    return move


def tree_sum(move, value):
    value = value + move(value, 0, 1)
    value = (value + move(value, 0, 2)) + (move(value, 1, 0) + move(value, 1, 2))
    return (value + move(value, 2, 0)) + (move(value, 4, 0) + move(value, 6, 0))


def scatter_fast(move, kept, sent, x_first):
    came = move(sent, 0, 1)
    (keep, send), = split_sum([(kept, came)], 2)
    steps = ((1, 0), (0, 2)) if x_first else ((0, 2), (1, 0))
    came = move(send, *steps[0])
    (keep, send), = split_sum([(keep, came)], 2)
    came = move(send, *steps[1])
    parts, = split_sum([(keep, came)], 4)
    return [parts[0], *(move(parts[b], 2 * b, 0) for b in (1, 2, 3))]


def scatter_plain(kept, sent, x_first):
    if x_first:
        parts = jnp.stack([kept, sent], axis=2).transpose(1, 2, 4, 3, 0, 5)
        parts = parts.reshape(4, parts.shape[2], -1)
    else:
        parts = jnp.stack([kept, sent], axis=1)
        rows, cols = parts.shape[-2:]
        parts = parts.reshape(4, 2, 4, rows, cols).swapaxes(1, 2).reshape(4, 8 * rows, cols)
    part = lax.psum_scatter(parts, "seq", scatter_dimension=0, tiled=True)[0].astype(F32)
    return lax.psum_scatter(part, "dp", scatter_dimension=1 if x_first else 0, tiled=True)


def local(
    frames, cotangent, lengths,
    input_weight, output_weight, expand_weight, reduce_weight, vector_copy,
    *states,
):
    rows, width = frames.shape
    seq, dp = lax.axis_size("seq"), lax.axis_size("dp")
    slab = rows * seq
    move = mover(dp, seq)
    own_s, own_d = lax.axis_index("seq"), lax.axis_index("dp")
    fast = dp == 8
    vectors = vector_copy.astype(F32)

    across = move(frames, 0, 2)
    near = move(frames, 0, 1)
    far = move(across, 0, 1)
    x_all = jnp.concatenate([frames, across, near, far], axis=0)

    first_end = lengths[0, 0]
    second_end = first_end + lengths[0, 1]
    third_end = second_end + lengths[0, 2]
    order = jnp.array([0, 2, 1, 3], jnp.int32) ^ own_s
    positions = (order[:, None] * rows + jnp.arange(rows, dtype=jnp.int32)[None, :]).reshape(slab, 1)
    segments = sum((positions >= end).astype(jnp.int32) for end in (first_end, second_end, third_end))
    lanes = jnp.arange(LANES, dtype=jnp.int32)[None, :]
    kmask = jnp.where((segments == lanes) | (lanes > 3), 0.0, MASK).astype(BF)
    qhot = (segments[:rows] == lanes).astype(BF)

    mixed, e, rinv, q, k, v, x_t = attend(x_all, input_weight, vectors, kmask, qhot)
    if fast:
        own = jnp.stack([own_s, own_d]).astype(jnp.int32)
    else:
        own = jnp.zeros((2,), jnp.int32)
    layer, gf, grad_mixed, red_s, red_k, exp_s, exp_k, out_s, out_k, vec_grad = middle(
        own, mixed, frames, cotangent, qhot, output_weight, expand_weight, reduce_weight, vectors
    )
    in_s1, in_k1, gx, vb1, dx = attend_back(
        0, own, e, q, k, v, grad_mixed, mixed, rinv, input_weight, x_t, gf, None
    )
    in_s2, in_k2, gx, vb2, dx_s, dx_k = attend_back(
        1, own, e, q, k, v, grad_mixed, mixed, rinv, input_weight, x_t, gx, dx
    )
    came = move(dx_s, 0, 1)
    (dx_keep, dx_send), = split_sum([(dx_k, came)], 2, (F32, BF))
    frames_gradient = frames_end(gx, dx_keep, move(dx_send, 0, 2))

    vb = jnp.concatenate([vb1, vb2], axis=1)[:2].reshape(2, -1, LANES)
    where = [(*GROUPS[0], *GROUPS[1]).index(p) for p in range(width // LANES)]
    vb = jnp.stack([vb[:, p] for p in where], axis=1).reshape(2, width)
    vec_grad = jnp.concatenate([vb, vec_grad[2:12]], axis=0)

    scattered = (
        (red_k, red_s, False), (exp_k, exp_s, True), (out_k, out_s, False), (in_k1, in_s1, False), (in_k2, in_s2, False)
    )
    if fast:
        totals = []
        for entry in scattered:
            parts = [p.astype(F32) for p in scatter_fast(move, *entry)]
            totals.append((parts[0] + parts[1]) + (parts[2] + parts[3]))
        vec_all = tree_sum(move, vec_grad)
        shape = (vec_grad.shape[0] // seq, width // dp)
        vec = lax.dynamic_slice(vec_all, (own_s * shape[0], own_d * shape[1]), shape)
    else:
        totals = [scatter_plain(*entry) for entry in scattered]
        vec = lax.psum_scatter(vec_grad, "seq", scatter_dimension=0, tiled=True)
        vec = lax.psum_scatter(vec, "dp", scatter_dimension=1, tiled=True)
    red, exp, out, in1, in2 = totals
    odd = own_s % 2 == 1
    even_cols = jnp.concatenate([in1[:, :128], in2[:, :128], in1[:, 128:], in2[:, 128:192]], axis=1)
    odd_cols = jnp.concatenate([in2[:, 64:128], in1[:, :256], in2[:, 128:], in1[:, 256:]], axis=1)
    inp = jnp.where(odd, odd_cols, even_cols)
    grads = [inp, out, exp, red, vec]
    squares = sum(jnp.sum(g * g) for g in grads)
    squares = jnp.full((8, LANES), squares, F32)
    squares = tree_sum(move, squares) if fast else lax.psum(squares, AXES)
    masters, firsts, seconds = states[:5], states[5:10], states[10:]
    hidden = expand_weight.shape[1]
    wide, narrow = 2.0 * width**-0.5, 2.0 * hidden**-0.5
    made = adam_all(
        squares, list(zip(masters, firsts, seconds)), grads,
        ((wide, 0.01), (wide, 0.01), (wide, 0.01), (narrow, 0.01), (0.5, 0.0)),
        (False, True, False, True, False),
    )
    return (layer, frames_gradient, made[0].reshape(()), *made[1:])


def solution(mesh):
    tokens, whole = P(("dp", "seq"), None), P()
    state = (P("dp", "seq"), *(P("seq", "dp"),) * 4)
    outs = tuple(s for s in state for _ in range(4))
    return jax.shard_map(
        local,
        mesh=mesh,
        in_specs=(tokens, tokens, P("dp", None), *(whole,) * 5, *state * 3),
        out_specs=(tokens, tokens, whole, *outs),
        check_vma=False,
    )
```

time: 1020 us -> 331 us (0.32)
  waiting for transfers between devices: 428 us -> 71.3 us
  matrix products: 174 us -> 0 us
  Pallas kernels: 0 us -> 161 us
  local copies, waits for them, and re-layouts: 168 us -> 19.5 us
  blocking collectives: 94.4 us -> 0 us
  other arithmetic: 103 us -> 20.5 us
  starting transfers between devices: 22 us -> 49.8 us
  between operations: 20.5 us -> 6.25 us
    unnamed x13 -> x0, waiting for transfers between devices: 252 us -> none
    dot_general x42 -> x0, matrix products: 174 us -> none  [the longest x9 29.6 us: block_weights(): jnp.einsum('qhd,khd->hqk', query_block, key_rows, preferred_element_type=...]
    reduce_scatter x5 -> x0, waiting for transfers between devices: 162 us -> none  [the longest x1 68.4 us: local(): lax.psum_scatter(partial_sums[2], 'dp', scatter_dimension=1, tiled=True)]
    pallas_call x0 -> x22, Pallas kernels: none -> 161 us  [the longest x16 49.6 us: split_sum(): pl.pallas_call(functools.partial(split_kernel, count), grid=(steps,), in_...]
    ppermute x0 -> x49, waiting for transfers between devices: none -> 71.3 us  [move(): return lax.ppermute(value, AXES, pairs)]
    ppermute x0 -> x49, starting transfers between devices: none -> 49.8 us  [move(): return lax.ppermute(value, AXES, pairs)]
    convert_element_type x16 -> x3, other arithmetic: 50.2 us -> 3.14 us  [the longest x1 1.36 us: local(): vectors = vector_copy.astype(F32)]
    all_to_all x1 -> x0, blocking collectives: 42.2 us -> none  [local(): lax.all_to_all(grad_stacked, 'seq', split_axis=0, concat_axis=2, tiled=True)]
  transfers between devices with their start and end apart: 14 -> 49, of which waited for: 9 -> 21; matrix products, arithmetic and copies ran while one was open for 36% -> 7% of each run, Pallas kernels for 0% -> 30%
where the time goes in v1:
time: 331 us; the launch traced here: 329 us
  Pallas kernels  161 us (49%)
  waiting for transfers between devices  71.3 us (22%)
  starting transfers between devices  49.8 us (15%)
  other arithmetic  20.5 us (6%)
  local copies, waits for them, and re-layouts  19.5 us (6%)
  between operations  6.25 us (2%)
    ppermute x49, waiting for transfers between devices, move(): return lax.ppermute(value, AXES, pairs)  71.3 us
    ppermute x49, starting transfers between devices, move(): return lax.ppermute(value, AXES, pairs)  49.8 us
    pallas_call x16, Pallas kernels, split_sum(): pl.pallas_call(functools.partial(split_kernel, count), grid=(steps,), in_...  49.6 us
    pallas_call x2, Pallas kernels, attend_back(): pl.pallas_call(functools.partial(back_kernel, group), grid_spec=pltpu.Pre...  42.7 us
    pallas_call x1, Pallas kernels, middle(): pl.pallas_call(mid_kernel, grid_spec=pltpu.PrefetchScalarGridSpec(num_sca...  30.6 us
    pallas_call x1, Pallas kernels, attend(): pl.pallas_call(attend_kernel, grid=(pairs,), in_specs=[full(x_all), cols(...  28.8 us
    unnamed x60, local copies, waits for them, and re-layouts  17.1 us
    reduce_sum x5, other arithmetic, local(): squares = sum((jnp.sum(g * g) for g in grads))  10.2 us
  transfers between devices with their start and end apart: 49, of which 21 were waited for; matrix products, arithmetic and copies ran while one was open for 7% of the time, Pallas kernels for 30%

profile of v1, /device:TPU:0, one launch (start us, length us, event | category | flops | bytes accessed | tf_op | source)
XLA Modules:
  0.0 328.9 jit_solution(6492317500109138046)
XLA Ops:
  1.2 2.6 collective-permute-start
  9.2 8.7 %collective-permute-done = bf16[384,768]{1,0:T(8,128)(2,1)S(1)} collective-permute-done((bf16[384,768]{1,0:T(8,128)(2,1)}, bf16[384,768]{1,0:T(8,128)(2,1)S(1)}, u32[]{:S(2)}, u32[]{:S(2)}) %collective-permute-start) | collective-permute-done | bytes 589856 | tf_op jit(solution)/shard_map/ppermute | solution.py:508
  20.9 2.6 pad_maximum_fusion.x_ref.xp_ref
  23.5 28.8 %attend.1 = (bf16[384,768]{1,0:T(8,128)(2,1)}, bf16[12,384,1536]{2,1,0:T(8,128)(2,1)}, f32[384,768]{1,0:T(8,128)}, bf16[384,768]{1,0:T(8,128)(2,1)}, bf16[1536,7...) custom-call(bf16[1536,768]{1,0:T(8,128)(2,1)} %pad_maximum_fusion.x_ref.xp_ref, ...), custom_call_target="tpu_custom_call" | custom-call | tf_op jit(solution)/shard_map/attend/pallas_call | solution.py:90
  52.3 30.6 %middle.1 = (bf16[384,768]{1,0:T(8,128)(2,1)}, f32[384,768]{1,0:T(8,128)}, bf16[384,768]{1,0:T(8,128)(2,1)}, bf16[2,8,96,768]{3,2,1,0:T(8,128)(2,1)}, bf16[2,8,9...) custom-call(s32[2]{0:T(128)} %pad_add_fusion.own_ref, ...), custom_call_target="tpu_custom_call" | custom-call | tf_op jit(solution)/shard_map/middle/pallas_call | solution.py:252
  85.5 25.2 %attend_back_0.1 = (bf16[2,8,96,384]{3,2,1,0:T(8,128)(2,1)}, bf16[2,8,96,384]{3,2,1,0:T(8,128)(2,1)}, f32[384,768]{1,0:T(8,128)}, f32[8,512]{1,0:T(8,128)}, f32[768,1536]{1,0:T(8,128)}) custom-call(s32[6]{0:T(128)} %pad_add_fusion.2.own_ref, bf16[12,384,1536]{2,1,0:T(8,128)(2,1)} %get-tuple-element.116.e_ref, bf16[384,768]{1,0:T(8,128)(2,1)} %get-tuple-element.117.q_ref, ...), custom_call_target="tpu_custom_call" | custom-call | tf_op jit(solution)/shard_map/attend_back_0/pallas_call | solution.py:410
  110.8 17.5 %attend_back_1.1 = (bf16[2,8,96,256]{3,2,1,0:T(8,128)(2,1)}, bf16[2,8,96,256]{3,2,1,0:T(8,128)(2,1)}, f32[384,768]{1,0:T(8,128)}, f32[8,256]{1,0:T(8,128)}, bf16...) custom-call(s32[4]{0:T(128)} %pad_add_fusion.1.own_ref, bf16[12,384,1536]{2,1,0:T(8,128)(2,1)} %get-tuple-element.116.e_ref, ...), custom_call_target="tpu_custom_call" | custom-call | tf_op jit(solution)/shard_map/attend_back_1/pallas_call | solution.py:410
  130.5 2.8 collective-permute-start.38
  134.1 1.5 collective-permute-done.38
  135.6 1.8 collective-permute-done.37
  138.0 3.7 %collective-permute-start.41 = (f32[12,768]{1,0:T(8,128)S(1)}, f32[12,768]{1,0:T(8,128)S(1)}, u32[]{:S(2)}, u32[]{:S(2)}) collective-permute-start(f32[12,768]{1,0:T(8,128)S(1)} %add_add_fusion.5), channel_id=1, source_target_pairs={{0,24},{1,25},{2,26},{3,27},{4,28},{5,29},{6,30},{7,31},{8,16},{9,... | collective-permute-start | bytes 110600 | tf_op jit(solution)/shard_map/ppermute | solution.py:508
  141.6 2.3 collective-permute-done.41
  143.9 2.7 collective-permute-done.40
  146.6 4.1 %collective-permute-done.39 = f32[12,768]{1,0:T(8,128)S(1)} collective-permute-done((f32[12,768]{1,0:T(8,128)S(1)}, f32[12,768]{1,0:T(8,128)S(1)}, u32[]{:S(2)}, u32[]{:S(2)}) %collective-permute-start.39) | collective-permute-done | bytes 36896 | tf_op jit(solution)/shard_map/ppermute | solution.py:508
  151.3 2.3 collective-permute-done.17
  154.6 3.5 %split_sum.23 = (bf16[768,192]{1,0:T(8,128)(2,1)}, bf16[768,192]{1,0:T(8,128)(2,1)}) custom-call(bf16[2,768,192]{2,1,0:T(8,128)(2,1)} %bitcast.47, bf16[2,768,192]{2,1,0:T(8,128)(2,1)} %bitcast.49), custom_call_target="tpu_custom_call" | custom-call | tf_op jit(solution)/shard_map/split_sum/pallas_call | solution.py:442
  158.7 3.5 %split_sum.17 = (bf16[768,256]{1,0:T(8,128)(2,1)}, bf16[768,256]{1,0:T(8,128)(2,1)}) custom-call(bf16[2,768,256]{2,1,0:T(8,128)(2,1)} %bitcast.48, bf16[2,768,256]{2,1,0:T(8,128)(2,1)} %bitcast.6.refs_1_), custom_call_target="tpu_custom_call" | custom-call | tf_op jit(solution)/shard_map/split_sum/pallas_call | solution.py:442
  162.2 7.6 %collective-permute-done.18 = bf16[768,192]{1,0:T(8,128)(2,1)S(1)} collective-permute-done((bf16[768,192]{1,0:T(8,128)(2,1)}, bf16[768,192]{1,0:T(8,128)(2,1)S(1)}, u32[]{:S(2)}, u32[]{:S(2)}) %collective-permute-start.18) | collective-permute-done | bytes 294944 | tf_op jit(solution)/shard_map/ppermute | solution.py:508
  171.0 3.2 split_sum.24
  174.2 1.5 collective-permute-start.19
  175.8 3.6 %split_sum.20 = (bf16[768,384]{1,0:T(8,128)(2,1)}, bf16[768,384]{1,0:T(8,128)(2,1)}) custom-call(bf16[2,768,384]{2,1,0:T(8,128)(2,1)} %bitcast.46, bf16[2,768,384]{2,1,0:T(8,128)(2,1)} %bitcast.12.refs_1_), custom_call_target="tpu_custom_call" | custom-call | tf_op jit(solution)/shard_map/split_sum/pallas_call | solution.py:442
  179.4 1.6 collective-permute-start.12
  181.0 4.3 %split_sum.26 = (bf16[1536,384]{1,0:T(8,128)(2,1)}, bf16[1536,384]{1,0:T(8,128)(2,1)}) custom-call(bf16[2,1536,384]{2,1,0:T(8,128)(2,1)} %bitcast.42, bf16[2,1536,384]{2,1,0:T(8,128)(2,1)} %bitcast.24.refs_1_), custom_call_target="tpu_custom_call" | custom-call | tf_op jit(solution)/shard_map/split_sum/pallas_call | solution.py:442
  185.9 1.7 split_sum.25
  188.3 3.2 split_sum.18
  191.9 1.5 collective-permute-start.7
  194.8 4.4 %split_sum.29 = (bf16[768,768]{1,0:T(8,128)(2,1)}, bf16[768,768]{1,0:T(8,128)(2,1)}) custom-call(bf16[2,768,768]{2,1,0:T(8,128)(2,1)} %bitcast.40, bf16[2,768,768]{2,1,0:T(8,128)(2,1)} %bitcast.41), custom_call_target="tpu_custom_call" | custom-call | tf_op jit(solution)/shard_map/split_sum/pallas_call | solution.py:442
  200.3 16.1 %collective-permute-done.7 = bf16[384,256]{1,0:T(8,128)(2,1)} collective-permute-done((bf16[384,256]{1,0:T(8,128)(2,1)}, bf16[384,256]{1,0:T(8,128)(2,1)}, u32[]{:S(2)}, u32[]{:S(2)}) %collective-permute-start.7) | collective-permute-done | bytes 196640 | tf_op jit(solution)/shard_map/ppermute | solution.py:508
  216.5 1.5 collective-permute-start.22
  218.0 2.0 multiply_reduce_fusion.4
  220.0 1.7 split_sum.19
  222.6 2.1 collective-permute-start.9
  224.7 2.3 collective-permute-start.10
  227.0 2.1 multiply_reduce_fusion.3
  229.1 4.0 %split_sum.16 = (f32[768,384]{1,0:T(8,128)}, bf16[768,384]{1,0:T(8,128)(2,1)}) custom-call(f32[2,768,384]{2,1,0:T(8,128)} %get-tuple-element.127.refs_0_, bf16[2,768,384]{2,1,0:T(8,128)(2,1)} %copy-done.1), custom_call_target="tpu_custom_call" | custom-call | tf_op jit(solution)/shard_map/split_sum/pallas_call | solution.py:442
  233.2 3.4 %split_sum.21 = (bf16[384,384]{1,0:T(8,128)(2,1)}, bf16[384,384]{1,0:T(8,128)(2,1)}) custom-call(bf16[2,384,384]{2,1,0:T(8,128)(2,1)} %bitcast.50, bf16[2,384,384]{2,1,0:T(8,128)(2,1)} %bitcast.14.refs_1_), custom_call_target="tpu_custom_call" | custom-call | tf_op jit(solution)/shard_map/split_sum/pallas_call | solution.py:442
  237.2 6.3 %collective-permute-done.13 = bf16[384,384]{1,0:T(8,128)(2,1)S(1)} collective-permute-done((bf16[384,384]{1,0:T(8,128)(2,1)}, bf16[384,384]{1,0:T(8,128)(2,1)S(1)}, u32[]{:S(2)}, u32[]{:S(2)}) %collective-permute-start.13) | collective-permute-done | bytes 294944 | tf_op jit(solution)/shard_map/ppermute | solution.py:508
  244.3 1.8 split_sum.22
  246.1 2.1 collective-permute-start.15
  248.2 2.3 collective-permute-start.16
  250.5 3.7 %split_sum.27 = (bf16[768,384]{1,0:T(8,128)(2,1)}, bf16[768,384]{1,0:T(8,128)(2,1)}) custom-call(bf16[2,768,384]{2,1,0:T(8,128)(2,1)} %bitcast.43, bf16[2,768,384]{2,1,0:T(8,128)(2,1)} %bitcast.26.refs_1_), custom_call_target="tpu_custom_call" | custom-call | tf_op jit(solution)/shard_map/split_sum/pallas_call | solution.py:442
  254.8 1.6 collective-permute-start.4
  256.4 3.6 %split_sum.30 = (bf16[384,768]{1,0:T(8,128)(2,1)}, bf16[384,768]{1,0:T(8,128)(2,1)}) custom-call(bf16[2,384,768]{2,1,0:T(8,128)(2,1)} %bitcast.44, bf16[2,384,768]{2,1,0:T(8,128)(2,1)} %bitcast.45), custom_call_target="tpu_custom_call" | custom-call | tf_op jit(solution)/shard_map/split_sum/pallas_call | solution.py:442
  260.7 9.2 %collective-permute-done.25 = bf16[768,384]{1,0:T(8,128)(2,1)S(1)} collective-permute-done((bf16[768,384]{1,0:T(8,128)(2,1)}, bf16[768,384]{1,0:T(8,128)(2,1)S(1)}, u32[]{:S(2)}, u32[]{:S(2)}) %collective-permute-start.25) | collective-permute-done | bytes 589856 | tf_op jit(solution)/shard_map/ppermute | solution.py:508
  270.7 2.0 split_sum.28
  272.8 2.8 collective-permute-start.27
  275.6 1.5 collective-permute-start.28
  277.2 1.4 multiply_reduce_fusion.2
  280.8 2.0 split_sum.31
  282.8 2.8 collective-permute-start.33
  285.6 1.5 collective-permute-start.34
  287.2 2.3 multiply_reduce_fusion.1
  290.7 2.1 collective-permute-done.34
  292.9 2.3 multiply_reduce_fusion
  298.2 1.4 collective-permute-start.45
  299.7 1.6 collective-permute-start.43
  303.3 1.7 collective-permute-start.48
  305.0 1.5 collective-permute-start.47
  311.3 5.2 %frames_end.1 = f32[384,768]{1,0:T(8,128)} custom-call(f32[384,768]{1,0:T(8,128)} %get-tuple-element.126.gx_ref, f32[768,384]{1,0:T(8,128)} %get-tuple-element.129.keep_ref, bf16[768,384]{1,0:T(8,128)(2,1)} %copy-done.6), custom_call_target="tpu_custom_call" | custom-call | tf_op jit(solution)/shard_map/frames_end/pallas_call | solution.py:458
  317.1 4.5 %adam.1 = (f32[1,1]{1,0:T(1,128)}, f32[96,576]{1,0:T(8,128)}, f32[96,576]{1,0:T(8,128)}, f32[96,576]{1,0:T(8,128)}, bf16[96,576]{1,0:T(8,128)(2,1)}, /*index=5*/...) custom-call(f32[8,128]{1,0:T(8,128)} %add_add_fusion.6.squares_ref, ...), custom_call_target="tpu_custom_call" | custom-call | tf_op jit(solution)/shard_map/adam/pallas_call | solution.py:498
  321.5 1.7 copy.62
  323.3 1.9 copy.59
  325.1 1.9 copy.60
  327.0 1.9 copy.61
  (153 shorter events, 35.9 us)
Async XLA Ops:
  0.7 20.2 %collective-permute-start.1 = (bf16[384,768]{1,0:T(8,128)(2,1)}, bf16[384,768]{1,0:T(8,128)(2,1)S(1)}, u32[]{:S(2)}, u32[]{:S(2)}) collective-permute-start(bf16[384,768]{1,0:T(8,128)(2,1)} %x_ref.1), channel_id=1, source_target_pairs={{0,1},{1,0},{2,3},{3,2},{4,5},{5,4},{6,7},{7,6},{8,9},{9,8},{10,11... | collective-permute-start | bytes 1769480 | tf_op jit(solution)/shard_map/ppermute | solution.py:508
  1.2 16.7 %collective-permute-start = (bf16[384,768]{1,0:T(8,128)(2,1)}, bf16[384,768]{1,0:T(8,128)(2,1)S(1)}, u32[]{:S(2)}, u32[]{:S(2)}) collective-permute-start(bf16[384,768]{1,0:T(8,128)(2,1)} %x_ref.1), channel_id=1, source_target_pairs={{0,2},{1,3},{2,0},{3,1},{4,6},{5,7},{6,4},{7,5},{8,10},{9,11},{10,... | collective-permute-start | bytes 1769480 | tf_op jit(solution)/shard_map/ppermute | solution.py:508
  17.9 3.0 collective-permute-start.2
  52.3 31.2 %copy-start.20 = (s32[4]{0:T(128)S(1)}, s32[4]{0:T(128)}, u32[]{:S(2)}) copy-start(s32[4]{0:T(128)} %constant.46.clone) | copy-start | bytes 52
  52.3 31.8 %copy-start.19 = (s32[2]{0:T(128)S(1)}, s32[2]{0:T(128)}, u32[]{:S(2)}) copy-start(s32[2]{0:T(128)} %constant.47.clone) | copy-start | bytes 28
  83.0 96.5 %collective-permute-start.23 = (bf16[2,2,4,192,384]{4,3,2,1,0:T(8,128)(2,1)}, bf16[2,2,4,192,384]{4,3,2,1,0:T(8,128)(2,1)}, u32[]{:S(2)}, u32[]{:S(2)}) collective-permute-start(bf16[2,2,4,192,384]{4,3,2,1,0:T(8,128)(2,1)} %get-tuple-element.162), channel_id=1, source_target_pairs={{0,1},{1,0},{2,3},{3,2},{4,5},{5,4},{6,7},{7,6},{8,9},{9,8},{10,11... | collective-permute-start | bytes 7077896 | tf_op jit(solution)/shard_map/ppermute | solution.py:508
  85.5 107.9 %collective-permute-start.29 = (bf16[2,8,96,768]{3,2,1,0:T(8,128)(2,1)}, bf16[2,8,96,768]{3,2,1,0:T(8,128)(2,1)S(1)}, u32[]{:S(2)}, u32[]{:S(2)}) collective-permute-start(bf16[2,8,96,768]{3,2,1,0:T(8,128)(2,1)} %get-tuple-element.172), channel_id=1, source_target_pairs={{0,1},{1,0},{2,3},{3,2},{4,5},{5,4},{6,7},{7,6},{8,9},{9,8},{10,11... | collective-permute-start | bytes 7077896 | tf_op jit(solution)/shard_map/ppermute | solution.py:508
  110.8 17.5 %copy-start.18 = (f32[8,512]{1,0:T(8,128)S(1)}, f32[8,512]{1,0:T(8,128)}, u32[]{:S(2)}) copy-start(f32[8,512]{1,0:T(8,128)} %get-tuple-element.181) | copy-start | bytes 49156
  110.8 40.6 %copy-start.24 = (bf16[2,8,96,192]{3,2,1,0:T(8,128)(2,1)S(1)}, bf16[2,8,96,192]{3,2,1,0:T(8,128)(2,1)}, u32[]{:S(2)}) copy-start(bf16[2,8,96,192]{3,2,1,0:T(8,128)(2,1)} %get-tuple-element.152) | copy-start | bytes 1769476
  129.1 1.4 collective-permute-start.35
  130.5 5.1 %collective-permute-start.38 = (f32[12,768]{1,0:T(8,128)S(1)}, f32[12,768]{1,0:T(8,128)S(1)}, u32[]{:S(2)}, u32[]{:S(2)}) collective-permute-start(f32[12,768]{1,0:T(8,128)S(1)} %fusion.13), channel_id=1, source_target_pairs={{0,6},{1,7},{2,4},{3,5},{4,2},{5,3},{6,0},{7,1},{8,14},{9,15},{10,... | collective-permute-start | bytes 110600 | tf_op jit(solution)/shard_map/ppermute | solution.py:508
  133.3 4.1 %collective-permute-start.37 = (f32[12,768]{1,0:T(8,128)S(1)}, f32[12,768]{1,0:T(8,128)S(1)}, u32[]{:S(2)}, u32[]{:S(2)}) collective-permute-start(f32[12,768]{1,0:T(8,128)S(1)} %fusion.13), channel_id=1, source_target_pairs={{0,4},{1,5},{2,6},{3,7},{4,0},{5,1},{6,2},{7,3},{8,12},{9,13},{10,... | collective-permute-start | bytes 110600 | tf_op jit(solution)/shard_map/ppermute | solution.py:508
  133.8 4.1 %collective-permute-start.36 = (f32[12,768]{1,0:T(8,128)S(1)}, f32[12,768]{1,0:T(8,128)S(1)}, u32[]{:S(2)}, u32[]{:S(2)}) collective-permute-start(f32[12,768]{1,0:T(8,128)S(1)} %fusion.13), channel_id=1, source_target_pairs={{0,2},{1,3},{2,0},{3,1},{4,6},{5,7},{6,4},{7,5},{8,10},{9,11},{10,... | collective-permute-start | bytes 110600 | tf_op jit(solution)/shard_map/ppermute | solution.py:508
  137.9 16.6 %copy-start.14 = (f32[12,768]{1,0:T(8,128)}, f32[12,768]{1,0:T(8,128)S(1)}, u32[]{:S(2)}) copy-start(f32[12,768]{1,0:T(8,128)S(1)} %add_add_fusion.5) | copy-start | bytes 110596
  138.0 6.0 %collective-permute-start.41 = (f32[12,768]{1,0:T(8,128)S(1)}, f32[12,768]{1,0:T(8,128)S(1)}, u32[]{:S(2)}, u32[]{:S(2)}) collective-permute-start(f32[12,768]{1,0:T(8,128)S(1)} %add_add_fusion.5), channel_id=1, source_target_pairs={{0,24},{1,25},{2,26},{3,27},{4,28},{5,29},{6,30},{7,31},{8,16},{9,... | collective-permute-start | bytes 110600 | tf_op jit(solution)/shard_map/ppermute | solution.py:508
  141.6 5.0 %collective-permute-start.40 = (f32[12,768]{1,0:T(8,128)S(1)}, f32[12,768]{1,0:T(8,128)S(1)}, u32[]{:S(2)}, u32[]{:S(2)}) collective-permute-start(f32[12,768]{1,0:T(8,128)S(1)} %add_add_fusion.5), channel_id=1, source_target_pairs={{0,16},{1,17},{2,18},{3,19},{4,20},{5,21},{6,22},{7,23},{8,24},{9,... | collective-permute-start | bytes 110600 | tf_op jit(solution)/shard_map/ppermute | solution.py:508
  141.6 16.5 %collective-permute-start.5 = (bf16[2,8,96,256]{3,2,1,0:T(8,128)(2,1)}, bf16[2,8,96,256]{3,2,1,0:T(8,128)(2,1)}, u32[]{:S(2)}, u32[]{:S(2)}) collective-permute-start(bf16[2,8,96,256]{3,2,1,0:T(8,128)(2,1)} %get-tuple-element.132), channel_id=1, source_target_pairs={{0,1},{1,0},{2,3},{3,2},{4,5},{5,4},{6,7},{7,6},{8,9},{9,8},{10,11... | collective-permute-start | bytes 2359304 | tf_op jit(solution)/shard_map/ppermute | solution.py:508
  143.9 6.8 %copy-start.21 = (f32[12,768]{1,0:T(8,128)}, f32[12,768]{1,0:T(8,128)S(1)}, u32[]{:S(2)}) copy-start(f32[12,768]{1,0:T(8,128)S(1)} %collective-permute-done.41) | copy-start | bytes 110596
  143.9 30.3 %collective-permute-start.11 = (bf16[2,8,96,384]{3,2,1,0:T(8,128)(2,1)}, bf16[2,8,96,384]{3,2,1,0:T(8,128)(2,1)}, u32[]{:S(2)}, u32[]{:S(2)}) collective-permute-start(bf16[2,8,96,384]{3,2,1,0:T(8,128)(2,1)} %get-tuple-element.142), channel_id=1, source_target_pairs={{0,1},{1,0},{2,3},{3,2},{4,5},{5,4},{6,7},{7,6},{8,9},{9,8},{10,11... | collective-permute-start | bytes 3538952 | tf_op jit(solution)/shard_map/ppermute | solution.py:508
  146.6 4.1 %copy-start.22 = (f32[12,768]{1,0:T(8,128)}, f32[12,768]{1,0:T(8,128)S(1)}, u32[]{:S(2)}) copy-start(f32[12,768]{1,0:T(8,128)S(1)} %collective-permute-done.40) | copy-start | bytes 110596
  146.6 4.1 %collective-permute-start.39 = (f32[12,768]{1,0:T(8,128)S(1)}, f32[12,768]{1,0:T(8,128)S(1)}, u32[]{:S(2)}, u32[]{:S(2)}) collective-permute-start(f32[12,768]{1,0:T(8,128)S(1)} %add_add_fusion.5), channel_id=1, source_target_pairs={{0,8},{1,9},{2,10},{3,11},{4,12},{5,13},{6,14},{7,15},{8,0},{9,1},... | collective-permute-start | bytes 110600 | tf_op jit(solution)/shard_map/ppermute | solution.py:508
  151.3 2.3 collective-permute-start.17
  154.5 68.1 %collective-permute-start.3 = (bf16[2,768,384]{2,1,0:T(8,128)(2,1)}, bf16[2,768,384]{2,1,0:T(8,128)(2,1)S(1)}, u32[]{:S(2)}, u32[]{:S(2)}) collective-permute-start(bf16[2,768,384]{2,1,0:T(8,128)(2,1)} %get-tuple-element.128), channel_id=1, source_target_pairs={{0,1},{1,0},{2,3},{3,2},{4,5},{5,4},{6,7},{7,6},{8,9},{9,8},{10,11... | collective-permute-start | bytes 3538952 | tf_op jit(solution)/shard_map/ppermute | solution.py:508
  158.1 11.6 %collective-permute-start.18 = (bf16[768,192]{1,0:T(8,128)(2,1)}, bf16[768,192]{1,0:T(8,128)(2,1)S(1)}, u32[]{:S(2)}, u32[]{:S(2)}) collective-permute-start(bf16[768,192]{1,0:T(8,128)(2,1)} %get-tuple-element.154), channel_id=1, source_target_pairs={{0,2},{1,3},{2,0},{3,1},{4,6},{5,7},{6,4},{7,5},{8,10},{9,11},{10,... | collective-permute-start | bytes 884744 | tf_op jit(solution)/shard_map/ppermute | solution.py:508
  170.5 17.0 %collective-permute-start.6 = (bf16[768,256]{1,0:T(8,128)(2,1)}, bf16[768,256]{1,0:T(8,128)(2,1)S(1)}, u32[]{:S(2)}, u32[]{:S(2)}) collective-permute-start(bf16[768,256]{1,0:T(8,128)(2,1)} %get-tuple-element.134), channel_id=1, source_target_pairs={{0,2},{1,3},{2,0},{3,1},{4,6},{5,7},{6,4},{7,5},{8,10},{9,11},{10,... | collective-permute-start | bytes 1179656 | tf_op jit(solution)/shard_map/ppermute | solution.py:508
  174.2 11.1 %collective-permute-start.19 = (bf16[384,192]{1,0:T(8,128)(2,1)}, bf16[384,192]{1,0:T(8,128)(2,1)}, u32[]{:S(2)}, u32[]{:S(2)}) collective-permute-start(bf16[384,192]{1,0:T(8,128)(2,1)} %get-tuple-element.156), channel_id=1, source_target_pairs={{0,4},{1,5},{2,6},{3,7},{4,0},{5,1},{6,2},{7,3},{8,12},{9,13},{10,... | collective-permute-start | bytes 442376 | tf_op jit(solution)/shard_map/ppermute | solution.py:508
  179.4 45.2 %collective-permute-start.12 = (bf16[768,384]{1,0:T(8,128)(2,1)}, bf16[768,384]{1,0:T(8,128)(2,1)}, u32[]{:S(2)}, u32[]{:S(2)}) collective-permute-start(bf16[768,384]{1,0:T(8,128)(2,1)} %get-tuple-element.144), channel_id=1, source_target_pairs={{0,2},{1,3},{2,0},{3,1},{4,6},{5,7},{6,4},{7,5},{8,10},{9,11},{10,... | collective-permute-start | bytes 1769480 | tf_op jit(solution)/shard_map/ppermute | solution.py:508
  185.3 65.2 %collective-permute-start.24 = (bf16[1536,384]{1,0:T(8,128)(2,1)}, bf16[1536,384]{1,0:T(8,128)(2,1)}, u32[]{:S(2)}, u32[]{:S(2)}) collective-permute-start(bf16[1536,384]{1,0:T(8,128)(2,1)} %get-tuple-element.164), channel_id=1, source_target_pairs={{0,4},{1,5},{2,6},{3,7},{4,0},{5,1},{6,2},{7,3},{8,12},{9,13},{10,... | collective-permute-start | bytes 3538952 | tf_op jit(solution)/shard_map/ppermute | solution.py:508
  187.6 4.4 %collective-permute-start.20 = (bf16[96,192]{1,0:T(8,128)(2,1)}, bf16[96,192]{1,0:T(8,128)(2,1)S(1)}, u32[]{:S(2)}, u32[]{:S(2)}) collective-permute-start(bf16[96,192]{1,0:T(8,128)(2,1)} %get-tuple-element.158), channel_id=1, source_target_pairs={{0,8},{1,9},{2,10},{3,11},{4,12},{5,13},{6,14},{7,15},{8,0},{9,1},... | collective-permute-start | bytes 110600 | tf_op jit(solution)/shard_map/ppermute | solution.py:508
  191.9 7.3 %copy-start.15 = (bf16[96,192]{1,0:T(8,128)(2,1)}, bf16[96,192]{1,0:T(8,128)(2,1)S(1)}, u32[]{:S(2)}) copy-start(bf16[96,192]{1,0:T(8,128)(2,1)S(1)} %collective-permute-done.20) | copy-start | bytes 110596
  191.9 24.5 %collective-permute-start.7 = (bf16[384,256]{1,0:T(8,128)(2,1)}, bf16[384,256]{1,0:T(8,128)(2,1)}, u32[]{:S(2)}, u32[]{:S(2)}) collective-permute-start(bf16[384,256]{1,0:T(8,128)(2,1)} %get-tuple-element.136), channel_id=1, source_target_pairs={{0,4},{1,5},{2,6},{3,7},{4,0},{5,1},{6,2},{7,3},{8,12},{9,13},{10,... | collective-permute-start | bytes 589832 | tf_op jit(solution)/shard_map/ppermute | solution.py:508
  193.4 5.7 %collective-permute-start.21 = (bf16[96,192]{1,0:T(8,128)(2,1)}, bf16[96,192]{1,0:T(8,128)(2,1)S(1)}, u32[]{:S(2)}, u32[]{:S(2)}) collective-permute-start(bf16[96,192]{1,0:T(8,128)(2,1)} %get-tuple-element.159), channel_id=1, source_target_pairs={{0,16},{1,17},{2,18},{3,19},{4,20},{5,21},{6,22},{7,23},{8,24},{9,... | collective-permute-start | bytes 110600 | tf_op jit(solution)/shard_map/ppermute | solution.py:508
  199.8 55.0 %collective-permute-start.30 = (bf16[768,768]{1,0:T(8,128)(2,1)}, bf16[768,768]{1,0:T(8,128)(2,1)S(1)}, u32[]{:S(2)}, u32[]{:S(2)}) collective-permute-start(bf16[768,768]{1,0:T(8,128)(2,1)} %get-tuple-element.174), channel_id=1, source_target_pairs={{0,2},{1,3},{2,0},{3,1},{4,6},{5,7},{6,4},{7,5},{8,10},{9,11},{10,... | collective-permute-start | bytes 3538952 | tf_op jit(solution)/shard_map/ppermute | solution.py:508
  216.5 6.1 %collective-permute-start.22 = (bf16[96,192]{1,0:T(8,128)(2,1)}, bf16[96,192]{1,0:T(8,128)(2,1)S(1)}, u32[]{:S(2)}, u32[]{:S(2)}) collective-permute-start(bf16[96,192]{1,0:T(8,128)(2,1)} %get-tuple-element.160), channel_id=1, source_target_pairs={{0,24},{1,25},{2,26},{3,27},{4,28},{5,29},{6,30},{7,31},{8,16},{9,... | collective-permute-start | bytes 110600 | tf_op jit(solution)/shard_map/ppermute | solution.py:508
  222.6 14.0 %collective-permute-start.8 = (bf16[96,256]{1,0:T(8,128)(2,1)}, bf16[96,256]{1,0:T(8,128)(2,1)S(1)}, u32[]{:S(2)}, u32[]{:S(2)}) collective-permute-start(bf16[96,256]{1,0:T(8,128)(2,1)} %get-tuple-element.138), channel_id=1, source_target_pairs={{0,8},{1,9},{2,10},{3,11},{4,12},{5,13},{6,14},{7,15},{8,0},{9,1},... | collective-permute-start | bytes 147464 | tf_op jit(solution)/shard_map/ppermute | solution.py:508
  222.6 6.5 %copy-start.1 = (bf16[2,768,384]{2,1,0:T(8,128)(2,1)}, bf16[2,768,384]{2,1,0:T(8,128)(2,1)S(1)}, u32[]{:S(2)}) copy-start(bf16[2,768,384]{2,1,0:T(8,128)(2,1)S(1)} %collective-permute-done.3.refs_1_) | copy-start | bytes 3538948
  222.6 14.6 %collective-permute-start.9 = (bf16[96,256]{1,0:T(8,128)(2,1)}, bf16[96,256]{1,0:T(8,128)(2,1)S(1)}, u32[]{:S(2)}, u32[]{:S(2)}) collective-permute-start(bf16[96,256]{1,0:T(8,128)(2,1)} %get-tuple-element.139), channel_id=1, source_target_pairs={{0,16},{1,17},{2,18},{3,19},{4,20},{5,21},{6,22},{7,23},{8,24},{9,... | collective-permute-start | bytes 147464 | tf_op jit(solution)/shard_map/ppermute | solution.py:508
  224.7 12.5 %collective-permute-start.10 = (bf16[96,256]{1,0:T(8,128)(2,1)}, bf16[96,256]{1,0:T(8,128)(2,1)S(1)}, u32[]{:S(2)}, u32[]{:S(2)}) collective-permute-start(bf16[96,256]{1,0:T(8,128)(2,1)} %get-tuple-element.140), channel_id=1, source_target_pairs={{0,24},{1,25},{2,26},{3,27},{4,28},{5,29},{6,30},{7,31},{8,16},{9,... | collective-permute-start | bytes 147464 | tf_op jit(solution)/shard_map/ppermute | solution.py:508
  229.1 8.1 %copy-start.17 = (bf16[96,256]{1,0:T(8,128)(2,1)S(1)}, bf16[96,256]{1,0:T(8,128)(2,1)}, u32[]{:S(2)}) copy-start(bf16[96,256]{1,0:T(8,128)(2,1)} %get-tuple-element.137) | copy-start | bytes 147460
  233.2 21.7 %copy-start.25 = (bf16[768,384]{1,0:T(8,128)(2,1)S(1)}, bf16[768,384]{1,0:T(8,128)(2,1)}, u32[]{:S(2)}) copy-start(bf16[768,384]{1,0:T(8,128)(2,1)} %get-tuple-element.130) | copy-start | bytes 1769476
  236.6 7.0 %collective-permute-start.13 = (bf16[384,384]{1,0:T(8,128)(2,1)}, bf16[384,384]{1,0:T(8,128)(2,1)S(1)}, u32[]{:S(2)}, u32[]{:S(2)}) collective-permute-start(bf16[384,384]{1,0:T(8,128)(2,1)} %get-tuple-element.146), channel_id=1, source_target_pairs={{0,4},{1,5},{2,6},{3,7},{4,0},{5,1},{6,2},{7,3},{8,12},{9,13},{10,... | collective-permute-start | bytes 884744 | tf_op jit(solution)/shard_map/ppermute | solution.py:508
  246.1 14.0 %collective-permute-start.14 = (bf16[96,384]{1,0:T(8,128)(2,1)}, bf16[96,384]{1,0:T(8,128)(2,1)S(1)}, u32[]{:S(2)}, u32[]{:S(2)}) collective-permute-start(bf16[96,384]{1,0:T(8,128)(2,1)} %get-tuple-element.148), channel_id=1, source_target_pairs={{0,8},{1,9},{2,10},{3,11},{4,12},{5,13},{6,14},{7,15},{8,0},{9,1},... | collective-permute-start | bytes 221192 | tf_op jit(solution)/shard_map/ppermute | solution.py:508
  246.1 14.5 %collective-permute-start.15 = (bf16[96,384]{1,0:T(8,128)(2,1)}, bf16[96,384]{1,0:T(8,128)(2,1)S(1)}, u32[]{:S(2)}, u32[]{:S(2)}) collective-permute-start(bf16[96,384]{1,0:T(8,128)(2,1)} %get-tuple-element.149), channel_id=1, source_target_pairs={{0,16},{1,17},{2,18},{3,19},{4,20},{5,21},{6,22},{7,23},{8,24},{9,... | collective-permute-start | bytes 221192 | tf_op jit(solution)/shard_map/ppermute | solution.py:508
  248.2 12.4 %collective-permute-start.16 = (bf16[96,384]{1,0:T(8,128)(2,1)}, bf16[96,384]{1,0:T(8,128)(2,1)S(1)}, u32[]{:S(2)}, u32[]{:S(2)}) collective-permute-start(bf16[96,384]{1,0:T(8,128)(2,1)} %get-tuple-element.150), channel_id=1, source_target_pairs={{0,24},{1,25},{2,26},{3,27},{4,28},{5,29},{6,30},{7,31},{8,16},{9,... | collective-permute-start | bytes 221192 | tf_op jit(solution)/shard_map/ppermute | solution.py:508
  250.5 10.1 %copy-start.13 = (bf16[96,384]{1,0:T(8,128)(2,1)S(1)}, bf16[96,384]{1,0:T(8,128)(2,1)}, u32[]{:S(2)}) copy-start(bf16[96,384]{1,0:T(8,128)(2,1)} %get-tuple-element.147) | copy-start | bytes 221188
  254.2 15.6 %collective-permute-start.25 = (bf16[768,384]{1,0:T(8,128)(2,1)}, bf16[768,384]{1,0:T(8,128)(2,1)S(1)}, u32[]{:S(2)}, u32[]{:S(2)}) collective-permute-start(bf16[768,384]{1,0:T(8,128)(2,1)} %get-tuple-element.166), channel_id=1, source_target_pairs={{0,2},{1,3},{2,0},{3,1},{4,6},{5,7},{6,4},{7,5},{8,10},{9,11},{10,... | collective-permute-start | bytes 1769480 | tf_op jit(solution)/shard_map/ppermute | solution.py:508
  254.8 55.6 %collective-permute-start.4 = (bf16[768,384]{1,0:T(8,128)(2,1)S(1)}, bf16[768,384]{1,0:T(8,128)(2,1)S(1)}, u32[]{:S(2)}, u32[]{:S(2)}) collective-permute-start(bf16[768,384]{1,0:T(8,128)(2,1)S(1)} %copy-done.25), channel_id=1, source_target_pairs={{0,2},{1,3},{2,0},{3,1},{4,6},{5,7},{6,4},{7,5},{8,10},{9,11},{10,... | collective-permute-start | bytes 1769480 | tf_op jit(solution)/shard_map/ppermute | solution.py:508
  260.1 19.9 %collective-permute-start.31 = (bf16[384,768]{1,0:T(8,128)(2,1)}, bf16[384,768]{1,0:T(8,128)(2,1)S(1)}, u32[]{:S(2)}, u32[]{:S(2)}) collective-permute-start(bf16[384,768]{1,0:T(8,128)(2,1)} %get-tuple-element.176), channel_id=1, source_target_pairs={{0,4},{1,5},{2,6},{3,7},{4,0},{5,1},{6,2},{7,3},{8,12},{9,13},{10,... | collective-permute-start | bytes 1769480 | tf_op jit(solution)/shard_map/ppermute | solution.py:508
  270.7 37.0 %copy-start.10 = (f32[768,96]{0,1:T(8,128)S(1)}, f32[768,96]{0,1:T(8,128)}, u32[]{:S(2)}) copy-start(f32[768,96]{0,1:T(8,128)} %param.37) | copy-start | bytes 884740
  272.7 35.9 %copy-start.11 = (f32[768,96]{0,1:T(8,128)S(1)}, f32[768,96]{0,1:T(8,128)}, u32[]{:S(2)}) copy-start(f32[768,96]{0,1:T(8,128)} %param.42) | copy-start | bytes 884740
  272.7 10.1 %collective-permute-start.26 = (bf16[192,384]{1,0:T(8,128)(2,1)}, bf16[192,384]{1,0:T(8,128)(2,1)S(1)}, u32[]{:S(2)}, u32[]{:S(2)}) collective-permute-start(bf16[192,384]{1,0:T(8,128)(2,1)} %get-tuple-element.168), channel_id=1, source_target_pairs={{0,8},{1,9},{2,10},{3,11},{4,12},{5,13},{6,14},{7,15},{8,0},{9,1},... | collective-permute-start | bytes 442376 | tf_op jit(solution)/shard_map/ppermute | solution.py:508
  272.8 12.8 %collective-permute-start.27 = (bf16[192,384]{1,0:T(8,128)(2,1)}, bf16[192,384]{1,0:T(8,128)(2,1)S(1)}, u32[]{:S(2)}, u32[]{:S(2)}) collective-permute-start(bf16[192,384]{1,0:T(8,128)(2,1)} %get-tuple-element.169), channel_id=1, source_target_pairs={{0,16},{1,17},{2,18},{3,19},{4,20},{5,21},{6,22},{7,23},{8,24},{9,... | collective-permute-start | bytes 442376 | tf_op jit(solution)/shard_map/ppermute | solution.py:508
  275.6 11.5 %collective-permute-start.28 = (bf16[192,384]{1,0:T(8,128)(2,1)}, bf16[192,384]{1,0:T(8,128)(2,1)S(1)}, u32[]{:S(2)}, u32[]{:S(2)}) collective-permute-start(bf16[192,384]{1,0:T(8,128)(2,1)} %get-tuple-element.170), channel_id=1, source_target_pairs={{0,24},{1,25},{2,26},{3,27},{4,28},{5,29},{6,30},{7,31},{8,16},{9,... | collective-permute-start | bytes 442376 | tf_op jit(solution)/shard_map/ppermute | solution.py:508
  278.6 30.9 %copy-start.12 = (f32[768,96]{0,1:T(8,128)S(1)}, f32[768,96]{0,1:T(8,128)}, u32[]{:S(2)}) copy-start(f32[768,96]{0,1:T(8,128)} %param.47) | copy-start | bytes 884740
  282.7 7.4 %collective-permute-start.32 = (bf16[96,768]{1,0:T(8,128)(2,1)}, bf16[96,768]{1,0:T(8,128)(2,1)S(1)}, u32[]{:S(2)}, u32[]{:S(2)}) collective-permute-start(bf16[96,768]{1,0:T(8,128)(2,1)} %get-tuple-element.178), channel_id=1, source_target_pairs={{0,8},{1,9},{2,10},{3,11},{4,12},{5,13},{6,14},{7,15},{8,0},{9,1},... | collective-permute-start | bytes 442376 | tf_op jit(solution)/shard_map/ppermute | solution.py:508
  282.8 7.9 %collective-permute-start.33 = (bf16[96,768]{1,0:T(8,128)(2,1)}, bf16[96,768]{1,0:T(8,128)(2,1)S(1)}, u32[]{:S(2)}, u32[]{:S(2)}) collective-permute-start(bf16[96,768]{1,0:T(8,128)(2,1)} %get-tuple-element.179), channel_id=1, source_target_pairs={{0,16},{1,17},{2,18},{3,19},{4,20},{5,21},{6,22},{7,23},{8,24},{9,... | collective-permute-start | bytes 442376 | tf_op jit(solution)/shard_map/ppermute | solution.py:508
  285.6 7.3 %collective-permute-start.34 = (bf16[96,768]{1,0:T(8,128)(2,1)}, bf16[96,768]{1,0:T(8,128)(2,1)S(1)}, u32[]{:S(2)}, u32[]{:S(2)}) collective-permute-start(bf16[96,768]{1,0:T(8,128)(2,1)} %get-tuple-element.180), channel_id=1, source_target_pairs={{0,24},{1,25},{2,26},{3,27},{4,28},{5,29},{6,30},{7,31},{8,16},{9,... | collective-permute-start | bytes 442376 | tf_op jit(solution)/shard_map/ppermute | solution.py:508
  296.5 1.2 collective-permute-start.42
  297.7 3.6 %collective-permute-start.44 = (f32[8,128]{1,0:T(8,128)S(1)}, f32[8,128]{1,0:T(8,128)S(1)}, u32[]{:S(2)}, u32[]{:S(2)}) collective-permute-start(f32[8,128]{1,0:T(8,128)S(1)} %broadcast_add_fusion), channel_id=1, source_target_pairs={{0,4},{1,5},{2,6},{3,7},{4,0},{5,1},{6,2},{7,3},{8,12},{9,13},{10,... | collective-permute-start | bytes 12296 | tf_op jit(solution)/shard_map/ppermute | solution.py:508
  298.2 4.5 %collective-permute-start.45 = (f32[8,128]{1,0:T(8,128)S(1)}, f32[8,128]{1,0:T(8,128)S(1)}, u32[]{:S(2)}, u32[]{:S(2)}) collective-permute-start(f32[8,128]{1,0:T(8,128)S(1)} %broadcast_add_fusion), channel_id=1, source_target_pairs={{0,6},{1,7},{2,4},{3,5},{4,2},{5,3},{6,0},{7,1},{8,14},{9,15},{10,... | collective-permute-start | bytes 12296 | tf_op jit(solution)/shard_map/ppermute | solution.py:508
  299.7 3.6 %collective-permute-start.43 = (f32[8,128]{1,0:T(8,128)S(1)}, f32[8,128]{1,0:T(8,128)S(1)}, u32[]{:S(2)}, u32[]{:S(2)}) collective-permute-start(f32[8,128]{1,0:T(8,128)S(1)} %broadcast_add_fusion), channel_id=1, source_target_pairs={{0,2},{1,3},{2,0},{3,1},{4,6},{5,7},{6,4},{7,5},{8,10},{9,11},{10,... | collective-permute-start | bytes 12296 | tf_op jit(solution)/shard_map/ppermute | solution.py:508
  303.3 13.2 %collective-permute-start.48 = (f32[8,128]{1,0:T(8,128)S(1)}, f32[8,128]{1,0:T(8,128)S(1)}, u32[]{:S(2)}, u32[]{:S(2)}) collective-permute-start(f32[8,128]{1,0:T(8,128)S(1)} %add_add_fusion.7), channel_id=1, source_target_pairs={{0,24},{1,25},{2,26},{3,27},{4,28},{5,29},{6,30},{7,31},{8,16},{9,... | collective-permute-start | bytes 12296 | tf_op jit(solution)/shard_map/ppermute | solution.py:508
  305.0 11.5 %collective-permute-start.47 = (f32[8,128]{1,0:T(8,128)S(1)}, f32[8,128]{1,0:T(8,128)S(1)}, u32[]{:S(2)}, u32[]{:S(2)}) collective-permute-start(f32[8,128]{1,0:T(8,128)S(1)} %add_add_fusion.7), channel_id=1, source_target_pairs={{0,16},{1,17},{2,18},{3,19},{4,20},{5,21},{6,22},{7,23},{8,24},{9,... | collective-permute-start | bytes 12296 | tf_op jit(solution)/shard_map/ppermute | solution.py:508
  306.5 10.0 %collective-permute-start.46 = (f32[8,128]{1,0:T(8,128)S(1)}, f32[8,128]{1,0:T(8,128)S(1)}, u32[]{:S(2)}, u32[]{:S(2)}) collective-permute-start(f32[8,128]{1,0:T(8,128)S(1)} %add_add_fusion.7), channel_id=1, source_target_pairs={{0,8},{1,9},{2,10},{3,11},{4,12},{5,13},{6,14},{7,15},{8,0},{9,1},... | collective-permute-start | bytes 12296 | tf_op jit(solution)/shard_map/ppermute | solution.py:508
  (11 other events, 9.8 us)

commit v2 on v1

v2 whole, which is shorter than its diff:
```python
import functools

import jax
import jax.numpy as jnp
from jax import lax
from jax.experimental import pallas as pl
from jax.experimental.pallas import tpu as pltpu
from jax.sharding import PartitionSpec as P

HD = 64
STEP = 10
LANES = 128
NORM_EPS = 1e-05
MASK = -float(2**30)
BF = jnp.bfloat16
F32 = jnp.float32
AXES = ("dp", "seq")

PLACES = (
    {
        0: ((0, 0, 0), (1, 1, 1), (2, 2, 2)),
        2: ((0, 0, 1), (1, 1, 2), (2, 3, 0)),
        3: ((0, 0, 2), (1, 2, 0), (2, 3, 1)),
        5: ((0, 1, 0), (1, 2, 1), (2, 3, 2)),
    },
    {
        1: ((0, 0, 0), (1, 1, 1), (2, 2, 1), (2, 3, 0)),
        4: ((0, 0, 1), (0, 1, 0), (1, 2, 0), (2, 3, 1)),
    },
)
WIDTHS = (3 * LANES, 2 * LANES)
CALLS = ((0, 2), (3, 5), (1, 4))


def params(**more):
    return pltpu.CompilerParams(vmem_limit_bytes=60 * 2**20, **more)


def cost(microseconds):
    return pl.CostEstimate(flops=int(microseconds * 4.4e9), bytes_accessed=0, transcendentals=0)


def dot(a, b):
    return lax.dot_general(a, b, (((1,), (0,)), ((), ())), preferred_element_type=F32)


def dot_t(a, b):
    return lax.dot_general(a, b, (((1,), (1,)), ((), ())), preferred_element_type=F32)


def attend_kernel(
    x0_ref, x1_ref, x2_ref, x3_ref, wq_ref, wk_ref, wv_ref, vec_ref, kmask_ref, qhot_ref,
    mixed_ref, e_ref, rinv_ref, q_ref, k_ref, v_ref, xt_ref, x_ref,
):
    rows = q_ref.shape[0]
    step = pl.program_id(0)

    @pl.when(step == 0)
    def _():
        for i, ref in enumerate((x0_ref, x1_ref, x2_ref, x3_ref)):
            x_ref[i * rows : (i + 1) * rows, :] = ref[...]

    xt_ref[...] = x_ref[:, pl.ds(pl.multiple_of(step * LANES, LANES), LANES)].T
    wkv = jnp.concatenate([wk_ref[...], wv_ref[...]], axis=1)
    kv = dot(x_ref[...], wkv)
    k = kv[:, :LANES].astype(BF)
    v = (kv[:, LANES:] + vec_ref[1:2, :]).astype(BF)
    q = (dot(x_ref[:rows, :], wq_ref[...]) + vec_ref[0:1, :]).astype(BF)
    q = q * jnp.asarray(HD**-0.5, BF)
    q_ref[...] = q
    k_ref[...] = k
    v_ref[...] = v
    keys = jnp.concatenate([k, kmask_ref[...]], axis=1)
    low = lax.broadcasted_iota(jnp.int32, (rows, LANES), 1) < HD
    outs, inverses = [], []
    for head in range(2):
        own = low if head == 0 else jnp.logical_not(low)
        qh = jnp.where(own, q, jnp.zeros_like(q))
        scores = dot_t(jnp.concatenate([qh, qhot_ref[...]], axis=1), keys)
        top = jnp.max(scores, axis=1, keepdims=True)
        e = jnp.exp(scores - top)
        total = jnp.sum(e, axis=1, keepdims=True)
        e_low = e.astype(BF)
        e_ref[head] = e_low
        outs.append(dot(e_low, v))
        inverses.append(1.0 / total)
    rinv = jnp.where(low, inverses[0], inverses[1])
    rinv_ref[...] = rinv
    mixed_ref[...] = (jnp.where(low, outs[0], outs[1]) * rinv).astype(BF)


def attend(blocks, input_weight, vectors, kmask, qhot):
    rows, width = blocks[0].shape
    slab = rows * len(blocks)
    pairs = width // LANES
    full = lambda a: pl.BlockSpec(a.shape, lambda p: (0,) * a.ndim)
    cols = lambda r, off=0: pl.BlockSpec((r, LANES), lambda p: (0, p + off))
    return pl.pallas_call(
        attend_kernel,
        grid=(pairs,),
        in_specs=[
            *map(full, blocks), cols(width), cols(width, pairs), cols(width, 2 * pairs),
            cols(vectors.shape[0]), full(kmask), full(qhot),
        ],
        out_specs=[
            cols(rows), pl.BlockSpec((2, rows, slab), lambda p: (p, 0, 0)), cols(rows), cols(rows),
            cols(slab), cols(slab), pl.BlockSpec((LANES, slab), lambda p: (p, 0)),
        ],
        out_shape=[
            jax.ShapeDtypeStruct((rows, width), BF),
            jax.ShapeDtypeStruct((2 * pairs, rows, slab), BF),
            jax.ShapeDtypeStruct((rows, width), F32),
            jax.ShapeDtypeStruct((rows, width), BF),
            jax.ShapeDtypeStruct((slab, width), BF),
            jax.ShapeDtypeStruct((slab, width), BF),
            jax.ShapeDtypeStruct((width, slab), BF),
        ],
        scratch_shapes=[pltpu.VMEM((slab, width), BF)],
        compiler_params=params(), cost_estimate=cost(29),
        name="attend",
    )(*blocks, input_weight, input_weight, input_weight, vectors, kmask, qhot)


def spot(d, own_d):
    rel = d ^ own_d
    return (rel & 1) * 4 + (rel >> 1)


def turn(j):
    return jnp.where(j < 2, 2 * j + 1, 2 * (j - 2))


def store_rows(ref, block, own_d):
    piece = block.shape[0] // 8
    for d in range(8):
        ref[0, spot(d, own_d)] = block[d * piece : (d + 1) * piece, :]


def reduce_kernel(own_ref, gbt_ref, act_ref, rk_ref):
    store_rows(rk_ref, dot(gbt_ref[...], act_ref[0]).astype(BF), own_ref[1])


def reduce_kept(own, gbt, act):
    width, rows = gbt.shape
    chunks, _, cut = act.shape
    return pl.pallas_call(
        reduce_kernel,
        grid_spec=pltpu.PrefetchScalarGridSpec(
            num_scalar_prefetch=1,
            grid=(2,),
            in_specs=[
                pl.BlockSpec((width, rows), lambda j, own: (0, 0)),
                pl.BlockSpec((1, rows, cut), lambda j, own: (j + 2, 0, 0)),
            ],
            out_specs=pl.BlockSpec((1, 8, width // 8, cut), lambda j, own: (j, 0, 0, 0)),
        ),
        out_shape=jax.ShapeDtypeStruct((2, 8, width // 8, cut), BF),
        compiler_params=params(), cost_estimate=cost(5),
        name="reduce_kept",
    )(own, gbt, act)


def ahead_kernel(
    own_ref, mixed_ref, x_ref, cot_ref, qhot_ref, wo_ref, we_ref, wr_ref, vec_ref,
    layer_ref, act_ref, slope_ref, norm1_ref, inv1_ref, hlt_ref, mt_ref, gs_ref, gb_ref, gbt, rs_ref, vg_ref,
    act, hid, hl, acc,
):
    step = pl.program_id(0)
    own_s, own_d = own_ref[0], own_ref[1]
    rows, width = x_ref.shape
    chunks = act.shape[0]
    j = lax.rem(step, chunks)
    shard = turn(j) ^ own_s
    row = lambda i: vec_ref[i : i + 1, :]

    @pl.when(step == 0)
    def _():
        z = x_ref[...].astype(F32) + dot(mixed_ref[...], wo_ref[...]) + row(2)
        center = z - jnp.mean(z, axis=1, keepdims=True)
        inverse = lax.rsqrt(jnp.mean(center * center, axis=1, keepdims=True) + NORM_EPS)
        normed = center * inverse
        hidden = normed * row(3) + row(4)
        hid[...] = hidden
        norm1_ref[...] = normed
        inv1_ref[...] = jnp.broadcast_to(inverse, inv1_ref.shape)
        low = hidden.astype(BF)
        hl[...] = low
        hlt_ref[...] = low.T
        mt_ref[...] = mixed_ref[...].T
        vg_ref[...] = jnp.zeros_like(vg_ref)

    @pl.when(step < chunks)
    def _():
        pre = dot(hl[...], we_ref[...]) + vec_ref[pl.ds(8 + shard, 1), :]
        cdf = 0.5 * (1.0 + lax.erf(pre * 0.7071067811865476))
        density = jnp.exp(-0.5 * pre * pre) * 0.3989422804014327
        low = (pre * cdf).astype(BF)
        act[j] = low
        act_ref[0] = low
        slope_ref[0] = cdf + pre * density
        part = dot(low, wr_ref[...])

        @pl.when(step == 0)
        def _():
            acc[...] = part

        @pl.when(step > 0)
        def _():
            acc[...] += part

    @pl.when(step == chunks - 1)
    def _():
        z = hid[...] + acc[...] + row(5)
        center = z - jnp.mean(z, axis=1, keepdims=True)
        inverse = lax.rsqrt(jnp.mean(center * center, axis=1, keepdims=True) + NORM_EPS)
        normed = center * inverse
        valid = 1.0 - qhot_ref[:, 3:4].astype(F32)
        layer_ref[...] = ((normed * row(6) + row(7)) * valid).astype(BF)
        gy = cot_ref[...].astype(F32) * valid
        vg_ref[6:7, :] = jnp.sum(gy * normed, axis=0, keepdims=True)
        vg_ref[7:8, :] = jnp.sum(gy, axis=0, keepdims=True)
        e = gy * row(6)
        grad = e - jnp.mean(e, axis=1, keepdims=True)
        grad = (grad - normed * jnp.mean(e * normed, axis=1, keepdims=True)) * inverse
        low = grad.astype(BF)
        vg_ref[5:6, :] = jnp.sum(low.astype(F32), axis=0, keepdims=True)
        gb_ref[...] = low
        gbt[...] = low.T
        gs_ref[...] = grad

    @pl.when(step >= chunks)
    def _():
        store_rows(rs_ref, dot(gbt[...], act[j]).astype(BF), own_d)


def ahead(own, mixed, frames, cotangent, qhot, output_weight, expand_weight, reduce_weight, vectors):
    rows, width = frames.shape
    hidden = expand_weight.shape[1]
    chunks = 4
    cut = hidden // chunks
    piece = width // 8
    first = lambda s: jnp.minimum(s, chunks - 1)
    shard_of = lambda s, own: turn(first(s)) ^ own[0]
    full = lambda shape: pl.BlockSpec(shape, lambda s, own: (0,) * len(shape))
    chunk = pl.BlockSpec((1, rows, cut), lambda s, own: (first(s), 0, 0))
    return pl.pallas_call(
        ahead_kernel,
        grid_spec=pltpu.PrefetchScalarGridSpec(
            num_scalar_prefetch=1,
            grid=(chunks + 2,),
            in_specs=[
                full(mixed.shape), full(frames.shape), full(cotangent.shape), full(qhot.shape),
                full(output_weight.shape),
                pl.BlockSpec((width, cut), lambda s, own: (0, shard_of(s, own))),
                pl.BlockSpec((cut, width), lambda s, own: (shard_of(s, own), 0)),
                full(vectors.shape),
            ],
            out_specs=[
                full((rows, width)), chunk, chunk, full((rows, width)), full((rows, LANES)),
                full((width, rows)), full((width, rows)), full((rows, width)), full((rows, width)), full((width, rows)),
                pl.BlockSpec((1, 8, piece, cut), lambda s, own: (jnp.maximum(s - chunks, 0), 0, 0, 0)),
                full((16, width)),
            ],
            scratch_shapes=[
                pltpu.VMEM((chunks, rows, cut), BF),
                pltpu.VMEM((rows, width), F32),
                pltpu.VMEM((rows, width), BF),
                pltpu.VMEM((rows, width), F32),
            ],
        ),
        out_shape=[
            jax.ShapeDtypeStruct((rows, width), BF),
            jax.ShapeDtypeStruct((chunks, rows, cut), BF),
            jax.ShapeDtypeStruct((chunks, rows, cut), F32),
            jax.ShapeDtypeStruct((rows, width), F32),
            jax.ShapeDtypeStruct((rows, LANES), F32),
            jax.ShapeDtypeStruct((width, rows), BF),
            jax.ShapeDtypeStruct((width, rows), BF),
            jax.ShapeDtypeStruct((rows, width), F32),
            jax.ShapeDtypeStruct((rows, width), BF),
            jax.ShapeDtypeStruct((width, rows), BF),
            jax.ShapeDtypeStruct((2, 8, piece, cut), BF),
            jax.ShapeDtypeStruct((16, width), F32),
        ],
        compiler_params=params(), cost_estimate=cost(20),
        name="ahead",
    )(own, mixed, frames, cotangent, qhot, output_weight, expand_weight, reduce_weight, vectors)


def behind_kernel(
    own_ref, slope_ref, gb_ref, gs_ref, norm1_ref, inv1_ref, hlt_ref, mt_ref, wo_ref, we_ref, wr_ref, vec_ref, _,
    gf_ref, gm_ref, es_ref, ek_ref, vg_ref,
    acc, tmp,
):
    j = pl.program_id(0)
    own_s, own_d = own_ref[0], own_ref[1]
    rows, width = gb_ref.shape
    shard = turn(j) ^ own_s
    row = lambda i: vec_ref[i : i + 1, :]
    piece, fourth = width // 8, width // 4

    @pl.when(j == 0)
    def _():
        acc[...] = gs_ref[...]
        vg_ref[...] = jnp.zeros_like(vg_ref)

    grad_act = dot_t(gb_ref[...], wr_ref[...])
    low = (grad_act * slope_ref[0]).astype(BF)
    vg_ref[pl.ds(8 + shard, 1), :] = jnp.sum(low.astype(F32), axis=0, keepdims=True)
    acc[...] += dot_t(low, we_ref[...])
    grad_e = dot(hlt_ref[...], low).astype(BF)
    tmp[...] = grad_e.reshape(tmp.shape)
    half = grad_e.shape[1] // 2
    rz = shard ^ (own_d >> 1)
    for part, ref in ((1, es_ref), (0, ek_ref)):
        for ry in range(2):
            for t in range(2):
                block = tmp[own_s ^ (2 * ry + part), :, t * half : (t + 1) * half]
                ref[ry, t ^ (own_d & 1), rz, :fourth, :] = block

    @pl.when(j == pl.num_programs(0) - 1)
    def _():
        gy = acc[...]
        normed = norm1_ref[...]
        vg_ref[3:4, :] = jnp.sum(gy * normed, axis=0, keepdims=True)
        vg_ref[4:5, :] = jnp.sum(gy, axis=0, keepdims=True)
        e = gy * row(3)
        grad = e - jnp.mean(e, axis=1, keepdims=True)
        grad = (grad - normed * jnp.mean(e * normed, axis=1, keepdims=True)) * inv1_ref[:, :1]
        gf_ref[...] = grad
        low = grad.astype(BF)
        vg_ref[2:3, :] = jnp.sum(low.astype(F32), axis=0, keepdims=True)
        gm_ref[...] = dot_t(low, wo_ref[...]).astype(BF)
        gat = low.T
        for part, ref in ((1, es_ref), (0, ek_ref)):
            for ry in range(2):
                start = pl.multiple_of((own_s ^ (2 * ry + part)) * fourth, fourth)
                out = dot_t(gat, mt_ref[pl.ds(start, fourth), :]).astype(BF)
                for d in range(8):
                    block = out[d * piece : (d + 1) * piece, :]
                    block = jnp.concatenate([block[: piece // 2], block[piece // 2 :]], axis=1)
                    ref[ry, (d & 1) ^ (own_d & 1), (d >> 1) ^ (own_d >> 1), fourth:, :] = block


def behind(own, slope, gb, gs, norm1, inv1, hlt, mt, output_weight, expand_weight, reduce_weight, vectors, after):
    rows, width = gb.shape
    hidden = expand_weight.shape[1]
    chunks = 4
    cut = hidden // chunks
    fourth, eighth = width // 4, hidden // 8
    shard_of = lambda s, own: turn(s) ^ own[0]
    full = lambda shape: pl.BlockSpec(shape, lambda s, own: (0,) * len(shape))
    spread = (2, 2, 4, fourth + width // 16, eighth)
    return pl.pallas_call(
        behind_kernel,
        grid_spec=pltpu.PrefetchScalarGridSpec(
            num_scalar_prefetch=1,
            grid=(chunks,),
            in_specs=[
                pl.BlockSpec((1, rows, cut), lambda s, own: (s, 0, 0)),
                full(gb.shape), full(gs.shape), full(norm1.shape), full(inv1.shape), full(hlt.shape), full(mt.shape),
                full(output_weight.shape),
                pl.BlockSpec((width, cut), lambda s, own: (0, shard_of(s, own))),
                pl.BlockSpec((cut, width), lambda s, own: (shard_of(s, own), 0)),
                full(vectors.shape), pl.BlockSpec(memory_space=pl.ANY),
            ],
            out_specs=[full((rows, width)), full((rows, width)), full(spread), full(spread), full((16, width))],
            scratch_shapes=[pltpu.VMEM((rows, width), F32), pltpu.VMEM((4, fourth, cut), BF)],
        ),
        out_shape=[
            jax.ShapeDtypeStruct((rows, width), F32),
            jax.ShapeDtypeStruct((rows, width), BF),
            jax.ShapeDtypeStruct(spread, BF),
            jax.ShapeDtypeStruct(spread, BF),
            jax.ShapeDtypeStruct((16, width), F32),
        ],
        compiler_params=params(), cost_estimate=cost(18),
        name="behind",
    )(own, slope, gb, gs, norm1, inv1, hlt, mt, output_weight, expand_weight, reduce_weight, vectors, after)


def back_kernel(group, pairs, first, last, own_ref, e_ref, q_ref, k_ref, v_ref, gm_ref, mixed_ref, rinv_ref, xt_ref,
                *rest):
    rest = list(rest[1:])
    gw_in_ref = None if first else rest.pop(0)
    vec_in = [rest.pop(0) for _ in range(4)] if group == 1 else []
    dq_ref, dkv_ref, vb_ref = rest[:3]
    rest = rest[3:]
    if last:
        gs_ref, gk_ref, gw, *vecs = rest
    else:
        (gw,) = rest
    i = pl.program_id(0)
    own_s, own_d = own_ref[0], own_ref[1]
    rows = q_ref.shape[0]
    q, k, v = q_ref[...], k_ref[...], v_ref[...]
    gm = gm_ref[...].astype(F32) * rinv_ref[...]
    both = gm * mixed_ref[...].astype(F32)
    gm_low = gm.astype(BF)
    gm_t = gm_low.T
    q_t = q.T
    low = lax.broadcasted_iota(jnp.int32, (rows, LANES), 1) < HD
    dqs, dks, dvs = [], [], []
    for head in range(2):
        own = low if head == 0 else jnp.logical_not(low)
        span = slice(head * HD, (head + 1) * HD)
        e = e_ref[head]
        inner = jnp.sum(jnp.where(own, both, 0.0), axis=1, keepdims=True)
        grad_e = dot_t(jnp.where(own, gm_low, jnp.zeros_like(gm_low)), v)
        ds = (e.astype(F32) * (grad_e - inner)).astype(BF)
        dqs.append(dot(ds, k))
        dks.append(dot(q_t[span, :], ds))
        dvs.append(dot(gm_t[span, :], e))
    dq = (jnp.where(low, dqs[0], dqs[1]) * HD**-0.5).astype(BF)
    dkv = jnp.concatenate([*dks, *dvs], axis=0).astype(BF)
    dq_ref[...] = dq
    dkv_ref[...] = dkv
    ones = jnp.ones((8, dkv.shape[1]), BF)
    bias = jnp.concatenate(
        [jnp.sum(dq.astype(F32), axis=0, keepdims=True), dot_t(ones, dkv[LANES:, :])[0:1, :]], axis=0
    )
    vb_ref[0:2, :] = bias

    if group == 1:

        @pl.when(i == 0)
        def _():
            vecs[0][...] = vec_in[0][...] + vec_in[1][...]
            for call, ref in zip(CALLS, vec_in[2:]):
                for n, p in enumerate(call):
                    vecs[0][0:2, p * LANES : (p + 1) * LANES] = ref[0:2, n * LANES : (n + 1) * LANES]

    if not first:

        @pl.when(i == 0)
        def _():
            gw[...] = gw_in_ref[...]

    grad_q = dot(xt_ref[:, :rows], dq).astype(BF)
    grad_kv = dot_t(xt_ref[...], dkv).astype(BF)
    piece = grad_q.shape[0] // 8
    blocks = [b.reshape(8, piece, LANES) for b in (grad_q, grad_kv[:, :LANES], grad_kv[:, LANES:])]
    for n, pair in enumerate(pairs):

        @pl.when(i == n)
        def _():
            for which, shard, place in PLACES[group][pair]:
                gw[shard, :, :piece, place * LANES : (place + 1) * LANES] = blocks[which]
            if group == 1:
                vecs[0][0:2, pair * LANES : (pair + 1) * LANES] = bias

    if last:

        @pl.when(i == len(pairs) - 1)
        def _():
            if group == 1:
                vec, tall = vecs[0][...], vecs[0].shape[1]
                for d in range(8):
                    turned = pltpu.roll(vec, (tall - piece * d) % tall, axis=1)[:, : gw.shape[3]]
                    for shard in range(4):
                        block = pltpu.roll(turned, (16 - 3 * shard) % 16, axis=0) if shard else turned
                        gw[shard, d, piece:, :] = block.astype(BF)
            for ref, part in ((gs_ref, 1), (gk_ref, 0)):
                for ry in range(2):
                    for d in range(8):
                        ref[ry, spot(d, own_d)] = gw[own_s ^ (2 * ry + part), d]


def attend_back(group, pairs, own, e, q, k, v, grad_mixed, mixed, rinv, x_t, after, gw=None, last=True, vecs=()):
    first = gw is None
    rows, width = q.shape
    slab = k.shape[0]
    piece = width // 8
    span = WIDTHS[group]
    own = jnp.concatenate([own, jnp.array(pairs, jnp.int32)])
    full = lambda shape: pl.BlockSpec(shape, lambda i, own: (0,) * len(shape))
    cols = lambda r: pl.BlockSpec((r, LANES), lambda i, own: (0, own[2 + i]))
    inputs = [e, q, k, v, grad_mixed, mixed, rinv, x_t, after]
    in_specs = [
        pl.BlockSpec((2, rows, slab), lambda i, own: (own[2 + i], 0, 0)),
        cols(rows), cols(slab), cols(slab), cols(rows), cols(rows), cols(rows), full(x_t.shape),
        pl.BlockSpec(memory_space=pl.ANY),
    ]
    out_shape = [
        jax.ShapeDtypeStruct((rows, len(pairs) * LANES), BF),
        jax.ShapeDtypeStruct((len(pairs) * 2 * LANES, slab), BF),
        jax.ShapeDtypeStruct((8, len(pairs) * LANES), F32),
    ]
    out_specs = [
        pl.BlockSpec((rows, LANES), lambda i, own: (0, i)),
        pl.BlockSpec((2 * LANES, slab), lambda i, own: (i, 0)),
        pl.BlockSpec((8, LANES), lambda i, own: (0, i)),
    ]
    scratch = []
    whole = (4, 8, piece + (16 if vecs else 0), span)
    if not first:
        inputs.append(gw)
        in_specs.append(full(whole))
    inputs += vecs
    in_specs += [full(a.shape) for a in vecs]
    if last:
        out_shape += [jax.ShapeDtypeStruct((2, *whole[1:]), BF)] * 2
        out_specs += [full((2, *whole[1:]))] * 2
        scratch.append(pltpu.VMEM(whole, BF))
        if vecs:
            scratch.append(pltpu.VMEM((16, width), F32))
    else:
        out_shape.append(jax.ShapeDtypeStruct(whole, BF))
        out_specs.append(full(whole))
    return pl.pallas_call(
        functools.partial(back_kernel, group, pairs, first, last),
        grid_spec=pltpu.PrefetchScalarGridSpec(
            num_scalar_prefetch=1, grid=(len(pairs),), in_specs=in_specs, out_specs=out_specs, scratch_shapes=scratch
        ),
        out_shape=out_shape,
        compiler_params=params(), cost_estimate=cost(12),
        name="attend_back",
    )(own, *inputs)


def frames_kernel(pairs, last, w_ref, gx_in_ref, after_ref, *refs):
    n = len(pairs)
    dqs, dkvs = refs[:n], refs[n : 2 * n]
    refs = list(refs[2 * n :])
    dx_ref = refs.pop(0) if last else None
    gx_ref, *outs, wkv = refs
    j = pl.program_id(0)
    width = gx_ref.shape[1]
    flat = [p for call in pairs for p in call]

    @pl.when(j == 0)
    def _():
        for i, p in enumerate(flat):
            for t in range(2):
                start = (1 + t) * width + p * LANES
                wkv[:, (2 * i + t) * LANES : (2 * i + t + 1) * LANES] = w_ref[:, start : start + LANES]
        wq = jnp.concatenate([w_ref[:, p * LANES : (p + 1) * LANES] for p in flat], axis=1)
        dq = jnp.concatenate([r[...] for r in dqs], axis=1)
        gx_ref[...] = gx_in_ref[...] + dot_t(dq, wq)

    made = dot(wkv[...], jnp.concatenate([r[...] for r in dkvs], axis=0))
    if not last:
        outs[0][0] = made
        return
    made = made + dx_ref[0]

    @pl.when(j < 2)
    def _():
        outs[0][0] = made.astype(BF)

    @pl.when(j >= 2)
    def _():
        outs[1][0] = made


def frames_back(input_weight, gx, after, pairs, dqs, dkvs, dx=None):
    rows, width = gx.shape
    last = dx is not None
    count = 2 * sum(map(len, pairs))
    full = lambda a: pl.BlockSpec(a.shape, lambda j: (0,) * a.ndim)
    column = lambda a: pl.BlockSpec((a.shape[0], rows), lambda j: (0, lax.rem(j + 2, 4)))
    block = lambda pick: pl.BlockSpec((1, width, rows), lambda j: (pick(j), 0, 0))
    if last:
        out_specs = [block(lambda j: jnp.minimum(j, 1)), block(lambda j: jnp.maximum(j - 2, 0))]
        out_shape = [jax.ShapeDtypeStruct((2, width, rows), BF), jax.ShapeDtypeStruct((2, width, rows), F32)]
    else:
        out_specs = [block(lambda j: j)]
        out_shape = [jax.ShapeDtypeStruct((4, width, rows), F32)]
    return pl.pallas_call(
        functools.partial(frames_kernel, pairs, last),
        grid=(4,),
        in_specs=[
            full(input_weight), full(gx), pl.BlockSpec(memory_space=pl.ANY), *map(full, dqs), *map(column, dkvs),
            *([block(lambda j: j)] if last else []),
        ],
        out_specs=[full(gx), *out_specs],
        out_shape=[jax.ShapeDtypeStruct((rows, width), F32), *out_shape],
        scratch_shapes=[pltpu.VMEM((width, count * LANES), BF)],
        compiler_params=params(), cost_estimate=cost(4 if last else 8),
        name="frames_back",
    )(input_weight, gx, after, *dqs, *dkvs, *([dx] if last else []))


def frames_end_kernel(gx_ref, keep_ref, came_ref, out_ref):
    out_ref[...] = gx_ref[...] + (keep_ref[0] + came_ref[0].astype(F32)).T


def frames_end(gx, keep, came):
    rows, width = gx.shape
    across = pl.BlockSpec((rows, LANES), lambda p: (0, p))
    down = pl.BlockSpec((1, LANES, rows), lambda p: (0, p, 0))
    return pl.pallas_call(
        frames_end_kernel,
        grid=(width // LANES,), in_specs=[across, down, down], out_specs=across,
        out_shape=jax.ShapeDtypeStruct((rows, width), F32), compiler_params=params(), cost_estimate=cost(5), name="frames_end",
    )(gx, keep, came)


def gather_kernel(plan, *refs):
    start, out = 0, sum(n for n, _ in plan) + 1
    for n, outs in plan:
        ins = refs[start : start + n]
        start += n
        for parts in outs:
            for i, part in enumerate(parts):
                terms = [r[part].astype(F32) for r in ins]
                while len(terms) > 1:
                    terms = [terms[t] + terms[t + 1] for t in range(0, len(terms), 2)]
                refs[out][i] = terms[0].astype(refs[out].dtype)
            out += 1


def gather(sums, after, steps=2):
    inputs, in_specs, out_shape, out_specs, plan = [], [], [], [], []
    for arrays, count, outs in sums:
        cols = arrays[0].shape[-1]
        rows = arrays[0].size // cols // count
        plan.append((len(arrays), tuple(parts for parts, _ in outs)))
        for a in arrays:
            inputs.append(a.reshape(count, rows, cols))
            in_specs.append(pl.BlockSpec((count, rows // steps, cols), lambda i: (0, i, 0)))
        for parts, kind in outs:
            out_shape.append(jax.ShapeDtypeStruct((len(parts), rows, cols), kind))
            out_specs.append(pl.BlockSpec((len(parts), rows // steps, cols), lambda i: (0, i, 0)))
    outs = pl.pallas_call(
        functools.partial(gather_kernel, plan),
        grid=(steps,), in_specs=[*in_specs, pl.BlockSpec(memory_space=pl.ANY)], out_specs=out_specs,
        out_shape=out_shape, compiler_params=params(), cost_estimate=cost(3), name="gather",
    )(*inputs, after)
    made = []
    for _, parts in plan:
        made.append(outs[: len(parts)])
        outs = outs[len(parts) :]
    return made


def finish_kernel(counts, own_ref, *refs):
    sums = []
    for n in counts:
        parts = [r[0].astype(F32) for r in refs[:n]]
        refs = refs[n:]
        while len(parts) > 1:
            parts = [parts[t] + parts[t + 1] for t in range(0, len(parts), 2)]
        sums.append(parts[0])
    inp_ref, out_ref, exp_ref, red_ref, vec_ref, sq_ref = refs
    red, exp, in1, in2 = sums
    rows = in1.shape[0]
    vec = in2[rows : rows + vec_ref.shape[0], : vec_ref.shape[1]]
    vec_ref[...] = vec
    in2 = in2[:rows]
    even = jnp.concatenate([in1[:, :128], in2[:, :128], in1[:, 128:], in2[:, 128:]], axis=1)
    odd = jnp.concatenate([in2[:, :128], in1[:, :256], in2[:, 128:], in1[:, 256:]], axis=1)
    odd = pltpu.roll(odd, odd.shape[1] - HD, axis=1)
    inp = jnp.where((own_ref[0] & 1) == 1, odd, even)[:, : inp_ref.shape[1]]
    tall = exp_ref.shape[0]
    out = exp[tall:, :]
    half = out_ref.shape[1]
    out = jnp.concatenate([out[:, :half], pltpu.roll(out, half, axis=1)[:, :half]], axis=0)
    inp_ref[...] = inp
    out_ref[...] = out
    exp_ref[...] = exp[:tall, :]
    red_ref[...] = red
    squares = jnp.zeros((1, 1), F32)
    for g in (inp, out, exp[:tall, :], red, vec):
        squares = squares + jnp.sum(jnp.sum(g * g, axis=0, keepdims=True), axis=1, keepdims=True)
    sq_ref[...] = jnp.broadcast_to(squares, sq_ref.shape)


def finish(own, red, exp, in1, in2):
    piece = in1[0].shape[1]
    tall = exp[0].shape[1] - piece // 2
    vmem = pl.BlockSpec(memory_space=pltpu.VMEM)
    inputs = [*red, *exp, *in1, *in2]
    return pl.pallas_call(
        functools.partial(finish_kernel, tuple(map(len, (red, exp, in1, in2)))),
        in_specs=[pl.BlockSpec(memory_space=pltpu.SMEM), *[vmem] * len(inputs)],
        out_specs=[vmem] * 6,
        out_shape=[
            jax.ShapeDtypeStruct((piece, 9 * HD), F32),
            jax.ShapeDtypeStruct((piece, 3 * HD), F32),
            jax.ShapeDtypeStruct((tall, exp[0].shape[2]), F32),
            jax.ShapeDtypeStruct(red[0].shape[1:], F32),
            jax.ShapeDtypeStruct((3, piece), F32),
            jax.ShapeDtypeStruct((8, LANES), F32),
        ],
        compiler_params=params(), cost_estimate=cost(3), name="finish",
    )(own, *inputs)


def adam_step(master, moment_one, moment_two, gradient, step_rate, decay_weight):
    new_one = 0.9 * moment_one + 0.1 * gradient
    new_two = 0.999 * moment_two + 0.001 * gradient * gradient
    corrected_one = new_one / (1.0 - 0.9**STEP)
    corrected_two = new_two / (1.0 - 0.999**STEP)
    new_master = master - step_rate * (
        corrected_one / (jnp.sqrt(corrected_two) + 1e-08) + decay_weight * master
    )
    return (new_one, new_two, new_master, new_master.astype(BF))


def adam_kernel(rates, turned, squares_ref, *refs):
    n = len(rates)
    ins, outs = refs[: 4 * n], refs[4 * n :]
    norm = jnp.sqrt(squares_ref[0:1, 0:1])
    outs[0][...] = norm
    factor = 1.0 / jnp.maximum(norm, 1.0)
    for a in range(n):
        master, one, two, grad = (r[...] for r in ins[4 * a : 4 * a + 4])
        if turned[a]:
            grad = grad.T
        made = adam_step(master, one, two, grad * factor, rates[a][0], rates[a][1])
        for b in range(4):
            outs[1 + 4 * a + b][...] = made[b]


def adam_all(squares, states, grads, rates, turned):
    inputs, out_shape = [squares], [jax.ShapeDtypeStruct((1, 1), F32)]
    for state, grad in zip(states, grads):
        inputs += [*state, grad]
        shape = state[0].shape
        out_shape += [jax.ShapeDtypeStruct(shape, F32)] * 3 + [jax.ShapeDtypeStruct(shape, BF)]
    vmem = pl.BlockSpec(memory_space=pltpu.VMEM)
    return pl.pallas_call(
        functools.partial(adam_kernel, rates, turned),
        in_specs=[vmem] * len(inputs), out_specs=[vmem] * len(out_shape), out_shape=out_shape,
        compiler_params=params(), cost_estimate=cost(5), name="adam",
    )(*inputs)


def mover(dp, seq):
    def move(value, bits_d, bits_s):
        pairs = [(d * seq + s, (d ^ bits_d) * seq + (s ^ bits_s)) for d in range(dp) for s in range(seq)]
        return lax.ppermute(value, AXES, pairs)

    return move


def tree_sum(move, value):
    value = value + move(value, 0, 1)
    value = (value + move(value, 0, 2)) + (move(value, 1, 0) + move(value, 1, 2))
    return (value + move(value, 2, 0)) + (move(value, 4, 0) + move(value, 6, 0))


def spread_out(move, parts):
    return [parts[0], *(move(parts[b], 2 * b, 0) for b in (1, 2, 3))]


def plane(move, parts):
    return [parts[0], move(parts[1], 1, 0), move(parts[2], 0, 2), move(parts[3], 1, 2)]


def scatter_plain(parts, dim):
    part = lax.psum_scatter(parts, "seq", scatter_dimension=0, tiled=True)[0].astype(F32)
    return lax.psum_scatter(part, "dp", scatter_dimension=dim, tiled=True)


def in_order(kept, sent):
    parts = jnp.stack([kept, sent], axis=1)
    rows, cols = parts.shape[-2:]
    return parts.reshape(4, 2, 4, rows, cols).swapaxes(1, 2).reshape(4, 8 * rows, cols)


HALVES = tuple((parts, BF) for parts in ((0, 2), (4, 6), (1, 5), (3, 7)))
PAIR = (((0,), BF), ((1,), BF))
QUARTERS = tuple(((part,), BF) for part in range(4))
ONE = (((0,), BF),)
Z_HALVES = (((0, 1), BF), ((2, 3), BF))


def both_ways(move, cut):
    y_keep, y_send, x_keep, x_send = cut
    return (y_keep, move(y_send, 0, 2)), (x_keep, move(x_send, 1, 0))


def turned_ways(move, y_cut, x_cut):
    return (y_cut[0], move(y_cut[1], 1, 0)), (x_cut[0], move(x_cut[1], 0, 2))


def reduce_fast(move, own, back, behind_of, input_weight, gbt, act, red_s, vec1):
    red_c = move(red_s, 0, 1)
    red_k = reduce_kept(own, gbt, act)
    (red,) = gather([((red_k, red_c), 8, HALVES)], red_k)
    red_y, red_x = both_ways(move, red)

    gf, grad_mixed, exp_s, exp_k, vec2 = behind_of(red[0])
    exp_c = move(exp_s, 0, 1)
    red_y, red_x = gather([(red_y, 2, PAIR), (red_x, 2, PAIR)], vec2)
    red_y, red_x = turned_ways(move, red_y, red_x)

    dq0, dkv0, vb0, gw = back(0, CALLS[0], grad_mixed, red_y[0], last=False)
    (red_k,), (red_s,), exp = gather([(red_y, 1, ONE), (red_x, 1, ONE), ((exp_k, exp_c), 8, HALVES)], vb0)
    red = red_k, move(red_s, 4, 0)
    exp_y, exp_x = both_ways(move, exp)

    dq1, dkv1, vb1, in_s1, in_k1 = back(0, CALLS[1], grad_mixed, red_k, gw=gw)
    in_c1 = move(in_s1, 0, 1)
    (red_k, red_s), exp_y, exp_x = gather([(red, 2, PAIR), (exp_y, 2, PAIR), (exp_x, 2, PAIR)], vb1)
    red = red_k, move(red_s, 2, 0)
    exp_y, exp_x = turned_ways(move, exp_y, exp_x)

    gx, dx = frames_back(input_weight, gf, red_k, CALLS[:2], (dq0, dq1), (dkv0, dkv1))
    (exp_k,), (exp_s,), in1 = gather([(exp_y, 1, ONE), (exp_x, 1, ONE), ((in_k1, in_c1), 4, QUARTERS)], gx)
    exp = exp_k, move(exp_s, 4, 0)
    in1 = plane(move, in1)

    dq2, dkv2, vb2, in_s2, in_k2 = back(1, CALLS[2], grad_mixed, exp_k, vecs=(vec1, vec2, vb0, vb1))
    in_c2 = move(in_s2, 0, 1)
    (exp_k, exp_s), (in1_k, in1_s) = gather([(exp, 2, PAIR), (in1, 4, Z_HALVES)], vb2, 1)
    in1 = in1_k, move(in1_s, 4, 0)
    (in2,) = gather([((in_k2, in_c2), 4, QUARTERS)], exp_k, 1)
    in2 = plane(move, in2)

    gx, dx_s, dx_k = frames_back(input_weight, gx, in2[0], CALLS[2:], (dq2,), (dkv2,), dx)
    dx_c = move(dx_s, 0, 1)
    in2, (in1_k, in1_s) = gather([(in2, 4, QUARTERS), (in1, 2, PAIR)], gx, 1)
    in2 = spread_out(move, in2)
    in1 = in1_k, move(in1_s, 2, 0)
    exp = exp_k, move(exp_s, 2, 0)
    ((dx_k, dx_s),) = gather([((dx_k, dx_c), 2, (((0,), F32), ((1,), BF)))], in1_k)
    return red, exp, in1, in2, gx, (dx_k, move(dx_s, 0, 2))


def reduce_plain(move, own, back, behind_of, input_weight, gbt, act, red_s, vec1):
    red_k = reduce_kept(own, gbt, act)
    gf, grad_mixed, exp_s, exp_k, vec2 = behind_of(red_k)
    dq0, dkv0, vb0, gw = back(0, CALLS[0], grad_mixed, vec2, last=False)
    dq1, dkv1, vb1, in_s1, in_k1 = back(0, CALLS[1], grad_mixed, vb0, gw=gw)
    dq2, dkv2, vb2, in_s2, in_k2 = back(1, CALLS[2], grad_mixed, vb1, vecs=(vec1, vec2, vb0, vb1))
    gx, dx = frames_back(input_weight, gf, vb2, CALLS[:2], (dq0, dq1), (dkv0, dkv1))
    gx, dx_s, dx_k = frames_back(input_weight, gx, vb2, CALLS[2:], (dq2,), (dkv2,), dx)
    ((dx_keep, dx_send),) = gather([((dx_k, move(dx_s, 0, 1)), 2, (((0,), F32), ((1,), BF)))], vb2)
    dx = dx_keep, move(dx_send, 0, 2)
    red = scatter_plain(in_order(red_k, red_s), 0)
    in1 = scatter_plain(in_order(in_k1, in_s1), 0)
    both = in_order(in_k2, in_s2)
    both = both.reshape(4, 8, -1, both.shape[-1])
    piece = in_k1.shape[2]
    in2 = scatter_plain(both[:, :, :piece].reshape(4, 8 * piece, -1), 0)
    vec = scatter_plain(both[:, :, piece : piece + 3, :piece].swapaxes(1, 2).reshape(4, 3, -1), 1)
    both = jnp.stack([exp_k, exp_s], axis=1).transpose(0, 1, 3, 2, 4, 5)
    tall, wide = both.shape[-2] - piece // 2, both.shape[-1]
    both = both.reshape(4, 8, -1, wide)
    exp = scatter_plain(both[:, :, :tall].swapaxes(1, 2).reshape(4, tall, 8 * wide), 1)
    out = both[:, :, tall:].reshape(4, 8, piece // 2, 2, wide // 2).swapaxes(2, 3)
    out = scatter_plain(out.reshape(4, 8 * piece, wide // 2), 0)
    even = jnp.concatenate([in1[:, :128], in2[:, :128], in1[:, 128:], in2[:, 128:192]], axis=1)
    odd = jnp.concatenate([in2[:, 64:128], in1[:, :256], in2[:, 128:], in1[:, 256:]], axis=1)
    inp = jnp.where(lax.axis_index("seq") % 2 == 1, odd, even)
    squares = sum(jnp.sum(g * g) for g in (inp, out, exp, red, vec))
    squares = lax.psum(jnp.full((8, LANES), squares, F32), AXES)
    return inp, out, exp, red, vec, squares, gx, dx


def local(
    frames, cotangent, lengths,
    input_weight, output_weight, expand_weight, reduce_weight, vector_copy,
    *states,
):
    rows, width = frames.shape
    seq, dp = lax.axis_size("seq"), lax.axis_size("dp")
    slab = rows * seq
    move = mover(dp, seq)
    own_s, own_d = lax.axis_index("seq"), lax.axis_index("dp")
    fast = dp == 8
    vectors = vector_copy.astype(F32)

    across = move(frames, 0, 2)
    near = move(frames, 0, 1)
    far = move(across, 0, 1)

    first_end = lengths[0, 0]
    second_end = first_end + lengths[0, 1]
    third_end = second_end + lengths[0, 2]
    order = jnp.array([0, 2, 1, 3], jnp.int32) ^ own_s
    positions = (order[:, None] * rows + jnp.arange(rows, dtype=jnp.int32)[None, :]).reshape(slab, 1)
    segments = sum((positions >= end).astype(jnp.int32) for end in (first_end, second_end, third_end))
    lanes = jnp.arange(LANES, dtype=jnp.int32)[None, :]
    kmask = jnp.where((segments == lanes) | (lanes > 3), 0.0, MASK).astype(BF)
    qhot = (segments[:rows] == lanes).astype(BF)
    if fast:
        own = jnp.stack([own_s, own_d]).astype(jnp.int32)
    else:
        own = jnp.zeros((2,), jnp.int32)

    mixed, e, rinv, q, k, v, x_t = attend((frames, across, near, far), input_weight, vectors, kmask, qhot)
    layer, act, slope, norm1, inv1, hlt, mt, gs, gb, gbt, red_s, vec1 = ahead(
        own, mixed, frames, cotangent, qhot, output_weight, expand_weight, reduce_weight, vectors
    )

    def behind_of(after):
        return behind(
            own, slope, gb, gs, norm1, inv1, hlt, mt, output_weight, expand_weight, reduce_weight, vectors, after
        )

    def back(group, pairs, grad_mixed, after, **more):
        return attend_back(group, pairs, own, e, q, k, v, grad_mixed, mixed, rinv, x_t, after, **more)

    if fast:
        red, exp, in1, in2, gx, dx = reduce_fast(move, own, back, behind_of, input_weight, gbt, act, red_s, vec1)
        inp, out, exp, red, vec, squares = finish(own, red, exp, in1, in2)
        squares = tree_sum(move, squares)
    else:
        inp, out, exp, red, vec, squares, gx, dx = reduce_plain(
            move, own, back, behind_of, input_weight, gbt, act, red_s, vec1
        )
    frames_gradient = frames_end(gx, *dx)

    grads = [inp, out, exp, red, vec]
    masters, firsts, seconds = (list(states[i : i + 5]) for i in (0, 5, 10))
    for group in (masters, firsts, seconds):
        group[3] = group[3].T
    hidden = expand_weight.shape[1]
    wide, narrow = 2.0 * width**-0.5, 2.0 * hidden**-0.5
    norm, *made = adam_all(
        squares, list(zip(masters, firsts, seconds)), grads,
        ((wide, 0.01), (wide, 0.01), (wide, 0.01), (narrow, 0.01), (0.5, 0.0)),
        (False, True, False, False, False),
    )
    made[12:16] = [m.T for m in made[12:16]]
    return (layer, frames_gradient, norm.reshape(()), *made)


def solution(mesh):
    tokens, whole = P(("dp", "seq"), None), P()
    state = (P("dp", "seq"), *(P("seq", "dp"),) * 4)
    outs = tuple(s for s in state for _ in range(4))
    return jax.shard_map(
        local,
        mesh=mesh,
        in_specs=(tokens, tokens, P("dp", None), *(whole,) * 5, *state * 3),
        out_specs=(tokens, tokens, whole, *outs),
        check_vma=False,
    )
```

time: 331 us -> 262 us (0.79)
  waiting for transfers between devices: 71.3 us -> 28.9 us
  other arithmetic: 20.5 us -> 8.36 us
  starting transfers between devices: 49.8 us -> 42.2 us
  local copies, waits for them, and re-layouts: 19.5 us -> 14.4 us
    ppermute x49 -> x39, waiting for transfers between devices: 71.3 us -> 28.9 us  [move(): return lax.ppermute(value, AXES, pairs)]
    reduce_sum x5 -> x0, other arithmetic: 10.2 us -> none  [local(): squares = sum((jnp.sum(g * g) for g in grads))]
    ppermute x49 -> x39, starting transfers between devices: 49.8 us -> 42.2 us  [move(): return lax.ppermute(value, AXES, pairs)]
    unnamed x60 -> x70, local copies, waits for them, and re-layouts: 17.1 us -> 13 us
    pallas_call x21 -> x20, Pallas kernels: 157 us -> 160 us  [the longest x3 37.6 us: attend_back(): pl.pallas_call(functools.partial(back_kernel, group, pairs, first, last),...]
  transfers between devices with their start and end apart: 49 -> 39, of which waited for: 21 -> 12; matrix products, arithmetic and copies ran while one was open for 7% -> 4% of each run, Pallas kernels for 30% -> 39%
where the time goes in v2:
time: 262 us; the launch traced here: 261 us
  Pallas kernels  164 us (63%)
  starting transfers between devices  42.2 us (16%)
  waiting for transfers between devices  28.9 us (11%)
  local copies, waits for them, and re-layouts  14.4 us (5%)
  other arithmetic  8.36 us (3%)
  between operations  3.05 us (1%)
    ppermute x39, starting transfers between devices, move(): return lax.ppermute(value, AXES, pairs)  42.2 us
    pallas_call x3, Pallas kernels, attend_back(): pl.pallas_call(functools.partial(back_kernel, group, pairs, first, last),...  37.6 us
    pallas_call x1, Pallas kernels, attend(): pl.pallas_call(attend_kernel, grid=(pairs,), in_specs=[*map(full, blocks)...  28.9 us
    ppermute x39, waiting for transfers between devices, move(): return lax.ppermute(value, AXES, pairs)  28.9 us
    pallas_call x9, Pallas kernels, gather(): pl.pallas_call(functools.partial(gather_kernel, plan), grid=(steps,), in_...  27.1 us
    pallas_call x1, Pallas kernels, behind(): pl.pallas_call(behind_kernel, grid_spec=pltpu.PrefetchScalarGridSpec(num_...  18.2 us
    pallas_call x2, Pallas kernels, frames_back(): pl.pallas_call(functools.partial(frames_kernel, pairs, last), grid=(4,),...  18 us
    pallas_call x1, Pallas kernels, ahead(): pl.pallas_call(ahead_kernel, grid_spec=pltpu.PrefetchScalarGridSpec(num_s...  17.9 us
  transfers between devices with their start and end apart: 39, of which 12 were waited for; matrix products, arithmetic and copies ran while one was open for 4% of the time, Pallas kernels for 39%

profile of v2, /device:TPU:0, one launch (start us, length us, event | category | flops | bytes accessed | tf_op | source)
XLA Modules:
  0.0 261.2 jit_solution(13263579373509160407)
XLA Ops:
  0.7 3.0 %collective-permute-start = (bf16[384,768]{1,0:T(8,128)(2,1)}, bf16[384,768]{1,0:T(8,128)(2,1)S(1)}, u32[]{:S(2)}, u32[]{:S(2)}) collective-permute-start(bf16[384,768]{1,0:T(8,128)(2,1)} %x_ref.1), channel_id=1, source_target_pairs={{0,2},{1,3},{2,0},{3,1},{4,6},{5,7},{6,4},{7,5},{8,10},{9,11},{10,... | collective-permute-start | bytes 1769480 | tf_op jit(solution)/shard_map/ppermute | solution.py:733
  3.7 1.4 fusion.5
  8.4 0.8 fusion.1.qhot_ref
  9.2 8.1 %collective-permute-done.x1_ref = bf16[384,768]{1,0:T(8,128)(2,1)S(1)} collective-permute-done((bf16[384,768]{1,0:T(8,128)(2,1)}, bf16[384,768]{1,0:T(8,128)(2,1)S(1)}, u32[]{:S(2)}, u32[]{:S(2)}) %collective-permute-start) | collective-permute-done | bytes 589856 | tf_op jit(solution)/shard_map/ppermute | solution.py:733
  17.9 1.4 convert_element_type.57.vec_ref
  19.3 1.2 pad_add_fusion.4
  20.5 1.1 select_convert_fusion.kmask_ref
  21.6 0.8 copy-done.11
  22.4 0.8 copy-done.15
  23.2 28.9 %attend.1 = (bf16[384,768]{1,0:T(8,128)(2,1)}, bf16[12,384,1536]{2,1,0:T(8,128)(2,1)}, f32[384,768]{1,0:T(8,128)}, bf16[384,768]{1,0:T(8,128)(2,1)}, bf16[1536,7...) custom-call(bf16[384,768]{1,0:T(8,128)(2,1)} %x_ref.1, bf16[384,768]{1,0:T(8,128)(2,1)} %copy-done.10, ...), custom_call_target="tpu_custom_call" | custom-call | flops 127600001024 | tf_op jit(solution)/shard_map/attend/pallas_call | solution.py:98
  52.2 17.9 %ahead.1 = (bf16[384,768]{1,0:T(8,128)(2,1)}, bf16[4,384,768]{2,1,0:T(8,128)(2,1)}, f32[4,384,768]{2,1,0:T(8,128)}, f32[384,768]{1,0:T(8,128)}, f32[384,128]{1,0...) custom-call(s32[2]{0:T(128)} %pad_add_fusion.own_ref, ...), custom_call_target="tpu_custom_call" | custom-call | flops 88000004096 | tf_op jit(solution)/shard_map/ahead/pallas_call | solution.py:246
  71.2 4.5 %reduce_kept.1.refs_2_ = bf16[2,8,96,768]{3,2,1,0:T(8,128)(2,1)} custom-call(s32[2]{0:T(128)} %pad_add_fusion.own_ref, bf16[768,384]{1,0:T(8,128)(2,1)} %get-tuple-element.144.gbt_ref, bf16[4,384,768]{2,1,0:T(8,128)(2,1)} %get-tuple-element.145.act_ref), custom_call_target="tpu_custom_call" | custom-call | flops 22000001024 | tf_op jit(solution)/shard_map/reduce_kept/pallas_call | solution.py:146
  75.7 1.5 copy-done.3
  77.2 3.7 %gather.9 = (bf16[2,192,768]{2,1,0:T(8,128)(2,1)}, bf16[2,192,768]{2,1,0:T(8,128)(2,1)}, bf16[2,192,768]{2,1,0:T(8,128)(2,1)}, bf16[2,192,768]{2,1,0:T(8,128)(2,1)}) custom-call(bf16[8,192,768]{2,1,0:T(8,128)(2,1)} %bitcast.49, bf16[8,192,768]{2,1,0:T(8,128)(2,1)} %bitcast.34, bf16[2,8,96,768]{3,2,1,0:T(8,128)(2,1)} %reduce_kept.1.refs_2_), custom_call_target="tpu_custom_call" | custom-call | flops 13200000000 | tf_op jit(solution)/shard_map/gather/pallas_call | solution.py:625
  80.8 1.7 collective-permute-start.4
  82.5 1.5 collective-permute-start.5
  84.0 18.2 %behind.1 = (f32[384,768]{1,0:T(8,128)}, bf16[384,768]{1,0:T(8,128)(2,1)}, bf16[2,2,4,240,384]{4,3,2,1,0:T(8,128)(2,1)}, bf16[2,2,4,240,384]{4,3,2,1,0:T(8,128)(2,1)}, f32[16,768]{1,0:T(8,128)}) custom-call(s32[2]{0:T(128)} %pad_add_fusion.own_ref, f32[4,384,768]{2,1,0:T(8,128)} %get-tuple-element.137.slope_ref, bf16[384,768]{1,0:T(8,128)(2,1)} %get-tuple-element.138.gb_ref, ...), custom_call_target="tpu_custom_call" | custom-call | flops 79200002048 | tf_op jit(solution)/shard_map/behind/pallas_call | solution.py:354
  102.3 0.8 copy-done.12
  103.4 2.5 gather.10
  106.7 11.9 %attend_back.3 = (bf16[384,256]{1,0:T(8,128)(2,1)}, bf16[512,1536]{1,0:T(8,128)(2,1)}, f32[8,256]{1,0:T(8,128)}, bf16[4,8,96,384]{3,2,1,0:T(8,128)(2,1)}) custom-call(s32[4]{0:T(128)} %get-tuple-element.250.own_ref, bf16[12,384,1536]{2,1,0:T(8,128)(2,1)} %get-tuple-element.159.e_ref, bf16[384,768]{1,0:T(8,128)(2,1)} %get-tuple-element.160.q_ref, ...), custom_call_target="tpu_custom_call" | custom-call | flops 52800000000 | tf_op jit(solution)/shard_map/attend_back/pallas_call | solution.py:510
  119.4 0.9 copy-done.2
  120.3 4.7 %gather.11 = (bf16[1,192,768]{2,1,0:T(8,128)(2,1)}, bf16[1,192,768]{2,1,0:T(8,128)(2,1)}, bf16[2,480,384]{2,1,0:T(8,128)(2,1)}, bf16[2,480,384]{2,1,0:T(8,128)(2...) custom-call(bf16[1,192,768]{2,1,0:T(8,128)(2,1)} %get-tuple-element.153.rest_0_.refs_0_, ...), custom_call_target="tpu_custom_call" | custom-call | flops 13200000000 | tf_op jit(solution)/shard_map/gather/pallas_call | solution.py:625
  125.1 1.8 collective-permute-start.10
  126.8 1.5 collective-permute-start.11
  128.3 2.6 collective-permute-start.9
  130.9 13.3 %attend_back.4 = (bf16[384,256]{1,0:T(8,128)(2,1)}, bf16[512,1536]{1,0:T(8,128)(2,1)}, f32[8,256]{1,0:T(8,128)}, bf16[2,8,96,384]{3,2,1,0:T(8,128)(2,1)}, bf16[2,8,96,384]{3,2,1,0:T(8,128)(2,1)}) custom-call(s32[4]{0:T(128)} %get-tuple-element.249.own_ref, bf16[12,384,1536]{2,1,0:T(8,128)(2,1)} %get-tuple-element.159.e_ref, ...), custom_call_target="tpu_custom_call" | custom-call | flops 52800000000 | tf_op jit(solution)/shard_map/attend_back/pallas_call | solution.py:510
  146.0 3.1 %gather.12 = (bf16[1,96,768]{2,1,0:T(8,128)(2,1)}, bf16[1,96,768]{2,1,0:T(8,128)(2,1)}, bf16[1,480,384]{2,1,0:T(8,128)(2,1)}, bf16[1,480,384]{2,1,0:T(8,128)(2,1...) custom-call(bf16[2,96,768]{2,1,0:T(8,128)(2,1)} %bitcast.57, bf16[2,96,768]{2,1,0:T(8,128)(2,1)} %bitcast.44, ...), custom_call_target="tpu_custom_call" | custom-call | flops 13200000000 | tf_op jit(solution)/shard_map/gather/pallas_call | solution.py:625
  149.0 1.5 collective-permute-start.12
  151.1 1.6 collective-permute-start.26
  152.7 9.3 %frames_back.2 = (f32[384,768]{1,0:T(8,128)}, f32[4,768,384]{2,1,0:T(8,128)}) custom-call(bf16[768,2304]{1,0:T(8,128)(2,1)} %w_ref.3, f32[384,768]{1,0:T(8,128)} %get-tuple-element.148.gx_in_ref, bf16[1,96,768]{2,1,0:T(8,128)(2,1)} %get-tuple-element.175.after_ref.refs_0_, bf16[384,256]{1,0:T(8,128)(2,1)} %get-tuple-element.176.refs_0_, ...), custom_call_target="tpu_custom_call" | custom-call | flops 35200000000 | tf_op jit(solution)/shard_map/frames_back/pallas_call | solution.py:569
  163.3 3.2 %gather.13 = (bf16[1,480,384]{2,1,0:T(8,128)(2,1)}, bf16[1,480,384]{2,1,0:T(8,128)(2,1)}, bf16[1,384,384]{2,1,0:T(8,128)(2,1)}, bf16[1,384,384]{2,1,0:T(8,128)(2...) custom-call(bf16[1,480,384]{2,1,0:T(8,128)(2,1)} %get-tuple-element.181.refs_0_, ...), custom_call_target="tpu_custom_call" | custom-call | flops 13200000000 | tf_op jit(solution)/shard_map/gather/pallas_call | solution.py:625
  166.5 2.7 %collective-permute-start.16 = (bf16[1,480,384]{2,1,0:T(8,128)(2,1)}, bf16[1,480,384]{2,1,0:T(8,128)(2,1)S(1)}, u32[]{:S(2)}, u32[]{:S(2)}) collective-permute-start(bf16[1,480,384]{2,1,0:T(8,128)(2,1)} %get-tuple-element.191), channel_id=1, source_target_pairs={{0,16},{1,17},{2,18},{3,19},{4,20},{5,21},{6,22},{7,23},{8,24},{9,... | collective-permute-start | bytes 1105928 | tf_op jit(solution)/shard_map/ppermute | solution.py:733
  169.7 1.5 collective-permute-start.18
  171.2 1.4 collective-permute-start.19
  172.6 12.4 %attend_back.5 = (bf16[384,256]{1,0:T(8,128)(2,1)}, bf16[512,1536]{1,0:T(8,128)(2,1)}, f32[8,256]{1,0:T(8,128)}, bf16[2,8,112,256]{3,2,1,0:T(8,128)(2,1)}, bf16[2,8,112,256]{3,2,1,0:T(8,128)(2,1)}) custom-call(s32[4]{0:T(128)} %get-tuple-element.247.own_ref, bf16[12,384,1536]{2,1,0:T(8,128)(2,1)} %get-tuple-element.159.e_ref, ...), custom_call_target="tpu_custom_call" | custom-call | flops 52800000000 | tf_op jit(solution)/shard_map/attend_back/pallas_call | solution.py:510
  186.1 2.3 gather.14
  188.8 0.9 copy-done.7
  189.7 2.4 gather.15
  192.7 1.5 collective-permute-start.22
  194.2 1.4 collective-permute-start.23
  195.6 8.7 %frames_back.3 = (f32[384,768]{1,0:T(8,128)}, bf16[2,768,384]{2,1,0:T(8,128)(2,1)}, f32[2,768,384]{2,1,0:T(8,128)}) custom-call(bf16[768,2304]{1,0:T(8,128)(2,1)} %w_ref.3, f32[384,768]{1,0:T(8,128)} %get-tuple-element.180.refs_6_.gx_in_ref, bf16[1,448,256]{2,1,0:T(8,128)(2,1)} %get-tuple-element.198.after_ref, bf16[384,256]{1,0:T(8,128)(2,1)} %get-tuple-element.199.refs_0_, ...), custom_call_target="tpu_custom_call" | custom-call | flops 17600000000 | tf_op jit(solution)/shard_map/frames_back/pallas_call | solution.py:569
  204.4 1.8 collective-permute-start.27
  207.0 2.2 gather.16
  209.5 1.7 collective-permute-start.29
  211.2 2.2 collective-permute-start.30
  214.0 1.0 collective-permute-done.29.refs_7_
  215.0 1.5 collective-permute-done.30.refs_8_
  216.5 3.1 %collective-permute-done.31.refs_9_ = bf16[1,112,256]{2,1,0:T(8,128)(2,1)S(1)} collective-permute-done((bf16[1,112,256]{2,1,0:T(8,128)(2,1)}, bf16[1,112,256]{2,1,0:T(8,128)(2,1)S(1)}, u32[]{:S(2)}, u32[]{:S(2)}) %collective-permute-start.31) | collective-permute-done | bytes 57376 | tf_op jit(solution)/shard_map/ppermute | solution.py:733
  220.3 2.4 finish.1
  222.7 1.4 collective-permute-done.32
  224.7 0.9 collective-permute-start.33
  225.7 1.5 collective-permute-start.34
  227.1 1.1 collective-permute-start.35
  228.3 0.9 collective-permute-done.34
  229.3 2.4 collective-permute-done.35
  231.6 1.3 collective-permute-start.37
  232.9 3.1 %collective-permute-start.38 = (f32[8,128]{1,0:T(8,128)S(1)}, f32[8,128]{1,0:T(8,128)S(1)}, u32[]{:S(2)}, u32[]{:S(2)}) collective-permute-start(f32[8,128]{1,0:T(8,128)S(1)} %add_add_fusion.1), channel_id=1, source_target_pairs={{0,24},{1,25},{2,26},{3,27},{4,28},{5,29},{6,30},{7,31},{8,16},{9,... | collective-permute-start | bytes 12296 | tf_op jit(solution)/shard_map/ppermute | solution.py:733
  236.2 2.1 collective-permute-done.38
  238.9 1.0 copy-done.5
  239.9 3.0 %gather.17 = (f32[1,768,384]{2,1,0:T(8,128)}, bf16[1,768,384]{2,1,0:T(8,128)(2,1)}) custom-call(f32[2,768,384]{2,1,0:T(8,128)} %get-tuple-element.203.refs_0_, bf16[2,768,384]{2,1,0:T(8,128)(2,1)} %copy-done.5, bf16[1,96,384]{2,1,0:T(8,128)(2,1)} %get-tuple-element.210.refs_2_.refs_4_), custom_call_target="tpu_custom_call" | custom-call | flops 13200000000 | tf_op jit(solution)/shard_map/gather/pallas_call | solution.py:625
  243.4 4.4 %adam.1 = (f32[1,1]{1,0:T(1,128)}, f32[96,576]{1,0:T(8,128)}, f32[96,576]{1,0:T(8,128)}, f32[96,576]{1,0:T(8,128)}, bf16[96,576]{1,0:T(8,128)(2,1)}, /*index=5*/...) custom-call(f32[8,128]{1,0:T(8,128)} %add_add_fusion.squares_ref, ...), custom_call_target="tpu_custom_call" | custom-call | flops 22000001024 | tf_op jit(solution)/shard_map/adam/pallas_call | solution.py:723
  247.9 7.3 %collective-permute-done.25.came_ref = bf16[1,768,384]{2,1,0:T(8,128)(2,1)S(1)} collective-permute-done((bf16[1,768,384]{2,1,0:T(8,128)(2,1)}, bf16[1,768,384]{2,1,0:T(8,128)(2,1)S(1)}, u32[]{:S(2)}, u32[]{:S(2)}) %collective-permute-start.25) | collective-permute-done | bytes 589856 | tf_op jit(solution)/shard_map/ppermute | solution.py:733
  255.1 0.8 copy-done.13
  256.0 5.2 %frames_end.1 = f32[384,768]{1,0:T(8,128)} custom-call(f32[384,768]{1,0:T(8,128)} %get-tuple-element.202.refs_6_.gx_ref, f32[1,768,384]{2,1,0:T(8,128)} %get-tuple-element.211.keep_ref, bf16[1,768,384]{2,1,0:T(8,128)(2,1)} %copy-done.13), custom_call_target="tpu_custom_call" | custom-call | flops 22000001024 | tf_op jit(solution)/shard_map/frames_end/pallas_call | solution.py:592
  (121 shorter events, 15.5 us)
Async XLA Ops:
  0.7 16.6 %collective-permute-start = (bf16[384,768]{1,0:T(8,128)(2,1)}, bf16[384,768]{1,0:T(8,128)(2,1)S(1)}, u32[]{:S(2)}, u32[]{:S(2)}) collective-permute-start(bf16[384,768]{1,0:T(8,128)(2,1)} %x_ref.1), channel_id=1, source_target_pairs={{0,2},{1,3},{2,0},{3,1},{4,6},{5,7},{6,4},{7,5},{8,10},{9,11},{10,... | collective-permute-start | bytes 1769480 | tf_op jit(solution)/shard_map/ppermute | solution.py:733
  3.7 17.9 %collective-permute-start.1 = (bf16[384,768]{1,0:T(8,128)(2,1)}, bf16[384,768]{1,0:T(8,128)(2,1)S(1)}, u32[]{:S(2)}, u32[]{:S(2)}) collective-permute-start(bf16[384,768]{1,0:T(8,128)(2,1)} %x_ref.1), channel_id=1, source_target_pairs={{0,1},{1,0},{2,3},{3,2},{4,5},{5,4},{6,7},{7,6},{8,9},{9,8},{10,11... | collective-permute-start | bytes 1769480 | tf_op jit(solution)/shard_map/ppermute | solution.py:733
  17.2 4.4 %copy-start.10 = (bf16[384,768]{1,0:T(8,128)(2,1)}, bf16[384,768]{1,0:T(8,128)(2,1)S(1)}, u32[]{:S(2)}) copy-start(bf16[384,768]{1,0:T(8,128)(2,1)S(1)} %collective-permute-done.x1_ref) | copy-start | bytes 1769476
  17.2 4.4 %collective-permute-start.2 = (bf16[384,768]{1,0:T(8,128)(2,1)S(1)}, bf16[384,768]{1,0:T(8,128)(2,1)S(1)}, u32[]{:S(2)}, u32[]{:S(2)}) collective-permute-start(bf16[384,768]{1,0:T(8,128)(2,1)S(1)} %collective-permute-done.x1_ref), channel_id=1, source_target_pairs={{0,1},{1,0},{2,3},{3,2},{4,5},{5,4},{6,7},{7,6},{8,9},{9,8},{10,11... | collective-permute-start | bytes 1769480 | tf_op jit(solution)/shard_map/ppermute | solution.py:733
  21.6 0.8 copy-start.11
  22.4 0.8 copy-start.15
  52.1 18.4 %copy-start = (s32[4]{0:T(128)S(1)}, s32[4]{0:T(128)}, u32[]{:S(2)}) copy-start(s32[4]{0:T(128)} %get-tuple-element.248) | copy-start | bytes 52
  52.1 18.4 %copy-start.1 = (s32[2]{0:T(128)S(1)}, s32[2]{0:T(128)}, u32[]{:S(2)}) copy-start(s32[2]{0:T(128)} %constant.28.clone) | copy-start | bytes 28
  70.1 5.6 %collective-permute-start.3 = (bf16[2,8,96,768]{3,2,1,0:T(8,128)(2,1)}, bf16[2,8,96,768]{3,2,1,0:T(8,128)(2,1)S(1)}, u32[]{:S(2)}, u32[]{:S(2)}) collective-permute-start(bf16[2,8,96,768]{3,2,1,0:T(8,128)(2,1)} %get-tuple-element.146), channel_id=1, source_target_pairs={{0,1},{1,0},{2,3},{3,2},{4,5},{5,4},{6,7},{7,6},{8,9},{9,8},{10,11... | collective-permute-start | bytes 7077896 | tf_op jit(solution)/shard_map/ppermute | solution.py:733
  75.7 1.5 copy-start.3
  80.8 21.5 %collective-permute-start.4 = (bf16[2,192,768]{2,1,0:T(8,128)(2,1)}, bf16[2,192,768]{2,1,0:T(8,128)(2,1)S(1)}, u32[]{:S(2)}, u32[]{:S(2)}) collective-permute-start(bf16[2,192,768]{2,1,0:T(8,128)(2,1)} %get-tuple-element.149), channel_id=1, source_target_pairs={{0,2},{1,3},{2,0},{3,1},{4,6},{5,7},{6,4},{7,5},{8,10},{9,11},{10,... | collective-permute-start | bytes 1769480 | tf_op jit(solution)/shard_map/ppermute | solution.py:733
  82.5 19.8 %collective-permute-start.5 = (bf16[2,192,768]{2,1,0:T(8,128)(2,1)}, bf16[2,192,768]{2,1,0:T(8,128)(2,1)S(1)}, u32[]{:S(2)}, u32[]{:S(2)}) collective-permute-start(bf16[2,192,768]{2,1,0:T(8,128)(2,1)} %get-tuple-element.151), channel_id=1, source_target_pairs={{0,4},{1,5},{2,6},{3,7},{4,0},{5,1},{6,2},{7,3},{8,12},{9,13},{10,... | collective-permute-start | bytes 1769480 | tf_op jit(solution)/shard_map/ppermute | solution.py:733
  102.2 16.4 %collective-permute-start.8 = (bf16[2,2,4,240,384]{4,3,2,1,0:T(8,128)(2,1)}, bf16[2,2,4,240,384]{4,3,2,1,0:T(8,128)(2,1)S(1)}, u32[]{:S(2)}, u32[]{:S(2)}) collective-permute-start(bf16[2,2,4,240,384]{4,3,2,1,0:T(8,128)(2,1)} %get-tuple-element.158), channel_id=1, source_target_pairs={{0,1},{1,0},{2,3},{3,2},{4,5},{5,4},{6,7},{7,6},{8,9},{9,8},{10,11... | collective-permute-start | bytes 8847368 | tf_op jit(solution)/shard_map/ppermute | solution.py:733
  102.3 0.8 copy-start.12
  102.3 1.0 copy-start.14
  105.8 12.7 %collective-permute-start.6 = (bf16[1,192,768]{2,1,0:T(8,128)(2,1)}, bf16[1,192,768]{2,1,0:T(8,128)(2,1)S(1)}, u32[]{:S(2)}, u32[]{:S(2)}) collective-permute-start(bf16[1,192,768]{2,1,0:T(8,128)(2,1)} %get-tuple-element.154), channel_id=1, source_target_pairs={{0,4},{1,5},{2,6},{3,7},{4,0},{5,1},{6,2},{7,3},{8,12},{9,13},{10,... | collective-permute-start | bytes 884744 | tf_op jit(solution)/shard_map/ppermute | solution.py:733
  106.4 12.2 %collective-permute-start.7 = (bf16[1,192,768]{2,1,0:T(8,128)(2,1)}, bf16[1,192,768]{2,1,0:T(8,128)(2,1)S(1)}, u32[]{:S(2)}, u32[]{:S(2)}) collective-permute-start(bf16[1,192,768]{2,1,0:T(8,128)(2,1)} %get-tuple-element.156), channel_id=1, source_target_pairs={{0,2},{1,3},{2,0},{3,1},{4,6},{5,7},{6,4},{7,5},{8,10},{9,11},{10,... | collective-permute-start | bytes 884744 | tf_op jit(solution)/shard_map/ppermute | solution.py:733
  118.6 1.7 copy-start.2
  125.1 19.3 %collective-permute-start.10 = (bf16[2,480,384]{2,1,0:T(8,128)(2,1)}, bf16[2,480,384]{2,1,0:T(8,128)(2,1)S(1)}, u32[]{:S(2)}, u32[]{:S(2)}) collective-permute-start(bf16[2,480,384]{2,1,0:T(8,128)(2,1)} %get-tuple-element.170), channel_id=1, source_target_pairs={{0,2},{1,3},{2,0},{3,1},{4,6},{5,7},{6,4},{7,5},{8,10},{9,11},{10,... | collective-permute-start | bytes 2211848 | tf_op jit(solution)/shard_map/ppermute | solution.py:733
  126.8 18.3 %collective-permute-start.11 = (bf16[2,480,384]{2,1,0:T(8,128)(2,1)}, bf16[2,480,384]{2,1,0:T(8,128)(2,1)S(1)}, u32[]{:S(2)}, u32[]{:S(2)}) collective-permute-start(bf16[2,480,384]{2,1,0:T(8,128)(2,1)} %get-tuple-element.172), channel_id=1, source_target_pairs={{0,4},{1,5},{2,6},{3,7},{4,0},{5,1},{6,2},{7,3},{8,12},{9,13},{10,... | collective-permute-start | bytes 2211848 | tf_op jit(solution)/shard_map/ppermute | solution.py:733
  128.3 16.0 %collective-permute-start.9 = (bf16[1,192,768]{2,1,0:T(8,128)(2,1)}, bf16[1,192,768]{2,1,0:T(8,128)(2,1)S(1)}, u32[]{:S(2)}, u32[]{:S(2)}) collective-permute-start(bf16[1,192,768]{2,1,0:T(8,128)(2,1)} %get-tuple-element.168), channel_id=1, source_target_pairs={{0,16},{1,17},{2,18},{3,19},{4,20},{5,21},{6,22},{7,23},{8,24},{9,... | collective-permute-start | bytes 884744 | tf_op jit(solution)/shard_map/ppermute | solution.py:733
  144.2 17.7 %collective-permute-start.14 = (bf16[2,8,96,384]{3,2,1,0:T(8,128)(2,1)}, bf16[2,8,96,384]{3,2,1,0:T(8,128)(2,1)S(1)}, u32[]{:S(2)}, u32[]{:S(2)}) collective-permute-start(bf16[2,8,96,384]{3,2,1,0:T(8,128)(2,1)} %get-tuple-element.186), channel_id=1, source_target_pairs={{0,1},{1,0},{2,3},{3,2},{4,5},{5,4},{6,7},{7,6},{8,9},{9,8},{10,11... | collective-permute-start | bytes 3538952 | tf_op jit(solution)/shard_map/ppermute | solution.py:733
  144.3 0.8 copy-start.22
  144.3 0.9 copy-start.8
  145.1 0.9 copy-start.9
  149.0 12.9 %collective-permute-start.12 = (bf16[1,480,384]{2,1,0:T(8,128)(2,1)}, bf16[1,480,384]{2,1,0:T(8,128)(2,1)S(1)}, u32[]{:S(2)}, u32[]{:S(2)}) collective-permute-start(bf16[1,480,384]{2,1,0:T(8,128)(2,1)} %get-tuple-element.182), channel_id=1, source_target_pairs={{0,4},{1,5},{2,6},{3,7},{4,0},{5,1},{6,2},{7,3},{8,12},{9,13},{10,... | collective-permute-start | bytes 1105928 | tf_op jit(solution)/shard_map/ppermute | solution.py:733
  150.6 11.4 %collective-permute-start.13 = (bf16[1,480,384]{2,1,0:T(8,128)(2,1)}, bf16[1,480,384]{2,1,0:T(8,128)(2,1)S(1)}, u32[]{:S(2)}, u32[]{:S(2)}) collective-permute-start(bf16[1,480,384]{2,1,0:T(8,128)(2,1)} %get-tuple-element.184), channel_id=1, source_target_pairs={{0,2},{1,3},{2,0},{3,1},{4,6},{5,7},{6,4},{7,5},{8,10},{9,11},{10,... | collective-permute-start | bytes 1105928 | tf_op jit(solution)/shard_map/ppermute | solution.py:733
  151.1 62.4 %collective-permute-start.26 = (bf16[1,96,768]{2,1,0:T(8,128)(2,1)}, bf16[1,96,768]{2,1,0:T(8,128)(2,1)}, u32[]{:S(2)}, u32[]{:S(2)}) collective-permute-start(bf16[1,96,768]{2,1,0:T(8,128)(2,1)} %get-tuple-element.213), channel_id=1, source_target_pairs={{0,8},{1,9},{2,10},{3,11},{4,12},{5,13},{6,14},{7,15},{8,0},{9,1},... | collective-permute-start | bytes 442376 | tf_op jit(solution)/shard_map/ppermute | solution.py:733
  162.0 0.9 copy-start.18
  162.0 1.3 copy-start.6
  166.5 18.7 %collective-permute-start.16 = (bf16[1,480,384]{2,1,0:T(8,128)(2,1)}, bf16[1,480,384]{2,1,0:T(8,128)(2,1)S(1)}, u32[]{:S(2)}, u32[]{:S(2)}) collective-permute-start(bf16[1,480,384]{2,1,0:T(8,128)(2,1)} %get-tuple-element.191), channel_id=1, source_target_pairs={{0,16},{1,17},{2,18},{3,19},{4,20},{5,21},{6,22},{7,23},{8,24},{9,... | collective-permute-start | bytes 1105928 | tf_op jit(solution)/shard_map/ppermute | solution.py:733
  169.1 15.9 %collective-permute-start.17 = (bf16[1,384,384]{2,1,0:T(8,128)(2,1)}, bf16[1,384,384]{2,1,0:T(8,128)(2,1)S(1)}, u32[]{:S(2)}, u32[]{:S(2)}) collective-permute-start(bf16[1,384,384]{2,1,0:T(8,128)(2,1)} %get-tuple-element.193), channel_id=1, source_target_pairs={{0,4},{1,5},{2,6},{3,7},{4,0},{5,1},{6,2},{7,3},{8,12},{9,13},{10,... | collective-permute-start | bytes 884744 | tf_op jit(solution)/shard_map/ppermute | solution.py:733
  169.7 15.5 %collective-permute-start.18 = (bf16[1,384,384]{2,1,0:T(8,128)(2,1)}, bf16[1,384,384]{2,1,0:T(8,128)(2,1)S(1)}, u32[]{:S(2)}, u32[]{:S(2)}) collective-permute-start(bf16[1,384,384]{2,1,0:T(8,128)(2,1)} %get-tuple-element.194), channel_id=1, source_target_pairs={{0,2},{1,3},{2,0},{3,1},{4,6},{5,7},{6,4},{7,5},{8,10},{9,11},{10,... | collective-permute-start | bytes 884744 | tf_op jit(solution)/shard_map/ppermute | solution.py:733
  171.2 14.0 %collective-permute-start.19 = (bf16[1,384,384]{2,1,0:T(8,128)(2,1)}, bf16[1,384,384]{2,1,0:T(8,128)(2,1)S(1)}, u32[]{:S(2)}, u32[]{:S(2)}) collective-permute-start(bf16[1,384,384]{2,1,0:T(8,128)(2,1)} %get-tuple-element.195), channel_id=1, source_target_pairs={{0,6},{1,7},{2,4},{3,5},{4,2},{5,3},{6,0},{7,1},{8,14},{9,15},{10,... | collective-permute-start | bytes 884744 | tf_op jit(solution)/shard_map/ppermute | solution.py:733
  185.1 3.7 %collective-permute-start.15 = (bf16[2,8,112,256]{3,2,1,0:T(8,128)(2,1)}, bf16[2,8,112,256]{3,2,1,0:T(8,128)(2,1)S(1)}, u32[]{:S(2)}, u32[]{:S(2)}) collective-permute-start(bf16[2,8,112,256]{3,2,1,0:T(8,128)(2,1)} %get-tuple-element.190), channel_id=1, source_target_pairs={{0,1},{1,0},{2,3},{3,2},{4,5},{5,4},{6,7},{7,6},{8,9},{9,8},{10,11... | collective-permute-start | bytes 2752520 | tf_op jit(solution)/shard_map/ppermute | solution.py:733
  185.2 0.9 copy-start.16
  188.4 15.9 %collective-permute-start.24 = (bf16[2,96,384]{2,1,0:T(8,128)(2,1)}, bf16[2,96,384]{2,1,0:T(8,128)(2,1)S(1)}, u32[]{:S(2)}, u32[]{:S(2)}) collective-permute-start(bf16[2,96,384]{2,1,0:T(8,128)(2,1)} %get-tuple-element.209), channel_id=1, source_target_pairs={{0,16},{1,17},{2,18},{3,19},{4,20},{5,21},{6,22},{7,23},{8,24},{9,... | collective-permute-start | bytes 442376 | tf_op jit(solution)/shard_map/ppermute | solution.py:733
  188.8 0.9 copy-start.7
  192.1 14.0 %collective-permute-start.21 = (bf16[1,448,256]{2,1,0:T(8,128)(2,1)}, bf16[1,448,256]{2,1,0:T(8,128)(2,1)S(1)}, u32[]{:S(2)}, u32[]{:S(2)}) collective-permute-start(bf16[1,448,256]{2,1,0:T(8,128)(2,1)} %get-tuple-element.205), channel_id=1, source_target_pairs={{0,4},{1,5},{2,6},{3,7},{4,0},{5,1},{6,2},{7,3},{8,12},{9,13},{10,... | collective-permute-start | bytes 688136 | tf_op jit(solution)/shard_map/ppermute | solution.py:733
  192.7 13.5 %collective-permute-start.22 = (bf16[1,448,256]{2,1,0:T(8,128)(2,1)}, bf16[1,448,256]{2,1,0:T(8,128)(2,1)S(1)}, u32[]{:S(2)}, u32[]{:S(2)}) collective-permute-start(bf16[1,448,256]{2,1,0:T(8,128)(2,1)} %get-tuple-element.206), channel_id=1, source_target_pairs={{0,2},{1,3},{2,0},{3,1},{4,6},{5,7},{6,4},{7,5},{8,10},{9,11},{10,... | collective-permute-start | bytes 688136 | tf_op jit(solution)/shard_map/ppermute | solution.py:733
  194.2 12.0 %collective-permute-start.23 = (bf16[1,448,256]{2,1,0:T(8,128)(2,1)}, bf16[1,448,256]{2,1,0:T(8,128)(2,1)S(1)}, u32[]{:S(2)}, u32[]{:S(2)}) collective-permute-start(bf16[1,448,256]{2,1,0:T(8,128)(2,1)} %get-tuple-element.207), channel_id=1, source_target_pairs={{0,6},{1,7},{2,4},{3,5},{4,2},{5,3},{6,0},{7,1},{8,14},{9,15},{10,... | collective-permute-start | bytes 688136 | tf_op jit(solution)/shard_map/ppermute | solution.py:733
  195.6 8.7 %copy-start.28 = (bf16[1,240,384]{2,1,0:T(8,128)(2,1)S(1)}, bf16[1,240,384]{2,1,0:T(8,128)(2,1)}, u32[]{:S(2)}) copy-start(bf16[1,240,384]{2,1,0:T(8,128)(2,1)} %get-tuple-element.214) | copy-start | bytes 552964
  204.3 1.8 copy-start.30
  204.4 9.6 %collective-permute-start.27 = (bf16[1,240,384]{2,1,0:T(8,128)(2,1)S(1)}, bf16[1,240,384]{2,1,0:T(8,128)(2,1)S(1)}, u32[]{:S(2)}, u32[]{:S(2)}) collective-permute-start(bf16[1,240,384]{2,1,0:T(8,128)(2,1)S(1)} %copy-done.28), channel_id=1, source_target_pairs={{0,8},{1,9},{2,10},{3,11},{4,12},{5,13},{6,14},{7,15},{8,0},{9,1},... | collective-permute-start | bytes 552968 | tf_op jit(solution)/shard_map/ppermute | solution.py:733
  206.2 0.8 copy-start.27
  207.0 7.0 %copy-start.4 = (bf16[2,768,384]{2,1,0:T(8,128)(2,1)S(1)}, bf16[2,768,384]{2,1,0:T(8,128)(2,1)}, u32[]{:S(2)}) copy-start(bf16[2,768,384]{2,1,0:T(8,128)(2,1)} %get-tuple-element.204) | copy-start | bytes 3538948
  209.2 10.4 %collective-permute-start.28 = (bf16[1,96,384]{2,1,0:T(8,128)(2,1)}, bf16[1,96,384]{2,1,0:T(8,128)(2,1)S(1)}, u32[]{:S(2)}, u32[]{:S(2)}) collective-permute-start(bf16[1,96,384]{2,1,0:T(8,128)(2,1)} %get-tuple-element.215), channel_id=1, source_target_pairs={{0,8},{1,9},{2,10},{3,11},{4,12},{5,13},{6,14},{7,15},{8,0},{9,1},... | collective-permute-start | bytes 221192 | tf_op jit(solution)/shard_map/ppermute | solution.py:733
  209.5 5.5 %collective-permute-start.29 = (bf16[1,112,256]{2,1,0:T(8,128)(2,1)}, bf16[1,112,256]{2,1,0:T(8,128)(2,1)S(1)}, u32[]{:S(2)}, u32[]{:S(2)}) collective-permute-start(bf16[1,112,256]{2,1,0:T(8,128)(2,1)} %get-tuple-element.217), channel_id=1, source_target_pairs={{0,8},{1,9},{2,10},{3,11},{4,12},{5,13},{6,14},{7,15},{8,0},{9,1},... | collective-permute-start | bytes 172040 | tf_op jit(solution)/shard_map/ppermute | solution.py:733
  211.2 5.3 %collective-permute-start.30 = (bf16[1,112,256]{2,1,0:T(8,128)(2,1)}, bf16[1,112,256]{2,1,0:T(8,128)(2,1)S(1)}, u32[]{:S(2)}, u32[]{:S(2)}) collective-permute-start(bf16[1,112,256]{2,1,0:T(8,128)(2,1)} %get-tuple-element.218), channel_id=1, source_target_pairs={{0,16},{1,17},{2,18},{3,19},{4,20},{5,21},{6,22},{7,23},{8,24},{9,... | collective-permute-start | bytes 172040 | tf_op jit(solution)/shard_map/ppermute | solution.py:733
  213.5 6.2 %collective-permute-start.31 = (bf16[1,112,256]{2,1,0:T(8,128)(2,1)}, bf16[1,112,256]{2,1,0:T(8,128)(2,1)S(1)}, u32[]{:S(2)}, u32[]{:S(2)}) collective-permute-start(bf16[1,112,256]{2,1,0:T(8,128)(2,1)} %get-tuple-element.219), channel_id=1, source_target_pairs={{0,24},{1,25},{2,26},{3,27},{4,28},{5,29},{6,30},{7,31},{8,16},{9,... | collective-permute-start | bytes 172040 | tf_op jit(solution)/shard_map/ppermute | solution.py:733
  213.9 5.7 %copy-start.29 = (bf16[1,240,384]{2,1,0:T(8,128)(2,1)}, bf16[1,240,384]{2,1,0:T(8,128)(2,1)S(1)}, u32[]{:S(2)}) copy-start(bf16[1,240,384]{2,1,0:T(8,128)(2,1)S(1)} %collective-permute-done.27.refs_3_) | copy-start | bytes 552964
  213.9 25.0 %collective-permute-start.20 = (bf16[2,768,384]{2,1,0:T(8,128)(2,1)S(1)}, bf16[2,768,384]{2,1,0:T(8,128)(2,1)S(1)}, u32[]{:S(2)}, u32[]{:S(2)}) collective-permute-start(bf16[2,768,384]{2,1,0:T(8,128)(2,1)S(1)} %copy-done.4), channel_id=1, source_target_pairs={{0,1},{1,0},{2,3},{3,2},{4,5},{5,4},{6,7},{7,6},{8,9},{9,8},{10,11... | collective-permute-start | bytes 3538952 | tf_op jit(solution)/shard_map/ppermute | solution.py:733
  215.0 4.7 %copy-start.32 = (bf16[1,112,256]{2,1,0:T(8,128)(2,1)}, bf16[1,112,256]{2,1,0:T(8,128)(2,1)S(1)}, u32[]{:S(2)}) copy-start(bf16[1,112,256]{2,1,0:T(8,128)(2,1)S(1)} %collective-permute-done.29.refs_7_) | copy-start | bytes 172036
  216.5 3.1 %copy-start.33 = (bf16[1,112,256]{2,1,0:T(8,128)(2,1)}, bf16[1,112,256]{2,1,0:T(8,128)(2,1)S(1)}, u32[]{:S(2)}) copy-start(bf16[1,112,256]{2,1,0:T(8,128)(2,1)S(1)} %collective-permute-done.30.refs_8_) | copy-start | bytes 172036
  222.7 1.4 collective-permute-start.32
  224.7 3.6 %collective-permute-start.33 = (f32[8,128]{1,0:T(8,128)S(1)}, f32[8,128]{1,0:T(8,128)S(1)}, u32[]{:S(2)}, u32[]{:S(2)}) collective-permute-start(f32[8,128]{1,0:T(8,128)S(1)} %add.97), channel_id=1, source_target_pairs={{0,2},{1,3},{2,0},{3,1},{4,6},{5,7},{6,4},{7,5},{8,10},{9,11},{10,... | collective-permute-start | bytes 12296 | tf_op jit(solution)/shard_map/ppermute | solution.py:733
  225.7 3.6 %collective-permute-start.34 = (f32[8,128]{1,0:T(8,128)S(1)}, f32[8,128]{1,0:T(8,128)S(1)}, u32[]{:S(2)}, u32[]{:S(2)}) collective-permute-start(f32[8,128]{1,0:T(8,128)S(1)} %add.97), channel_id=1, source_target_pairs={{0,4},{1,5},{2,6},{3,7},{4,0},{5,1},{6,2},{7,3},{8,12},{9,13},{10,... | collective-permute-start | bytes 12296 | tf_op jit(solution)/shard_map/ppermute | solution.py:733
  227.1 4.5 %collective-permute-start.35 = (f32[8,128]{1,0:T(8,128)S(1)}, f32[8,128]{1,0:T(8,128)S(1)}, u32[]{:S(2)}, u32[]{:S(2)}) collective-permute-start(f32[8,128]{1,0:T(8,128)S(1)} %add.97), channel_id=1, source_target_pairs={{0,6},{1,7},{2,4},{3,5},{4,2},{5,3},{6,0},{7,1},{8,14},{9,15},{10,... | collective-permute-start | bytes 12296 | tf_op jit(solution)/shard_map/ppermute | solution.py:733
  231.6 4.4 %collective-permute-start.36 = (f32[8,128]{1,0:T(8,128)S(1)}, f32[8,128]{1,0:T(8,128)S(1)}, u32[]{:S(2)}, u32[]{:S(2)}) collective-permute-start(f32[8,128]{1,0:T(8,128)S(1)} %add_add_fusion.1), channel_id=1, source_target_pairs={{0,8},{1,9},{2,10},{3,11},{4,12},{5,13},{6,14},{7,15},{8,0},{9,1},... | collective-permute-start | bytes 12296 | tf_op jit(solution)/shard_map/ppermute | solution.py:733
  231.6 4.6 %collective-permute-start.37 = (f32[8,128]{1,0:T(8,128)S(1)}, f32[8,128]{1,0:T(8,128)S(1)}, u32[]{:S(2)}, u32[]{:S(2)}) collective-permute-start(f32[8,128]{1,0:T(8,128)S(1)} %add_add_fusion.1), channel_id=1, source_target_pairs={{0,16},{1,17},{2,18},{3,19},{4,20},{5,21},{6,22},{7,23},{8,24},{9,... | collective-permute-start | bytes 12296 | tf_op jit(solution)/shard_map/ppermute | solution.py:733
  232.9 5.4 %collective-permute-start.38 = (f32[8,128]{1,0:T(8,128)S(1)}, f32[8,128]{1,0:T(8,128)S(1)}, u32[]{:S(2)}, u32[]{:S(2)}) collective-permute-start(f32[8,128]{1,0:T(8,128)S(1)} %add_add_fusion.1), channel_id=1, source_target_pairs={{0,24},{1,25},{2,26},{3,27},{4,28},{5,29},{6,30},{7,31},{8,16},{9,... | collective-permute-start | bytes 12296 | tf_op jit(solution)/shard_map/ppermute | solution.py:733
  238.9 1.0 copy-start.5
  242.9 12.2 %collective-permute-start.25 = (bf16[1,768,384]{2,1,0:T(8,128)(2,1)}, bf16[1,768,384]{2,1,0:T(8,128)(2,1)S(1)}, u32[]{:S(2)}, u32[]{:S(2)}) collective-permute-start(bf16[1,768,384]{2,1,0:T(8,128)(2,1)} %get-tuple-element.212), channel_id=1, source_target_pairs={{0,2},{1,3},{2,0},{3,1},{4,6},{5,7},{6,4},{7,5},{8,10},{9,11},{10,... | collective-permute-start | bytes 1769480 | tf_op jit(solution)/shard_map/ppermute | solution.py:733
  255.1 0.8 copy-start.13
  (10 other events, 7.2 us)

commit v3 on v2

--- a/solution.py
+++ b/solution.py
@@ -32,12 +32,16 @@
 CALLS = ((0, 2), (3, 5), (1, 4))
 
 
-def params(**more):
-    return pltpu.CompilerParams(vmem_limit_bytes=60 * 2**20, **more)
+def params(mebibytes):
+    return pltpu.CompilerParams(vmem_limit_bytes=mebibytes * 2**20)
 
 
 def cost(microseconds):
     return pl.CostEstimate(flops=int(microseconds * 4.4e9), bytes_accessed=0, transcendentals=0)
+
+
+def in_hbm(array):
+    return pltpu.with_memory_space_constraint(array, pltpu.HBM)
 
 
 def dot(a, b):
@@ -54,71 +58,82 @@
 ):
     rows = q_ref.shape[0]
     step = pl.program_id(0)
+    wide = wq_ref.shape[1]
+    pairs = wide // LANES
 
     @pl.when(step == 0)
     def _():
         for i, ref in enumerate((x0_ref, x1_ref, x2_ref, x3_ref)):
             x_ref[i * rows : (i + 1) * rows, :] = ref[...]
 
-    xt_ref[...] = x_ref[:, pl.ds(pl.multiple_of(step * LANES, LANES), LANES)].T
-    wkv = jnp.concatenate([wk_ref[...], wv_ref[...]], axis=1)
-    kv = dot(x_ref[...], wkv)
-    k = kv[:, :LANES].astype(BF)
-    v = (kv[:, LANES:] + vec_ref[1:2, :]).astype(BF)
+    xt_ref[...] = x_ref[:, pl.ds(pl.multiple_of(step * wide, LANES), wide)].T
+    k = dot(x_ref[...], wk_ref[...]).astype(BF)
+    v = (dot(x_ref[...], wv_ref[...]) + vec_ref[1:2, :]).astype(BF)
     q = (dot(x_ref[:rows, :], wq_ref[...]) + vec_ref[0:1, :]).astype(BF)
     q = q * jnp.asarray(HD**-0.5, BF)
     q_ref[...] = q
     k_ref[...] = k
     v_ref[...] = v
-    keys = jnp.concatenate([k, kmask_ref[...]], axis=1)
     low = lax.broadcasted_iota(jnp.int32, (rows, LANES), 1) < HD
-    outs, inverses = [], []
-    for head in range(2):
-        own = low if head == 0 else jnp.logical_not(low)
-        qh = jnp.where(own, q, jnp.zeros_like(q))
-        scores = dot_t(jnp.concatenate([qh, qhot_ref[...]], axis=1), keys)
-        top = jnp.max(scores, axis=1, keepdims=True)
-        e = jnp.exp(scores - top)
-        total = jnp.sum(e, axis=1, keepdims=True)
-        e_low = e.astype(BF)
-        e_ref[head] = e_low
-        outs.append(dot(e_low, v))
-        inverses.append(1.0 / total)
-    rinv = jnp.where(low, inverses[0], inverses[1])
-    rinv_ref[...] = rinv
-    mixed_ref[...] = (jnp.where(low, outs[0], outs[1]) * rinv).astype(BF)
+    part = lambda a, p: a[:, p * LANES : (p + 1) * LANES]
+    keys = [jnp.concatenate([part(k, p), kmask_ref[...]], axis=1) for p in range(pairs)]
+    values = [jnp.concatenate([part(v, p), jnp.ones((v.shape[0], LANES), BF)], axis=1) for p in range(pairs)]
+
+    def score(head):
+        qh = part(q, head // 2)
+        qh = jnp.where(low if head % 2 == 0 else jnp.logical_not(low), qh, jnp.zeros_like(qh))
+        return dot_t(jnp.concatenate([qh, qhot_ref[...]], axis=1), keys[head // 2])
+
+    following = score(0)
+    done = []
+    for head in range(2 * pairs):
+        scores = following
+        if head + 1 < 2 * pairs:
+            following = score(head + 1)
+        e = jnp.exp(scores - jnp.max(scores, axis=1, keepdims=True)).astype(BF)
+        e_ref[head] = e
+        both = dot(e, values[head // 2])
+        done.append((both[:, :LANES], 1.0 / both[:, LANES:]))
+        if head % 2 == 1:
+            (out0, rinv0), (out1, rinv1) = done[-2:]
+            span = slice(head // 2 * LANES, (head // 2 + 1) * LANES)
+            rinv = jnp.where(low, rinv0, rinv1)
+            rinv_ref[:, span] = rinv
+            mixed_ref[:, span] = (jnp.where(low, out0, out1) * rinv).astype(BF)
 
 
 def attend(blocks, input_weight, vectors, kmask, qhot):
     rows, width = blocks[0].shape
     slab = rows * len(blocks)
-    pairs = width // LANES
+    wide = 2 * LANES
+    steps = width // wide
+    weight = in_hbm(input_weight)
     full = lambda a: pl.BlockSpec(a.shape, lambda p: (0,) * a.ndim)
-    cols = lambda r, off=0: pl.BlockSpec((r, LANES), lambda p: (0, p + off))
+    cols = lambda r, off=0: pl.BlockSpec((r, wide), lambda p: (0, p + off))
     return pl.pallas_call(
         attend_kernel,
-        grid=(pairs,),
+        grid=(steps,),
         in_specs=[
-            *map(full, blocks), cols(width), cols(width, pairs), cols(width, 2 * pairs),
+            *map(full, blocks), cols(width), cols(width, steps), cols(width, 2 * steps),
             cols(vectors.shape[0]), full(kmask), full(qhot),
         ],
         out_specs=[
-            cols(rows), pl.BlockSpec((2, rows, slab), lambda p: (p, 0, 0)), cols(rows), cols(rows),
-            cols(slab), cols(slab), pl.BlockSpec((LANES, slab), lambda p: (p, 0)),
+            cols(rows), pl.BlockSpec((wide // HD, rows, slab), lambda p: (p, 0, 0)), cols(rows), cols(rows),
+            cols(slab), cols(slab), pl.BlockSpec((wide, slab), lambda p: (p, 0)),
         ],
         out_shape=[
             jax.ShapeDtypeStruct((rows, width), BF),
-            jax.ShapeDtypeStruct((2 * pairs, rows, slab), BF),
-            jax.ShapeDtypeStruct((rows, width), F32),
-            jax.ShapeDtypeStruct((rows, width), BF),
-            jax.ShapeDtypeStruct((slab, width), BF),
-            jax.ShapeDtypeStruct((slab, width), BF),
-            jax.ShapeDtypeStruct((width, slab), BF),
+            pltpu.HBM((width // HD, rows, slab), BF),
+            pltpu.HBM((rows, width), F32),
+            pltpu.HBM((rows, width), BF),
+            pltpu.HBM((slab, width), BF),
+            pltpu.HBM((slab, width), BF),
+            pltpu.HBM((width, slab), BF),
         ],
         scratch_shapes=[pltpu.VMEM((slab, width), BF)],
-        compiler_params=params(), cost_estimate=cost(29),
+        compiler_params=params(40), cost_estimate=cost(20),
         name="attend",
-    )(*blocks, input_weight, input_weight, input_weight, vectors, kmask, qhot)
+    )(in_hbm(blocks[0]), *blocks[1:], weight, weight, weight, vectors, kmask, qhot)
 
 
 def spot(d, own_d):
@@ -155,7 +170,7 @@
             out_specs=pl.BlockSpec((1, 8, width // 8, cut), lambda j, own: (j, 0, 0, 0)),
         ),
         out_shape=jax.ShapeDtypeStruct((2, 8, width // 8, cut), BF),
-        compiler_params=params(), cost_estimate=cost(5),
+        compiler_params=params(12), cost_estimate=cost(5),
         name="reduce_kept",
     )(own, gbt, act)
 
@@ -282,7 +297,7 @@
             jax.ShapeDtypeStruct((2, 8, piece, cut), BF),
             jax.ShapeDtypeStruct((16, width), F32),
         ],
-        compiler_params=params(), cost_estimate=cost(20),
+        compiler_params=params(22), cost_estimate=cost(20),
         name="ahead",
     )(own, mixed, frames, cotangent, qhot, output_weight, expand_weight, reduce_weight, vectors)
 
@@ -374,7 +389,7 @@
             jax.ShapeDtypeStruct(spread, BF),
             jax.ShapeDtypeStruct((16, width), F32),
         ],
-        compiler_params=params(), cost_estimate=cost(18),
+        compiler_params=params(20), cost_estimate=cost(18),
         name="behind",
     )(own, slope, gb, gs, norm1, inv1, hlt, mt, output_weight, expand_weight, reduce_weight, vectors, after)
 
@@ -475,7 +490,7 @@
     own = jnp.concatenate([own, jnp.array(pairs, jnp.int32)])
     full = lambda shape: pl.BlockSpec(shape, lambda i, own: (0,) * len(shape))
     cols = lambda r: pl.BlockSpec((r, LANES), lambda i, own: (0, own[2 + i]))
-    inputs = [e, q, k, v, grad_mixed, mixed, rinv, x_t, after]
+    inputs = [in_hbm(e), q, k, v, grad_mixed, mixed, rinv, x_t, after]
     in_specs = [
         pl.BlockSpec((2, rows, slab), lambda i, own: (own[2 + i], 0, 0)),
         cols(rows), cols(slab), cols(slab), cols(rows), cols(rows), cols(rows), full(x_t.shape),
@@ -513,7 +528,7 @@
             num_scalar_prefetch=1, grid=(len(pairs),), in_specs=in_specs, out_specs=out_specs, scratch_shapes=scratch
         ),
         out_shape=out_shape,
-        compiler_params=params(), cost_estimate=cost(12),
+        compiler_params=params(20), cost_estimate=cost(12),
         name="attend_back",
     )(own, *inputs)
 
@@ -576,12 +591,13 @@
         out_specs=[full(gx), *out_specs],
         out_shape=[jax.ShapeDtypeStruct((rows, width), F32), *out_shape],
         scratch_shapes=[pltpu.VMEM((width, count * LANES), BF)],
-        compiler_params=params(), cost_estimate=cost(4 if last else 8),
+        compiler_params=params(16), cost_estimate=cost(4 if last else 8),
         name="frames_back",
     )(input_weight, gx, after, *dqs, *dkvs, *([dx] if last else []))
 
 
-def frames_end_kernel(gx_ref, keep_ref, came_ref, out_ref):
+def frames_end_kernel(gx_ref, keep_ref, came_ref, out_ref, token_ref):
+    token_ref[...] = jnp.zeros_like(token_ref)
     out_ref[...] = gx_ref[...] + (keep_ref[0] + came_ref[0].astype(F32)).T
 
 
@@ -591,8 +607,9 @@
     down = pl.BlockSpec((1, LANES, rows), lambda p: (0, p, 0))
     return pl.pallas_call(
         frames_end_kernel,
-        grid=(width // LANES,), in_specs=[across, down, down], out_specs=across,
-        out_shape=jax.ShapeDtypeStruct((rows, width), F32), compiler_params=params(), cost_estimate=cost(5), name="frames_end",
+        grid=(width // LANES,), in_specs=[across, down, down],
+        out_specs=[across, pl.BlockSpec((8, LANES), lambda p: (0, 0))],
+        out_shape=[jax.ShapeDtypeStruct((rows, width), F32), jax.ShapeDtypeStruct((8, LANES), F32)], compiler_params=params(8), cost_estimate=cost(5), name="frames_end",
     )(gx, keep, came)
 
 
@@ -625,7 +642,7 @@
     outs = pl.pallas_call(
         functools.partial(gather_kernel, plan),
         grid=(steps,), in_specs=[*in_specs, pl.BlockSpec(memory_space=pl.ANY)], out_specs=out_specs,
-        out_shape=out_shape, compiler_params=params(), cost_estimate=cost(3), name="gather",
+        out_shape=out_shape, compiler_params=params(14), cost_estimate=cost(3), name="gather",
     )(*inputs, after)
     made = []
     for _, parts in plan:
@@ -642,7 +659,7 @@
         while len(parts) > 1:
             parts = [parts[t] + parts[t + 1] for t in range(0, len(parts), 2)]
         sums.append(parts[0])
-    inp_ref, out_ref, exp_ref, red_ref, vec_ref, sq_ref = refs
+    inp_ref, out_ref, exp_ref, red_ref, vec_ref, sq_ref = refs[1:]
     red, exp, in1, in2 = sums
     rows = in1.shape[0]
     vec = in2[rows : rows + vec_ref.shape[0], : vec_ref.shape[1]]
@@ -666,14 +683,16 @@
     sq_ref[...] = jnp.broadcast_to(squares, sq_ref.shape)
 
 
-def finish(own, red, exp, in1, in2):
+def finish(own, red, exp, in1, in2, after):
     piece = in1[0].shape[1]
     tall = exp[0].shape[1] - piece // 2
     vmem = pl.BlockSpec(memory_space=pltpu.VMEM)
     inputs = [*red, *exp, *in1, *in2]
     return pl.pallas_call(
         functools.partial(finish_kernel, tuple(map(len, (red, exp, in1, in2)))),
-        in_specs=[pl.BlockSpec(memory_space=pltpu.SMEM), *[vmem] * len(inputs)],
+        in_specs=[
+            pl.BlockSpec(memory_space=pltpu.SMEM), *[vmem] * len(inputs), pl.BlockSpec(memory_space=pl.ANY)
+        ],
         out_specs=[vmem] * 6,
         out_shape=[
             jax.ShapeDtypeStruct((piece, 9 * HD), F32),
@@ -683,8 +702,8 @@
             jax.ShapeDtypeStruct((3, piece), F32),
             jax.ShapeDtypeStruct((8, LANES), F32),
         ],
-        compiler_params=params(), cost_estimate=cost(3), name="finish",
-    )(own, *inputs)
+        compiler_params=params(8), cost_estimate=cost(3), name="finish",
+    )(own, *inputs, after)
 
 
 def adam_step(master, moment_one, moment_two, gradient, step_rate, decay_weight):
@@ -698,7 +717,7 @@
     return (new_one, new_two, new_master, new_master.astype(BF))
 
 
-def adam_kernel(rates, turned, squares_ref, *refs):
+def adam_kernel(rates, turned, squares_ref, _, *refs):
     n = len(rates)
     ins, outs = refs[: 4 * n], refs[4 * n :]
     norm = jnp.sqrt(squares_ref[0:1, 0:1])
@@ -713,8 +732,8 @@
             outs[1 + 4 * a + b][...] = made[b]
 
 
-def adam_all(squares, states, grads, rates, turned):
-    inputs, out_shape = [squares], [jax.ShapeDtypeStruct((1, 1), F32)]
+def adam_all(squares, after, states, grads, rates, turned):
+    inputs, out_shape = [squares, after], [jax.ShapeDtypeStruct((1, 1), F32)]
     for state, grad in zip(states, grads):
         inputs += [*state, grad]
         shape = state[0].shape
@@ -722,8 +741,8 @@
     vmem = pl.BlockSpec(memory_space=pltpu.VMEM)
     return pl.pallas_call(
         functools.partial(adam_kernel, rates, turned),
-        in_specs=[vmem] * len(inputs), out_specs=[vmem] * len(out_shape), out_shape=out_shape,
-        compiler_params=params(), cost_estimate=cost(5), name="adam",
+        in_specs=[vmem, pl.BlockSpec(memory_space=pl.ANY), *[vmem] * (len(inputs) - 2)], out_specs=[vmem] * len(out_shape), out_shape=out_shape,
+        compiler_params=params(16), cost_estimate=cost(5), name="adam",
     )(*inputs)
 
 
@@ -897,13 +916,13 @@
 
     if fast:
         red, exp, in1, in2, gx, dx = reduce_fast(move, own, back, behind_of, input_weight, gbt, act, red_s, vec1)
-        inp, out, exp, red, vec, squares = finish(own, red, exp, in1, in2)
+        inp, out, exp, red, vec, squares = finish(own, red, exp, in1, in2, dx[0])
         squares = tree_sum(move, squares)
     else:
         inp, out, exp, red, vec, squares, gx, dx = reduce_plain(
             move, own, back, behind_of, input_weight, gbt, act, red_s, vec1
         )
-    frames_gradient = frames_end(gx, *dx)
+    frames_gradient, token = frames_end(gx, *dx)
 
     grads = [inp, out, exp, red, vec]
     masters, firsts, seconds = (list(states[i : i + 5]) for i in (0, 5, 10))
@@ -912,7 +931,7 @@
     hidden = expand_weight.shape[1]
     wide, narrow = 2.0 * width**-0.5, 2.0 * hidden**-0.5
     norm, *made = adam_all(
-        squares, list(zip(masters, firsts, seconds)), grads,
+        squares, token, list(zip(masters, firsts, seconds)), grads,
         ((wide, 0.01), (wide, 0.01), (wide, 0.01), (narrow, 0.01), (0.5, 0.0)),
         (False, True, False, False, False),
     )

time: 262 us -> 183 us (0.70)
  Pallas kernels: 164 us -> 93.7 us
  local copies, waits for them, and re-layouts: 14.4 us -> 2.43 us
  waiting for transfers between devices: 28.9 us -> 33.7 us
  other arithmetic: 8.36 us -> 3.92 us
  starting transfers between devices: 42.2 us -> 45.8 us
    pallas_call x9, Pallas kernels: 27.1 us -> 6.64 us  [gather(): pl.pallas_call(functools.partial(gather_kernel, plan), grid=(steps,), in_...]
    unnamed x70 -> x60, local copies, waits for them, and re-layouts: 13 us -> 1.05 us
    pallas_call x3, Pallas kernels: 37.6 us -> 27.6 us  [attend_back(): pl.pallas_call(functools.partial(back_kernel, group, pairs, first, last),...]
    pallas_call x1, Pallas kernels: 28.9 us -> 19 us  [attend(): pl.pallas_call(attend_kernel, grid=(steps,), in_specs=[*map(full, blocks)...]
    pallas_call x2, Pallas kernels: 18 us -> 8.62 us  [frames_back(): pl.pallas_call(functools.partial(frames_kernel, pairs, last), grid=(4,),...]
    pallas_call x1, Pallas kernels: 18.2 us -> 11.3 us  [behind(): pl.pallas_call(behind_kernel, grid_spec=pltpu.PrefetchScalarGridSpec(num_...]
    pallas_call x1, Pallas kernels: 17.9 us -> 12.1 us  [ahead(): pl.pallas_call(ahead_kernel, grid_spec=pltpu.PrefetchScalarGridSpec(num_s...]
    ppermute x39, waiting for transfers between devices: 28.9 us -> 33.7 us  [move(): return lax.ppermute(value, AXES, pairs)]
  transfers between devices with their start and end apart: 39 -> 39, of which waited for: 12 -> 17; matrix products, arithmetic and copies ran while one was open for 4% -> 3% of each run, Pallas kernels for 39% -> 30%
where the time goes in v3:
time: 183 us
  Pallas kernels  93.7 us (51%)
  starting transfers between devices  45.8 us (25%)
  waiting for transfers between devices  33.7 us (18%)
  other arithmetic  3.92 us (2%)
  between operations  3.39 us (2%)
  local copies, waits for them, and re-layouts  2.43 us (1%)
    ppermute x39, starting transfers between devices, move(): return lax.ppermute(value, AXES, pairs)  45.8 us
    ppermute x39, waiting for transfers between devices, move(): return lax.ppermute(value, AXES, pairs)  33.7 us
    pallas_call x3, Pallas kernels, attend_back(): pl.pallas_call(functools.partial(back_kernel, group, pairs, first, last),...  27.6 us
    pallas_call x1, Pallas kernels, attend(): pl.pallas_call(attend_kernel, grid=(steps,), in_specs=[*map(full, blocks)...  19 us
    pallas_call x1, Pallas kernels, ahead(): pl.pallas_call(ahead_kernel, grid_spec=pltpu.PrefetchScalarGridSpec(num_s...  12.1 us
    pallas_call x1, Pallas kernels, behind(): pl.pallas_call(behind_kernel, grid_spec=pltpu.PrefetchScalarGridSpec(num_...  11.3 us
    pallas_call x2, Pallas kernels, frames_back(): pl.pallas_call(functools.partial(frames_kernel, pairs, last), grid=(4,),...  8.62 us
    pallas_call x9, Pallas kernels, gather(): pl.pallas_call(functools.partial(gather_kernel, plan), grid=(steps,), in_...  6.64 us
  transfers between devices with their start and end apart: 39, of which 17 were waited for; matrix products, arithmetic and copies ran while one was open for 3% of the time, Pallas kernels for 30%

profile of v3, /device:TPU:0, one launch (start us, length us, event | category | flops | bytes accessed | tf_op | source)
XLA Modules:
  0.0 182.9 jit_solution(7216527858940402456)
XLA Ops:
  0.7 3.0 %collective-permute-start = (bf16[384,768]{1,0:T(8,128)(2,1)}, bf16[384,768]{1,0:T(8,128)(2,1)S(1)}, u32[]{:S(2)}, u32[]{:S(2)}) collective-permute-start(bf16[384,768]{1,0:T(8,128)(2,1)} %x_ref.1), channel_id=1, source_target_pairs={{0,2},{1,3},{2,0},{3,1},{4,6},{5,7},{6,4},{7,5},{8,10},{9,11},{10,... | collective-permute-start | bytes 1769480 | tf_op jit(solution)/shard_map/ppermute | solution.py:752
  3.7 1.4 fusion.5
  5.0 0.7 xor_multiply_fusion
  7.7 0.7 convert_add_fusion
  8.5 8.7 %collective-permute-done.x1_ref = bf16[384,768]{1,0:T(8,128)(2,1)S(1)} collective-permute-done((bf16[384,768]{1,0:T(8,128)(2,1)}, bf16[384,768]{1,0:T(8,128)(2,1)S(1)}, u32[]{:S(2)}, u32[]{:S(2)}) %collective-permute-start) | collective-permute-done | bytes 589856 | tf_op jit(solution)/shard_map/ppermute | solution.py:752
  17.3 0.7 convert_element_type.57.vec_ref
  18.1 1.2 pad_add_fusion.4
  19.7 19.0 %attend.1 = (bf16[384,768]{1,0:T(8,128)(2,1)S(1)}, bf16[12,384,1536]{2,1,0:T(8,128)(2,1)}, f32[384,768]{1,0:T(8,128)}, bf16[384,768]{1,0:T(8,128)(2,1)}, bf16[15...) custom-call(bf16[384,768]{1,0:T(8,128)(2,1)} %x_ref.1, ...), custom_call_target="tpu_custom_call" | custom-call | flops 88000004096 | tf_op jit(solution)/shard_map/attend/pallas_call | solution.py:113
  38.8 12.1 %ahead.1 = (bf16[384,768]{1,0:T(8,128)(2,1)}, bf16[4,384,768]{2,1,0:T(8,128)(2,1)S(1)}, f32[4,384,768]{2,1,0:T(8,128)S(1)}, f32[384,768]{1,0:T(8,128)S(1)}, f32[...) custom-call(s32[2]{0:T(128)S(1)} %pad_add_fusion.own_ref, ...), custom_call_target="tpu_custom_call" | custom-call | flops 88000004096 | tf_op jit(solution)/shard_map/ahead/pallas_call | solution.py:261
  50.9 0.5 collective-permute-start.3
  51.5 2.1 %reduce_kept.1.refs_2_ = bf16[2,8,96,768]{3,2,1,0:T(8,128)(2,1)S(1)} custom-call(s32[2]{0:T(128)S(1)} %pad_add_fusion.own_ref, bf16[768,384]{1,0:T(8,128)(2,1)S(1)} %get-tuple-element.146.gbt_ref, bf16[4,384,768]{2,1,0:T(8,128)(2,1)S(1)} %get-tuple-element.147.act_ref), custom_call_target="tpu_custom_call" | custom-call | flops 22000001024 | tf_op jit(solution)/shard_map/reduce_kept/pallas_call | solution.py:161
  53.6 1.9 %collective-permute-done.3 = bf16[2,8,96,768]{3,2,1,0:T(8,128)(2,1)S(1)} collective-permute-done((bf16[2,8,96,768]{3,2,1,0:T(8,128)(2,1)S(1)}, bf16[2,8,96,768]{3,2,1,0:T(8,128)(2,1)S(1)}, u32[]{:S(2)}, u32[]{:S(2)}) %collective-permute-start.3) | collective-permute-done | bytes 2359328 | tf_op jit(solution)/shard_map/ppermute | solution.py:752
  55.5 1.1 gather.9
  56.6 1.8 collective-permute-start.4
  58.4 1.5 collective-permute-start.5
  59.9 11.3 %behind.1 = (f32[384,768]{1,0:T(8,128)S(1)}, bf16[384,768]{1,0:T(8,128)(2,1)S(1)}, bf16[2,2,4,240,384]{4,3,2,1,0:T(8,128)(2,1)S(1)}, bf16[2,2,4,240,384]{4,3,2,1,0:T(8,128)(2,1)S(1)}, f32[16,768]{1,0:T(8,128)S(1)}) custom-call(s32[2]{0:T(128)S(1)} %pad_add_fusion.own_ref, f32[4,384,768]{2,1,0:T(8,128)S(1)} %get-tuple-element.139.slope_ref, ...), custom_call_target="tpu_custom_call" | custom-call | flops 79200002048 | tf_op jit(solution)/shard_map/behind/pallas_call | solution.py:369
  71.3 0.9 collective-permute-done.4.refs_1_
  72.3 1.5 collective-permute-done.5.refs_3_
  73.8 0.5 gather.10
  74.3 1.6 collective-permute-start.6
  77.2 8.6 %attend_back.3 = (bf16[384,256]{1,0:T(8,128)(2,1)S(1)}, bf16[512,1536]{1,0:T(8,128)(2,1)S(1)}, f32[8,256]{1,0:T(8,128)S(1)}, bf16[4,8,96,384]{3,2,1,0:T(8,128)(2,1)S(1)}) custom-call(s32[4]{0:T(128)S(1)} %get-tuple-element.254.own_ref, bf16[12,384,1536]{2,1,0:T(8,128)(2,1)} %get-tuple-element.161.e_ref, bf16[384,768]{1,0:T(8,128)(2,1)S(1)} %copy-done.23, ...), custom_call_target="tpu_custom_call" | custom-call | flops 52800000000 | tf_op jit(solution)/shard_map/attend_back/pallas_call | solution.py:525
  85.9 1.8 gather.11
  87.7 0.7 collective-permute-start.10
  88.4 1.3 collective-permute-start.11
  89.7 2.6 %collective-permute-start.9 = (bf16[1,192,768]{2,1,0:T(8,128)(2,1)S(1)}, bf16[1,192,768]{2,1,0:T(8,128)(2,1)S(1)}, u32[]{:S(2)}, u32[]{:S(2)}) collective-permute-start(bf16[1,192,768]{2,1,0:T(8,128)(2,1)S(1)} %get-tuple-element.170), channel_id=1, source_target_pairs={{0,16},{1,17},{2,18},{3,19},{4,20},{5,21},{6,22},{7,23},{8,24},{9,... | collective-permute-start | bytes 884744 | tf_op jit(solution)/shard_map/ppermute | solution.py:752
  92.3 9.6 %attend_back.4 = (bf16[384,256]{1,0:T(8,128)(2,1)S(1)}, bf16[512,1536]{1,0:T(8,128)(2,1)S(1)}, f32[8,256]{1,0:T(8,128)S(1)}, bf16[2,8,96,384]{3,2,1,0:T(8,128)(2,1)S(1)}, bf16[2,8,96,384]{3,2,1,0:T(8,128)(2,1)S(1)}) custom-call(s32[4]{0:T(128)S(1)} %get-tuple-element.253.own_ref, bf16[12,384,1536]{2,1,0:T(8,128)(2,1)} %get-tuple-element.161.e_ref, ...), custom_call_target="tpu_custom_call" | custom-call | flops 52800000000 | tf_op jit(solution)/shard_map/attend_back/pallas_call | solution.py:525
  102.0 2.6 %collective-permute-done.9 = bf16[1,192,768]{2,1,0:T(8,128)(2,1)S(1)} collective-permute-done((bf16[1,192,768]{2,1,0:T(8,128)(2,1)S(1)}, bf16[1,192,768]{2,1,0:T(8,128)(2,1)S(1)}, u32[]{:S(2)}, u32[]{:S(2)}) %collective-permute-start.9) | collective-permute-done | bytes 294944 | tf_op jit(solution)/shard_map/ppermute | solution.py:752
  104.7 0.7 collective-permute-done.10.refs_3_
  105.7 1.4 gather.12
  107.1 1.5 collective-permute-start.12
  108.6 1.4 collective-permute-start.13
  110.0 1.6 collective-permute-start.26
  111.6 5.3 %frames_back.2 = (f32[384,768]{1,0:T(8,128)S(1)}, f32[4,768,384]{2,1,0:T(8,128)S(1)}) custom-call(bf16[768,2304]{1,0:T(8,128)(2,1)S(1)} %copy-done, f32[384,768]{1,0:T(8,128)S(1)} %get-tuple-element.150.gx_in_ref, bf16[1,96,768]{2,1,0:T(8,128)(2,1)S(1)} %get-tuple-element.177.after_ref.refs_0_, bf16[384,256]{1,0:T(8,128)(2,1)S(1)} %get-tuple-element.178.refs_0_, ...), custom_call_target="tpu_custom_call" | custom-call | flops 35200000000 | tf_op jit(solution)/shard_map/frames_back/pallas_call | solution.py:584
  116.9 0.8 gather.13
  117.7 2.6 %collective-permute-start.16 = (bf16[1,480,384]{2,1,0:T(8,128)(2,1)S(1)}, bf16[1,480,384]{2,1,0:T(8,128)(2,1)S(1)}, u32[]{:S(2)}, u32[]{:S(2)}) collective-permute-start(bf16[1,480,384]{2,1,0:T(8,128)(2,1)S(1)} %get-tuple-element.193), channel_id=1, source_target_pairs={{0,16},{1,17},{2,18},{3,19},{4,20},{5,21},{6,22},{7,23},{8,24},{9,... | collective-permute-start | bytes 1105928 | tf_op jit(solution)/shard_map/ppermute | solution.py:752
  120.3 0.5 collective-permute-start.17
  120.9 1.3 collective-permute-start.18
  122.2 1.6 collective-permute-start.19
  123.8 9.3 %attend_back.5 = (bf16[384,256]{1,0:T(8,128)(2,1)S(1)}, bf16[512,1536]{1,0:T(8,128)(2,1)S(1)}, f32[8,256]{1,0:T(8,128)S(1)}, bf16[2,8,112,256]{3,2,1,0:T(8,128)(2,1)S(1)}, bf16[2,8,112,256]{3,2,1,0:T(8,128)(2,1)S(1)}) custom-call(s32[4]{0:T(128)S(1)} %get-tuple-element.251.own_ref, bf16[12,384,1536]{2,1,0:T(8,128)(2,1)} %get-tuple-element.161.e_ref, ...), custom_call_target="tpu_custom_call" | custom-call | flops 52800000000 | tf_op jit(solution)/shard_map/attend_back/pallas_call | solution.py:525
  133.6 0.6 collective-permute-done.16
  134.5 1.2 collective-permute-done.15
  135.9 0.6 collective-permute-start.21
  136.5 1.3 collective-permute-start.22
  137.8 1.6 collective-permute-start.23
  139.5 3.3 %frames_back.3 = (f32[384,768]{1,0:T(8,128)S(1)}, bf16[2,768,384]{2,1,0:T(8,128)(2,1)S(1)}, f32[2,768,384]{2,1,0:T(8,128)S(1)}) custom-call(bf16[768,2304]{1,0:T(8,128)(2,1)S(1)} %copy-done, f32[384,768]{1,0:T(8,128)S(1)} %get-tuple-element.182.refs_6_.gx_in_ref, bf16[1,448,256]{2,1,0:T(8,128)(2,1)S(1)} %get-tuple-element.200.after_ref, ...), custom_call_target="tpu_custom_call" | custom-call | flops 17600000000 | tf_op jit(solution)/shard_map/frames_back/pallas_call | solution.py:584
  142.8 1.1 collective-permute-done.24.refs_5_
  143.9 1.9 %collective-permute-start.27 = (bf16[1,240,384]{2,1,0:T(8,128)(2,1)S(1)}, bf16[1,240,384]{2,1,0:T(8,128)(2,1)S(1)}, u32[]{:S(2)}, u32[]{:S(2)}) collective-permute-start(bf16[1,240,384]{2,1,0:T(8,128)(2,1)S(1)} %get-tuple-element.217), channel_id=1, source_target_pairs={{0,8},{1,9},{2,10},{3,11},{4,12},{5,13},{6,14},{7,15},{8,0},{9,1},... | collective-permute-start | bytes 552968 | tf_op jit(solution)/shard_map/ppermute | solution.py:752
  145.8 3.5 %collective-permute-done.23 = bf16[1,448,256]{2,1,0:T(8,128)(2,1)S(1)} collective-permute-done((bf16[1,448,256]{2,1,0:T(8,128)(2,1)S(1)}, bf16[1,448,256]{2,1,0:T(8,128)(2,1)S(1)}, u32[]{:S(2)}, u32[]{:S(2)}) %collective-permute-start.23) | collective-permute-done | bytes 229408 | tf_op jit(solution)/shard_map/ppermute | solution.py:752
  149.5 2.9 %collective-permute-start.28 = (bf16[1,96,384]{2,1,0:T(8,128)(2,1)S(1)}, bf16[1,96,384]{2,1,0:T(8,128)(2,1)S(1)}, u32[]{:S(2)}, u32[]{:S(2)}) collective-permute-start(bf16[1,96,384]{2,1,0:T(8,128)(2,1)S(1)} %get-tuple-element.218), channel_id=1, source_target_pairs={{0,8},{1,9},{2,10},{3,11},{4,12},{5,13},{6,14},{7,15},{8,0},{9,1},... | collective-permute-start | bytes 221192 | tf_op jit(solution)/shard_map/ppermute | solution.py:752
  152.8 4.0 %collective-permute-start.31 = (bf16[1,112,256]{2,1,0:T(8,128)(2,1)S(1)}, bf16[1,112,256]{2,1,0:T(8,128)(2,1)S(1)}, u32[]{:S(2)}, u32[]{:S(2)}) collective-permute-start(bf16[1,112,256]{2,1,0:T(8,128)(2,1)S(1)} %get-tuple-element.222), channel_id=1, source_target_pairs={{0,24},{1,25},{2,26},{3,27},{4,28},{5,29},{6,30},{7,31},{8,16},{9,... | collective-permute-start | bytes 172040 | tf_op jit(solution)/shard_map/ppermute | solution.py:752
  156.8 0.5 gather.17
  157.3 0.7 collective-permute-start.25
  158.0 1.6 collective-permute-done.31.refs_9_
  159.6 1.2 finish.1
  160.8 1.2 collective-permute-done.32
  162.0 0.7 collective-permute-start.33
  162.7 1.1 collective-permute-start.34
  163.8 1.7 collective-permute-start.35
  165.5 4.5 %collective-permute-done.33 = f32[8,128]{1,0:T(8,128)S(1)} collective-permute-done((f32[8,128]{1,0:T(8,128)S(1)}, f32[8,128]{1,0:T(8,128)S(1)}, u32[]{:S(2)}, u32[]{:S(2)}) %collective-permute-start.33) | collective-permute-done | bytes 4128 | tf_op jit(solution)/shard_map/ppermute | solution.py:752
  170.0 1.9 %collective-permute-start.37 = (f32[8,128]{1,0:T(8,128)S(1)}, f32[8,128]{1,0:T(8,128)S(1)}, u32[]{:S(2)}, u32[]{:S(2)}) collective-permute-start(f32[8,128]{1,0:T(8,128)S(1)} %add_add_fusion.1), channel_id=1, source_target_pairs={{0,16},{1,17},{2,18},{3,19},{4,20},{5,21},{6,22},{7,23},{8,24},{9,... | collective-permute-start | bytes 12296 | tf_op jit(solution)/shard_map/ppermute | solution.py:752
  172.0 2.4 %collective-permute-start.38 = (f32[8,128]{1,0:T(8,128)S(1)}, f32[8,128]{1,0:T(8,128)S(1)}, u32[]{:S(2)}, u32[]{:S(2)}) collective-permute-start(f32[8,128]{1,0:T(8,128)S(1)} %add_add_fusion.1), channel_id=1, source_target_pairs={{0,24},{1,25},{2,26},{3,27},{4,28},{5,29},{6,30},{7,31},{8,16},{9,... | collective-permute-start | bytes 12296 | tf_op jit(solution)/shard_map/ppermute | solution.py:752
  174.6 2.8 %collective-permute-done.38 = f32[8,128]{1,0:T(8,128)S(1)} collective-permute-done((f32[8,128]{1,0:T(8,128)S(1)}, f32[8,128]{1,0:T(8,128)S(1)}, u32[]{:S(2)}, u32[]{:S(2)}) %collective-permute-start.38) | collective-permute-done | bytes 4128 | tf_op jit(solution)/shard_map/ppermute | solution.py:752
  177.6 2.7 %frames_end.1 = (f32[384,768]{1,0:T(8,128)}, f32[8,128]{1,0:T(8,128)S(1)}) custom-call(f32[384,768]{1,0:T(8,128)S(1)} %get-tuple-element.204.refs_6_.gx_ref, f32[1,768,384]{2,1,0:T(8,128)S(1)} %get-tuple-element.213.keep_ref.refs_10_, bf16[1,768,384]{2,1,0:T(8,128)(2,1)S(1)} %collective-permute-done.25.came_ref), custom_call_target="tpu_custom_call" | custom-call | flops 22000001024 | tf_op jit(solution)/shard_map/frames_end/pallas_call | solution.py:608
  180.4 2.4 %adam.1 = (f32[1,1]{1,0:T(1,128)}, f32[96,576]{1,0:T(8,128)}, f32[96,576]{1,0:T(8,128)}, f32[96,576]{1,0:T(8,128)}, bf16[96,576]{1,0:T(8,128)(2,1)}, /*index=5*/...) custom-call(f32[8,128]{1,0:T(8,128)S(1)} %add_add_fusion.squares_ref, ...), custom_call_target="tpu_custom_call" | custom-call | flops 22000001024 | tf_op jit(solution)/shard_map/adam/pallas_call | solution.py:742
  (113 shorter events, 4.5 us)
Async XLA Ops:
  0.7 16.6 %collective-permute-start = (bf16[384,768]{1,0:T(8,128)(2,1)}, bf16[384,768]{1,0:T(8,128)(2,1)S(1)}, u32[]{:S(2)}, u32[]{:S(2)}) collective-permute-start(bf16[384,768]{1,0:T(8,128)(2,1)} %x_ref.1), channel_id=1, source_target_pairs={{0,2},{1,3},{2,0},{3,1},{4,6},{5,7},{6,4},{7,5},{8,10},{9,11},{10,... | collective-permute-start | bytes 1769480 | tf_op jit(solution)/shard_map/ppermute | solution.py:752
  3.7 16.0 %collective-permute-start.1 = (bf16[384,768]{1,0:T(8,128)(2,1)}, bf16[384,768]{1,0:T(8,128)(2,1)S(1)}, u32[]{:S(2)}, u32[]{:S(2)}) collective-permute-start(bf16[384,768]{1,0:T(8,128)(2,1)} %x_ref.1), channel_id=1, source_target_pairs={{0,1},{1,0},{2,3},{3,2},{4,5},{5,4},{6,7},{7,6},{8,9},{9,8},{10,11... | collective-permute-start | bytes 1769480 | tf_op jit(solution)/shard_map/ppermute | solution.py:752
  17.2 2.4 %collective-permute-start.2 = (bf16[384,768]{1,0:T(8,128)(2,1)S(1)}, bf16[384,768]{1,0:T(8,128)(2,1)S(1)}, u32[]{:S(2)}, u32[]{:S(2)}) collective-permute-start(bf16[384,768]{1,0:T(8,128)(2,1)S(1)} %collective-permute-done.x1_ref), channel_id=1, source_target_pairs={{0,1},{1,0},{2,3},{3,2},{4,5},{5,4},{6,7},{7,6},{8,9},{9,8},{10,11... | collective-permute-start | bytes 1769480 | tf_op jit(solution)/shard_map/ppermute | solution.py:752
  19.3 19.4 %slice-start = ((s8[4718592]{0:T(1024)(128)(4,1)}), s8[4194304]{0:T(1024)(128)(4,1)S(1)}, s32[]{:S(2)}) async-start(s8[4718592]{0:T(1024)(128)(4,1)} %bitcast.33), calls=%async_computation | async-start | bytes 8388608
  19.3 19.4 %slice-start.2 = ((s8[4718592]{0:T(1024)(128)(4,1)}), s8[4194304]{0:T(1024)(128)(4,1)S(1)}, s32[]{:S(2)}) async-start(s8[4718592]{0:T(1024)(128)(4,1)} %bitcast.35), calls=%async_computation.2 | async-start | bytes 8388608
  19.6 19.1 %slice-start.1 = ((s8[4718592]{0:T(1024)(128)(4,1)}), s8[524288]{0:T(1024)(128)(4,1)S(1)}, s32[]{:S(2)}) async-start(s8[4718592]{0:T(1024)(128)(4,1)} %bitcast.33), calls=%async_computation.1 | async-start | bytes 1048576
  19.6 19.1 %slice-start.3 = ((s8[4718592]{0:T(1024)(128)(4,1)}), s8[524288]{0:T(1024)(128)(4,1)S(1)}, s32[]{:S(2)}) async-start(s8[4718592]{0:T(1024)(128)(4,1)} %bitcast.35), calls=%async_computation.3 | async-start | bytes 1048576
  19.6 19.1 %copy-start.1 = (bf16[768,768]{1,0:T(8,128)(2,1)S(1)}, bf16[768,768]{1,0:T(8,128)(2,1)}, u32[]{:S(2)}) copy-start(bf16[768,768]{1,0:T(8,128)(2,1)} %wo_ref.3) | copy-start | bytes 3538948
  19.6 19.1 %copy-start.2 = (bf16[384,768]{1,0:T(8,128)(2,1)S(1)}, bf16[384,768]{1,0:T(8,128)(2,1)}, u32[]{:S(2)}) copy-start(bf16[384,768]{1,0:T(8,128)(2,1)} %x_ref.1) | copy-start | bytes 1769476
  19.6 19.1 %copy-start.3 = (bf16[384,768]{1,0:T(8,128)(2,1)S(1)}, bf16[384,768]{1,0:T(8,128)(2,1)}, u32[]{:S(2)}) copy-start(bf16[384,768]{1,0:T(8,128)(2,1)} %cot_ref.1) | copy-start | bytes 1769476
  38.8 12.6 %copy-start.24 = (s32[4]{0:T(128)S(1)}, s32[4]{0:T(128)}, u32[]{:S(2)}) copy-start(s32[4]{0:T(128)} %get-tuple-element.252) | copy-start | bytes 52
  38.8 12.6 %copy-start.25 = (s32[2]{0:T(128)S(1)}, s32[2]{0:T(128)}, u32[]{:S(2)}) copy-start(s32[2]{0:T(128)} %constant.28.clone) | copy-start | bytes 28
  50.9 4.7 %collective-permute-start.3 = (bf16[2,8,96,768]{3,2,1,0:T(8,128)(2,1)S(1)}, bf16[2,8,96,768]{3,2,1,0:T(8,128)(2,1)S(1)}, u32[]{:S(2)}, u32[]{:S(2)}) collective-permute-start(bf16[2,8,96,768]{3,2,1,0:T(8,128)(2,1)S(1)} %get-tuple-element.148), channel_id=1, source_target_pairs={{0,1},{1,0},{2,3},{3,2},{4,5},{5,4},{6,7},{7,6},{8,9},{9,8},{10,11... | collective-permute-start | bytes 7077896 | tf_op jit(solution)/shard_map/ppermute | solution.py:752
  56.6 15.7 %collective-permute-start.4 = (bf16[2,192,768]{2,1,0:T(8,128)(2,1)S(1)}, bf16[2,192,768]{2,1,0:T(8,128)(2,1)S(1)}, u32[]{:S(2)}, u32[]{:S(2)}) collective-permute-start(bf16[2,192,768]{2,1,0:T(8,128)(2,1)S(1)} %get-tuple-element.151), channel_id=1, source_target_pairs={{0,2},{1,3},{2,0},{3,1},{4,6},{5,7},{6,4},{7,5},{8,10},{9,11},{10,... | collective-permute-start | bytes 1769480 | tf_op jit(solution)/shard_map/ppermute | solution.py:752
  58.4 15.3 %collective-permute-start.5 = (bf16[2,192,768]{2,1,0:T(8,128)(2,1)S(1)}, bf16[2,192,768]{2,1,0:T(8,128)(2,1)S(1)}, u32[]{:S(2)}, u32[]{:S(2)}) collective-permute-start(bf16[2,192,768]{2,1,0:T(8,128)(2,1)S(1)} %get-tuple-element.153), channel_id=1, source_target_pairs={{0,4},{1,5},{2,6},{3,7},{4,0},{5,1},{6,2},{7,3},{8,12},{9,13},{10,... | collective-permute-start | bytes 1769480 | tf_op jit(solution)/shard_map/ppermute | solution.py:752
  71.3 14.6 %collective-permute-start.8 = (bf16[2,2,4,240,384]{4,3,2,1,0:T(8,128)(2,1)S(1)}, bf16[2,2,4,240,384]{4,3,2,1,0:T(8,128)(2,1)S(1)}, u32[]{:S(2)}, u32[]{:S(2)}) collective-permute-start(bf16[2,2,4,240,384]{4,3,2,1,0:T(8,128)(2,1)S(1)} %get-tuple-element.160), channel_id=1, source_target_pairs={{0,1},{1,0},{2,3},{3,2},{4,5},{5,4},{6,7},{7,6},{8,9},{9,8},{10,11... | collective-permute-start | bytes 8847368 | tf_op jit(solution)/shard_map/ppermute | solution.py:752
  73.7 3.1 %copy-start.21 = (bf16[768,1536]{1,0:T(8,128)(2,1)S(1)}, bf16[768,1536]{1,0:T(8,128)(2,1)}, u32[]{:S(2)}) copy-start(bf16[768,1536]{1,0:T(8,128)(2,1)} %get-tuple-element.167.xt_ref) | copy-start | bytes 7077892
  73.7 3.4 %copy-start.22 = (f32[384,768]{1,0:T(8,128)S(1)}, f32[384,768]{1,0:T(8,128)}, u32[]{:S(2)}) copy-start(f32[384,768]{1,0:T(8,128)} %get-tuple-element.166.rinv_ref) | copy-start | bytes 3538948
  73.7 3.5 %copy-start.23 = (bf16[384,768]{1,0:T(8,128)(2,1)S(1)}, bf16[384,768]{1,0:T(8,128)(2,1)}, u32[]{:S(2)}) copy-start(bf16[384,768]{1,0:T(8,128)(2,1)} %get-tuple-element.162.q_ref) | copy-start | bytes 1769476
  74.3 11.6 %collective-permute-start.6 = (bf16[1,192,768]{2,1,0:T(8,128)(2,1)S(1)}, bf16[1,192,768]{2,1,0:T(8,128)(2,1)S(1)}, u32[]{:S(2)}, u32[]{:S(2)}) collective-permute-start(bf16[1,192,768]{2,1,0:T(8,128)(2,1)S(1)} %get-tuple-element.156), channel_id=1, source_target_pairs={{0,4},{1,5},{2,6},{3,7},{4,0},{5,1},{6,2},{7,3},{8,12},{9,13},{10,... | collective-permute-start | bytes 884744 | tf_op jit(solution)/shard_map/ppermute | solution.py:752
  75.8 10.0 %collective-permute-start.7 = (bf16[1,192,768]{2,1,0:T(8,128)(2,1)S(1)}, bf16[1,192,768]{2,1,0:T(8,128)(2,1)S(1)}, u32[]{:S(2)}, u32[]{:S(2)}) collective-permute-start(bf16[1,192,768]{2,1,0:T(8,128)(2,1)S(1)} %get-tuple-element.158), channel_id=1, source_target_pairs={{0,2},{1,3},{2,0},{3,1},{4,6},{5,7},{6,4},{7,5},{8,10},{9,11},{10,... | collective-permute-start | bytes 884744 | tf_op jit(solution)/shard_map/ppermute | solution.py:752
  87.7 17.7 %collective-permute-start.10 = (bf16[2,480,384]{2,1,0:T(8,128)(2,1)S(1)}, bf16[2,480,384]{2,1,0:T(8,128)(2,1)S(1)}, u32[]{:S(2)}, u32[]{:S(2)}) collective-permute-start(bf16[2,480,384]{2,1,0:T(8,128)(2,1)S(1)} %get-tuple-element.172), channel_id=1, source_target_pairs={{0,2},{1,3},{2,0},{3,1},{4,6},{5,7},{6,4},{7,5},{8,10},{9,11},{10,... | collective-permute-start | bytes 2211848 | tf_op jit(solution)/shard_map/ppermute | solution.py:752
  88.4 17.3 %collective-permute-start.11 = (bf16[2,480,384]{2,1,0:T(8,128)(2,1)S(1)}, bf16[2,480,384]{2,1,0:T(8,128)(2,1)S(1)}, u32[]{:S(2)}, u32[]{:S(2)}) collective-permute-start(bf16[2,480,384]{2,1,0:T(8,128)(2,1)S(1)} %get-tuple-element.174), channel_id=1, source_target_pairs={{0,4},{1,5},{2,6},{3,7},{4,0},{5,1},{6,2},{7,3},{8,12},{9,13},{10,... | collective-permute-start | bytes 2211848 | tf_op jit(solution)/shard_map/ppermute | solution.py:752
  89.7 14.9 %collective-permute-start.9 = (bf16[1,192,768]{2,1,0:T(8,128)(2,1)S(1)}, bf16[1,192,768]{2,1,0:T(8,128)(2,1)S(1)}, u32[]{:S(2)}, u32[]{:S(2)}) collective-permute-start(bf16[1,192,768]{2,1,0:T(8,128)(2,1)S(1)} %get-tuple-element.170), channel_id=1, source_target_pairs={{0,16},{1,17},{2,18},{3,19},{4,20},{5,21},{6,22},{7,23},{8,24},{9,... | collective-permute-start | bytes 884744 | tf_op jit(solution)/shard_map/ppermute | solution.py:752
  102.0 15.0 %collective-permute-start.14 = (bf16[2,8,96,384]{3,2,1,0:T(8,128)(2,1)S(1)}, bf16[2,8,96,384]{3,2,1,0:T(8,128)(2,1)S(1)}, u32[]{:S(2)}, u32[]{:S(2)}) collective-permute-start(bf16[2,8,96,384]{3,2,1,0:T(8,128)(2,1)S(1)} %get-tuple-element.188), channel_id=1, source_target_pairs={{0,1},{1,0},{2,3},{3,2},{4,5},{5,4},{6,7},{7,6},{8,9},{9,8},{10,11... | collective-permute-start | bytes 3538952 | tf_op jit(solution)/shard_map/ppermute | solution.py:752
  105.7 5.9 %copy-start = (bf16[768,2304]{1,0:T(8,128)(2,1)S(1)}, bf16[768,2304]{1,0:T(8,128)(2,1)}, u32[]{:S(2)}) copy-start(bf16[768,2304]{1,0:T(8,128)(2,1)} %w_ref.3) | copy-start | bytes 10616836
  107.1 9.8 %collective-permute-start.12 = (bf16[1,480,384]{2,1,0:T(8,128)(2,1)S(1)}, bf16[1,480,384]{2,1,0:T(8,128)(2,1)S(1)}, u32[]{:S(2)}, u32[]{:S(2)}) collective-permute-start(bf16[1,480,384]{2,1,0:T(8,128)(2,1)S(1)} %get-tuple-element.184), channel_id=1, source_target_pairs={{0,4},{1,5},{2,6},{3,7},{4,0},{5,1},{6,2},{7,3},{8,12},{9,13},{10,... | collective-permute-start | bytes 1105928 | tf_op jit(solution)/shard_map/ppermute | solution.py:752
  108.6 8.3 %collective-permute-start.13 = (bf16[1,480,384]{2,1,0:T(8,128)(2,1)S(1)}, bf16[1,480,384]{2,1,0:T(8,128)(2,1)S(1)}, u32[]{:S(2)}, u32[]{:S(2)}) collective-permute-start(bf16[1,480,384]{2,1,0:T(8,128)(2,1)S(1)} %get-tuple-element.186), channel_id=1, source_target_pairs={{0,2},{1,3},{2,0},{3,1},{4,6},{5,7},{6,4},{7,5},{8,10},{9,11},{10,... | collective-permute-start | bytes 1105928 | tf_op jit(solution)/shard_map/ppermute | solution.py:752
  110.0 42.4 %collective-permute-start.26 = (bf16[1,96,768]{2,1,0:T(8,128)(2,1)}, bf16[1,96,768]{2,1,0:T(8,128)(2,1)}, u32[]{:S(2)}, u32[]{:S(2)}) collective-permute-start(bf16[1,96,768]{2,1,0:T(8,128)(2,1)} %get-tuple-element.216), channel_id=1, source_target_pairs={{0,8},{1,9},{2,10},{3,11},{4,12},{5,13},{6,14},{7,15},{8,0},{9,1},... | collective-permute-start | bytes 442376 | tf_op jit(solution)/shard_map/ppermute | solution.py:752
  117.7 16.5 %collective-permute-start.16 = (bf16[1,480,384]{2,1,0:T(8,128)(2,1)S(1)}, bf16[1,480,384]{2,1,0:T(8,128)(2,1)S(1)}, u32[]{:S(2)}, u32[]{:S(2)}) collective-permute-start(bf16[1,480,384]{2,1,0:T(8,128)(2,1)S(1)} %get-tuple-element.193), channel_id=1, source_target_pairs={{0,16},{1,17},{2,18},{3,19},{4,20},{5,21},{6,22},{7,23},{8,24},{9,... | collective-permute-start | bytes 1105928 | tf_op jit(solution)/shard_map/ppermute | solution.py:752
  120.3 12.8 %collective-permute-start.17 = (bf16[1,384,384]{2,1,0:T(8,128)(2,1)S(1)}, bf16[1,384,384]{2,1,0:T(8,128)(2,1)S(1)}, u32[]{:S(2)}, u32[]{:S(2)}) collective-permute-start(bf16[1,384,384]{2,1,0:T(8,128)(2,1)S(1)} %get-tuple-element.195), channel_id=1, source_target_pairs={{0,4},{1,5},{2,6},{3,7},{4,0},{5,1},{6,2},{7,3},{8,12},{9,13},{10,... | collective-permute-start | bytes 884744 | tf_op jit(solution)/shard_map/ppermute | solution.py:752
  120.9 12.7 %collective-permute-start.18 = (bf16[1,384,384]{2,1,0:T(8,128)(2,1)S(1)}, bf16[1,384,384]{2,1,0:T(8,128)(2,1)S(1)}, u32[]{:S(2)}, u32[]{:S(2)}) collective-permute-start(bf16[1,384,384]{2,1,0:T(8,128)(2,1)S(1)} %get-tuple-element.196), channel_id=1, source_target_pairs={{0,2},{1,3},{2,0},{3,1},{4,6},{5,7},{6,4},{7,5},{8,10},{9,11},{10,... | collective-permute-start | bytes 884744 | tf_op jit(solution)/shard_map/ppermute | solution.py:752
  122.2 11.4 %collective-permute-start.19 = (bf16[1,384,384]{2,1,0:T(8,128)(2,1)S(1)}, bf16[1,384,384]{2,1,0:T(8,128)(2,1)S(1)}, u32[]{:S(2)}, u32[]{:S(2)}) collective-permute-start(bf16[1,384,384]{2,1,0:T(8,128)(2,1)S(1)} %get-tuple-element.197), channel_id=1, source_target_pairs={{0,6},{1,7},{2,4},{3,5},{4,2},{5,3},{6,0},{7,1},{8,14},{9,15},{10,... | collective-permute-start | bytes 884744 | tf_op jit(solution)/shard_map/ppermute | solution.py:752
  133.2 2.5 %collective-permute-start.15 = (bf16[2,8,112,256]{3,2,1,0:T(8,128)(2,1)S(1)}, bf16[2,8,112,256]{3,2,1,0:T(8,128)(2,1)S(1)}, u32[]{:S(2)}, u32[]{:S(2)}) collective-permute-start(bf16[2,8,112,256]{3,2,1,0:T(8,128)(2,1)S(1)} %get-tuple-element.192), channel_id=1, source_target_pairs={{0,1},{1,0},{2,3},{3,2},{4,5},{5,4},{6,7},{7,6},{8,9},{9,8},{10,11... | collective-permute-start | bytes 2752520 | tf_op jit(solution)/shard_map/ppermute | solution.py:752
  134.5 9.4 %collective-permute-start.24 = (bf16[2,96,384]{2,1,0:T(8,128)(2,1)S(1)}, bf16[2,96,384]{2,1,0:T(8,128)(2,1)S(1)}, u32[]{:S(2)}, u32[]{:S(2)}) collective-permute-start(bf16[2,96,384]{2,1,0:T(8,128)(2,1)S(1)} %get-tuple-element.211), channel_id=1, source_target_pairs={{0,16},{1,17},{2,18},{3,19},{4,20},{5,21},{6,22},{7,23},{8,24},{9,... | collective-permute-start | bytes 442376 | tf_op jit(solution)/shard_map/ppermute | solution.py:752
  135.9 9.9 %collective-permute-start.21 = (bf16[1,448,256]{2,1,0:T(8,128)(2,1)S(1)}, bf16[1,448,256]{2,1,0:T(8,128)(2,1)S(1)}, u32[]{:S(2)}, u32[]{:S(2)}) collective-permute-start(bf16[1,448,256]{2,1,0:T(8,128)(2,1)S(1)} %get-tuple-element.207), channel_id=1, source_target_pairs={{0,4},{1,5},{2,6},{3,7},{4,0},{5,1},{6,2},{7,3},{8,12},{9,13},{10,... | collective-permute-start | bytes 688136 | tf_op jit(solution)/shard_map/ppermute | solution.py:752
  136.5 9.3 %collective-permute-start.22 = (bf16[1,448,256]{2,1,0:T(8,128)(2,1)S(1)}, bf16[1,448,256]{2,1,0:T(8,128)(2,1)S(1)}, u32[]{:S(2)}, u32[]{:S(2)}) collective-permute-start(bf16[1,448,256]{2,1,0:T(8,128)(2,1)S(1)} %get-tuple-element.208), channel_id=1, source_target_pairs={{0,2},{1,3},{2,0},{3,1},{4,6},{5,7},{6,4},{7,5},{8,10},{9,11},{10,... | collective-permute-start | bytes 688136 | tf_op jit(solution)/shard_map/ppermute | solution.py:752
  137.8 11.5 %collective-permute-start.23 = (bf16[1,448,256]{2,1,0:T(8,128)(2,1)S(1)}, bf16[1,448,256]{2,1,0:T(8,128)(2,1)S(1)}, u32[]{:S(2)}, u32[]{:S(2)}) collective-permute-start(bf16[1,448,256]{2,1,0:T(8,128)(2,1)S(1)} %get-tuple-element.209), channel_id=1, source_target_pairs={{0,6},{1,7},{2,4},{3,5},{4,2},{5,3},{6,0},{7,1},{8,14},{9,15},{10,... | collective-permute-start | bytes 688136 | tf_op jit(solution)/shard_map/ppermute | solution.py:752
  143.9 13.4 %collective-permute-start.27 = (bf16[1,240,384]{2,1,0:T(8,128)(2,1)S(1)}, bf16[1,240,384]{2,1,0:T(8,128)(2,1)S(1)}, u32[]{:S(2)}, u32[]{:S(2)}) collective-permute-start(bf16[1,240,384]{2,1,0:T(8,128)(2,1)S(1)} %get-tuple-element.217), channel_id=1, source_target_pairs={{0,8},{1,9},{2,10},{3,11},{4,12},{5,13},{6,14},{7,15},{8,0},{9,1},... | collective-permute-start | bytes 552968 | tf_op jit(solution)/shard_map/ppermute | solution.py:752
  145.8 7.0 %collective-permute-start.20 = (bf16[2,768,384]{2,1,0:T(8,128)(2,1)S(1)}, bf16[2,768,384]{2,1,0:T(8,128)(2,1)S(1)}, u32[]{:S(2)}, u32[]{:S(2)}) collective-permute-start(bf16[2,768,384]{2,1,0:T(8,128)(2,1)S(1)} %get-tuple-element.206), channel_id=1, source_target_pairs={{0,1},{1,0},{2,3},{3,2},{4,5},{5,4},{6,7},{7,6},{8,9},{9,8},{10,11... | collective-permute-start | bytes 3538952 | tf_op jit(solution)/shard_map/ppermute | solution.py:752
  149.5 10.1 %collective-permute-start.28 = (bf16[1,96,384]{2,1,0:T(8,128)(2,1)S(1)}, bf16[1,96,384]{2,1,0:T(8,128)(2,1)S(1)}, u32[]{:S(2)}, u32[]{:S(2)}) collective-permute-start(bf16[1,96,384]{2,1,0:T(8,128)(2,1)S(1)} %get-tuple-element.218), channel_id=1, source_target_pairs={{0,8},{1,9},{2,10},{3,11},{4,12},{5,13},{6,14},{7,15},{8,0},{9,1},... | collective-permute-start | bytes 221192 | tf_op jit(solution)/shard_map/ppermute | solution.py:752
  152.4 5.6 %collective-permute-start.29 = (bf16[1,112,256]{2,1,0:T(8,128)(2,1)S(1)}, bf16[1,112,256]{2,1,0:T(8,128)(2,1)S(1)}, u32[]{:S(2)}, u32[]{:S(2)}) collective-permute-start(bf16[1,112,256]{2,1,0:T(8,128)(2,1)S(1)} %get-tuple-element.220), channel_id=1, source_target_pairs={{0,8},{1,9},{2,10},{3,11},{4,12},{5,13},{6,14},{7,15},{8,0},{9,1},... | collective-permute-start | bytes 172040 | tf_op jit(solution)/shard_map/ppermute | solution.py:752
  152.4 5.5 %collective-permute-start.30 = (bf16[1,112,256]{2,1,0:T(8,128)(2,1)S(1)}, bf16[1,112,256]{2,1,0:T(8,128)(2,1)S(1)}, u32[]{:S(2)}, u32[]{:S(2)}) collective-permute-start(bf16[1,112,256]{2,1,0:T(8,128)(2,1)S(1)} %get-tuple-element.221), channel_id=1, source_target_pairs={{0,16},{1,17},{2,18},{3,19},{4,20},{5,21},{6,22},{7,23},{8,24},{9,... | collective-permute-start | bytes 172040 | tf_op jit(solution)/shard_map/ppermute | solution.py:752
  152.8 6.8 %collective-permute-start.31 = (bf16[1,112,256]{2,1,0:T(8,128)(2,1)S(1)}, bf16[1,112,256]{2,1,0:T(8,128)(2,1)S(1)}, u32[]{:S(2)}, u32[]{:S(2)}) collective-permute-start(bf16[1,112,256]{2,1,0:T(8,128)(2,1)S(1)} %get-tuple-element.222), channel_id=1, source_target_pairs={{0,24},{1,25},{2,26},{3,27},{4,28},{5,29},{6,30},{7,31},{8,16},{9,... | collective-permute-start | bytes 172040 | tf_op jit(solution)/shard_map/ppermute | solution.py:752
  157.3 20.2 %collective-permute-start.25 = (bf16[1,768,384]{2,1,0:T(8,128)(2,1)S(1)}, bf16[1,768,384]{2,1,0:T(8,128)(2,1)S(1)}, u32[]{:S(2)}, u32[]{:S(2)}) collective-permute-start(bf16[1,768,384]{2,1,0:T(8,128)(2,1)S(1)} %get-tuple-element.214), channel_id=1, source_target_pairs={{0,2},{1,3},{2,0},{3,1},{4,6},{5,7},{6,4},{7,5},{8,10},{9,11},{10,... | collective-permute-start | bytes 1769480 | tf_op jit(solution)/shard_map/ppermute | solution.py:752
  160.8 1.2 collective-permute-start.32
  162.0 8.0 %collective-permute-start.33 = (f32[8,128]{1,0:T(8,128)S(1)}, f32[8,128]{1,0:T(8,128)S(1)}, u32[]{:S(2)}, u32[]{:S(2)}) collective-permute-start(f32[8,128]{1,0:T(8,128)S(1)} %add.97), channel_id=1, source_target_pairs={{0,2},{1,3},{2,0},{3,1},{4,6},{5,7},{6,4},{7,5},{8,10},{9,11},{10,... | collective-permute-start | bytes 12296 | tf_op jit(solution)/shard_map/ppermute | solution.py:752
  162.7 7.3 %collective-permute-start.34 = (f32[8,128]{1,0:T(8,128)S(1)}, f32[8,128]{1,0:T(8,128)S(1)}, u32[]{:S(2)}, u32[]{:S(2)}) collective-permute-start(f32[8,128]{1,0:T(8,128)S(1)} %add.97), channel_id=1, source_target_pairs={{0,4},{1,5},{2,6},{3,7},{4,0},{5,1},{6,2},{7,3},{8,12},{9,13},{10,... | collective-permute-start | bytes 12296 | tf_op jit(solution)/shard_map/ppermute | solution.py:752
  163.8 6.2 %collective-permute-start.35 = (f32[8,128]{1,0:T(8,128)S(1)}, f32[8,128]{1,0:T(8,128)S(1)}, u32[]{:S(2)}, u32[]{:S(2)}) collective-permute-start(f32[8,128]{1,0:T(8,128)S(1)} %add.97), channel_id=1, source_target_pairs={{0,6},{1,7},{2,4},{3,5},{4,2},{5,3},{6,0},{7,1},{8,14},{9,15},{10,... | collective-permute-start | bytes 12296 | tf_op jit(solution)/shard_map/ppermute | solution.py:752
  170.0 4.5 %collective-permute-start.36 = (f32[8,128]{1,0:T(8,128)S(1)}, f32[8,128]{1,0:T(8,128)S(1)}, u32[]{:S(2)}, u32[]{:S(2)}) collective-permute-start(f32[8,128]{1,0:T(8,128)S(1)} %add_add_fusion.1), channel_id=1, source_target_pairs={{0,8},{1,9},{2,10},{3,11},{4,12},{5,13},{6,14},{7,15},{8,0},{9,1},... | collective-permute-start | bytes 12296 | tf_op jit(solution)/shard_map/ppermute | solution.py:752
  170.0 4.6 %collective-permute-start.37 = (f32[8,128]{1,0:T(8,128)S(1)}, f32[8,128]{1,0:T(8,128)S(1)}, u32[]{:S(2)}, u32[]{:S(2)}) collective-permute-start(f32[8,128]{1,0:T(8,128)S(1)} %add_add_fusion.1), channel_id=1, source_target_pairs={{0,16},{1,17},{2,18},{3,19},{4,20},{5,21},{6,22},{7,23},{8,24},{9,... | collective-permute-start | bytes 12296 | tf_op jit(solution)/shard_map/ppermute | solution.py:752
  172.0 5.4 %collective-permute-start.38 = (f32[8,128]{1,0:T(8,128)S(1)}, f32[8,128]{1,0:T(8,128)S(1)}, u32[]{:S(2)}, u32[]{:S(2)}) collective-permute-start(f32[8,128]{1,0:T(8,128)S(1)} %add_add_fusion.1), channel_id=1, source_target_pairs={{0,24},{1,25},{2,26},{3,27},{4,28},{5,29},{6,30},{7,31},{8,16},{9,... | collective-permute-start | bytes 12296 | tf_op jit(solution)/shard_map/ppermute | solution.py:752
  177.4 2.9 %copy-start.4 = (f32[192,384]{1,0:T(8,128)S(1)}, f32[192,384]{1,0:T(8,128)}, u32[]{:S(2)}) copy-start(f32[192,384]{1,0:T(8,128)} %refs_8_.1) | copy-start | bytes 884740
  177.4 2.9 %copy-start.5 = (f32[192,384]{1,0:T(8,128)S(1)}, f32[192,384]{1,0:T(8,128)}, u32[]{:S(2)}) copy-start(f32[192,384]{1,0:T(8,128)} %refs_9_.1) | copy-start | bytes 884740
  177.4 2.9 %copy-start.6 = (f32[192,384]{1,0:T(8,128)S(1)}, f32[192,384]{1,0:T(8,128)}, u32[]{:S(2)}) copy-start(f32[192,384]{1,0:T(8,128)} %refs_10_.1) | copy-start | bytes 884740
  177.4 2.9 %copy-start.7 = (f32[768,96]{0,1:T(8,128)S(1)}, f32[768,96]{0,1:T(8,128)}, u32[]{:S(2)}) copy-start(f32[768,96]{0,1:T(8,128)} %param.38) | copy-start | bytes 884740
  177.4 2.9 %copy-start.8 = (f32[768,96]{0,1:T(8,128)S(1)}, f32[768,96]{0,1:T(8,128)}, u32[]{:S(2)}) copy-start(f32[768,96]{0,1:T(8,128)} %param.43) | copy-start | bytes 884740
  177.4 2.9 %copy-start.9 = (f32[768,96]{0,1:T(8,128)S(1)}, f32[768,96]{0,1:T(8,128)}, u32[]{:S(2)}) copy-start(f32[768,96]{0,1:T(8,128)} %param.48) | copy-start | bytes 884740
  177.4 2.9 %copy-start.10 = (f32[96,576]{1,0:T(8,128)S(1)}, f32[96,576]{1,0:T(8,128)}, u32[]{:S(2)}) copy-start(f32[96,576]{1,0:T(8,128)} %refs_0_.1) | copy-start | bytes 663556
  177.5 2.9 %copy-start.11 = (f32[96,576]{1,0:T(8,128)S(1)}, f32[96,576]{1,0:T(8,128)}, u32[]{:S(2)}) copy-start(f32[96,576]{1,0:T(8,128)} %refs_1_.1) | copy-start | bytes 663556
  177.5 2.9 %copy-start.12 = (f32[96,576]{1,0:T(8,128)S(1)}, f32[96,576]{1,0:T(8,128)}, u32[]{:S(2)}) copy-start(f32[96,576]{1,0:T(8,128)} %refs_2_.1) | copy-start | bytes 663556
  177.5 2.9 %copy-start.13 = (f32[192,96]{1,0:T(8,128)S(1)}, f32[192,96]{1,0:T(8,128)}, u32[]{:S(2)}) copy-start(f32[192,96]{1,0:T(8,128)} %refs_4_.1) | copy-start | bytes 221188
  177.5 2.9 %copy-start.14 = (f32[192,96]{1,0:T(8,128)S(1)}, f32[192,96]{1,0:T(8,128)}, u32[]{:S(2)}) copy-start(f32[192,96]{1,0:T(8,128)} %refs_5_.1) | copy-start | bytes 221188
  177.5 2.9 %copy-start.15 = (f32[192,96]{1,0:T(8,128)S(1)}, f32[192,96]{1,0:T(8,128)}, u32[]{:S(2)}) copy-start(f32[192,96]{1,0:T(8,128)} %refs_6_.1) | copy-start | bytes 221188
  (5 other events, 13.8 us)

commit v4 on v3

--- a/solution.py
+++ b/solution.py
@@ -52,88 +52,204 @@
     return lax.dot_general(a, b, (((1,), (1,)), ((), ())), preferred_element_type=F32)
 
 
-def attend_kernel(
-    x0_ref, x1_ref, x2_ref, x3_ref, wq_ref, wk_ref, wv_ref, vec_ref, kmask_ref, qhot_ref,
-    mixed_ref, e_ref, rinv_ref, q_ref, k_ref, v_ref, xt_ref, x_ref,
-):
-    rows = q_ref.shape[0]
-    step = pl.program_id(0)
-    wide = wq_ref.shape[1]
+def softmax_half(q, k, v, kmask, qhot, e_ref):
+    rows, wide = q.shape
     pairs = wide // LANES
-
-    @pl.when(step == 0)
-    def _():
-        for i, ref in enumerate((x0_ref, x1_ref, x2_ref, x3_ref)):
-            x_ref[i * rows : (i + 1) * rows, :] = ref[...]
-
-    xt_ref[...] = x_ref[:, pl.ds(pl.multiple_of(step * wide, LANES), wide)].T
-    k = dot(x_ref[...], wk_ref[...]).astype(BF)
-    v = (dot(x_ref[...], wv_ref[...]) + vec_ref[1:2, :]).astype(BF)
-    q = (dot(x_ref[:rows, :], wq_ref[...]) + vec_ref[0:1, :]).astype(BF)
-    q = q * jnp.asarray(HD**-0.5, BF)
-    q_ref[...] = q
-    k_ref[...] = k
-    v_ref[...] = v
     low = lax.broadcasted_iota(jnp.int32, (rows, LANES), 1) < HD
     part = lambda a, p: a[:, p * LANES : (p + 1) * LANES]
-    keys = [jnp.concatenate([part(k, p), kmask_ref[...]], axis=1) for p in range(pairs)]
+    keys = [jnp.concatenate([part(k, p), kmask], axis=1) for p in range(pairs)]
     values = [jnp.concatenate([part(v, p), jnp.ones((v.shape[0], LANES), BF)], axis=1) for p in range(pairs)]
 
     def score(head):
         qh = part(q, head // 2)
         qh = jnp.where(low if head % 2 == 0 else jnp.logical_not(low), qh, jnp.zeros_like(qh))
-        return dot_t(jnp.concatenate([qh, qhot_ref[...]], axis=1), keys[head // 2])
+        return dot_t(jnp.concatenate([qh, qhot], axis=1), keys[head // 2])
 
     following = score(0)
-    done = []
+    done, results = [], []
     for head in range(2 * pairs):
         scores = following
         if head + 1 < 2 * pairs:
             following = score(head + 1)
-        e = jnp.exp(scores - jnp.max(scores, axis=1, keepdims=True)).astype(BF)
+        top = jnp.max(scores, axis=1, keepdims=True)
+        e = jnp.exp(scores - top).astype(BF)
         e_ref[head] = e
         both = dot(e, values[head // 2])
-        done.append((both[:, :LANES], 1.0 / both[:, LANES:]))
+        done.append((top, both[:, LANES:], both[:, :LANES]))
         if head % 2 == 1:
-            (out0, rinv0), (out1, rinv1) = done[-2:]
-            span = slice(head // 2 * LANES, (head // 2 + 1) * LANES)
-            rinv = jnp.where(low, rinv0, rinv1)
-            rinv_ref[:, span] = rinv
-            mixed_ref[:, span] = (jnp.where(low, out0, out1) * rinv).astype(BF)
-
-
-def attend(blocks, input_weight, vectors, kmask, qhot):
+            results.append([jnp.where(low, a, b) for a, b in zip(*done[-2:])])
+    return results
+
+
+def segment_of(lengths_ref, rows, first):
+    own = lax.axis_index("seq")
+    at = lax.broadcasted_iota(jnp.int32, (rows, LANES), 0)
+    half = rows // 2
+    place = jnp.where(at < half, (first ^ own) * half + at, ((first + 1) ^ own) * half + at - half)
+    segments, end = jnp.zeros((rows, LANES), jnp.int32), 0
+    for n in range(lengths_ref.shape[1]):
+        end = end + lengths_ref[0, n]
+        segments = segments + (place >= end).astype(jnp.int32)
+    return segments
+
+
+def key_mask(lengths_ref, rows, first):
+    lanes = lax.broadcasted_iota(jnp.int32, (rows, LANES), 1)
+    segments = segment_of(lengths_ref, rows, first)
+    return jnp.where((segments == lanes) | (lanes > 3), 0.0, MASK).astype(BF)
+
+
+def project_half(x_ref, blocks, wk_ref, wv_ref, vec_ref, k_ref, v_ref, xt_ref):
+    step = pl.program_id(0)
+    wide = wk_ref.shape[1]
+    rows = blocks[0].shape[0]
+
+    @pl.when(step == 0)
+    def _():
+        for i, ref in enumerate(blocks):
+            x_ref[i * rows : (i + 1) * rows, :] = ref[...]
+
+    xt_ref[...] = x_ref[:, pl.ds(pl.multiple_of(step * wide, LANES), wide)].T
+    k = dot(x_ref[...], wk_ref[...]).astype(BF)
+    v = (dot(x_ref[...], wv_ref[...]) + vec_ref[1:2, :].astype(F32)).astype(BF)
+    k_ref[...] = k
+    v_ref[...] = v
+    return k, v
+
+
+def attend_near_kernel(
+    lengths_ref, x0_ref, x1_ref, wk_ref, wv_ref, vec_ref, wq_ref,
+    e_ref, k_ref, v_ref, xt_ref, q_ref, top_ref, sum_ref, out_ref, qhot_ref, wide_ref, x_ref, kmask,
+):
+    rows, slab = q_ref.shape[0], x_ref.shape[0]
+
+    @pl.when(pl.program_id(0) == 0)
+    def _():
+        kmask[...] = key_mask(lengths_ref, slab, 0)
+        lanes = lax.broadcasted_iota(jnp.int32, (rows, LANES), 1)
+        qhot_ref[...] = (segment_of(lengths_ref, slab, 0)[:rows] == lanes).astype(F32).astype(BF)
+
+    wide_ref[...] = vec_ref[...].astype(F32)
+    k, v = project_half(x_ref, (x0_ref, x1_ref), wk_ref, wv_ref, vec_ref, k_ref, v_ref, xt_ref)
+    q = (dot(x_ref[:rows, :], wq_ref[...]) + vec_ref[0:1, :].astype(F32)).astype(BF)
+    q = q * jnp.asarray(HD**-0.5, BF)
+    q_ref[...] = q
+    for p, made in enumerate(softmax_half(q, k, v, kmask[...], qhot_ref[...], e_ref)):
+        for ref, value in zip((top_ref, sum_ref, out_ref), made):
+            ref[:, p * LANES : (p + 1) * LANES] = value
+
+
+def pass_kernel(x_ref, _, out_ref):
+    out_ref[...] = x_ref[...]
+
+
+def pass_on(x, after):
+    whole = pl.BlockSpec(x.shape, lambda i: (0, 0))
+    return pl.pallas_call(
+        pass_kernel,
+        grid=(1,), in_specs=[whole, pl.BlockSpec(memory_space=pl.ANY)], out_specs=whole,
+        out_shape=jax.ShapeDtypeStruct(x.shape, x.dtype),
+        compiler_params=params(6), cost_estimate=cost(1), name="pass_on",
+    )(x, after)
+
+
+def project_kernel(x_ref, xp_ref, wk_ref, wv_ref, vec_ref, _, k_ref, v_ref, xt_ref):
+    xt_ref[...] = xp_ref[...].T
+    k_ref[...] = dot(x_ref[...], wk_ref[...]).astype(BF)
+    v_ref[...] = (dot(x_ref[...], wv_ref[...]) + vec_ref[1:2, :]).astype(BF)
+
+
+def project(x, input_weight, vectors, after):
+    rows, width = x.shape
+    wide = 3 * LANES
+    steps = width // wide
+    weight = in_hbm(input_weight)
+    cols = lambda r, off=0: pl.BlockSpec((r, wide), lambda p: (0, p + off))
+    down = pl.BlockSpec((wide, rows), lambda p: (p, 0))
+    return pl.pallas_call(
+        project_kernel,
+        grid=(steps,),
+        in_specs=[
+            pl.BlockSpec((rows, width), lambda p: (0, 0)), cols(rows), cols(width, steps), cols(width, 2 * steps),
+            cols(vectors.shape[0]), pl.BlockSpec(memory_space=pl.ANY),
+        ],
+        out_specs=[cols(rows), cols(rows), down],
+        out_shape=[jax.ShapeDtypeStruct((rows, width), BF)] * 2 + [jax.ShapeDtypeStruct((width, rows), BF)],
+        compiler_params=params(12), cost_estimate=cost(5),
+        name="project",
+    )(x, x, weight, weight, vectors, after)
+
+
+def attend_far_kernel(
+    lengths_ref, x0_ref, wk_ref, wv_ref, vec_ref, qhot_ref, q_ref, top_ref, sum_ref, out_ref, k0_ref, v0_ref, xt0_ref,
+    e_ref, k_ref, v_ref, xt_ref, mixed_ref, near_ref, far_ref, x_ref, kmask,
+):
+    rows = x0_ref.shape[0]
+
+    @pl.when(pl.program_id(0) == 0)
+    def _():
+        kmask[...] = key_mask(lengths_ref, 2 * rows, 2)
+
+    project_half(
+        x_ref, (x0_ref,), wk_ref, wv_ref, vec_ref, k_ref.at[rows:, :], v_ref.at[rows:, :], xt_ref.at[:, rows:]
+    )
+    k_ref[:rows, :] = k0_ref[...]
+    v_ref[:rows, :] = v0_ref[...]
+    xt_ref[:, :rows] = xt0_ref[...]
+    k, v = k_ref[...], v_ref[...]
+    for p, (top, total, out) in enumerate(softmax_half(q_ref[...], k, v, kmask[...], qhot_ref[...], e_ref)):
+        span = slice(p * LANES, (p + 1) * LANES)
+        both = jnp.maximum(top, top_ref[:, span])
+        near, far = jnp.exp(top_ref[:, span] - both), jnp.exp(top - both)
+        rinv = 1.0 / (near * sum_ref[:, span] + far * total)
+        near, far = near * rinv, far * rinv
+        near_ref[:, span] = near
+        far_ref[:, span] = far
+        mixed_ref[:, span] = (out_ref[:, span] * near + out * far).astype(BF)
+
+
+def attend(lengths, blocks, input_weight, vectors, near=()):
     rows, width = blocks[0].shape
-    slab = rows * len(blocks)
+    slab = 2 * rows
     wide = 2 * LANES
     steps = width // wide
     weight = in_hbm(input_weight)
-    full = lambda a: pl.BlockSpec(a.shape, lambda p: (0,) * a.ndim)
+    full = lambda shape: pl.BlockSpec(shape, lambda p: (0,) * len(shape))
     cols = lambda r, off=0: pl.BlockSpec((r, wide), lambda p: (0, p + off))
+    down = lambda c: pl.BlockSpec((wide, c), lambda p: (p, 0))
+    inputs = [lengths, *blocks, weight, weight, vectors]
+    in_specs = [
+        pl.BlockSpec(memory_space=pltpu.SMEM), *(full(b.shape) for b in blocks), cols(width, steps), cols(width, 2 * steps), cols(vectors.shape[0]),
+    ]
+    out_specs = [
+        pl.BlockSpec((wide // HD, rows, slab), lambda p: (p, 0, 0)), cols(slab), cols(slab), down(slab),
+    ]
+    out_shape = [
+        pltpu.HBM((width // HD, rows, slab), BF), pltpu.HBM((slab, width), BF), pltpu.HBM((slab, width), BF),
+        pltpu.HBM((width, slab), BF),
+    ]
+    if near:
+        inputs += near
+        in_specs += [full((rows, LANES)), *[cols(rows)] * 6, down(rows)]
+        out_specs += [cols(rows)] * 3
+        out_shape += [jax.ShapeDtypeStruct((rows, width), BF), *[pltpu.HBM((rows, width), F32)] * 2]
+    else:
+        inputs[1] = in_hbm(inputs[1])
+        inputs.append(weight)
+        in_specs.append(cols(width))
+        out_specs += [*[cols(rows)] * 4, full((rows, LANES)), cols(vectors.shape[0])]
+        out_shape += [
+            jax.ShapeDtypeStruct((rows, width), BF), *[jax.ShapeDtypeStruct((rows, width), F32)] * 3,
+            jax.ShapeDtypeStruct((rows, LANES), BF), jax.ShapeDtypeStruct(vectors.shape, F32),
+        ]
     return pl.pallas_call(
-        attend_kernel,
-        grid=(steps,),
-        in_specs=[
-            *map(full, blocks), cols(width), cols(width, steps), cols(width, 2 * steps),
-            cols(vectors.shape[0]), full(kmask), full(qhot),
-        ],
-        out_specs=[
-            cols(rows), pl.BlockSpec((wide // HD, rows, slab), lambda p: (p, 0, 0)), cols(rows), cols(rows),
-            cols(slab), cols(slab), pl.BlockSpec((wide, slab), lambda p: (p, 0)),
-        ],
-        out_shape=[
-            jax.ShapeDtypeStruct((rows, width), BF),
-            pltpu.HBM((width // HD, rows, slab), BF),
-            pltpu.HBM((rows, width), F32),
-            pltpu.HBM((rows, width), BF),
-            pltpu.HBM((slab, width), BF),
-            pltpu.HBM((slab, width), BF),
-            pltpu.HBM((width, slab), BF),
-        ],
-        scratch_shapes=[pltpu.VMEM((slab, width), BF)],
-        compiler_params=params(40), cost_estimate=cost(20),
+        attend_far_kernel if near else attend_near_kernel,
+        grid=(steps,), in_specs=in_specs, out_specs=out_specs,
+        scratch_shapes=[pltpu.VMEM((rows * len(blocks), width), BF), pltpu.VMEM((slab, LANES), BF)],
+        out_shape=out_shape,
+        compiler_params=params(28), cost_estimate=cost(11),
         name="attend",
-    )(in_hbm(blocks[0]), *blocks[1:], weight, weight, weight, vectors, kmask, qhot)
+    )(*inputs)
 
 
 def spot(d, own_d):
@@ -143,6 +259,16 @@
 
 def turn(j):
     return jnp.where(j < 2, 2 * j + 1, 2 * (j - 2))
+
+
+def by_rows(rows, body):
+    block = rows // 4
+
+    def step(i, carry):
+        body(pl.ds(pl.multiple_of(i * block, block), block))
+        return carry
+
+    lax.fori_loop(0, 4, step, 0)
 
 
 def store_rows(ref, block, own_d):
@@ -190,17 +316,21 @@
 
     @pl.when(step == 0)
     def _():
-        z = x_ref[...].astype(F32) + dot(mixed_ref[...], wo_ref[...]) + row(2)
-        center = z - jnp.mean(z, axis=1, keepdims=True)
-        inverse = lax.rsqrt(jnp.mean(center * center, axis=1, keepdims=True) + NORM_EPS)
-        normed = center * inverse
-        hidden = normed * row(3) + row(4)
-        hid[...] = hidden
-        norm1_ref[...] = normed
-        inv1_ref[...] = jnp.broadcast_to(inverse, inv1_ref.shape)
-        low = hidden.astype(BF)
-        hl[...] = low
-        hlt_ref[...] = low.T
+        acc[...] = dot(mixed_ref[...], wo_ref[...])
+
+        def first_norm(at):
+            z = x_ref[at, :].astype(F32) + acc[at, :] + row(2)
+            center = z - jnp.mean(z, axis=1, keepdims=True)
+            inverse = lax.rsqrt(jnp.mean(center * center, axis=1, keepdims=True) + NORM_EPS)
+            normed = center * inverse
+            hidden = normed * row(3) + row(4)
+            hid[at, :] = hidden
+            norm1_ref[at, :] = normed
+            inv1_ref[at, :] = jnp.broadcast_to(inverse, (z.shape[0], LANES))
+            hl[at, :] = hidden.astype(BF)
+
+        by_rows(rows, first_norm)
+        hlt_ref[...] = hl[...].T
         mt_ref[...] = mixed_ref[...].T
         vg_ref[...] = jnp.zeros_like(vg_ref)
 
@@ -225,23 +355,26 @@
 
     @pl.when(step == chunks - 1)
     def _():
-        z = hid[...] + acc[...] + row(5)
-        center = z - jnp.mean(z, axis=1, keepdims=True)
-        inverse = lax.rsqrt(jnp.mean(center * center, axis=1, keepdims=True) + NORM_EPS)
-        normed = center * inverse
-        valid = 1.0 - qhot_ref[:, 3:4].astype(F32)
-        layer_ref[...] = ((normed * row(6) + row(7)) * valid).astype(BF)
-        gy = cot_ref[...].astype(F32) * valid
-        vg_ref[6:7, :] = jnp.sum(gy * normed, axis=0, keepdims=True)
-        vg_ref[7:8, :] = jnp.sum(gy, axis=0, keepdims=True)
-        e = gy * row(6)
-        grad = e - jnp.mean(e, axis=1, keepdims=True)
-        grad = (grad - normed * jnp.mean(e * normed, axis=1, keepdims=True)) * inverse
-        low = grad.astype(BF)
-        vg_ref[5:6, :] = jnp.sum(low.astype(F32), axis=0, keepdims=True)
-        gb_ref[...] = low
-        gbt[...] = low.T
-        gs_ref[...] = grad
+        def second_norm(at):
+            z = hid[at, :] + acc[at, :] + row(5)
+            center = z - jnp.mean(z, axis=1, keepdims=True)
+            inverse = lax.rsqrt(jnp.mean(center * center, axis=1, keepdims=True) + NORM_EPS)
+            normed = center * inverse
+            valid = 1.0 - qhot_ref[at, :][:, 3:4].astype(F32)
+            layer_ref[at, :] = ((normed * row(6) + row(7)) * valid).astype(BF)
+            gy = cot_ref[at, :].astype(F32) * valid
+            e = gy * row(6)
+            grad = e - jnp.mean(e, axis=1, keepdims=True)
+            grad = (grad - normed * jnp.mean(e * normed, axis=1, keepdims=True)) * inverse
+            low = grad.astype(BF)
+            vg_ref[5:6, :] += jnp.sum(low.astype(F32), axis=0, keepdims=True)
+            vg_ref[6:7, :] += jnp.sum(gy * normed, axis=0, keepdims=True)
+            vg_ref[7:8, :] += jnp.sum(gy, axis=0, keepdims=True)
+            gb_ref[at, :] = low
+            gs_ref[at, :] = grad
+
+        by_rows(rows, second_norm)
+        gbt[...] = gb_ref[...].T
 
     @pl.when(step >= chunks)
     def _():
@@ -305,7 +438,7 @@
 def behind_kernel(
     own_ref, slope_ref, gb_ref, gs_ref, norm1_ref, inv1_ref, hlt_ref, mt_ref, wo_ref, we_ref, wr_ref, vec_ref, _,
     gf_ref, gm_ref, es_ref, ek_ref, vg_ref,
-    acc, tmp,
+    acc, tmp, ga,
 ):
     j = pl.program_id(0)
     own_s, own_d = own_ref[0], own_ref[1]
@@ -335,18 +468,22 @@
 
     @pl.when(j == pl.num_programs(0) - 1)
     def _():
-        gy = acc[...]
-        normed = norm1_ref[...]
-        vg_ref[3:4, :] = jnp.sum(gy * normed, axis=0, keepdims=True)
-        vg_ref[4:5, :] = jnp.sum(gy, axis=0, keepdims=True)
-        e = gy * row(3)
-        grad = e - jnp.mean(e, axis=1, keepdims=True)
-        grad = (grad - normed * jnp.mean(e * normed, axis=1, keepdims=True)) * inv1_ref[:, :1]
-        gf_ref[...] = grad
-        low = grad.astype(BF)
-        vg_ref[2:3, :] = jnp.sum(low.astype(F32), axis=0, keepdims=True)
-        gm_ref[...] = dot_t(low, wo_ref[...]).astype(BF)
-        gat = low.T
+        def first_back(at):
+            gy = acc[at, :]
+            normed = norm1_ref[at, :]
+            e = gy * row(3)
+            grad = e - jnp.mean(e, axis=1, keepdims=True)
+            grad = (grad - normed * jnp.mean(e * normed, axis=1, keepdims=True)) * inv1_ref[at, :][:, :1]
+            gf_ref[at, :] = grad
+            rounded = grad.astype(BF)
+            vg_ref[2:3, :] += jnp.sum(rounded.astype(F32), axis=0, keepdims=True)
+            vg_ref[3:4, :] += jnp.sum(gy * normed, axis=0, keepdims=True)
+            vg_ref[4:5, :] += jnp.sum(gy, axis=0, keepdims=True)
+            ga[at, :] = rounded
+
+        by_rows(rows, first_back)
+        gm_ref[...] = dot_t(ga[...], wo_ref[...]).astype(BF)
+        gat = ga[...].T
         for part, ref in ((1, es_ref), (0, ek_ref)):
             for ry in range(2):
                 start = pl.multiple_of((own_s ^ (2 * ry + part)) * fourth, fourth)
@@ -380,7 +517,9 @@
                 full(vectors.shape), pl.BlockSpec(memory_space=pl.ANY),
             ],
             out_specs=[full((rows, width)), full((rows, width)), full(spread), full(spread), full((16, width))],
-            scratch_shapes=[pltpu.VMEM((rows, width), F32), pltpu.VMEM((4, fourth, cut), BF)],
+            scratch_shapes=[
+                pltpu.VMEM((rows, width), F32), pltpu.VMEM((4, fourth, cut), BF), pltpu.VMEM((rows, width), BF),
+            ],
         ),
         out_shape=[
             jax.ShapeDtypeStruct((rows, width), F32),
@@ -394,9 +533,8 @@
     )(own, slope, gb, gs, norm1, inv1, hlt, mt, output_weight, expand_weight, reduce_weight, vectors, after)
 
 
-def back_kernel(group, pairs, first, last, own_ref, e_ref, q_ref, k_ref, v_ref, gm_ref, mixed_ref, rinv_ref, xt_ref,
-                *rest):
-    rest = list(rest[1:])
+def back_kernel(group, pairs, first, last, own_ref, q_ref, gm_ref, mixed_ref, *rest):
+    halves, rest = (rest[:5], rest[5:10]), list(rest[11:])
     gw_in_ref = None if first else rest.pop(0)
     vec_in = [rest.pop(0) for _ in range(4)] if group == 1 else []
     dq_ref, dkv_ref, vb_ref = rest[:3]
@@ -408,26 +546,29 @@
     i = pl.program_id(0)
     own_s, own_d = own_ref[0], own_ref[1]
     rows = q_ref.shape[0]
-    q, k, v = q_ref[...], k_ref[...], v_ref[...]
-    gm = gm_ref[...].astype(F32) * rinv_ref[...]
-    both = gm * mixed_ref[...].astype(F32)
-    gm_low = gm.astype(BF)
-    gm_t = gm_low.T
-    q_t = q.T
+    q_t = q_ref[...].T
     low = lax.broadcasted_iota(jnp.int32, (rows, LANES), 1) < HD
-    dqs, dks, dvs = [], [], []
-    for head in range(2):
-        own = low if head == 0 else jnp.logical_not(low)
-        span = slice(head * HD, (head + 1) * HD)
-        e = e_ref[head]
-        inner = jnp.sum(jnp.where(own, both, 0.0), axis=1, keepdims=True)
-        grad_e = dot_t(jnp.where(own, gm_low, jnp.zeros_like(gm_low)), v)
-        ds = (e.astype(F32) * (grad_e - inner)).astype(BF)
-        dqs.append(dot(ds, k))
-        dks.append(dot(q_t[span, :], ds))
-        dvs.append(dot(gm_t[span, :], e))
+    dqs, dkvs = [0.0, 0.0], []
+    for e_ref, k_ref, v_ref, rinv_ref, _ in halves:
+        k, v = k_ref[...], v_ref[...]
+        gm = gm_ref[...].astype(F32) * rinv_ref[...]
+        both = gm * mixed_ref[...].astype(F32)
+        gm_low = gm.astype(BF)
+        gm_t = gm_low.T
+        dks, dvs = [], []
+        for head in range(2):
+            own = low if head == 0 else jnp.logical_not(low)
+            span = slice(head * HD, (head + 1) * HD)
+            e = e_ref[head]
+            inner = jnp.sum(jnp.where(own, both, 0.0), axis=1, keepdims=True)
+            grad_e = dot_t(jnp.where(own, gm_low, jnp.zeros_like(gm_low)), v)
+            ds = (e.astype(F32) * (grad_e - inner)).astype(BF)
+            dqs[head] = dqs[head] + dot(ds, k)
+            dks.append(dot(q_t[span, :], ds))
+            dvs.append(dot(gm_t[span, :], e))
+        dkvs.append(jnp.concatenate([*dks, *dvs], axis=0).astype(BF))
     dq = (jnp.where(low, dqs[0], dqs[1]) * HD**-0.5).astype(BF)
-    dkv = jnp.concatenate([*dks, *dvs], axis=0).astype(BF)
+    dkv = jnp.concatenate(dkvs, axis=1)
     dq_ref[...] = dq
     dkv_ref[...] = dkv
     ones = jnp.ones((8, dkv.shape[1]), BF)
@@ -451,8 +592,8 @@
         def _():
             gw[...] = gw_in_ref[...]
 
-    grad_q = dot(xt_ref[:, :rows], dq).astype(BF)
-    grad_kv = dot_t(xt_ref[...], dkv).astype(BF)
+    grad_q = dot(halves[0][4][:, :rows], dq).astype(BF)
+    grad_kv = sum(dot_t(half[4][...], part) for half, part in zip(halves, dkvs)).astype(BF)
     piece = grad_q.shape[0] // 8
     blocks = [b.reshape(8, piece, LANES) for b in (grad_q, grad_kv[:, :LANES], grad_kv[:, LANES:])]
     for n, pair in enumerate(pairs):
@@ -481,21 +622,26 @@
                         ref[ry, spot(d, own_d)] = gw[own_s ^ (2 * ry + part), d]
 
 
-def attend_back(group, pairs, own, e, q, k, v, grad_mixed, mixed, rinv, x_t, after, gw=None, last=True, vecs=()):
+def attend_back(group, pairs, own, q, grad_mixed, mixed, halves, after, gw=None, last=True, vecs=()):
     first = gw is None
     rows, width = q.shape
-    slab = k.shape[0]
+    half = halves[0][1].shape[0]
+    slab = 2 * half
     piece = width // 8
     span = WIDTHS[group]
-    own = jnp.concatenate([own, jnp.array(pairs, jnp.int32)])
+    pair_of = lambda i: jnp.where(i == 0, pairs[0], pairs[1])
     full = lambda shape: pl.BlockSpec(shape, lambda i, own: (0,) * len(shape))
-    cols = lambda r: pl.BlockSpec((r, LANES), lambda i, own: (0, own[2 + i]))
-    inputs = [in_hbm(e), q, k, v, grad_mixed, mixed, rinv, x_t, after]
-    in_specs = [
-        pl.BlockSpec((2, rows, slab), lambda i, own: (own[2 + i], 0, 0)),
-        cols(rows), cols(slab), cols(slab), cols(rows), cols(rows), cols(rows), full(x_t.shape),
-        pl.BlockSpec(memory_space=pl.ANY),
-    ]
+    cols = lambda r: pl.BlockSpec((r, LANES), lambda i, own: (0, pair_of(i)))
+    inputs = [q, grad_mixed, mixed]
+    in_specs = [cols(rows)] * 3
+    for e, k, v, rinv, x_t in halves:
+        inputs += [in_hbm(e), k, v, rinv, x_t]
+        in_specs += [
+            pl.BlockSpec((2, rows, half), lambda i, own: (pair_of(i), 0, 0)),
+            cols(half), cols(half), cols(rows), full(x_t.shape),
+        ]
+    inputs.append(after)
+    in_specs.append(pl.BlockSpec(memory_space=pl.ANY))
     out_shape = [
         jax.ShapeDtypeStruct((rows, len(pairs) * LANES), BF),
         jax.ShapeDtypeStruct((len(pairs) * 2 * LANES, slab), BF),
@@ -573,7 +719,7 @@
     last = dx is not None
     count = 2 * sum(map(len, pairs))
     full = lambda a: pl.BlockSpec(a.shape, lambda j: (0,) * a.ndim)
-    column = lambda a: pl.BlockSpec((a.shape[0], rows), lambda j: (0, lax.rem(j + 2, 4)))
+    column = lambda a: pl.BlockSpec((a.shape[0], rows), lambda j: (0, turn(j)))
     block = lambda pick: pl.BlockSpec((1, width, rows), lambda j: (pick(j), 0, 0))
     if last:
         out_specs = [block(lambda j: jnp.minimum(j, 1)), block(lambda j: jnp.maximum(j - 2, 0))]
@@ -717,7 +863,7 @@
     return (new_one, new_two, new_master, new_master.astype(BF))
 
 
-def adam_kernel(rates, turned, squares_ref, _, *refs):
+def adam_kernel(rates, turned, squares_ref, *refs):
     n = len(rates)
     ins, outs = refs[: 4 * n], refs[4 * n :]
     norm = jnp.sqrt(squares_ref[0:1, 0:1])
@@ -732,8 +878,8 @@
             outs[1 + 4 * a + b][...] = made[b]
 
 
-def adam_all(squares, after, states, grads, rates, turned):
-    inputs, out_shape = [squares, after], [jax.ShapeDtypeStruct((1, 1), F32)]
+def adam_all(squares, states, grads, rates, turned):
+    inputs, out_shape = [squares], [jax.ShapeDtypeStruct((1, 1), F32)]
     for state, grad in zip(states, grads):
         inputs += [*state, grad]
         shape = state[0].shape
@@ -741,7 +887,7 @@
     vmem = pl.BlockSpec(memory_space=pltpu.VMEM)
     return pl.pallas_call(
         functools.partial(adam_kernel, rates, turned),
-        in_specs=[vmem, pl.BlockSpec(memory_space=pl.ANY), *[vmem] * (len(inputs) - 2)], out_specs=[vmem] * len(out_shape), out_shape=out_shape,
+        in_specs=[vmem] * len(inputs), out_specs=[vmem] * len(out_shape), out_shape=out_shape,
         compiler_params=params(16), cost_estimate=cost(5), name="adam",
     )(*inputs)
 
@@ -754,10 +900,10 @@
     return move
 
 
-def tree_sum(move, value):
+def tree_sum(move, value, token):
     value = value + move(value, 0, 1)
     value = (value + move(value, 0, 2)) + (move(value, 1, 0) + move(value, 1, 2))
-    return (value + move(value, 2, 0)) + (move(value, 4, 0) + move(value, 6, 0))
+    return (value + move(value, 2, 0)) + (move(value, 4, 0) + move(value, 6, 0)) + token
 
 
 def spread_out(move, parts):
@@ -877,31 +1023,20 @@
 ):
     rows, width = frames.shape
     seq, dp = lax.axis_size("seq"), lax.axis_size("dp")
-    slab = rows * seq
     move = mover(dp, seq)
     own_s, own_d = lax.axis_index("seq"), lax.axis_index("dp")
     fast = dp == 8
-    vectors = vector_copy.astype(F32)
-
+
+    near = move(frames, 0, 1)
     across = move(frames, 0, 2)
-    near = move(frames, 0, 1)
+    own = jnp.stack([own_s, own_d]).astype(jnp.int32) if fast else jnp.zeros((2,), jnp.int32)
+
+    e0, k0, v0, xt0, q, *stats, qhot, vectors = attend(lengths, (frames, near), input_weight, vector_copy)
+    across = pass_on(across, stats[0])
     far = move(across, 0, 1)
-
-    first_end = lengths[0, 0]
-    second_end = first_end + lengths[0, 1]
-    third_end = second_end + lengths[0, 2]
-    order = jnp.array([0, 2, 1, 3], jnp.int32) ^ own_s
-    positions = (order[:, None] * rows + jnp.arange(rows, dtype=jnp.int32)[None, :]).reshape(slab, 1)
-    segments = sum((positions >= end).astype(jnp.int32) for end in (first_end, second_end, third_end))
-    lanes = jnp.arange(LANES, dtype=jnp.int32)[None, :]
-    kmask = jnp.where((segments == lanes) | (lanes > 3), 0.0, MASK).astype(BF)
-    qhot = (segments[:rows] == lanes).astype(BF)
-    if fast:
-        own = jnp.stack([own_s, own_d]).astype(jnp.int32)
-    else:
-        own = jnp.zeros((2,), jnp.int32)
-
-    mixed, e, rinv, q, k, v, x_t = attend((frames, across, near, far), input_weight, vectors, kmask, qhot)
+    rest = qhot, q, *stats, *project(across, input_weight, vectors, stats[0])
+    e1, k1, v1, xt1, mixed, rinv0, rinv1 = attend(lengths, (far,), input_weight, vectors, rest)
+    halves = (e0, k0, v0, rinv0, xt0), (e1, k1, v1, rinv1, xt1)
     layer, act, slope, norm1, inv1, hlt, mt, gs, gb, gbt, red_s, vec1 = ahead(
         own, mixed, frames, cotangent, qhot, output_weight, expand_weight, reduce_weight, vectors
     )
@@ -912,17 +1047,19 @@
         )
 
     def back(group, pairs, grad_mixed, after, **more):
-        return attend_back(group, pairs, own, e, q, k, v, grad_mixed, mixed, rinv, x_t, after, **more)
+        return attend_back(group, pairs, own, q, grad_mixed, mixed, halves, after, **more)
 
     if fast:
         red, exp, in1, in2, gx, dx = reduce_fast(move, own, back, behind_of, input_weight, gbt, act, red_s, vec1)
         inp, out, exp, red, vec, squares = finish(own, red, exp, in1, in2, dx[0])
-        squares = tree_sum(move, squares)
+        frames_gradient, token = frames_end(gx, *dx)
+        squares = tree_sum(move, squares, token)
     else:
         inp, out, exp, red, vec, squares, gx, dx = reduce_plain(
             move, own, back, behind_of, input_weight, gbt, act, red_s, vec1
         )
-    frames_gradient, token = frames_end(gx, *dx)
+        frames_gradient, token = frames_end(gx, *dx)
+        squares = squares + token
 
     grads = [inp, out, exp, red, vec]
     masters, firsts, seconds = (list(states[i : i + 5]) for i in (0, 5, 10))
@@ -931,7 +1068,7 @@
     hidden = expand_weight.shape[1]
     wide, narrow = 2.0 * width**-0.5, 2.0 * hidden**-0.5
     norm, *made = adam_all(
-        squares, token, list(zip(masters, firsts, seconds)), grads,
+        squares, list(zip(masters, firsts, seconds)), grads,
         ((wide, 0.01), (wide, 0.01), (wide, 0.01), (narrow, 0.01), (0.5, 0.0)),
         (False, True, False, False, False),
     )

time: 183 us -> 175 us (0.956)
  Pallas kernels: 93.7 us -> 103 us
  waiting for transfers between devices: 33.7 us -> 26.7 us
  starting transfers between devices: 45.8 us -> 40.9 us
  other arithmetic: 3.92 us -> 0.09 us
  between operations: 3.39 us -> 1.53 us
    ppermute x39, waiting for transfers between devices: 33.7 us -> 26.7 us  [move(): return lax.ppermute(value, AXES, pairs)]
    pallas_call x1 -> x4, Pallas kernels: 19 us -> 25.5 us  [the longest x2 22.2 us: attend(): pl.pallas_call(attend_far_kernel if near else attend_near_kernel, grid=(s...]
    ppermute x39, starting transfers between devices: 45.8 us -> 40.9 us  [move(): return lax.ppermute(value, AXES, pairs)]
  transfers between devices with their start and end apart: 39 -> 39, of which waited for: 17 -> 18; matrix products, arithmetic and copies ran while one was open for 3% -> 0% of each run, Pallas kernels for 30% -> 42%
where the time goes in v4:
time: 175 us
  Pallas kernels  103 us (59%)
  starting transfers between devices  40.9 us (23%)
  waiting for transfers between devices  26.7 us (15%)
  local copies, waits for them, and re-layouts  2.75 us (2%)
    ppermute x39, starting transfers between devices, move(): return lax.ppermute(value, AXES, pairs)  40.9 us
    pallas_call x3, Pallas kernels, attend_back(): pl.pallas_call(functools.partial(back_kernel, group, pairs, first, last),...  28.8 us
    ppermute x39, waiting for transfers between devices, move(): return lax.ppermute(value, AXES, pairs)  26.7 us
    pallas_call x2, Pallas kernels, attend(): pl.pallas_call(attend_far_kernel if near else attend_near_kernel, grid=(s...  22.2 us
    pallas_call x1, Pallas kernels, ahead(): pl.pallas_call(ahead_kernel, grid_spec=pltpu.PrefetchScalarGridSpec(num_s...  13.2 us
    pallas_call x1, Pallas kernels, behind(): pl.pallas_call(behind_kernel, grid_spec=pltpu.PrefetchScalarGridSpec(num_...  11.7 us
    pallas_call x2, Pallas kernels, frames_back(): pl.pallas_call(functools.partial(frames_kernel, pairs, last), grid=(4,),...  8.62 us
    pallas_call x9, Pallas kernels, gather(): pl.pallas_call(functools.partial(gather_kernel, plan), grid=(steps,), in_...  6.62 us
  transfers between devices with their start and end apart: 39, of which 18 were waited for; matrix products, arithmetic and copies ran while one was open for 0% of the time, Pallas kernels for 42%

profile of v4, /device:TPU:0, one launch (start us, length us, event | category | flops | bytes accessed | tf_op | source)
XLA Modules:
  0.0 174.8 jit_solution(10096091138597849562)
XLA Ops:
  0.7 0.5 collective-permute-start.1
  1.2 2.6 %collective-permute-start = (bf16[384,768]{1,0:T(8,128)(2,1)}, bf16[384,768]{1,0:T(8,128)(2,1)S(1)}, u32[]{:S(2)}, u32[]{:S(2)}) collective-permute-start(bf16[384,768]{1,0:T(8,128)(2,1)} %x_ref.1), channel_id=1, source_target_pairs={{0,2},{1,3},{2,0},{3,1},{4,6},{5,7},{6,4},{7,5},{8,10},{9,11},{10,... | collective-permute-start | bytes 1769480 | tf_op jit(solution)/shard_map/ppermute | solution.py:898
  3.9 0.7 copy-done.16
  4.6 0.7 copy-done.20
  5.2 11.8 %attend.2 = (bf16[12,384,768]{2,1,0:T(8,128)(2,1)}, bf16[768,768]{1,0:T(8,128)(2,1)}, bf16[768,768]{1,0:T(8,128)(2,1)}, bf16[768,768]{1,0:T(8,128)(2,1)}, bf16[3...) custom-call(s32[1,3]{1,0:T(1,128)S(1)} %copy-done.20, ...), custom_call_target="tpu_custom_call" | custom-call | flops 48399998976 | tf_op jit(solution)/shard_map/attend/pallas_call | solution.py:245
  17.0 0.9 collective-permute-done.x_ref
  18.0 3.2 %project.1 = (bf16[384,768]{1,0:T(8,128)(2,1)S(1)}, bf16[384,768]{1,0:T(8,128)(2,1)S(1)}, bf16[768,384]{1,0:T(8,128)(2,1)S(1)}) custom-call(bf16[384,768]{1,0:T(8,128)(2,1)S(1)} %pass_on.1.x_ref.xp_ref, bf16[384,768]{1,0:T(8,128)(2,1)S(1)} %pass_on.1.x_ref.xp_ref, bf16[768,2304]{1,0:T(8,128)(2,1)} %w_ref.3, bf16[768,2304]{1,0:T(8,128)(2,1)} %w_ref.3, ...), custom_call_target="tpu_custom_call" | custom-call | flops 22000001024 | tf_op jit(solution)/shard_map/project/pallas_call | solution.py:169
  21.3 10.5 %attend.3 = (bf16[12,384,768]{2,1,0:T(8,128)(2,1)}, bf16[768,768]{1,0:T(8,128)(2,1)}, bf16[768,768]{1,0:T(8,128)(2,1)}, bf16[768,768]{1,0:T(8,128)(2,1)}, bf16[3...) custom-call(s32[1,3]{1,0:T(1,128)S(1)} %copy-done.20, ...), custom_call_target="tpu_custom_call" | custom-call | flops 48399998976 | tf_op jit(solution)/shard_map/attend/pallas_call | solution.py:245
  31.9 13.2 %ahead.1 = (bf16[384,768]{1,0:T(8,128)(2,1)}, bf16[4,384,768]{2,1,0:T(8,128)(2,1)S(1)}, f32[4,384,768]{2,1,0:T(8,128)S(1)}, f32[384,768]{1,0:T(8,128)S(1)}, f32[...) custom-call(s32[2]{0:T(128)S(1)} %pad_add_fusion.own_ref, ...), custom_call_target="tpu_custom_call" | custom-call | flops 88000004096 | tf_op jit(solution)/shard_map/ahead/pallas_call | solution.py:394
  45.5 2.1 %reduce_kept.1.refs_2_ = bf16[2,8,96,768]{3,2,1,0:T(8,128)(2,1)S(1)} custom-call(s32[2]{0:T(128)S(1)} %pad_add_fusion.own_ref, bf16[768,384]{1,0:T(8,128)(2,1)S(1)} %get-tuple-element.168.gbt_ref, bf16[4,384,768]{2,1,0:T(8,128)(2,1)S(1)} %get-tuple-element.169.act_ref), custom_call_target="tpu_custom_call" | custom-call | flops 22000001024 | tf_op jit(solution)/shard_map/reduce_kept/pallas_call | solution.py:287
  47.7 2.0 %collective-permute-done.3 = bf16[2,8,96,768]{3,2,1,0:T(8,128)(2,1)S(1)} collective-permute-done((bf16[2,8,96,768]{3,2,1,0:T(8,128)(2,1)S(1)}, bf16[2,8,96,768]{3,2,1,0:T(8,128)(2,1)S(1)}, u32[]{:S(2)}, u32[]{:S(2)}) %collective-permute-start.3) | collective-permute-done | bytes 2359328 | tf_op jit(solution)/shard_map/ppermute | solution.py:898
  49.7 1.1 gather.9
  50.8 1.8 %collective-permute-start.4 = (bf16[2,192,768]{2,1,0:T(8,128)(2,1)S(1)}, bf16[2,192,768]{2,1,0:T(8,128)(2,1)S(1)}, u32[]{:S(2)}, u32[]{:S(2)}) collective-permute-start(bf16[2,192,768]{2,1,0:T(8,128)(2,1)S(1)} %get-tuple-element.173), channel_id=1, source_target_pairs={{0,2},{1,3},{2,0},{3,1},{4,6},{5,7},{6,4},{7,5},{8,10},{9,11},{10,... | collective-permute-start | bytes 1769480 | tf_op jit(solution)/shard_map/ppermute | solution.py:898
  52.6 1.5 collective-permute-start.5
  54.1 11.7 %behind.1 = (f32[384,768]{1,0:T(8,128)S(1)}, bf16[384,768]{1,0:T(8,128)(2,1)S(1)}, bf16[2,2,4,240,384]{4,3,2,1,0:T(8,128)(2,1)S(1)}, bf16[2,2,4,240,384]{4,3,2,1,0:T(8,128)(2,1)S(1)}, f32[16,768]{1,0:T(8,128)S(1)}) custom-call(s32[2]{0:T(128)S(1)} %pad_add_fusion.own_ref, f32[4,384,768]{2,1,0:T(8,128)S(1)} %get-tuple-element.161.slope_ref, ...), custom_call_target="tpu_custom_call" | custom-call | flops 79200002048 | tf_op jit(solution)/shard_map/behind/pallas_call | solution.py:506
  65.9 0.6 collective-permute-done.4.refs_1_
  66.5 1.5 collective-permute-done.5.refs_3_
  68.5 1.6 collective-permute-start.6
  71.8 9.3 %attend_back.3 = (bf16[384,256]{1,0:T(8,128)(2,1)S(1)}, bf16[512,1536]{1,0:T(8,128)(2,1)S(1)}, f32[8,256]{1,0:T(8,128)S(1)}, bf16[4,8,96,384]{3,2,1,0:T(8,128)(2,1)S(1)}) custom-call(s32[2]{0:T(128)S(1)} %pad_add_fusion.own_ref, bf16[384,768]{1,0:T(8,128)(2,1)S(1)} %copy-done.32, bf16[384,768]{1,0:T(8,128)(2,1)S(1)} %get-tuple-element.183.gm_ref, ...), custom_call_target="tpu_custom_call" | custom-call | flops 52800000000 | tf_op jit(solution)/shard_map/attend_back/pallas_call | solution.py:671
  81.1 1.8 %gather.11 = (bf16[1,192,768]{2,1,0:T(8,128)(2,1)S(1)}, bf16[1,192,768]{2,1,0:T(8,128)(2,1)S(1)}, bf16[2,480,384]{2,1,0:T(8,128)(2,1)S(1)}, bf16[2,480,384]{2,1,...) custom-call(bf16[1,192,768]{2,1,0:T(8,128)(2,1)S(1)} %get-tuple-element.177.rest_10_.refs_0_, ...), custom_call_target="tpu_custom_call" | custom-call | flops 13200000000 | tf_op jit(solution)/shard_map/gather/pallas_call | solution.py:788
  82.9 2.7 %collective-permute-start.9 = (bf16[1,192,768]{2,1,0:T(8,128)(2,1)S(1)}, bf16[1,192,768]{2,1,0:T(8,128)(2,1)S(1)}, u32[]{:S(2)}, u32[]{:S(2)}) collective-permute-start(bf16[1,192,768]{2,1,0:T(8,128)(2,1)S(1)} %get-tuple-element.196), channel_id=1, source_target_pairs={{0,16},{1,17},{2,18},{3,19},{4,20},{5,21},{6,22},{7,23},{8,24},{9,... | collective-permute-start | bytes 884744 | tf_op jit(solution)/shard_map/ppermute | solution.py:898
  86.1 1.5 collective-permute-start.11
  87.5 10.0 %attend_back.4 = (bf16[384,256]{1,0:T(8,128)(2,1)S(1)}, bf16[512,1536]{1,0:T(8,128)(2,1)S(1)}, f32[8,256]{1,0:T(8,128)S(1)}, bf16[2,8,96,384]{3,2,1,0:T(8,128)(2,1)S(1)}, bf16[2,8,96,384]{3,2,1,0:T(8,128)(2,1)S(1)}) custom-call(s32[2]{0:T(128)S(1)} %pad_add_fusion.own_ref, bf16[384,768]{1,0:T(8,128)(2,1)S(1)} %copy-done.32, ...), custom_call_target="tpu_custom_call" | custom-call | flops 52800000000 | tf_op jit(solution)/shard_map/attend_back/pallas_call | solution.py:671
  97.6 0.7 collective-permute-done.9
  98.3 4.6 %collective-permute-done.10.refs_3_ = bf16[2,480,384]{2,1,0:T(8,128)(2,1)S(1)} collective-permute-done((bf16[2,480,384]{2,1,0:T(8,128)(2,1)S(1)}, bf16[2,480,384]{2,1,0:T(8,128)(2,1)S(1)}, u32[]{:S(2)}, u32[]{:S(2)}) %collective-permute-start.10) | collective-permute-done | bytes 737312 | tf_op jit(solution)/shard_map/ppermute | solution.py:898
  103.2 1.4 gather.12
  104.6 1.6 collective-permute-start.26
  106.2 1.5 collective-permute-start.12
  107.7 1.4 collective-permute-start.13
  109.1 5.3 %frames_back.2 = (f32[384,768]{1,0:T(8,128)S(1)}, f32[4,768,384]{2,1,0:T(8,128)S(1)}) custom-call(bf16[768,2304]{1,0:T(8,128)(2,1)S(1)} %copy-done, f32[384,768]{1,0:T(8,128)S(1)} %get-tuple-element.172.gx_in_ref, bf16[1,96,768]{2,1,0:T(8,128)(2,1)S(1)} %get-tuple-element.203.after_ref.refs_0_, bf16[384,256]{1,0:T(8,128)(2,1)S(1)} %get-tuple-element.204.refs_0_, ...), custom_call_target="tpu_custom_call" | custom-call | flops 35200000000 | tf_op jit(solution)/shard_map/frames_back/pallas_call | solution.py:730
  114.4 1.1 collective-permute-done.13.refs_3_
  115.5 0.8 gather.13
  116.2 0.6 collective-permute-start.17
  116.8 1.3 collective-permute-start.18
  118.1 1.6 collective-permute-start.19
  120.2 9.6 %attend_back.5 = (bf16[384,256]{1,0:T(8,128)(2,1)S(1)}, bf16[512,1536]{1,0:T(8,128)(2,1)S(1)}, f32[8,256]{1,0:T(8,128)S(1)}, bf16[2,8,112,256]{3,2,1,0:T(8,128)(2,1)S(1)}, bf16[2,8,112,256]{3,2,1,0:T(8,128)(2,1)S(1)}) custom-call(s32[2]{0:T(128)S(1)} %pad_add_fusion.own_ref, bf16[384,768]{1,0:T(8,128)(2,1)S(1)} %copy-done.32, ...), custom_call_target="tpu_custom_call" | custom-call | flops 52800000000 | tf_op jit(solution)/shard_map/attend_back/pallas_call | solution.py:671
  129.8 4.7 %collective-permute-done.16 = bf16[1,480,384]{2,1,0:T(8,128)(2,1)S(1)} collective-permute-done((bf16[1,480,384]{2,1,0:T(8,128)(2,1)S(1)}, bf16[1,480,384]{2,1,0:T(8,128)(2,1)S(1)}, u32[]{:S(2)}, u32[]{:S(2)}) %collective-permute-start.16) | collective-permute-done | bytes 368672 | tf_op jit(solution)/shard_map/ppermute | solution.py:898
  135.0 0.8 collective-permute-start.21
  135.8 1.2 collective-permute-start.22
  137.0 1.6 collective-permute-start.23
  138.6 3.3 %frames_back.3 = (f32[384,768]{1,0:T(8,128)S(1)}, bf16[2,768,384]{2,1,0:T(8,128)(2,1)S(1)}, f32[2,768,384]{2,1,0:T(8,128)S(1)}) custom-call(bf16[768,2304]{1,0:T(8,128)(2,1)S(1)} %copy-done, f32[384,768]{1,0:T(8,128)S(1)} %get-tuple-element.208.refs_6_.gx_in_ref, bf16[1,448,256]{2,1,0:T(8,128)(2,1)S(1)} %get-tuple-element.226.after_ref, ...), custom_call_target="tpu_custom_call" | custom-call | flops 17600000000 | tf_op jit(solution)/shard_map/frames_back/pallas_call | solution.py:730
  142.0 1.0 collective-permute-start.27
  143.0 0.6 collective-permute-done.21
  143.5 0.7 collective-permute-done.22
  144.3 2.3 %collective-permute-done.23 = bf16[1,448,256]{2,1,0:T(8,128)(2,1)S(1)} collective-permute-done((bf16[1,448,256]{2,1,0:T(8,128)(2,1)S(1)}, bf16[1,448,256]{2,1,0:T(8,128)(2,1)S(1)}, u32[]{:S(2)}, u32[]{:S(2)}) %collective-permute-start.23) | collective-permute-done | bytes 229408 | tf_op jit(solution)/shard_map/ppermute | solution.py:898
  146.7 1.1 collective-permute-start.29
  147.8 1.7 collective-permute-start.30
  149.5 1.7 collective-permute-start.31
  151.5 0.5 gather.17
  152.0 1.2 collective-permute-start.25
  153.2 2.4 %collective-permute-done.31.refs_9_ = bf16[1,112,256]{2,1,0:T(8,128)(2,1)S(1)} collective-permute-done((bf16[1,112,256]{2,1,0:T(8,128)(2,1)S(1)}, bf16[1,112,256]{2,1,0:T(8,128)(2,1)S(1)}, u32[]{:S(2)}, u32[]{:S(2)}) %collective-permute-start.31) | collective-permute-done | bytes 57376 | tf_op jit(solution)/shard_map/ppermute | solution.py:898
  155.6 0.5 collective-permute-done.28.refs_5_
  156.1 1.2 finish.1
  157.4 1.2 collective-permute-done.32
  158.6 1.7 collective-permute-start.35
  160.3 0.8 collective-permute-start.34
  161.1 0.9 collective-permute-start.33
  162.0 1.1 collective-permute-done.35
  163.2 0.7 collective-permute-done.34
  163.9 0.8 collective-permute-done.33
  164.9 2.3 %collective-permute-start.38 = (f32[8,128]{1,0:T(8,128)S(1)}, f32[8,128]{1,0:T(8,128)S(1)}, u32[]{:S(2)}, u32[]{:S(2)}) collective-permute-start(f32[8,128]{1,0:T(8,128)S(1)} %add_add_fusion.1), channel_id=1, source_target_pairs={{0,24},{1,25},{2,26},{3,27},{4,28},{5,29},{6,30},{7,31},{8,16},{9,... | collective-permute-start | bytes 12296 | tf_op jit(solution)/shard_map/ppermute | solution.py:898
  167.5 1.8 %collective-permute-start.36 = (f32[8,128]{1,0:T(8,128)S(1)}, f32[8,128]{1,0:T(8,128)S(1)}, u32[]{:S(2)}, u32[]{:S(2)}) collective-permute-start(f32[8,128]{1,0:T(8,128)S(1)} %add_add_fusion.1), channel_id=1, source_target_pairs={{0,8},{1,9},{2,10},{3,11},{4,12},{5,13},{6,14},{7,15},{8,0},{9,1},... | collective-permute-start | bytes 12296 | tf_op jit(solution)/shard_map/ppermute | solution.py:898
  169.4 2.7 %frames_end.1 = (f32[384,768]{1,0:T(8,128)}, f32[8,128]{1,0:T(8,128)S(1)}) custom-call(f32[384,768]{1,0:T(8,128)S(1)} %get-tuple-element.230.refs_6_.gx_ref, f32[1,768,384]{2,1,0:T(8,128)S(1)} %get-tuple-element.239.keep_ref.refs_10_, bf16[1,768,384]{2,1,0:T(8,128)(2,1)S(1)} %collective-permute-done.25.came_ref), custom_call_target="tpu_custom_call" | custom-call | flops 22000001024 | tf_op jit(solution)/shard_map/frames_end/pallas_call | solution.py:754
  172.2 2.4 %adam.1 = (f32[1,1]{1,0:T(1,128)}, f32[96,576]{1,0:T(8,128)}, f32[96,576]{1,0:T(8,128)}, f32[96,576]{1,0:T(8,128)}, bf16[96,576]{1,0:T(8,128)(2,1)}, /*index=5*/...) custom-call(f32[8,128]{1,0:T(8,128)S(1)} %add_add_fusion.squares_ref, ...), custom_call_target="tpu_custom_call" | custom-call | flops 22000001024 | tf_op jit(solution)/shard_map/adam/pallas_call | solution.py:888
  (118 shorter events, 5.9 us)
Async XLA Ops:
  0.7 3.2 %collective-permute-start.1 = (bf16[384,768]{1,0:T(8,128)(2,1)}, bf16[384,768]{1,0:T(8,128)(2,1)S(1)}, u32[]{:S(2)}, u32[]{:S(2)}) collective-permute-start(bf16[384,768]{1,0:T(8,128)(2,1)} %x_ref.1), channel_id=1, source_target_pairs={{0,1},{1,0},{2,3},{3,2},{4,5},{5,4},{6,7},{7,6},{8,9},{9,8},{10,11... | collective-permute-start | bytes 1769480 | tf_op jit(solution)/shard_map/ppermute | solution.py:898
  1.2 16.7 %collective-permute-start = (bf16[384,768]{1,0:T(8,128)(2,1)}, bf16[384,768]{1,0:T(8,128)(2,1)S(1)}, u32[]{:S(2)}, u32[]{:S(2)}) collective-permute-start(bf16[384,768]{1,0:T(8,128)(2,1)} %x_ref.1), channel_id=1, source_target_pairs={{0,2},{1,3},{2,0},{3,1},{4,6},{5,7},{6,4},{7,5},{8,10},{9,11},{10,... | collective-permute-start | bytes 1769480 | tf_op jit(solution)/shard_map/ppermute | solution.py:898
  17.0 4.3 %copy-start.31 = (bf16[384,768]{1,0:T(8,128)(2,1)}, bf16[384,768]{1,0:T(8,128)(2,1)S(1)}, u32[]{:S(2)}) copy-start(bf16[384,768]{1,0:T(8,128)(2,1)S(1)} %get-tuple-element.153.q_ref) | copy-start | bytes 1769476
  17.9 3.3 %collective-permute-start.2 = (bf16[384,768]{1,0:T(8,128)(2,1)S(1)}, bf16[384,768]{1,0:T(8,128)(2,1)S(1)}, u32[]{:S(2)}, u32[]{:S(2)}) collective-permute-start(bf16[384,768]{1,0:T(8,128)(2,1)S(1)} %pass_on.1.x_ref.xp_ref), channel_id=1, source_target_pairs={{0,1},{1,0},{2,3},{3,2},{4,5},{5,4},{6,7},{7,6},{8,9},{9,8},{10,11... | collective-permute-start | bytes 1769480 | tf_op jit(solution)/shard_map/ppermute | solution.py:898
  18.0 13.8 %slice-start = ((s8[4718592]{0:T(1024)(128)(4,1)}), s8[4194304]{0:T(1024)(128)(4,1)S(1)}, s32[]{:S(2)}) async-start(s8[4718592]{0:T(1024)(128)(4,1)} %bitcast.30), calls=%async_computation | async-start | bytes 8388608
  18.0 13.8 %slice-start.2 = ((s8[4718592]{0:T(1024)(128)(4,1)}), s8[4194304]{0:T(1024)(128)(4,1)S(1)}, s32[]{:S(2)}) async-start(s8[4718592]{0:T(1024)(128)(4,1)} %bitcast.32), calls=%async_computation.2 | async-start | bytes 8388608
  21.3 10.6 %slice-start.1 = ((s8[4718592]{0:T(1024)(128)(4,1)}), s8[524288]{0:T(1024)(128)(4,1)S(1)}, s32[]{:S(2)}) async-start(s8[4718592]{0:T(1024)(128)(4,1)} %bitcast.30), calls=%async_computation.1 | async-start | bytes 1048576
  21.3 10.6 %slice-start.3 = ((s8[4718592]{0:T(1024)(128)(4,1)}), s8[524288]{0:T(1024)(128)(4,1)S(1)}, s32[]{:S(2)}) async-start(s8[4718592]{0:T(1024)(128)(4,1)} %bitcast.32), calls=%async_computation.3 | async-start | bytes 1048576
  21.3 10.6 %copy-start.1 = (bf16[768,768]{1,0:T(8,128)(2,1)S(1)}, bf16[768,768]{1,0:T(8,128)(2,1)}, u32[]{:S(2)}) copy-start(bf16[768,768]{1,0:T(8,128)(2,1)} %wo_ref.3) | copy-start | bytes 3538948
  21.3 10.6 %copy-start.2 = (bf16[384,768]{1,0:T(8,128)(2,1)S(1)}, bf16[384,768]{1,0:T(8,128)(2,1)}, u32[]{:S(2)}) copy-start(bf16[384,768]{1,0:T(8,128)(2,1)} %x_ref.1) | copy-start | bytes 1769476
  21.3 10.6 %copy-start.3 = (bf16[384,768]{1,0:T(8,128)(2,1)S(1)}, bf16[384,768]{1,0:T(8,128)(2,1)}, u32[]{:S(2)}) copy-start(bf16[384,768]{1,0:T(8,128)(2,1)} %cot_ref.1) | copy-start | bytes 1769476
  45.1 4.6 %collective-permute-start.3 = (bf16[2,8,96,768]{3,2,1,0:T(8,128)(2,1)S(1)}, bf16[2,8,96,768]{3,2,1,0:T(8,128)(2,1)S(1)}, u32[]{:S(2)}, u32[]{:S(2)}) collective-permute-start(bf16[2,8,96,768]{3,2,1,0:T(8,128)(2,1)S(1)} %get-tuple-element.170), channel_id=1, source_target_pairs={{0,1},{1,0},{2,3},{3,2},{4,5},{5,4},{6,7},{7,6},{8,9},{9,8},{10,11... | collective-permute-start | bytes 7077896 | tf_op jit(solution)/shard_map/ppermute | solution.py:898
  50.8 15.7 %collective-permute-start.4 = (bf16[2,192,768]{2,1,0:T(8,128)(2,1)S(1)}, bf16[2,192,768]{2,1,0:T(8,128)(2,1)S(1)}, u32[]{:S(2)}, u32[]{:S(2)}) collective-permute-start(bf16[2,192,768]{2,1,0:T(8,128)(2,1)S(1)} %get-tuple-element.173), channel_id=1, source_target_pairs={{0,2},{1,3},{2,0},{3,1},{4,6},{5,7},{6,4},{7,5},{8,10},{9,11},{10,... | collective-permute-start | bytes 1769480 | tf_op jit(solution)/shard_map/ppermute | solution.py:898
  52.6 15.3 %collective-permute-start.5 = (bf16[2,192,768]{2,1,0:T(8,128)(2,1)S(1)}, bf16[2,192,768]{2,1,0:T(8,128)(2,1)S(1)}, u32[]{:S(2)}, u32[]{:S(2)}) collective-permute-start(bf16[2,192,768]{2,1,0:T(8,128)(2,1)S(1)} %get-tuple-element.175), channel_id=1, source_target_pairs={{0,4},{1,5},{2,6},{3,7},{4,0},{5,1},{6,2},{7,3},{8,12},{9,13},{10,... | collective-permute-start | bytes 1769480 | tf_op jit(solution)/shard_map/ppermute | solution.py:898
  65.8 15.3 %collective-permute-start.8 = (bf16[2,2,4,240,384]{4,3,2,1,0:T(8,128)(2,1)S(1)}, bf16[2,2,4,240,384]{4,3,2,1,0:T(8,128)(2,1)S(1)}, u32[]{:S(2)}, u32[]{:S(2)}) collective-permute-start(bf16[2,2,4,240,384]{4,3,2,1,0:T(8,128)(2,1)S(1)} %get-tuple-element.182), channel_id=1, source_target_pairs={{0,1},{1,0},{2,3},{3,2},{4,5},{5,4},{6,7},{7,6},{8,9},{9,8},{10,11... | collective-permute-start | bytes 8847368 | tf_op jit(solution)/shard_map/ppermute | solution.py:898
  68.5 12.6 %collective-permute-start.6 = (bf16[1,192,768]{2,1,0:T(8,128)(2,1)S(1)}, bf16[1,192,768]{2,1,0:T(8,128)(2,1)S(1)}, u32[]{:S(2)}, u32[]{:S(2)}) collective-permute-start(bf16[1,192,768]{2,1,0:T(8,128)(2,1)S(1)} %get-tuple-element.178), channel_id=1, source_target_pairs={{0,4},{1,5},{2,6},{3,7},{4,0},{5,1},{6,2},{7,3},{8,12},{9,13},{10,... | collective-permute-start | bytes 884744 | tf_op jit(solution)/shard_map/ppermute | solution.py:898
  70.1 11.0 %collective-permute-start.7 = (bf16[1,192,768]{2,1,0:T(8,128)(2,1)S(1)}, bf16[1,192,768]{2,1,0:T(8,128)(2,1)S(1)}, u32[]{:S(2)}, u32[]{:S(2)}) collective-permute-start(bf16[1,192,768]{2,1,0:T(8,128)(2,1)S(1)} %get-tuple-element.180), channel_id=1, source_target_pairs={{0,2},{1,3},{2,0},{3,1},{4,6},{5,7},{6,4},{7,5},{8,10},{9,11},{10,... | collective-permute-start | bytes 884744 | tf_op jit(solution)/shard_map/ppermute | solution.py:898
  82.9 15.4 %collective-permute-start.9 = (bf16[1,192,768]{2,1,0:T(8,128)(2,1)S(1)}, bf16[1,192,768]{2,1,0:T(8,128)(2,1)S(1)}, u32[]{:S(2)}, u32[]{:S(2)}) collective-permute-start(bf16[1,192,768]{2,1,0:T(8,128)(2,1)S(1)} %get-tuple-element.196), channel_id=1, source_target_pairs={{0,16},{1,17},{2,18},{3,19},{4,20},{5,21},{6,22},{7,23},{8,24},{9,... | collective-permute-start | bytes 884744 | tf_op jit(solution)/shard_map/ppermute | solution.py:898
  85.5 17.4 %collective-permute-start.10 = (bf16[2,480,384]{2,1,0:T(8,128)(2,1)S(1)}, bf16[2,480,384]{2,1,0:T(8,128)(2,1)S(1)}, u32[]{:S(2)}, u32[]{:S(2)}) collective-permute-start(bf16[2,480,384]{2,1,0:T(8,128)(2,1)S(1)} %get-tuple-element.198), channel_id=1, source_target_pairs={{0,2},{1,3},{2,0},{3,1},{4,6},{5,7},{6,4},{7,5},{8,10},{9,11},{10,... | collective-permute-start | bytes 2211848 | tf_op jit(solution)/shard_map/ppermute | solution.py:898
  86.1 17.2 %collective-permute-start.11 = (bf16[2,480,384]{2,1,0:T(8,128)(2,1)S(1)}, bf16[2,480,384]{2,1,0:T(8,128)(2,1)S(1)}, u32[]{:S(2)}, u32[]{:S(2)}) collective-permute-start(bf16[2,480,384]{2,1,0:T(8,128)(2,1)S(1)} %get-tuple-element.200), channel_id=1, source_target_pairs={{0,4},{1,5},{2,6},{3,7},{4,0},{5,1},{6,2},{7,3},{8,12},{9,13},{10,... | collective-permute-start | bytes 2211848 | tf_op jit(solution)/shard_map/ppermute | solution.py:898
  97.5 17.9 %collective-permute-start.14 = (bf16[2,8,96,384]{3,2,1,0:T(8,128)(2,1)S(1)}, bf16[2,8,96,384]{3,2,1,0:T(8,128)(2,1)S(1)}, u32[]{:S(2)}, u32[]{:S(2)}) collective-permute-start(bf16[2,8,96,384]{3,2,1,0:T(8,128)(2,1)S(1)} %get-tuple-element.214), channel_id=1, source_target_pairs={{0,1},{1,0},{2,3},{3,2},{4,5},{5,4},{6,7},{7,6},{8,9},{9,8},{10,11... | collective-permute-start | bytes 3538952 | tf_op jit(solution)/shard_map/ppermute | solution.py:898
  103.2 5.9 %copy-start = (bf16[768,2304]{1,0:T(8,128)(2,1)S(1)}, bf16[768,2304]{1,0:T(8,128)(2,1)}, u32[]{:S(2)}) copy-start(bf16[768,2304]{1,0:T(8,128)(2,1)} %w_ref.3) | copy-start | bytes 10616836
  104.6 44.9 %collective-permute-start.26 = (bf16[1,96,768]{2,1,0:T(8,128)(2,1)}, bf16[1,96,768]{2,1,0:T(8,128)(2,1)}, u32[]{:S(2)}, u32[]{:S(2)}) collective-permute-start(bf16[1,96,768]{2,1,0:T(8,128)(2,1)} %get-tuple-element.242), channel_id=1, source_target_pairs={{0,8},{1,9},{2,10},{3,11},{4,12},{5,13},{6,14},{7,15},{8,0},{9,1},... | collective-permute-start | bytes 442376 | tf_op jit(solution)/shard_map/ppermute | solution.py:898
  106.2 8.2 %collective-permute-start.12 = (bf16[1,480,384]{2,1,0:T(8,128)(2,1)S(1)}, bf16[1,480,384]{2,1,0:T(8,128)(2,1)S(1)}, u32[]{:S(2)}, u32[]{:S(2)}) collective-permute-start(bf16[1,480,384]{2,1,0:T(8,128)(2,1)S(1)} %get-tuple-element.210), channel_id=1, source_target_pairs={{0,4},{1,5},{2,6},{3,7},{4,0},{5,1},{6,2},{7,3},{8,12},{9,13},{10,... | collective-permute-start | bytes 1105928 | tf_op jit(solution)/shard_map/ppermute | solution.py:898
  107.7 7.8 %collective-permute-start.13 = (bf16[1,480,384]{2,1,0:T(8,128)(2,1)S(1)}, bf16[1,480,384]{2,1,0:T(8,128)(2,1)S(1)}, u32[]{:S(2)}, u32[]{:S(2)}) collective-permute-start(bf16[1,480,384]{2,1,0:T(8,128)(2,1)S(1)} %get-tuple-element.212), channel_id=1, source_target_pairs={{0,2},{1,3},{2,0},{3,1},{4,6},{5,7},{6,4},{7,5},{8,10},{9,11},{10,... | collective-permute-start | bytes 1105928 | tf_op jit(solution)/shard_map/ppermute | solution.py:898
  115.5 4.7 %copy-start.30 = (f32[16,768]{1,0:T(8,128)S(1)}, f32[16,768]{1,0:T(8,128)}, u32[]{:S(2)}) copy-start(f32[16,768]{1,0:T(8,128)} %copy-done.29) | copy-start | bytes 147460
  116.2 13.5 %collective-permute-start.17 = (bf16[1,384,384]{2,1,0:T(8,128)(2,1)S(1)}, bf16[1,384,384]{2,1,0:T(8,128)(2,1)S(1)}, u32[]{:S(2)}, u32[]{:S(2)}) collective-permute-start(bf16[1,384,384]{2,1,0:T(8,128)(2,1)S(1)} %get-tuple-element.221), channel_id=1, source_target_pairs={{0,4},{1,5},{2,6},{3,7},{4,0},{5,1},{6,2},{7,3},{8,12},{9,13},{10,... | collective-permute-start | bytes 884744 | tf_op jit(solution)/shard_map/ppermute | solution.py:898
  116.8 13.0 %collective-permute-start.18 = (bf16[1,384,384]{2,1,0:T(8,128)(2,1)S(1)}, bf16[1,384,384]{2,1,0:T(8,128)(2,1)S(1)}, u32[]{:S(2)}, u32[]{:S(2)}) collective-permute-start(bf16[1,384,384]{2,1,0:T(8,128)(2,1)S(1)} %get-tuple-element.222), channel_id=1, source_target_pairs={{0,2},{1,3},{2,0},{3,1},{4,6},{5,7},{6,4},{7,5},{8,10},{9,11},{10,... | collective-permute-start | bytes 884744 | tf_op jit(solution)/shard_map/ppermute | solution.py:898
  118.1 11.7 %collective-permute-start.19 = (bf16[1,384,384]{2,1,0:T(8,128)(2,1)S(1)}, bf16[1,384,384]{2,1,0:T(8,128)(2,1)S(1)}, u32[]{:S(2)}, u32[]{:S(2)}) collective-permute-start(bf16[1,384,384]{2,1,0:T(8,128)(2,1)S(1)} %get-tuple-element.223), channel_id=1, source_target_pairs={{0,6},{1,7},{2,4},{3,5},{4,2},{5,3},{6,0},{7,1},{8,14},{9,15},{10,... | collective-permute-start | bytes 884744 | tf_op jit(solution)/shard_map/ppermute | solution.py:898
  119.8 14.7 %collective-permute-start.16 = (bf16[1,480,384]{2,1,0:T(8,128)(2,1)S(1)}, bf16[1,480,384]{2,1,0:T(8,128)(2,1)S(1)}, u32[]{:S(2)}, u32[]{:S(2)}) collective-permute-start(bf16[1,480,384]{2,1,0:T(8,128)(2,1)S(1)} %get-tuple-element.219), channel_id=1, source_target_pairs={{0,16},{1,17},{2,18},{3,19},{4,20},{5,21},{6,22},{7,23},{8,24},{9,... | collective-permute-start | bytes 1105928 | tf_op jit(solution)/shard_map/ppermute | solution.py:898
  129.7 5.1 %collective-permute-start.15 = (bf16[2,8,112,256]{3,2,1,0:T(8,128)(2,1)S(1)}, bf16[2,8,112,256]{3,2,1,0:T(8,128)(2,1)S(1)}, u32[]{:S(2)}, u32[]{:S(2)}) collective-permute-start(bf16[2,8,112,256]{3,2,1,0:T(8,128)(2,1)S(1)} %get-tuple-element.218), channel_id=1, source_target_pairs={{0,1},{1,0},{2,3},{3,2},{4,5},{5,4},{6,7},{7,6},{8,9},{9,8},{10,11... | collective-permute-start | bytes 2752520 | tf_op jit(solution)/shard_map/ppermute | solution.py:898
  134.7 7.2 %collective-permute-start.24 = (bf16[2,96,384]{2,1,0:T(8,128)(2,1)S(1)}, bf16[2,96,384]{2,1,0:T(8,128)(2,1)S(1)}, u32[]{:S(2)}, u32[]{:S(2)}) collective-permute-start(bf16[2,96,384]{2,1,0:T(8,128)(2,1)S(1)} %get-tuple-element.237), channel_id=1, source_target_pairs={{0,16},{1,17},{2,18},{3,19},{4,20},{5,21},{6,22},{7,23},{8,24},{9,... | collective-permute-start | bytes 442376 | tf_op jit(solution)/shard_map/ppermute | solution.py:898
  135.0 8.5 %collective-permute-start.21 = (bf16[1,448,256]{2,1,0:T(8,128)(2,1)S(1)}, bf16[1,448,256]{2,1,0:T(8,128)(2,1)S(1)}, u32[]{:S(2)}, u32[]{:S(2)}) collective-permute-start(bf16[1,448,256]{2,1,0:T(8,128)(2,1)S(1)} %get-tuple-element.233), channel_id=1, source_target_pairs={{0,4},{1,5},{2,6},{3,7},{4,0},{5,1},{6,2},{7,3},{8,12},{9,13},{10,... | collective-permute-start | bytes 688136 | tf_op jit(solution)/shard_map/ppermute | solution.py:898
  135.8 8.5 %collective-permute-start.22 = (bf16[1,448,256]{2,1,0:T(8,128)(2,1)S(1)}, bf16[1,448,256]{2,1,0:T(8,128)(2,1)S(1)}, u32[]{:S(2)}, u32[]{:S(2)}) collective-permute-start(bf16[1,448,256]{2,1,0:T(8,128)(2,1)S(1)} %get-tuple-element.234), channel_id=1, source_target_pairs={{0,2},{1,3},{2,0},{3,1},{4,6},{5,7},{6,4},{7,5},{8,10},{9,11},{10,... | collective-permute-start | bytes 688136 | tf_op jit(solution)/shard_map/ppermute | solution.py:898
  137.0 9.6 %collective-permute-start.23 = (bf16[1,448,256]{2,1,0:T(8,128)(2,1)S(1)}, bf16[1,448,256]{2,1,0:T(8,128)(2,1)S(1)}, u32[]{:S(2)}, u32[]{:S(2)}) collective-permute-start(bf16[1,448,256]{2,1,0:T(8,128)(2,1)S(1)} %get-tuple-element.235), channel_id=1, source_target_pairs={{0,6},{1,7},{2,4},{3,5},{4,2},{5,3},{6,0},{7,1},{8,14},{9,15},{10,... | collective-permute-start | bytes 688136 | tf_op jit(solution)/shard_map/ppermute | solution.py:898
  142.0 10.1 %collective-permute-start.27 = (bf16[1,240,384]{2,1,0:T(8,128)(2,1)S(1)}, bf16[1,240,384]{2,1,0:T(8,128)(2,1)S(1)}, u32[]{:S(2)}, u32[]{:S(2)}) collective-permute-start(bf16[1,240,384]{2,1,0:T(8,128)(2,1)S(1)} %get-tuple-element.243), channel_id=1, source_target_pairs={{0,8},{1,9},{2,10},{3,11},{4,12},{5,13},{6,14},{7,15},{8,0},{9,1},... | collective-permute-start | bytes 552968 | tf_op jit(solution)/shard_map/ppermute | solution.py:898
  143.5 7.6 %collective-permute-start.20 = (bf16[2,768,384]{2,1,0:T(8,128)(2,1)S(1)}, bf16[2,768,384]{2,1,0:T(8,128)(2,1)S(1)}, u32[]{:S(2)}, u32[]{:S(2)}) collective-permute-start(bf16[2,768,384]{2,1,0:T(8,128)(2,1)S(1)} %get-tuple-element.232), channel_id=1, source_target_pairs={{0,1},{1,0},{2,3},{3,2},{4,5},{5,4},{6,7},{7,6},{8,9},{9,8},{10,11... | collective-permute-start | bytes 3538952 | tf_op jit(solution)/shard_map/ppermute | solution.py:898
  146.7 6.5 %collective-permute-start.29 = (bf16[1,112,256]{2,1,0:T(8,128)(2,1)S(1)}, bf16[1,112,256]{2,1,0:T(8,128)(2,1)S(1)}, u32[]{:S(2)}, u32[]{:S(2)}) collective-permute-start(bf16[1,112,256]{2,1,0:T(8,128)(2,1)S(1)} %get-tuple-element.246), channel_id=1, source_target_pairs={{0,8},{1,9},{2,10},{3,11},{4,12},{5,13},{6,14},{7,15},{8,0},{9,1},... | collective-permute-start | bytes 172040 | tf_op jit(solution)/shard_map/ppermute | solution.py:898
  147.8 5.4 %collective-permute-start.30 = (bf16[1,112,256]{2,1,0:T(8,128)(2,1)S(1)}, bf16[1,112,256]{2,1,0:T(8,128)(2,1)S(1)}, u32[]{:S(2)}, u32[]{:S(2)}) collective-permute-start(bf16[1,112,256]{2,1,0:T(8,128)(2,1)S(1)} %get-tuple-element.247), channel_id=1, source_target_pairs={{0,16},{1,17},{2,18},{3,19},{4,20},{5,21},{6,22},{7,23},{8,24},{9,... | collective-permute-start | bytes 172040 | tf_op jit(solution)/shard_map/ppermute | solution.py:898
  149.5 6.1 %collective-permute-start.31 = (bf16[1,112,256]{2,1,0:T(8,128)(2,1)S(1)}, bf16[1,112,256]{2,1,0:T(8,128)(2,1)S(1)}, u32[]{:S(2)}, u32[]{:S(2)}) collective-permute-start(bf16[1,112,256]{2,1,0:T(8,128)(2,1)S(1)} %get-tuple-element.248), channel_id=1, source_target_pairs={{0,24},{1,25},{2,26},{3,27},{4,28},{5,29},{6,30},{7,31},{8,16},{9,... | collective-permute-start | bytes 172040 | tf_op jit(solution)/shard_map/ppermute | solution.py:898
  151.2 5.0 %collective-permute-start.28 = (bf16[1,96,384]{2,1,0:T(8,128)(2,1)S(1)}, bf16[1,96,384]{2,1,0:T(8,128)(2,1)S(1)}, u32[]{:S(2)}, u32[]{:S(2)}) collective-permute-start(bf16[1,96,384]{2,1,0:T(8,128)(2,1)S(1)} %get-tuple-element.244), channel_id=1, source_target_pairs={{0,8},{1,9},{2,10},{3,11},{4,12},{5,13},{6,14},{7,15},{8,0},{9,1},... | collective-permute-start | bytes 221192 | tf_op jit(solution)/shard_map/ppermute | solution.py:898
  152.0 17.3 %collective-permute-start.25 = (bf16[1,768,384]{2,1,0:T(8,128)(2,1)S(1)}, bf16[1,768,384]{2,1,0:T(8,128)(2,1)S(1)}, u32[]{:S(2)}, u32[]{:S(2)}) collective-permute-start(bf16[1,768,384]{2,1,0:T(8,128)(2,1)S(1)} %get-tuple-element.240), channel_id=1, source_target_pairs={{0,2},{1,3},{2,0},{3,1},{4,6},{5,7},{6,4},{7,5},{8,10},{9,11},{10,... | collective-permute-start | bytes 1769480 | tf_op jit(solution)/shard_map/ppermute | solution.py:898
  157.4 1.2 collective-permute-start.32
  158.6 4.6 %collective-permute-start.35 = (f32[8,128]{1,0:T(8,128)S(1)}, f32[8,128]{1,0:T(8,128)S(1)}, u32[]{:S(2)}, u32[]{:S(2)}) collective-permute-start(f32[8,128]{1,0:T(8,128)S(1)} %add.24), channel_id=1, source_target_pairs={{0,6},{1,7},{2,4},{3,5},{4,2},{5,3},{6,0},{7,1},{8,14},{9,15},{10,... | collective-permute-start | bytes 12296 | tf_op jit(solution)/shard_map/ppermute | solution.py:898
  160.3 3.6 %collective-permute-start.34 = (f32[8,128]{1,0:T(8,128)S(1)}, f32[8,128]{1,0:T(8,128)S(1)}, u32[]{:S(2)}, u32[]{:S(2)}) collective-permute-start(f32[8,128]{1,0:T(8,128)S(1)} %add.24), channel_id=1, source_target_pairs={{0,4},{1,5},{2,6},{3,7},{4,0},{5,1},{6,2},{7,3},{8,12},{9,13},{10,... | collective-permute-start | bytes 12296 | tf_op jit(solution)/shard_map/ppermute | solution.py:898
  161.1 3.6 %collective-permute-start.33 = (f32[8,128]{1,0:T(8,128)S(1)}, f32[8,128]{1,0:T(8,128)S(1)}, u32[]{:S(2)}, u32[]{:S(2)}) collective-permute-start(f32[8,128]{1,0:T(8,128)S(1)} %add.24), channel_id=1, source_target_pairs={{0,2},{1,3},{2,0},{3,1},{4,6},{5,7},{6,4},{7,5},{8,10},{9,11},{10,... | collective-permute-start | bytes 12296 | tf_op jit(solution)/shard_map/ppermute | solution.py:898
  164.7 7.4 %copy-start.4 = (f32[192,384]{1,0:T(8,128)S(1)}, f32[192,384]{1,0:T(8,128)}, u32[]{:S(2)}) copy-start(f32[192,384]{1,0:T(8,128)} %refs_8_.1) | copy-start | bytes 884740
  164.7 7.4 %copy-start.5 = (f32[192,384]{1,0:T(8,128)S(1)}, f32[192,384]{1,0:T(8,128)}, u32[]{:S(2)}) copy-start(f32[192,384]{1,0:T(8,128)} %refs_9_.1) | copy-start | bytes 884740
  164.7 7.4 %copy-start.6 = (f32[192,384]{1,0:T(8,128)S(1)}, f32[192,384]{1,0:T(8,128)}, u32[]{:S(2)}) copy-start(f32[192,384]{1,0:T(8,128)} %refs_10_.1) | copy-start | bytes 884740
  164.8 7.4 %copy-start.7 = (f32[768,96]{0,1:T(8,128)S(1)}, f32[768,96]{0,1:T(8,128)}, u32[]{:S(2)}) copy-start(f32[768,96]{0,1:T(8,128)} %param.34) | copy-start | bytes 884740
  164.8 7.4 %copy-start.8 = (f32[768,96]{0,1:T(8,128)S(1)}, f32[768,96]{0,1:T(8,128)}, u32[]{:S(2)}) copy-start(f32[768,96]{0,1:T(8,128)} %param.39) | copy-start | bytes 884740
  164.8 7.4 %copy-start.9 = (f32[768,96]{0,1:T(8,128)S(1)}, f32[768,96]{0,1:T(8,128)}, u32[]{:S(2)}) copy-start(f32[768,96]{0,1:T(8,128)} %param.44) | copy-start | bytes 884740
  164.8 7.4 %copy-start.10 = (f32[96,576]{1,0:T(8,128)S(1)}, f32[96,576]{1,0:T(8,128)}, u32[]{:S(2)}) copy-start(f32[96,576]{1,0:T(8,128)} %refs_0_.1) | copy-start | bytes 663556
  164.8 7.4 %copy-start.11 = (f32[96,576]{1,0:T(8,128)S(1)}, f32[96,576]{1,0:T(8,128)}, u32[]{:S(2)}) copy-start(f32[96,576]{1,0:T(8,128)} %refs_1_.1) | copy-start | bytes 663556
  164.8 7.4 %copy-start.12 = (f32[96,576]{1,0:T(8,128)S(1)}, f32[96,576]{1,0:T(8,128)}, u32[]{:S(2)}) copy-start(f32[96,576]{1,0:T(8,128)} %refs_2_.1) | copy-start | bytes 663556
  164.8 7.4 %copy-start.13 = (f32[192,96]{1,0:T(8,128)S(1)}, f32[192,96]{1,0:T(8,128)}, u32[]{:S(2)}) copy-start(f32[192,96]{1,0:T(8,128)} %refs_4_.1) | copy-start | bytes 221188
  164.8 7.3 %copy-start.14 = (f32[192,96]{1,0:T(8,128)S(1)}, f32[192,96]{1,0:T(8,128)}, u32[]{:S(2)}) copy-start(f32[192,96]{1,0:T(8,128)} %refs_5_.1) | copy-start | bytes 221188
  164.9 7.3 %copy-start.15 = (f32[192,96]{1,0:T(8,128)S(1)}, f32[192,96]{1,0:T(8,128)}, u32[]{:S(2)}) copy-start(f32[192,96]{1,0:T(8,128)} %refs_6_.1) | copy-start | bytes 221188
  164.9 7.3 %copy-start.17 = (f32[3,96]{1,0:T(4,128)S(1)}, f32[3,96]{1,0:T(4,128)}, u32[]{:S(2)}) copy-start(f32[3,96]{1,0:T(4,128)} %refs_16_.1) | copy-start | bytes 3460
  164.9 7.3 %copy-start.18 = (f32[3,96]{1,0:T(4,128)S(1)}, f32[3,96]{1,0:T(4,128)}, u32[]{:S(2)}) copy-start(f32[3,96]{1,0:T(4,128)} %refs_17_.1) | copy-start | bytes 3460
  164.9 7.3 %copy-start.19 = (f32[3,96]{1,0:T(4,128)S(1)}, f32[3,96]{1,0:T(4,128)}, u32[]{:S(2)}) copy-start(f32[3,96]{1,0:T(4,128)} %refs_18_.1) | copy-start | bytes 3460
  164.9 7.2 %collective-permute-start.38 = (f32[8,128]{1,0:T(8,128)S(1)}, f32[8,128]{1,0:T(8,128)S(1)}, u32[]{:S(2)}, u32[]{:S(2)}) collective-permute-start(f32[8,128]{1,0:T(8,128)S(1)} %add_add_fusion.1), channel_id=1, source_target_pairs={{0,24},{1,25},{2,26},{3,27},{4,28},{5,29},{6,30},{7,31},{8,16},{9,... | collective-permute-start | bytes 12296 | tf_op jit(solution)/shard_map/ppermute | solution.py:898
  167.2 4.9 %collective-permute-start.37 = (f32[8,128]{1,0:T(8,128)S(1)}, f32[8,128]{1,0:T(8,128)S(1)}, u32[]{:S(2)}, u32[]{:S(2)}) collective-permute-start(f32[8,128]{1,0:T(8,128)S(1)} %add_add_fusion.1), channel_id=1, source_target_pairs={{0,16},{1,17},{2,18},{3,19},{4,20},{5,21},{6,22},{7,23},{8,24},{9,... | collective-permute-start | bytes 12296 | tf_op jit(solution)/shard_map/ppermute | solution.py:898
  167.5 4.5 %collective-permute-start.36 = (f32[8,128]{1,0:T(8,128)S(1)}, f32[8,128]{1,0:T(8,128)S(1)}, u32[]{:S(2)}, u32[]{:S(2)}) collective-permute-start(f32[8,128]{1,0:T(8,128)S(1)} %add_add_fusion.1), channel_id=1, source_target_pairs={{0,8},{1,9},{2,10},{3,11},{4,12},{5,13},{6,14},{7,15},{8,0},{9,1},... | collective-permute-start | bytes 12296 | tf_op jit(solution)/shard_map/ppermute | solution.py:898
  (12 other events, 31.2 us)

commit v5 on v4

--- a/solution.py
+++ b/solution.py
@@ -261,14 +261,14 @@
     return jnp.where(j < 2, 2 * j + 1, 2 * (j - 2))
 
 
-def by_rows(rows, body):
-    block = rows // 4
+def by_rows(rows, body, blocks=4):
+    block = rows // blocks
 
     def step(i, carry):
         body(pl.ds(pl.multiple_of(i * block, block), block))
         return carry
 
-    lax.fori_loop(0, 4, step, 0)
+    lax.fori_loop(0, blocks, step, 0)
 
 
 def store_rows(ref, block, own_d):
@@ -277,34 +277,46 @@
         ref[0, spot(d, own_d)] = block[d * piece : (d + 1) * piece, :]
 
 
-def reduce_kernel(own_ref, gbt_ref, act_ref, rk_ref):
+def reduce_kernel(own_ref, gbt_ref, act_ref, hl_ref, mixed_ref, rk_ref, hlt_ref, mt_ref):
     store_rows(rk_ref, dot(gbt_ref[...], act_ref[0]).astype(BF), own_ref[1])
 
-
-def reduce_kept(own, gbt, act):
+    @pl.when(pl.program_id(0) == 0)
+    def _():
+        hlt_ref[...] = hl_ref[...].T
+        mt_ref[...] = mixed_ref[...].T
+
+
+def reduce_kept(own, gbt, act, hl, mixed):
     width, rows = gbt.shape
     chunks, _, cut = act.shape
+    full = lambda a: pl.BlockSpec(a, lambda j, own: (0, 0))
     return pl.pallas_call(
         reduce_kernel,
         grid_spec=pltpu.PrefetchScalarGridSpec(
             num_scalar_prefetch=1,
             grid=(2,),
             in_specs=[
-                pl.BlockSpec((width, rows), lambda j, own: (0, 0)),
-                pl.BlockSpec((1, rows, cut), lambda j, own: (j + 2, 0, 0)),
+                full((width, rows)), pl.BlockSpec((1, rows, cut), lambda j, own: (j + 2, 0, 0)),
+                full((rows, width)), full((rows, width)),
             ],
-            out_specs=pl.BlockSpec((1, 8, width // 8, cut), lambda j, own: (j, 0, 0, 0)),
+            out_specs=[
+                pl.BlockSpec((1, 8, width // 8, cut), lambda j, own: (j, 0, 0, 0)), full((width, rows)),
+                full((width, rows)),
+            ],
         ),
-        out_shape=jax.ShapeDtypeStruct((2, 8, width // 8, cut), BF),
+        out_shape=[
+            jax.ShapeDtypeStruct((2, 8, width // 8, cut), BF),
+            jax.ShapeDtypeStruct((width, rows), BF), jax.ShapeDtypeStruct((width, rows), BF),
+        ],
         compiler_params=params(12), cost_estimate=cost(5),
         name="reduce_kept",
-    )(own, gbt, act)
+    )(own, gbt, act, hl, mixed)
 
 
 def ahead_kernel(
     own_ref, mixed_ref, x_ref, cot_ref, qhot_ref, wo_ref, we_ref, wr_ref, vec_ref,
-    layer_ref, act_ref, slope_ref, norm1_ref, inv1_ref, hlt_ref, mt_ref, gs_ref, gb_ref, gbt, rs_ref, vg_ref,
-    act, hid, hl, acc,
+    layer_ref, act_ref, slope_ref, norm1_ref, inv1_ref, hl, gs_ref, gb_ref, gbt, rs_ref, vg_ref,
+    act, hid, acc,
 ):
     step = pl.program_id(0)
     own_s, own_d = own_ref[0], own_ref[1]
@@ -329,9 +341,7 @@
             inv1_ref[at, :] = jnp.broadcast_to(inverse, (z.shape[0], LANES))
             hl[at, :] = hidden.astype(BF)
 
-        by_rows(rows, first_norm)
-        hlt_ref[...] = hl[...].T
-        mt_ref[...] = mixed_ref[...].T
+        by_rows(rows, first_norm, 2)
         vg_ref[...] = jnp.zeros_like(vg_ref)
 
     @pl.when(step < chunks)
@@ -373,7 +383,7 @@
             gb_ref[at, :] = low
             gs_ref[at, :] = grad
 
-        by_rows(rows, second_norm)
+        by_rows(rows, second_norm, 2)
         gbt[...] = gb_ref[...].T
 
     @pl.when(step >= chunks)
@@ -405,14 +415,13 @@
             ],
             out_specs=[
                 full((rows, width)), chunk, chunk, full((rows, width)), full((rows, LANES)),
-                full((width, rows)), full((width, rows)), full((rows, width)), full((rows, width)), full((width, rows)),
+                full((rows, width)), full((rows, width)), full((rows, width)), full((width, rows)),
                 pl.BlockSpec((1, 8, piece, cut), lambda s, own: (jnp.maximum(s - chunks, 0), 0, 0, 0)),
                 full((16, width)),
             ],
             scratch_shapes=[
                 pltpu.VMEM((chunks, rows, cut), BF),
                 pltpu.VMEM((rows, width), F32),
-                pltpu.VMEM((rows, width), BF),
                 pltpu.VMEM((rows, width), F32),
             ],
         ),
@@ -422,8 +431,7 @@
             jax.ShapeDtypeStruct((chunks, rows, cut), F32),
             jax.ShapeDtypeStruct((rows, width), F32),
             jax.ShapeDtypeStruct((rows, LANES), F32),
-            jax.ShapeDtypeStruct((width, rows), BF),
-            jax.ShapeDtypeStruct((width, rows), BF),
+            jax.ShapeDtypeStruct((rows, width), BF),
             jax.ShapeDtypeStruct((rows, width), F32),
             jax.ShapeDtypeStruct((rows, width), BF),
             jax.ShapeDtypeStruct((width, rows), BF),
@@ -622,7 +630,7 @@
                         ref[ry, spot(d, own_d)] = gw[own_s ^ (2 * ry + part), d]
 
 
-def attend_back(group, pairs, own, q, grad_mixed, mixed, halves, after, gw=None, last=True, vecs=()):
+def attend_back(group, pairs, own, q, grad_mixed, mixed, halves, after, gw=None, last=True, vecs=(), time=12):
     first = gw is None
     rows, width = q.shape
     half = halves[0][1].shape[0]
@@ -674,7 +682,7 @@
             num_scalar_prefetch=1, grid=(len(pairs),), in_specs=in_specs, out_specs=out_specs, scratch_shapes=scratch
         ),
         out_shape=out_shape,
-        compiler_params=params(20), cost_estimate=cost(12),
+        compiler_params=params(20), cost_estimate=cost(time),
         name="attend_back",
     )(own, *inputs)
 
@@ -773,7 +781,7 @@
             out += 1
 
 
-def gather(sums, after, steps=2):
+def gather(sums, after, steps=2, time=3):
     inputs, in_specs, out_shape, out_specs, plan = [], [], [], [], []
     for arrays, count, outs in sums:
         cols = arrays[0].shape[-1]
@@ -788,7 +796,7 @@
     outs = pl.pallas_call(
         functools.partial(gather_kernel, plan),
         grid=(steps,), in_specs=[*in_specs, pl.BlockSpec(memory_space=pl.ANY)], out_specs=out_specs,
-        out_shape=out_shape, compiler_params=params(14), cost_estimate=cost(3), name="gather",
+        out_shape=out_shape, compiler_params=params(14), cost_estimate=cost(time), name="gather",
     )(*inputs, after)
     made = []
     for _, parts in plan:
@@ -797,16 +805,42 @@
     return made
 
 
-def finish_kernel(counts, own_ref, *refs):
-    sums = []
-    for n in counts:
-        parts = [r[0].astype(F32) for r in refs[:n]]
-        refs = refs[n:]
-        while len(parts) > 1:
-            parts = [parts[t] + parts[t + 1] for t in range(0, len(parts), 2)]
-        sums.append(parts[0])
+def join_kernel(a_ref, a_came_ref, b_ref, b_came_ref, _, a_keep_ref, b_keep_ref, send_ref):
+    start = 0
+    for ref, came_ref, keep_ref in ((a_ref, a_came_ref, a_keep_ref), (b_ref, b_came_ref, b_keep_ref)):
+        total = ref[...].astype(F32) + came_ref[...].astype(F32)
+        rows = total.shape[1]
+        keep_ref[...] = total[0]
+        send_ref[start : start + rows, :] = total[1].astype(BF)
+        start += rows
+
+
+def join(a, b, after):
+    inputs, out_shape = [], []
+    for arrays in (a, b):
+        cols = arrays[0].shape[-1]
+        rows = arrays[0].size // cols // 2
+        inputs += [r.reshape(2, rows, cols) for r in arrays]
+        out_shape.append(jax.ShapeDtypeStruct((rows, cols), F32))
+    out_shape.append(jax.ShapeDtypeStruct((sum(o.shape[0] for o in out_shape), cols), BF))
+    vmem = pl.BlockSpec(memory_space=pltpu.VMEM)
+    return pl.pallas_call(
+        join_kernel,
+        in_specs=[*[vmem] * 4, pl.BlockSpec(memory_space=pl.ANY)], out_specs=[vmem] * 3, out_shape=out_shape,
+        compiler_params=params(8), cost_estimate=cost(3), name="join",
+    )(*inputs, after)
+
+
+def finish_kernel(own_ref, *refs):
+    read = lambda ref: ref[0].astype(F32)
+    exp_ref, in1_ref, both_ref = refs[2:5]
+    tall = exp_ref.shape[0]
+    red = read(refs[0]) + read(refs[1])
+    exp = exp_ref[...] + both_ref[:tall, :].astype(F32)
+    in1 = in1_ref[...] + both_ref[tall:, :].astype(F32)
+    in2 = (read(refs[5]) + read(refs[6])) + (read(refs[7]) + read(refs[8]))
+    refs = refs[9:]
     inp_ref, out_ref, exp_ref, red_ref, vec_ref, sq_ref = refs[1:]
-    red, exp, in1, in2 = sums
     rows = in1.shape[0]
     vec = in2[rows : rows + vec_ref.shape[0], : vec_ref.shape[1]]
     vec_ref[...] = vec
@@ -829,13 +863,13 @@
     sq_ref[...] = jnp.broadcast_to(squares, sq_ref.shape)
 
 
-def finish(own, red, exp, in1, in2, after):
-    piece = in1[0].shape[1]
-    tall = exp[0].shape[1] - piece // 2
+def finish(own, red, others, in2, after):
+    piece = others[1].shape[0]
+    tall = others[0].shape[0] - piece // 2
     vmem = pl.BlockSpec(memory_space=pltpu.VMEM)
-    inputs = [*red, *exp, *in1, *in2]
+    inputs = [*red, *others, *in2]
     return pl.pallas_call(
-        functools.partial(finish_kernel, tuple(map(len, (red, exp, in1, in2)))),
+        finish_kernel,
         in_specs=[
             pl.BlockSpec(memory_space=pltpu.SMEM), *[vmem] * len(inputs), pl.BlockSpec(memory_space=pl.ANY)
         ],
@@ -843,7 +877,7 @@
         out_shape=[
             jax.ShapeDtypeStruct((piece, 9 * HD), F32),
             jax.ShapeDtypeStruct((piece, 3 * HD), F32),
-            jax.ShapeDtypeStruct((tall, exp[0].shape[2]), F32),
+            jax.ShapeDtypeStruct((tall, others[0].shape[1]), F32),
             jax.ShapeDtypeStruct(red[0].shape[1:], F32),
             jax.ShapeDtypeStruct((3, piece), F32),
             jax.ShapeDtypeStruct((8, LANES), F32),
@@ -902,8 +936,8 @@
 
 def tree_sum(move, value, token):
     value = value + move(value, 0, 1)
-    value = (value + move(value, 0, 2)) + (move(value, 1, 0) + move(value, 1, 2))
-    return (value + move(value, 2, 0)) + (move(value, 4, 0) + move(value, 6, 0)) + token
+    value = (value + move(value, 2, 0)) + (move(value, 4, 0) + move(value, 6, 0))
+    return (value + move(value, 0, 2)) + (move(value, 1, 0) + move(value, 1, 2)) + token
 
 
 def spread_out(move, parts):
@@ -941,53 +975,56 @@
     return (y_cut[0], move(y_cut[1], 1, 0)), (x_cut[0], move(x_cut[1], 0, 2))
 
 
-def reduce_fast(move, own, back, behind_of, input_weight, gbt, act, red_s, vec1):
+def reduce_fast(move, kept_of, back, behind_of, input_weight, red_s, vec1):
     red_c = move(red_s, 0, 1)
-    red_k = reduce_kept(own, gbt, act)
+    red_k, *turned = kept_of()
     (red,) = gather([((red_k, red_c), 8, HALVES)], red_k)
     red_y, red_x = both_ways(move, red)
 
-    gf, grad_mixed, exp_s, exp_k, vec2 = behind_of(red[0])
+    gf, grad_mixed, exp_s, exp_k, vec2 = behind_of(red[0], turned)
     exp_c = move(exp_s, 0, 1)
-    red_y, red_x = gather([(red_y, 2, PAIR), (red_x, 2, PAIR)], vec2)
+    red_y, red_x = gather([(red_y, 2, PAIR), (red_x, 2, PAIR)], vec2, time=12)
     red_y, red_x = turned_ways(move, red_y, red_x)
-
-    dq0, dkv0, vb0, gw = back(0, CALLS[0], grad_mixed, red_y[0], last=False)
-    (red_k,), (red_s,), exp = gather([(red_y, 1, ONE), (red_x, 1, ONE), ((exp_k, exp_c), 8, HALVES)], vb0)
+    (exp,) = gather([((exp_k, exp_c), 8, HALVES)], red_y[0])
+    exp_y, exp_x = both_ways(move, exp)
+
+    dq0, dkv0, vb0, gw = back(0, CALLS[0], grad_mixed, exp[0], last=False)
+    (red_k,), (red_s,) = gather([(red_y, 1, ONE), (red_x, 1, ONE)], vb0)
     red = red_k, move(red_s, 4, 0)
-    exp_y, exp_x = both_ways(move, exp)
-
-    dq1, dkv1, vb1, in_s1, in_k1 = back(0, CALLS[1], grad_mixed, red_k, gw=gw)
+
+    dq1, dkv1, vb1, in_s1, in_k1 = back(0, CALLS[1], grad_mixed, red_k, gw=gw, time=1)
     in_c1 = move(in_s1, 0, 1)
-    (red_k, red_s), exp_y, exp_x = gather([(red, 2, PAIR), (exp_y, 2, PAIR), (exp_x, 2, PAIR)], vb1)
-    red = red_k, move(red_s, 2, 0)
+    exp_y, exp_x = gather([(exp_y, 2, PAIR), (exp_x, 2, PAIR)], vb1)
     exp_y, exp_x = turned_ways(move, exp_y, exp_x)
 
-    gx, dx = frames_back(input_weight, gf, red_k, CALLS[:2], (dq0, dq1), (dkv0, dkv1))
-    (exp_k,), (exp_s,), in1 = gather([(exp_y, 1, ONE), (exp_x, 1, ONE), ((in_k1, in_c1), 4, QUARTERS)], gx)
+    gx, dx = frames_back(input_weight, gf, exp_y[0], CALLS[:2], (dq0, dq1), (dkv0, dkv1))
+    (exp_k,), (exp_s,), in1, (red_k, red_s) = gather(
+        [(exp_y, 1, ONE), (exp_x, 1, ONE), ((in_k1, in_c1), 4, QUARTERS), (red, 2, PAIR)], gx
+    )
     exp = exp_k, move(exp_s, 4, 0)
     in1 = plane(move, in1)
+    red = red_k, move(red_s, 2, 0)
 
     dq2, dkv2, vb2, in_s2, in_k2 = back(1, CALLS[2], grad_mixed, exp_k, vecs=(vec1, vec2, vb0, vb1))
     in_c2 = move(in_s2, 0, 1)
-    (exp_k, exp_s), (in1_k, in1_s) = gather([(exp, 2, PAIR), (in1, 4, Z_HALVES)], vb2, 1)
+    ((in1_k, in1_s),) = gather([(in1, 4, Z_HALVES)], vb2, 1)
     in1 = in1_k, move(in1_s, 4, 0)
-    (in2,) = gather([((in_k2, in_c2), 4, QUARTERS)], exp_k, 1)
+    (in2,) = gather([((in_k2, in_c2), 4, QUARTERS)], in1_k, 1)
     in2 = plane(move, in2)
 
     gx, dx_s, dx_k = frames_back(input_weight, gx, in2[0], CALLS[2:], (dq2,), (dkv2,), dx)
     dx_c = move(dx_s, 0, 1)
-    in2, (in1_k, in1_s) = gather([(in2, 4, QUARTERS), (in1, 2, PAIR)], gx, 1)
+    exp_k, in1_k, both_s = join(exp, in1, gx)
+    both_c = move(both_s, 2, 0)
+    (in2,) = gather([(in2, 4, QUARTERS)], exp_k, 1)
     in2 = spread_out(move, in2)
-    in1 = in1_k, move(in1_s, 2, 0)
-    exp = exp_k, move(exp_s, 2, 0)
-    ((dx_k, dx_s),) = gather([((dx_k, dx_c), 2, (((0,), F32), ((1,), BF)))], in1_k)
-    return red, exp, in1, in2, gx, (dx_k, move(dx_s, 0, 2))
-
-
-def reduce_plain(move, own, back, behind_of, input_weight, gbt, act, red_s, vec1):
-    red_k = reduce_kept(own, gbt, act)
-    gf, grad_mixed, exp_s, exp_k, vec2 = behind_of(red_k)
+    ((dx_k, dx_s),) = gather([((dx_k, dx_c), 2, (((0,), F32), ((1,), BF)))], in2[0])
+    return red, (exp_k, in1_k, both_c), in2, gx, (dx_k, move(dx_s, 0, 2))
+
+
+def reduce_plain(move, kept_of, back, behind_of, input_weight, red_s, vec1):
+    red_k, *turned = kept_of()
+    gf, grad_mixed, exp_s, exp_k, vec2 = behind_of(red_k, turned)
     dq0, dkv0, vb0, gw = back(0, CALLS[0], grad_mixed, vec2, last=False)
     dq1, dkv1, vb1, in_s1, in_k1 = back(0, CALLS[1], grad_mixed, vb0, gw=gw)
     dq2, dkv2, vb2, in_s2, in_k2 = back(1, CALLS[2], grad_mixed, vb1, vecs=(vec1, vec2, vb0, vb1))
@@ -1027,8 +1064,8 @@
     own_s, own_d = lax.axis_index("seq"), lax.axis_index("dp")
     fast = dp == 8
 
+    across = move(frames, 0, 2)
     near = move(frames, 0, 1)
-    across = move(frames, 0, 2)
     own = jnp.stack([own_s, own_d]).astype(jnp.int32) if fast else jnp.zeros((2,), jnp.int32)
 
     e0, k0, v0, xt0, q, *stats, qhot, vectors = attend(lengths, (frames, near), input_weight, vector_copy)
@@ -1037,26 +1074,29 @@
     rest = qhot, q, *stats, *project(across, input_weight, vectors, stats[0])
     e1, k1, v1, xt1, mixed, rinv0, rinv1 = attend(lengths, (far,), input_weight, vectors, rest)
     halves = (e0, k0, v0, rinv0, xt0), (e1, k1, v1, rinv1, xt1)
-    layer, act, slope, norm1, inv1, hlt, mt, gs, gb, gbt, red_s, vec1 = ahead(
+    layer, act, slope, norm1, inv1, hl, gs, gb, gbt, red_s, vec1 = ahead(
         own, mixed, frames, cotangent, qhot, output_weight, expand_weight, reduce_weight, vectors
     )
 
-    def behind_of(after):
+    def kept_of():
+        return reduce_kept(own, gbt, act, hl, mixed)
+
+    def behind_of(after, turned):
         return behind(
-            own, slope, gb, gs, norm1, inv1, hlt, mt, output_weight, expand_weight, reduce_weight, vectors, after
+            own, slope, gb, gs, norm1, inv1, *turned, output_weight, expand_weight, reduce_weight, vectors, after
         )
 
     def back(group, pairs, grad_mixed, after, **more):
         return attend_back(group, pairs, own, q, grad_mixed, mixed, halves, after, **more)
 
     if fast:
-        red, exp, in1, in2, gx, dx = reduce_fast(move, own, back, behind_of, input_weight, gbt, act, red_s, vec1)
-        inp, out, exp, red, vec, squares = finish(own, red, exp, in1, in2, dx[0])
+        red, others, in2, gx, dx = reduce_fast(move, kept_of, back, behind_of, input_weight, red_s, vec1)
+        inp, out, exp, red, vec, squares = finish(own, red, others, in2, dx[0])
         frames_gradient, token = frames_end(gx, *dx)
         squares = tree_sum(move, squares, token)
     else:
         inp, out, exp, red, vec, squares, gx, dx = reduce_plain(
-            move, own, back, behind_of, input_weight, gbt, act, red_s, vec1
+            move, kept_of, back, behind_of, input_weight, red_s, vec1
         )
         frames_gradient, token = frames_end(gx, *dx)
         squares = squares + token

time: 175 us -> 170 us (0.971)
  Pallas kernels: 103 us -> 101 us
    ppermute x39 -> x38, starting transfers between devices: 40.9 us -> 39.2 us  [move(): return lax.ppermute(value, AXES, pairs)]
    ppermute x39 -> x38, waiting for transfers between devices: 26.7 us -> 25.3 us  [move(): return lax.ppermute(value, AXES, pairs)]
    pallas_call x9 -> x10, Pallas kernels: 6.62 us -> 6.04 us  [gather(): pl.pallas_call(functools.partial(gather_kernel, plan), grid=(steps,), in_...]
  transfers between devices with their start and end apart: 39 -> 38, of which waited for: 18 -> 16; matrix products, arithmetic and copies ran while one was open for 0% -> 0% of each run, Pallas kernels for 42% -> 44%
where the time goes in v5:
time: 170 us
  Pallas kernels  101 us (59%)
  starting transfers between devices  39.2 us (23%)
  waiting for transfers between devices  25.3 us (15%)
  local copies, waits for them, and re-layouts  2.43 us (1%)
    ppermute x38, starting transfers between devices, move(): return lax.ppermute(value, AXES, pairs)  39.2 us
    pallas_call x3, Pallas kernels, attend_back(): pl.pallas_call(functools.partial(back_kernel, group, pairs, first, last),...  28.7 us
    ppermute x38, waiting for transfers between devices, move(): return lax.ppermute(value, AXES, pairs)  25.3 us
    pallas_call x2, Pallas kernels, attend(): pl.pallas_call(attend_far_kernel if near else attend_near_kernel, grid=(s...  22.2 us
    pallas_call x1, Pallas kernels, ahead(): pl.pallas_call(ahead_kernel, grid_spec=pltpu.PrefetchScalarGridSpec(num_s...  12.2 us
    pallas_call x1, Pallas kernels, behind(): pl.pallas_call(behind_kernel, grid_spec=pltpu.PrefetchScalarGridSpec(num_...  11.7 us
    pallas_call x2, Pallas kernels, frames_back(): pl.pallas_call(functools.partial(frames_kernel, pairs, last), grid=(4,),...  8.87 us
    pallas_call x10, Pallas kernels, gather(): pl.pallas_call(functools.partial(gather_kernel, plan), grid=(steps,), in_...  6.04 us
  transfers between devices with their start and end apart: 38, of which 16 were waited for; matrix products, arithmetic and copies ran while one was open for 0% of the time, Pallas kernels for 44%

profile of v5, /device:TPU:0, one launch (start us, length us, event | category | flops | bytes accessed | tf_op | source)
XLA Modules:
  0.0 169.9 jit_solution(9404185262723601319)
XLA Ops:
  0.7 0.5 collective-permute-start.1
  1.2 2.6 %collective-permute-start = (bf16[384,768]{1,0:T(8,128)(2,1)}, bf16[384,768]{1,0:T(8,128)(2,1)S(1)}, u32[]{:S(2)}, u32[]{:S(2)}) collective-permute-start(bf16[384,768]{1,0:T(8,128)(2,1)} %x_ref.1), channel_id=1, source_target_pairs={{0,2},{1,3},{2,0},{3,1},{4,6},{5,7},{6,4},{7,5},{8,10},{9,11},{10,... | collective-permute-start | bytes 1769480 | tf_op jit(solution)/shard_map/ppermute | solution.py:932
  3.9 0.7 copy-done.28
  4.6 0.7 copy-done.32
  5.2 11.8 %attend.2 = (bf16[12,384,768]{2,1,0:T(8,128)(2,1)}, bf16[768,768]{1,0:T(8,128)(2,1)}, bf16[768,768]{1,0:T(8,128)(2,1)}, bf16[768,768]{1,0:T(8,128)(2,1)}, bf16[3...) custom-call(s32[1,3]{1,0:T(1,128)S(1)} %copy-done.32, ...), custom_call_target="tpu_custom_call" | custom-call | flops 48399998976 | tf_op jit(solution)/shard_map/attend/pallas_call | solution.py:245
  17.0 0.9 collective-permute-done.x_ref
  18.0 3.2 %project.1 = (bf16[384,768]{1,0:T(8,128)(2,1)S(1)}, bf16[384,768]{1,0:T(8,128)(2,1)S(1)}, bf16[768,384]{1,0:T(8,128)(2,1)S(1)}) custom-call(bf16[384,768]{1,0:T(8,128)(2,1)S(1)} %pass_on.1.x_ref.xp_ref, bf16[384,768]{1,0:T(8,128)(2,1)S(1)} %pass_on.1.x_ref.xp_ref, bf16[768,2304]{1,0:T(8,128)(2,1)} %w_ref.3, bf16[768,2304]{1,0:T(8,128)(2,1)} %w_ref.3, ...), custom_call_target="tpu_custom_call" | custom-call | flops 22000001024 | tf_op jit(solution)/shard_map/project/pallas_call | solution.py:169
  21.3 10.4 %attend.3 = (bf16[12,384,768]{2,1,0:T(8,128)(2,1)}, bf16[768,768]{1,0:T(8,128)(2,1)}, bf16[768,768]{1,0:T(8,128)(2,1)}, bf16[768,768]{1,0:T(8,128)(2,1)}, bf16[3...) custom-call(s32[1,3]{1,0:T(1,128)S(1)} %copy-done.32, ...), custom_call_target="tpu_custom_call" | custom-call | flops 48399998976 | tf_op jit(solution)/shard_map/attend/pallas_call | solution.py:245
  31.8 12.2 %ahead.1 = (bf16[384,768]{1,0:T(8,128)(2,1)}, bf16[4,384,768]{2,1,0:T(8,128)(2,1)S(1)}, f32[4,384,768]{2,1,0:T(8,128)S(1)}, f32[384,768]{1,0:T(8,128)S(1)}, f32[...) custom-call(s32[2]{0:T(128)S(1)} %pad_add_fusion.own_ref, ...), custom_call_target="tpu_custom_call" | custom-call | flops 88000004096 | tf_op jit(solution)/shard_map/ahead/pallas_call | solution.py:404
  44.0 0.4 collective-permute-start.3
  44.5 2.5 %reduce_kept.1 = (bf16[2,8,96,768]{3,2,1,0:T(8,128)(2,1)S(1)}, bf16[768,384]{1,0:T(8,128)(2,1)S(1)}, bf16[768,384]{1,0:T(8,128)(2,1)S(1)}) custom-call(s32[2]{0:T(128)S(1)} %pad_add_fusion.own_ref, bf16[768,384]{1,0:T(8,128)(2,1)S(1)} %get-tuple-element.167.gbt_ref, bf16[4,384,768]{2,1,0:T(8,128)(2,1)S(1)} %get-tuple-element.168.act_ref, ...), custom_call_target="tpu_custom_call" | custom-call | flops 22000001024 | tf_op jit(solution)/shard_map/reduce_kept/pallas_call | solution.py:293
  46.9 1.7 collective-permute-done.3
  48.6 1.1 gather.10
  49.7 1.8 %collective-permute-start.5 = (bf16[2,192,768]{2,1,0:T(8,128)(2,1)S(1)}, bf16[2,192,768]{2,1,0:T(8,128)(2,1)S(1)}, u32[]{:S(2)}, u32[]{:S(2)}) collective-permute-start(bf16[2,192,768]{2,1,0:T(8,128)(2,1)S(1)} %get-tuple-element.178), channel_id=1, source_target_pairs={{0,2},{1,3},{2,0},{3,1},{4,6},{5,7},{6,4},{7,5},{8,10},{9,11},{10,... | collective-permute-start | bytes 1769480 | tf_op jit(solution)/shard_map/ppermute | solution.py:932
  51.5 1.5 collective-permute-start.6
  53.0 11.7 %behind.1 = (f32[384,768]{1,0:T(8,128)S(1)}, bf16[384,768]{1,0:T(8,128)(2,1)S(1)}, bf16[2,2,4,240,384]{4,3,2,1,0:T(8,128)(2,1)S(1)}, bf16[2,2,4,240,384]{4,3,2,1,0:T(8,128)(2,1)S(1)}, f32[16,768]{1,0:T(8,128)S(1)}) custom-call(s32[2]{0:T(128)S(1)} %pad_add_fusion.own_ref, f32[4,384,768]{2,1,0:T(8,128)S(1)} %get-tuple-element.162.slope_ref, ...), custom_call_target="tpu_custom_call" | custom-call | flops 79200002048 | tf_op jit(solution)/shard_map/behind/pallas_call | solution.py:514
  64.8 0.6 collective-permute-done.5.refs_1_
  65.4 1.5 collective-permute-done.6.refs_3_
  66.8 0.5 gather.11
  67.3 1.6 collective-permute-start.9
  68.9 0.5 collective-permute-start.10
  69.4 0.7 collective-permute-done.4
  70.2 1.7 gather.12
  71.9 0.9 collective-permute-start.7
  72.7 0.5 collective-permute-start.8
  74.2 9.3 %attend_back.3 = (bf16[384,256]{1,0:T(8,128)(2,1)S(1)}, bf16[512,1536]{1,0:T(8,128)(2,1)S(1)}, f32[8,256]{1,0:T(8,128)S(1)}, bf16[4,8,96,384]{3,2,1,0:T(8,128)(2,1)S(1)}) custom-call(s32[2]{0:T(128)S(1)} %pad_add_fusion.own_ref, bf16[384,768]{1,0:T(8,128)(2,1)S(1)} %copy-done.9, bf16[384,768]{1,0:T(8,128)(2,1)S(1)} %get-tuple-element.187.gm_ref, ...), custom_call_target="tpu_custom_call" | custom-call | flops 52800000000 | tf_op jit(solution)/shard_map/attend_back/pallas_call | solution.py:679
  83.6 2.7 %collective-permute-start.14 = (bf16[1,192,768]{2,1,0:T(8,128)(2,1)S(1)}, bf16[1,192,768]{2,1,0:T(8,128)(2,1)S(1)}, u32[]{:S(2)}, u32[]{:S(2)}) collective-permute-start(bf16[1,192,768]{2,1,0:T(8,128)(2,1)S(1)} %get-tuple-element.216), channel_id=1, source_target_pairs={{0,16},{1,17},{2,18},{3,19},{4,20},{5,21},{6,22},{7,23},{8,24},{9,... | collective-permute-start | bytes 884744 | tf_op jit(solution)/shard_map/ppermute | solution.py:932
  86.3 9.9 %attend_back.4 = (bf16[384,256]{1,0:T(8,128)(2,1)S(1)}, bf16[512,1536]{1,0:T(8,128)(2,1)S(1)}, f32[8,256]{1,0:T(8,128)S(1)}, bf16[2,8,96,384]{3,2,1,0:T(8,128)(2,1)S(1)}, bf16[2,8,96,384]{3,2,1,0:T(8,128)(2,1)S(1)}) custom-call(s32[2]{0:T(128)S(1)} %pad_add_fusion.own_ref, bf16[384,768]{1,0:T(8,128)(2,1)S(1)} %copy-done.9, ...), custom_call_target="tpu_custom_call" | custom-call | flops 4400000000 | tf_op jit(solution)/shard_map/attend_back/pallas_call | solution.py:679
  96.4 0.7 gather.14
  97.1 0.7 collective-permute-start.11
  97.9 1.2 collective-permute-start.12
  99.1 5.3 %frames_back.2 = (f32[384,768]{1,0:T(8,128)S(1)}, f32[4,768,384]{2,1,0:T(8,128)S(1)}) custom-call(bf16[768,2304]{1,0:T(8,128)(2,1)S(1)} %copy-done.12, f32[384,768]{1,0:T(8,128)S(1)} %get-tuple-element.175.gx_in_ref, bf16[1,480,384]{2,1,0:T(8,128)(2,1)S(1)} %get-tuple-element.205.after_ref.refs_0_, bf16[384,256]{1,0:T(8,128)(2,1)S(1)} %get-tuple-element.206.refs_0_, ...), custom_call_target="tpu_custom_call" | custom-call | flops 35200000000 | tf_op jit(solution)/shard_map/frames_back/pallas_call | solution.py:738
  104.4 3.7 %collective-permute-done.11.refs_1_ = bf16[1,480,384]{2,1,0:T(8,128)(2,1)S(1)} collective-permute-done((bf16[1,480,384]{2,1,0:T(8,128)(2,1)S(1)}, bf16[1,480,384]{2,1,0:T(8,128)(2,1)S(1)}, u32[]{:S(2)}, u32[]{:S(2)}) %collective-permute-start.11) | collective-permute-done | bytes 368672 | tf_op jit(solution)/shard_map/ppermute | solution.py:932
  108.6 0.9 gather.15
  109.4 1.7 collective-permute-start.26
  111.1 1.3 collective-permute-start.16
  112.4 0.8 collective-permute-start.17
  113.2 1.4 collective-permute-start.18
  114.9 9.5 %attend_back.5 = (bf16[384,256]{1,0:T(8,128)(2,1)S(1)}, bf16[512,1536]{1,0:T(8,128)(2,1)S(1)}, f32[8,256]{1,0:T(8,128)S(1)}, bf16[2,8,112,256]{3,2,1,0:T(8,128)(2,1)S(1)}, bf16[2,8,112,256]{3,2,1,0:T(8,128)(2,1)S(1)}) custom-call(s32[2]{0:T(128)S(1)} %pad_add_fusion.own_ref, bf16[384,768]{1,0:T(8,128)(2,1)S(1)} %copy-done.9, ...), custom_call_target="tpu_custom_call" | custom-call | flops 52800000000 | tf_op jit(solution)/shard_map/attend_back/pallas_call | solution.py:679
  124.5 1.9 %collective-permute-done.17 = bf16[1,384,384]{2,1,0:T(8,128)(2,1)S(1)} collective-permute-done((bf16[1,384,384]{2,1,0:T(8,128)(2,1)S(1)}, bf16[1,384,384]{2,1,0:T(8,128)(2,1)S(1)}, u32[]{:S(2)}, u32[]{:S(2)}) %collective-permute-start.17) | collective-permute-done | bytes 294944 | tf_op jit(solution)/shard_map/ppermute | solution.py:932
  126.6 0.8 collective-permute-start.24
  127.6 1.4 collective-permute-start.20
  129.0 0.8 collective-permute-start.21
  129.8 3.6 %frames_back.3 = (f32[384,768]{1,0:T(8,128)S(1)}, bf16[2,768,384]{2,1,0:T(8,128)(2,1)S(1)}, f32[2,768,384]{2,1,0:T(8,128)S(1)}) custom-call(bf16[768,2304]{1,0:T(8,128)(2,1)S(1)} %copy-done.12, f32[384,768]{1,0:T(8,128)S(1)} %get-tuple-element.210.refs_8_.gx_in_ref, bf16[1,448,256]{2,1,0:T(8,128)(2,1)S(1)} %get-tuple-element.227.after_ref, ...), custom_call_target="tpu_custom_call" | custom-call | flops 17600000000 | tf_op jit(solution)/shard_map/frames_back/pallas_call | solution.py:738
  133.4 1.8 %collective-permute-done.23 = bf16[1,480,384]{2,1,0:T(8,128)(2,1)S(1)} collective-permute-done((bf16[1,480,384]{2,1,0:T(8,128)(2,1)S(1)}, bf16[1,480,384]{2,1,0:T(8,128)(2,1)S(1)}, u32[]{:S(2)}, u32[]{:S(2)}) %collective-permute-start.23) | collective-permute-done | bytes 368672 | tf_op jit(solution)/shard_map/ppermute | solution.py:932
  135.2 1.6 collective-permute-start.22
  136.8 1.5 collective-permute-done.24.b_came_ref
  138.6 5.0 %collective-permute-done.22 = bf16[1,448,256]{2,1,0:T(8,128)(2,1)S(1)} collective-permute-done((bf16[1,448,256]{2,1,0:T(8,128)(2,1)S(1)}, bf16[1,448,256]{2,1,0:T(8,128)(2,1)S(1)}, u32[]{:S(2)}, u32[]{:S(2)}) %collective-permute-start.22) | collective-permute-done | bytes 229408 | tf_op jit(solution)/shard_map/ppermute | solution.py:932
  143.8 0.5 collective-permute-start.29
  144.3 3.8 %collective-permute-start.30 = (bf16[1,112,256]{2,1,0:T(8,128)(2,1)S(1)}, bf16[1,112,256]{2,1,0:T(8,128)(2,1)S(1)}, u32[]{:S(2)}, u32[]{:S(2)}) collective-permute-start(bf16[1,112,256]{2,1,0:T(8,128)(2,1)S(1)} %get-tuple-element.250), channel_id=1, source_target_pairs={{0,24},{1,25},{2,26},{3,27},{4,28},{5,29},{6,30},{7,31},{8,16},{9,... | collective-permute-start | bytes 172040 | tf_op jit(solution)/shard_map/ppermute | solution.py:932
  148.2 0.5 gather.19
  148.7 1.3 collective-permute-start.25
  150.0 1.0 collective-permute-done.30.refs_8_
  151.0 0.8 finish.1
  151.9 1.2 collective-permute-done.31
  153.1 3.1 %collective-permute-start.34 = (f32[8,128]{1,0:T(8,128)S(1)}, f32[8,128]{1,0:T(8,128)S(1)}, u32[]{:S(2)}, u32[]{:S(2)}) collective-permute-start(f32[8,128]{1,0:T(8,128)S(1)} %add.24), channel_id=1, source_target_pairs={{0,24},{1,25},{2,26},{3,27},{4,28},{5,29},{6,30},{7,31},{8,16},{9,... | collective-permute-start | bytes 12296 | tf_op jit(solution)/shard_map/ppermute | solution.py:932
  156.2 1.3 collective-permute-start.32
  157.4 1.0 collective-permute-done.34
  158.5 2.2 %collective-permute-done.33 = f32[8,128]{1,0:T(8,128)S(1)} collective-permute-done((f32[8,128]{1,0:T(8,128)S(1)}, f32[8,128]{1,0:T(8,128)S(1)}, u32[]{:S(2)}, u32[]{:S(2)}) %collective-permute-start.33) | collective-permute-done | bytes 4128 | tf_op jit(solution)/shard_map/ppermute | solution.py:932
  160.9 1.6 collective-permute-start.37
  162.5 1.1 collective-permute-start.36
  163.6 0.8 collective-permute-start.35
  164.4 2.7 %frames_end.1 = (f32[384,768]{1,0:T(8,128)}, f32[8,128]{1,0:T(8,128)S(1)}) custom-call(f32[384,768]{1,0:T(8,128)S(1)} %get-tuple-element.231._.gx_ref, f32[1,768,384]{2,1,0:T(8,128)S(1)} %get-tuple-element.241.keep_ref.refs_9_, bf16[1,768,384]{2,1,0:T(8,128)(2,1)S(1)} %collective-permute-done.25.came_ref), custom_call_target="tpu_custom_call" | custom-call | flops 22000001024 | tf_op jit(solution)/shard_map/frames_end/pallas_call | solution.py:762
  167.4 2.4 %adam.1 = (f32[1,1]{1,0:T(1,128)}, f32[96,576]{1,0:T(8,128)}, f32[96,576]{1,0:T(8,128)}, f32[96,576]{1,0:T(8,128)}, bf16[96,576]{1,0:T(8,128)(2,1)}, /*index=5*/...) custom-call(f32[8,128]{1,0:T(8,128)S(1)} %add_add_fusion.squares_ref, ...), custom_call_target="tpu_custom_call" | custom-call | flops 22000001024 | tf_op jit(solution)/shard_map/adam/pallas_call | solution.py:922
  (122 shorter events, 3.4 us)
Async XLA Ops:
  0.7 3.2 %collective-permute-start.1 = (bf16[384,768]{1,0:T(8,128)(2,1)}, bf16[384,768]{1,0:T(8,128)(2,1)S(1)}, u32[]{:S(2)}, u32[]{:S(2)}) collective-permute-start(bf16[384,768]{1,0:T(8,128)(2,1)} %x_ref.1), channel_id=1, source_target_pairs={{0,1},{1,0},{2,3},{3,2},{4,5},{5,4},{6,7},{7,6},{8,9},{9,8},{10,11... | collective-permute-start | bytes 1769480 | tf_op jit(solution)/shard_map/ppermute | solution.py:932
  1.2 16.7 %collective-permute-start = (bf16[384,768]{1,0:T(8,128)(2,1)}, bf16[384,768]{1,0:T(8,128)(2,1)S(1)}, u32[]{:S(2)}, u32[]{:S(2)}) collective-permute-start(bf16[384,768]{1,0:T(8,128)(2,1)} %x_ref.1), channel_id=1, source_target_pairs={{0,2},{1,3},{2,0},{3,1},{4,6},{5,7},{6,4},{7,5},{8,10},{9,11},{10,... | collective-permute-start | bytes 1769480 | tf_op jit(solution)/shard_map/ppermute | solution.py:932
  17.0 4.2 %copy-start.8 = (bf16[384,768]{1,0:T(8,128)(2,1)}, bf16[384,768]{1,0:T(8,128)(2,1)S(1)}, u32[]{:S(2)}) copy-start(bf16[384,768]{1,0:T(8,128)(2,1)S(1)} %get-tuple-element.154.q_ref) | copy-start | bytes 1769476
  17.9 3.3 %collective-permute-start.2 = (bf16[384,768]{1,0:T(8,128)(2,1)S(1)}, bf16[384,768]{1,0:T(8,128)(2,1)S(1)}, u32[]{:S(2)}, u32[]{:S(2)}) collective-permute-start(bf16[384,768]{1,0:T(8,128)(2,1)S(1)} %pass_on.1.x_ref.xp_ref), channel_id=1, source_target_pairs={{0,1},{1,0},{2,3},{3,2},{4,5},{5,4},{6,7},{7,6},{8,9},{9,8},{10,11... | collective-permute-start | bytes 1769480 | tf_op jit(solution)/shard_map/ppermute | solution.py:932
  18.0 13.7 %slice-start = ((s8[4718592]{0:T(1024)(128)(4,1)}), s8[4194304]{0:T(1024)(128)(4,1)S(1)}, s32[]{:S(2)}) async-start(s8[4718592]{0:T(1024)(128)(4,1)} %bitcast.31), calls=%async_computation | async-start | bytes 8388608
  18.0 13.7 %slice-start.2 = ((s8[4718592]{0:T(1024)(128)(4,1)}), s8[4194304]{0:T(1024)(128)(4,1)S(1)}, s32[]{:S(2)}) async-start(s8[4718592]{0:T(1024)(128)(4,1)} %bitcast.33), calls=%async_computation.2 | async-start | bytes 8388608
  21.2 10.5 %slice-start.1 = ((s8[4718592]{0:T(1024)(128)(4,1)}), s8[524288]{0:T(1024)(128)(4,1)S(1)}, s32[]{:S(2)}) async-start(s8[4718592]{0:T(1024)(128)(4,1)} %bitcast.31), calls=%async_computation.1 | async-start | bytes 1048576
  21.3 10.5 %slice-start.3 = ((s8[4718592]{0:T(1024)(128)(4,1)}), s8[524288]{0:T(1024)(128)(4,1)S(1)}, s32[]{:S(2)}) async-start(s8[4718592]{0:T(1024)(128)(4,1)} %bitcast.33), calls=%async_computation.3 | async-start | bytes 1048576
  21.3 10.5 %copy-start.13 = (bf16[768,768]{1,0:T(8,128)(2,1)S(1)}, bf16[768,768]{1,0:T(8,128)(2,1)}, u32[]{:S(2)}) copy-start(bf16[768,768]{1,0:T(8,128)(2,1)} %wo_ref.3) | copy-start | bytes 3538948
  21.3 10.5 %copy-start.14 = (bf16[384,768]{1,0:T(8,128)(2,1)S(1)}, bf16[384,768]{1,0:T(8,128)(2,1)}, u32[]{:S(2)}) copy-start(bf16[384,768]{1,0:T(8,128)(2,1)} %x_ref.1) | copy-start | bytes 1769476
  21.3 10.5 %copy-start.15 = (bf16[384,768]{1,0:T(8,128)(2,1)S(1)}, bf16[384,768]{1,0:T(8,128)(2,1)}, u32[]{:S(2)}) copy-start(bf16[384,768]{1,0:T(8,128)(2,1)} %cot_ref.1) | copy-start | bytes 1769476
  31.8 12.7 %copy-start.10 = (bf16[384,768]{1,0:T(8,128)(2,1)}, bf16[384,768]{1,0:T(8,128)(2,1)S(1)}, u32[]{:S(2)}) copy-start(bf16[384,768]{1,0:T(8,128)(2,1)S(1)} %get-tuple-element.160.mixed_ref) | copy-start | bytes 1769476
  44.0 4.6 %collective-permute-start.3 = (bf16[2,8,96,768]{3,2,1,0:T(8,128)(2,1)S(1)}, bf16[2,8,96,768]{3,2,1,0:T(8,128)(2,1)S(1)}, u32[]{:S(2)}, u32[]{:S(2)}) collective-permute-start(bf16[2,8,96,768]{3,2,1,0:T(8,128)(2,1)S(1)} %get-tuple-element.173), channel_id=1, source_target_pairs={{0,1},{1,0},{2,3},{3,2},{4,5},{5,4},{6,7},{7,6},{8,9},{9,8},{10,11... | collective-permute-start | bytes 7077896 | tf_op jit(solution)/shard_map/ppermute | solution.py:932
  49.7 15.7 %collective-permute-start.5 = (bf16[2,192,768]{2,1,0:T(8,128)(2,1)S(1)}, bf16[2,192,768]{2,1,0:T(8,128)(2,1)S(1)}, u32[]{:S(2)}, u32[]{:S(2)}) collective-permute-start(bf16[2,192,768]{2,1,0:T(8,128)(2,1)S(1)} %get-tuple-element.178), channel_id=1, source_target_pairs={{0,2},{1,3},{2,0},{3,1},{4,6},{5,7},{6,4},{7,5},{8,10},{9,11},{10,... | collective-permute-start | bytes 1769480 | tf_op jit(solution)/shard_map/ppermute | solution.py:932
  51.5 15.3 %collective-permute-start.6 = (bf16[2,192,768]{2,1,0:T(8,128)(2,1)S(1)}, bf16[2,192,768]{2,1,0:T(8,128)(2,1)S(1)}, u32[]{:S(2)}, u32[]{:S(2)}) collective-permute-start(bf16[2,192,768]{2,1,0:T(8,128)(2,1)S(1)} %get-tuple-element.180), channel_id=1, source_target_pairs={{0,4},{1,5},{2,6},{3,7},{4,0},{5,1},{6,2},{7,3},{8,12},{9,13},{10,... | collective-permute-start | bytes 1769480 | tf_op jit(solution)/shard_map/ppermute | solution.py:932
  64.7 5.4 %collective-permute-start.4 = (bf16[2,2,4,240,384]{4,3,2,1,0:T(8,128)(2,1)S(1)}, bf16[2,2,4,240,384]{4,3,2,1,0:T(8,128)(2,1)S(1)}, u32[]{:S(2)}, u32[]{:S(2)}) collective-permute-start(bf16[2,2,4,240,384]{4,3,2,1,0:T(8,128)(2,1)S(1)} %get-tuple-element.177), channel_id=1, source_target_pairs={{0,1},{1,0},{2,3},{3,2},{4,5},{5,4},{6,7},{7,6},{8,9},{9,8},{10,11... | collective-permute-start | bytes 8847368 | tf_op jit(solution)/shard_map/ppermute | solution.py:932
  67.3 16.1 %collective-permute-start.9 = (bf16[1,192,768]{2,1,0:T(8,128)(2,1)S(1)}, bf16[1,192,768]{2,1,0:T(8,128)(2,1)S(1)}, u32[]{:S(2)}, u32[]{:S(2)}) collective-permute-start(bf16[1,192,768]{2,1,0:T(8,128)(2,1)S(1)} %get-tuple-element.198), channel_id=1, source_target_pairs={{0,4},{1,5},{2,6},{3,7},{4,0},{5,1},{6,2},{7,3},{8,12},{9,13},{10,... | collective-permute-start | bytes 884744 | tf_op jit(solution)/shard_map/ppermute | solution.py:932
  68.9 14.5 %collective-permute-start.10 = (bf16[1,192,768]{2,1,0:T(8,128)(2,1)S(1)}, bf16[1,192,768]{2,1,0:T(8,128)(2,1)S(1)}, u32[]{:S(2)}, u32[]{:S(2)}) collective-permute-start(bf16[1,192,768]{2,1,0:T(8,128)(2,1)S(1)} %get-tuple-element.200), channel_id=1, source_target_pairs={{0,2},{1,3},{2,0},{3,1},{4,6},{5,7},{6,4},{7,5},{8,10},{9,11},{10,... | collective-permute-start | bytes 884744 | tf_op jit(solution)/shard_map/ppermute | solution.py:932
  70.2 4.0 %copy-start.11 = (bf16[384,768]{1,0:T(8,128)(2,1)S(1)}, bf16[384,768]{1,0:T(8,128)(2,1)}, u32[]{:S(2)}) copy-start(bf16[384,768]{1,0:T(8,128)(2,1)} %copy-done.10) | copy-start | bytes 1769476
  71.9 24.5 %collective-permute-start.7 = (bf16[2,480,384]{2,1,0:T(8,128)(2,1)S(1)}, bf16[2,480,384]{2,1,0:T(8,128)(2,1)S(1)}, u32[]{:S(2)}, u32[]{:S(2)}) collective-permute-start(bf16[2,480,384]{2,1,0:T(8,128)(2,1)S(1)} %get-tuple-element.184), channel_id=1, source_target_pairs={{0,2},{1,3},{2,0},{3,1},{4,6},{5,7},{6,4},{7,5},{8,10},{9,11},{10,... | collective-permute-start | bytes 2211848 | tf_op jit(solution)/shard_map/ppermute | solution.py:932
  72.7 23.6 %collective-permute-start.8 = (bf16[2,480,384]{2,1,0:T(8,128)(2,1)S(1)}, bf16[2,480,384]{2,1,0:T(8,128)(2,1)S(1)}, u32[]{:S(2)}, u32[]{:S(2)}) collective-permute-start(bf16[2,480,384]{2,1,0:T(8,128)(2,1)S(1)} %get-tuple-element.186), channel_id=1, source_target_pairs={{0,4},{1,5},{2,6},{3,7},{4,0},{5,1},{6,2},{7,3},{8,12},{9,13},{10,... | collective-permute-start | bytes 2211848 | tf_op jit(solution)/shard_map/ppermute | solution.py:932
  83.6 20.8 %collective-permute-start.14 = (bf16[1,192,768]{2,1,0:T(8,128)(2,1)S(1)}, bf16[1,192,768]{2,1,0:T(8,128)(2,1)S(1)}, u32[]{:S(2)}, u32[]{:S(2)}) collective-permute-start(bf16[1,192,768]{2,1,0:T(8,128)(2,1)S(1)} %get-tuple-element.216), channel_id=1, source_target_pairs={{0,16},{1,17},{2,18},{3,19},{4,20},{5,21},{6,22},{7,23},{8,24},{9,... | collective-permute-start | bytes 884744 | tf_op jit(solution)/shard_map/ppermute | solution.py:932
  96.3 12.3 %collective-permute-start.13 = (bf16[2,8,96,384]{3,2,1,0:T(8,128)(2,1)S(1)}, bf16[2,8,96,384]{3,2,1,0:T(8,128)(2,1)S(1)}, u32[]{:S(2)}, u32[]{:S(2)}) collective-permute-start(bf16[2,8,96,384]{3,2,1,0:T(8,128)(2,1)S(1)} %get-tuple-element.215), channel_id=1, source_target_pairs={{0,1},{1,0},{2,3},{3,2},{4,5},{5,4},{6,7},{7,6},{8,9},{9,8},{10,11... | collective-permute-start | bytes 3538952 | tf_op jit(solution)/shard_map/ppermute | solution.py:932
  97.1 11.0 %collective-permute-start.11 = (bf16[1,480,384]{2,1,0:T(8,128)(2,1)S(1)}, bf16[1,480,384]{2,1,0:T(8,128)(2,1)S(1)}, u32[]{:S(2)}, u32[]{:S(2)}) collective-permute-start(bf16[1,480,384]{2,1,0:T(8,128)(2,1)S(1)} %get-tuple-element.211), channel_id=1, source_target_pairs={{0,4},{1,5},{2,6},{3,7},{4,0},{5,1},{6,2},{7,3},{8,12},{9,13},{10,... | collective-permute-start | bytes 1105928 | tf_op jit(solution)/shard_map/ppermute | solution.py:932
  97.9 10.7 %collective-permute-start.12 = (bf16[1,480,384]{2,1,0:T(8,128)(2,1)S(1)}, bf16[1,480,384]{2,1,0:T(8,128)(2,1)S(1)}, u32[]{:S(2)}, u32[]{:S(2)}) collective-permute-start(bf16[1,480,384]{2,1,0:T(8,128)(2,1)S(1)} %get-tuple-element.213), channel_id=1, source_target_pairs={{0,2},{1,3},{2,0},{3,1},{4,6},{5,7},{6,4},{7,5},{8,10},{9,11},{10,... | collective-permute-start | bytes 1105928 | tf_op jit(solution)/shard_map/ppermute | solution.py:932
  108.6 6.4 %copy-start.34 = (f32[16,768]{1,0:T(8,128)S(1)}, f32[16,768]{1,0:T(8,128)}, u32[]{:S(2)}) copy-start(f32[16,768]{1,0:T(8,128)} %copy-done.33) | copy-start | bytes 147460
  109.4 39.3 %collective-permute-start.26 = (bf16[1,96,768]{2,1,0:T(8,128)(2,1)S(1)}, bf16[1,96,768]{2,1,0:T(8,128)(2,1)S(1)}, u32[]{:S(2)}, u32[]{:S(2)}) collective-permute-start(bf16[1,96,768]{2,1,0:T(8,128)(2,1)S(1)} %get-tuple-element.245), channel_id=1, source_target_pairs={{0,8},{1,9},{2,10},{3,11},{4,12},{5,13},{6,14},{7,15},{8,0},{9,1},... | collective-permute-start | bytes 442376 | tf_op jit(solution)/shard_map/ppermute | solution.py:932
  111.1 13.4 %collective-permute-start.16 = (bf16[1,384,384]{2,1,0:T(8,128)(2,1)S(1)}, bf16[1,384,384]{2,1,0:T(8,128)(2,1)S(1)}, u32[]{:S(2)}, u32[]{:S(2)}) collective-permute-start(bf16[1,384,384]{2,1,0:T(8,128)(2,1)S(1)} %get-tuple-element.222), channel_id=1, source_target_pairs={{0,4},{1,5},{2,6},{3,7},{4,0},{5,1},{6,2},{7,3},{8,12},{9,13},{10,... | collective-permute-start | bytes 884744 | tf_op jit(solution)/shard_map/ppermute | solution.py:932
  112.4 14.0 %collective-permute-start.17 = (bf16[1,384,384]{2,1,0:T(8,128)(2,1)S(1)}, bf16[1,384,384]{2,1,0:T(8,128)(2,1)S(1)}, u32[]{:S(2)}, u32[]{:S(2)}) collective-permute-start(bf16[1,384,384]{2,1,0:T(8,128)(2,1)S(1)} %get-tuple-element.223), channel_id=1, source_target_pairs={{0,2},{1,3},{2,0},{3,1},{4,6},{5,7},{6,4},{7,5},{8,10},{9,11},{10,... | collective-permute-start | bytes 884744 | tf_op jit(solution)/shard_map/ppermute | solution.py:932
  113.2 13.2 %collective-permute-start.18 = (bf16[1,384,384]{2,1,0:T(8,128)(2,1)S(1)}, bf16[1,384,384]{2,1,0:T(8,128)(2,1)S(1)}, u32[]{:S(2)}, u32[]{:S(2)}) collective-permute-start(bf16[1,384,384]{2,1,0:T(8,128)(2,1)S(1)} %get-tuple-element.224), channel_id=1, source_target_pairs={{0,6},{1,7},{2,4},{3,5},{4,2},{5,3},{6,0},{7,1},{8,14},{9,15},{10,... | collective-permute-start | bytes 884744 | tf_op jit(solution)/shard_map/ppermute | solution.py:932
  114.6 20.7 %collective-permute-start.23 = (bf16[1,480,384]{2,1,0:T(8,128)(2,1)S(1)}, bf16[1,480,384]{2,1,0:T(8,128)(2,1)S(1)}, u32[]{:S(2)}, u32[]{:S(2)}) collective-permute-start(bf16[1,480,384]{2,1,0:T(8,128)(2,1)S(1)} %get-tuple-element.237), channel_id=1, source_target_pairs={{0,16},{1,17},{2,18},{3,19},{4,20},{5,21},{6,22},{7,23},{8,24},{9,... | collective-permute-start | bytes 1105928 | tf_op jit(solution)/shard_map/ppermute | solution.py:932
  124.5 2.9 %collective-permute-start.15 = (bf16[2,8,112,256]{3,2,1,0:T(8,128)(2,1)S(1)}, bf16[2,8,112,256]{3,2,1,0:T(8,128)(2,1)S(1)}, u32[]{:S(2)}, u32[]{:S(2)}) collective-permute-start(bf16[2,8,112,256]{3,2,1,0:T(8,128)(2,1)S(1)} %get-tuple-element.220), channel_id=1, source_target_pairs={{0,1},{1,0},{2,3},{3,2},{4,5},{5,4},{6,7},{7,6},{8,9},{9,8},{10,11... | collective-permute-start | bytes 2752520 | tf_op jit(solution)/shard_map/ppermute | solution.py:932
  126.6 11.7 %collective-permute-start.24 = (bf16[2,96,384]{2,1,0:T(8,128)(2,1)S(1)}, bf16[2,96,384]{2,1,0:T(8,128)(2,1)S(1)}, u32[]{:S(2)}, u32[]{:S(2)}) collective-permute-start(bf16[2,96,384]{2,1,0:T(8,128)(2,1)S(1)} %get-tuple-element.238), channel_id=1, source_target_pairs={{0,16},{1,17},{2,18},{3,19},{4,20},{5,21},{6,22},{7,23},{8,24},{9,... | collective-permute-start | bytes 442376 | tf_op jit(solution)/shard_map/ppermute | solution.py:932
  127.6 10.9 %collective-permute-start.20 = (bf16[1,448,256]{2,1,0:T(8,128)(2,1)S(1)}, bf16[1,448,256]{2,1,0:T(8,128)(2,1)S(1)}, u32[]{:S(2)}, u32[]{:S(2)}) collective-permute-start(bf16[1,448,256]{2,1,0:T(8,128)(2,1)S(1)} %get-tuple-element.234), channel_id=1, source_target_pairs={{0,4},{1,5},{2,6},{3,7},{4,0},{5,1},{6,2},{7,3},{8,12},{9,13},{10,... | collective-permute-start | bytes 688136 | tf_op jit(solution)/shard_map/ppermute | solution.py:932
  129.0 9.6 %collective-permute-start.21 = (bf16[1,448,256]{2,1,0:T(8,128)(2,1)S(1)}, bf16[1,448,256]{2,1,0:T(8,128)(2,1)S(1)}, u32[]{:S(2)}, u32[]{:S(2)}) collective-permute-start(bf16[1,448,256]{2,1,0:T(8,128)(2,1)S(1)} %get-tuple-element.235), channel_id=1, source_target_pairs={{0,2},{1,3},{2,0},{3,1},{4,6},{5,7},{6,4},{7,5},{8,10},{9,11},{10,... | collective-permute-start | bytes 688136 | tf_op jit(solution)/shard_map/ppermute | solution.py:932
  135.2 8.3 %collective-permute-start.22 = (bf16[1,448,256]{2,1,0:T(8,128)(2,1)S(1)}, bf16[1,448,256]{2,1,0:T(8,128)(2,1)S(1)}, u32[]{:S(2)}, u32[]{:S(2)}) collective-permute-start(bf16[1,448,256]{2,1,0:T(8,128)(2,1)S(1)} %get-tuple-element.236), channel_id=1, source_target_pairs={{0,6},{1,7},{2,4},{3,5},{4,2},{5,3},{6,0},{7,1},{8,14},{9,15},{10,... | collective-permute-start | bytes 688136 | tf_op jit(solution)/shard_map/ppermute | solution.py:932
  138.4 11.6 %collective-permute-start.27 = (bf16[336,384]{1,0:T(8,128)(2,1)S(1)}, bf16[336,384]{1,0:T(8,128)(2,1)S(1)}, u32[]{:S(2)}, u32[]{:S(2)}) collective-permute-start(bf16[336,384]{1,0:T(8,128)(2,1)S(1)} %get-tuple-element.247), channel_id=1, source_target_pairs={{0,8},{1,9},{2,10},{3,11},{4,12},{5,13},{6,14},{7,15},{8,0},{9,1},... | collective-permute-start | bytes 774152 | tf_op jit(solution)/shard_map/ppermute | solution.py:932
  138.5 5.8 %collective-permute-start.19 = (bf16[2,768,384]{2,1,0:T(8,128)(2,1)S(1)}, bf16[2,768,384]{2,1,0:T(8,128)(2,1)S(1)}, u32[]{:S(2)}, u32[]{:S(2)}) collective-permute-start(bf16[2,768,384]{2,1,0:T(8,128)(2,1)S(1)} %get-tuple-element.233), channel_id=1, source_target_pairs={{0,1},{1,0},{2,3},{3,2},{4,5},{5,4},{6,7},{7,6},{8,9},{9,8},{10,11... | collective-permute-start | bytes 3538952 | tf_op jit(solution)/shard_map/ppermute | solution.py:932
  143.7 6.3 %collective-permute-start.28 = (bf16[1,112,256]{2,1,0:T(8,128)(2,1)S(1)}, bf16[1,112,256]{2,1,0:T(8,128)(2,1)S(1)}, u32[]{:S(2)}, u32[]{:S(2)}) collective-permute-start(bf16[1,112,256]{2,1,0:T(8,128)(2,1)S(1)} %get-tuple-element.248), channel_id=1, source_target_pairs={{0,8},{1,9},{2,10},{3,11},{4,12},{5,13},{6,14},{7,15},{8,0},{9,1},... | collective-permute-start | bytes 172040 | tf_op jit(solution)/shard_map/ppermute | solution.py:932
  143.8 6.2 %collective-permute-start.29 = (bf16[1,112,256]{2,1,0:T(8,128)(2,1)S(1)}, bf16[1,112,256]{2,1,0:T(8,128)(2,1)S(1)}, u32[]{:S(2)}, u32[]{:S(2)}) collective-permute-start(bf16[1,112,256]{2,1,0:T(8,128)(2,1)S(1)} %get-tuple-element.249), channel_id=1, source_target_pairs={{0,16},{1,17},{2,18},{3,19},{4,20},{5,21},{6,22},{7,23},{8,24},{9,... | collective-permute-start | bytes 172040 | tf_op jit(solution)/shard_map/ppermute | solution.py:932
  144.3 6.7 %collective-permute-start.30 = (bf16[1,112,256]{2,1,0:T(8,128)(2,1)S(1)}, bf16[1,112,256]{2,1,0:T(8,128)(2,1)S(1)}, u32[]{:S(2)}, u32[]{:S(2)}) collective-permute-start(bf16[1,112,256]{2,1,0:T(8,128)(2,1)S(1)} %get-tuple-element.250), channel_id=1, source_target_pairs={{0,24},{1,25},{2,26},{3,27},{4,28},{5,29},{6,30},{7,31},{8,16},{9,... | collective-permute-start | bytes 172040 | tf_op jit(solution)/shard_map/ppermute | solution.py:932
  148.7 15.7 %collective-permute-start.25 = (bf16[1,768,384]{2,1,0:T(8,128)(2,1)S(1)}, bf16[1,768,384]{2,1,0:T(8,128)(2,1)S(1)}, u32[]{:S(2)}, u32[]{:S(2)}) collective-permute-start(bf16[1,768,384]{2,1,0:T(8,128)(2,1)S(1)} %get-tuple-element.242), channel_id=1, source_target_pairs={{0,2},{1,3},{2,0},{3,1},{4,6},{5,7},{6,4},{7,5},{8,10},{9,11},{10,... | collective-permute-start | bytes 1769480 | tf_op jit(solution)/shard_map/ppermute | solution.py:932
  151.9 1.2 collective-permute-start.31
  153.1 5.4 %collective-permute-start.34 = (f32[8,128]{1,0:T(8,128)S(1)}, f32[8,128]{1,0:T(8,128)S(1)}, u32[]{:S(2)}, u32[]{:S(2)}) collective-permute-start(f32[8,128]{1,0:T(8,128)S(1)} %add.24), channel_id=1, source_target_pairs={{0,24},{1,25},{2,26},{3,27},{4,28},{5,29},{6,30},{7,31},{8,16},{9,... | collective-permute-start | bytes 12296 | tf_op jit(solution)/shard_map/ppermute | solution.py:932
  156.2 4.5 %collective-permute-start.33 = (f32[8,128]{1,0:T(8,128)S(1)}, f32[8,128]{1,0:T(8,128)S(1)}, u32[]{:S(2)}, u32[]{:S(2)}) collective-permute-start(f32[8,128]{1,0:T(8,128)S(1)} %add.24), channel_id=1, source_target_pairs={{0,16},{1,17},{2,18},{3,19},{4,20},{5,21},{6,22},{7,23},{8,24},{9,... | collective-permute-start | bytes 12296 | tf_op jit(solution)/shard_map/ppermute | solution.py:932
  156.2 4.5 %collective-permute-start.32 = (f32[8,128]{1,0:T(8,128)S(1)}, f32[8,128]{1,0:T(8,128)S(1)}, u32[]{:S(2)}, u32[]{:S(2)}) collective-permute-start(f32[8,128]{1,0:T(8,128)S(1)} %add.24), channel_id=1, source_target_pairs={{0,8},{1,9},{2,10},{3,11},{4,12},{5,13},{6,14},{7,15},{8,0},{9,1},... | collective-permute-start | bytes 12296 | tf_op jit(solution)/shard_map/ppermute | solution.py:932
  160.7 6.6 %copy-start.16 = (f32[192,384]{1,0:T(8,128)S(1)}, f32[192,384]{1,0:T(8,128)}, u32[]{:S(2)}) copy-start(f32[192,384]{1,0:T(8,128)} %refs_8_.1) | copy-start | bytes 884740
  160.7 6.6 %copy-start.17 = (f32[192,384]{1,0:T(8,128)S(1)}, f32[192,384]{1,0:T(8,128)}, u32[]{:S(2)}) copy-start(f32[192,384]{1,0:T(8,128)} %refs_9_.1) | copy-start | bytes 884740
  160.7 6.6 %copy-start.18 = (f32[192,384]{1,0:T(8,128)S(1)}, f32[192,384]{1,0:T(8,128)}, u32[]{:S(2)}) copy-start(f32[192,384]{1,0:T(8,128)} %refs_10_.1) | copy-start | bytes 884740
  160.7 6.6 %copy-start.19 = (f32[768,96]{0,1:T(8,128)S(1)}, f32[768,96]{0,1:T(8,128)}, u32[]{:S(2)}) copy-start(f32[768,96]{0,1:T(8,128)} %param.34) | copy-start | bytes 884740
  160.7 6.6 %copy-start.20 = (f32[768,96]{0,1:T(8,128)S(1)}, f32[768,96]{0,1:T(8,128)}, u32[]{:S(2)}) copy-start(f32[768,96]{0,1:T(8,128)} %param.39) | copy-start | bytes 884740
  160.7 6.6 %copy-start.21 = (f32[768,96]{0,1:T(8,128)S(1)}, f32[768,96]{0,1:T(8,128)}, u32[]{:S(2)}) copy-start(f32[768,96]{0,1:T(8,128)} %param.44) | copy-start | bytes 884740
  160.8 6.6 %copy-start.22 = (f32[96,576]{1,0:T(8,128)S(1)}, f32[96,576]{1,0:T(8,128)}, u32[]{:S(2)}) copy-start(f32[96,576]{1,0:T(8,128)} %refs_0_.1) | copy-start | bytes 663556
  160.8 6.5 %copy-start.23 = (f32[96,576]{1,0:T(8,128)S(1)}, f32[96,576]{1,0:T(8,128)}, u32[]{:S(2)}) copy-start(f32[96,576]{1,0:T(8,128)} %refs_1_.1) | copy-start | bytes 663556
  160.8 6.5 %copy-start.24 = (f32[96,576]{1,0:T(8,128)S(1)}, f32[96,576]{1,0:T(8,128)}, u32[]{:S(2)}) copy-start(f32[96,576]{1,0:T(8,128)} %refs_2_.1) | copy-start | bytes 663556
  160.8 6.5 %copy-start.25 = (f32[192,96]{1,0:T(8,128)S(1)}, f32[192,96]{1,0:T(8,128)}, u32[]{:S(2)}) copy-start(f32[192,96]{1,0:T(8,128)} %refs_4_.1) | copy-start | bytes 221188
  160.8 6.5 %copy-start.26 = (f32[192,96]{1,0:T(8,128)S(1)}, f32[192,96]{1,0:T(8,128)}, u32[]{:S(2)}) copy-start(f32[192,96]{1,0:T(8,128)} %refs_5_.1) | copy-start | bytes 221188
  160.8 6.5 %copy-start.27 = (f32[192,96]{1,0:T(8,128)S(1)}, f32[192,96]{1,0:T(8,128)}, u32[]{:S(2)}) copy-start(f32[192,96]{1,0:T(8,128)} %refs_6_.1) | copy-start | bytes 221188
  160.8 6.5 %copy-start.29 = (f32[3,96]{1,0:T(4,128)S(1)}, f32[3,96]{1,0:T(4,128)}, u32[]{:S(2)}) copy-start(f32[3,96]{1,0:T(4,128)} %refs_16_.1) | copy-start | bytes 3460
  160.8 6.5 %copy-start.30 = (f32[3,96]{1,0:T(4,128)S(1)}, f32[3,96]{1,0:T(4,128)}, u32[]{:S(2)}) copy-start(f32[3,96]{1,0:T(4,128)} %refs_17_.1) | copy-start | bytes 3460
  160.9 6.5 %copy-start.31 = (f32[3,96]{1,0:T(4,128)S(1)}, f32[3,96]{1,0:T(4,128)}, u32[]{:S(2)}) copy-start(f32[3,96]{1,0:T(4,128)} %refs_18_.1) | copy-start | bytes 3460
  160.9 6.2 %collective-permute-start.37 = (f32[8,128]{1,0:T(8,128)S(1)}, f32[8,128]{1,0:T(8,128)S(1)}, u32[]{:S(2)}, u32[]{:S(2)}) collective-permute-start(f32[8,128]{1,0:T(8,128)S(1)} %add_add_fusion.1), channel_id=1, source_target_pairs={{0,6},{1,7},{2,4},{3,5},{4,2},{5,3},{6,0},{7,1},{8,14},{9,15},{10,... | collective-permute-start | bytes 12296 | tf_op jit(solution)/shard_map/ppermute | solution.py:932
  162.5 4.6 %collective-permute-start.36 = (f32[8,128]{1,0:T(8,128)S(1)}, f32[8,128]{1,0:T(8,128)S(1)}, u32[]{:S(2)}, u32[]{:S(2)}) collective-permute-start(f32[8,128]{1,0:T(8,128)S(1)} %add_add_fusion.1), channel_id=1, source_target_pairs={{0,4},{1,5},{2,6},{3,7},{4,0},{5,1},{6,2},{7,3},{8,12},{9,13},{10,... | collective-permute-start | bytes 12296 | tf_op jit(solution)/shard_map/ppermute | solution.py:932
  163.6 3.6 %collective-permute-start.35 = (f32[8,128]{1,0:T(8,128)S(1)}, f32[8,128]{1,0:T(8,128)S(1)}, u32[]{:S(2)}, u32[]{:S(2)}) collective-permute-start(f32[8,128]{1,0:T(8,128)S(1)} %add_add_fusion.1), channel_id=1, source_target_pairs={{0,2},{1,3},{2,0},{3,1},{4,6},{5,7},{6,4},{7,5},{8,10},{9,11},{10,... | collective-permute-start | bytes 12296 | tf_op jit(solution)/shard_map/ppermute | solution.py:932
  (13 other events, 36.5 us)

commit v6 on v5

--- a/solution.py
+++ b/solution.py
@@ -757,11 +757,12 @@
 
 def frames_end(gx, keep, came):
     rows, width = gx.shape
-    across = pl.BlockSpec((rows, LANES), lambda p: (0, p))
-    down = pl.BlockSpec((1, LANES, rows), lambda p: (0, p, 0))
+    wide = 3 * LANES
+    across = pl.BlockSpec((rows, wide), lambda p: (0, p))
+    down = pl.BlockSpec((1, wide, rows), lambda p: (0, p, 0))
     return pl.pallas_call(
         frames_end_kernel,
-        grid=(width // LANES,), in_specs=[across, down, down],
+        grid=(width // wide,), in_specs=[across, down, down],
         out_specs=[across, pl.BlockSpec((8, LANES), lambda p: (0, 0))],
         out_shape=[jax.ShapeDtypeStruct((rows, width), F32), jax.ShapeDtypeStruct((8, LANES), F32)], compiler_params=params(8), cost_estimate=cost(5), name="frames_end",
     )(gx, keep, came)
@@ -978,14 +979,14 @@
 def reduce_fast(move, kept_of, back, behind_of, input_weight, red_s, vec1):
     red_c = move(red_s, 0, 1)
     red_k, *turned = kept_of()
-    (red,) = gather([((red_k, red_c), 8, HALVES)], red_k)
+    (red,) = gather([((red_k, red_c), 8, HALVES)], red_k, 3)
     red_y, red_x = both_ways(move, red)
 
     gf, grad_mixed, exp_s, exp_k, vec2 = behind_of(red[0], turned)
     exp_c = move(exp_s, 0, 1)
     red_y, red_x = gather([(red_y, 2, PAIR), (red_x, 2, PAIR)], vec2, time=12)
     red_y, red_x = turned_ways(move, red_y, red_x)
-    (exp,) = gather([((exp_k, exp_c), 8, HALVES)], red_y[0])
+    (exp,) = gather([((exp_k, exp_c), 8, HALVES)], red_y[0], 3)
     exp_y, exp_x = both_ways(move, exp)
 
     dq0, dkv0, vb0, gw = back(0, CALLS[0], grad_mixed, exp[0], last=False)

time: 170 us -> 170 us (level)
  transfers between devices with their start and end apart: 38 -> 38, of which waited for: 16 -> 17; matrix products, arithmetic and copies ran while one was open for 0% -> 0% of each run, Pallas kernels for 44% -> 43%
where the time goes in v6:
time: 170 us
  Pallas kernels  99.9 us (59%)
  starting transfers between devices  39.1 us (23%)
  waiting for transfers between devices  26.8 us (16%)
  local copies, waits for them, and re-layouts  2.42 us (1%)
    ppermute x38, starting transfers between devices, move(): return lax.ppermute(value, AXES, pairs)  39.1 us
    pallas_call x3, Pallas kernels, attend_back(): pl.pallas_call(functools.partial(back_kernel, group, pairs, first, last),...  28.5 us
    ppermute x38, waiting for transfers between devices, move(): return lax.ppermute(value, AXES, pairs)  26.8 us
    pallas_call x2, Pallas kernels, attend(): pl.pallas_call(attend_far_kernel if near else attend_near_kernel, grid=(s...  22.2 us
    pallas_call x1, Pallas kernels, ahead(): pl.pallas_call(ahead_kernel, grid_spec=pltpu.PrefetchScalarGridSpec(num_s...  12.2 us
    pallas_call x1, Pallas kernels, behind(): pl.pallas_call(behind_kernel, grid_spec=pltpu.PrefetchScalarGridSpec(num_...  11.7 us
    pallas_call x2, Pallas kernels, frames_back(): pl.pallas_call(functools.partial(frames_kernel, pairs, last), grid=(4,),...  8.61 us
    pallas_call x10, Pallas kernels, gather(): pl.pallas_call(functools.partial(gather_kernel, plan), grid=(steps,), in_...  6.3 us
  transfers between devices with their start and end apart: 38, of which 17 were waited for; matrix products, arithmetic and copies ran while one was open for 0% of the time, Pallas kernels for 43%

profile of v6, /device:TPU:0, one launch (start us, length us, event | category | flops | bytes accessed | tf_op | source)
XLA Modules:
  0.0 170.0 jit_solution(13653047874049583016)
XLA Ops:
  0.7 0.5 collective-permute-start.1
  1.2 2.6 %collective-permute-start = (bf16[384,768]{1,0:T(8,128)(2,1)}, bf16[384,768]{1,0:T(8,128)(2,1)S(1)}, u32[]{:S(2)}, u32[]{:S(2)}) collective-permute-start(bf16[384,768]{1,0:T(8,128)(2,1)} %x_ref.1), channel_id=1, source_target_pairs={{0,2},{1,3},{2,0},{3,1},{4,6},{5,7},{6,4},{7,5},{8,10},{9,11},{10,... | collective-permute-start | bytes 1769480 | tf_op jit(solution)/shard_map/ppermute | solution.py:933
  3.9 0.7 copy-done.28
  4.6 0.7 copy-done.32
  5.2 11.8 %attend.2 = (bf16[12,384,768]{2,1,0:T(8,128)(2,1)}, bf16[768,768]{1,0:T(8,128)(2,1)}, bf16[768,768]{1,0:T(8,128)(2,1)}, bf16[768,768]{1,0:T(8,128)(2,1)}, bf16[3...) custom-call(s32[1,3]{1,0:T(1,128)S(1)} %copy-done.32, ...), custom_call_target="tpu_custom_call" | custom-call | flops 48399998976 | tf_op jit(solution)/shard_map/attend/pallas_call | solution.py:245
  17.0 0.9 collective-permute-done.x_ref
  18.0 3.2 %project.1 = (bf16[384,768]{1,0:T(8,128)(2,1)S(1)}, bf16[384,768]{1,0:T(8,128)(2,1)S(1)}, bf16[768,384]{1,0:T(8,128)(2,1)S(1)}) custom-call(bf16[384,768]{1,0:T(8,128)(2,1)S(1)} %pass_on.1.x_ref.xp_ref, bf16[384,768]{1,0:T(8,128)(2,1)S(1)} %pass_on.1.x_ref.xp_ref, bf16[768,2304]{1,0:T(8,128)(2,1)} %w_ref.3, bf16[768,2304]{1,0:T(8,128)(2,1)} %w_ref.3, ...), custom_call_target="tpu_custom_call" | custom-call | flops 22000001024 | tf_op jit(solution)/shard_map/project/pallas_call | solution.py:169
  21.3 10.4 %attend.3 = (bf16[12,384,768]{2,1,0:T(8,128)(2,1)}, bf16[768,768]{1,0:T(8,128)(2,1)}, bf16[768,768]{1,0:T(8,128)(2,1)}, bf16[768,768]{1,0:T(8,128)(2,1)}, bf16[3...) custom-call(s32[1,3]{1,0:T(1,128)S(1)} %copy-done.32, ...), custom_call_target="tpu_custom_call" | custom-call | flops 48399998976 | tf_op jit(solution)/shard_map/attend/pallas_call | solution.py:245
  31.8 12.2 %ahead.1 = (bf16[384,768]{1,0:T(8,128)(2,1)}, bf16[4,384,768]{2,1,0:T(8,128)(2,1)S(1)}, f32[4,384,768]{2,1,0:T(8,128)S(1)}, f32[384,768]{1,0:T(8,128)S(1)}, f32[...) custom-call(s32[2]{0:T(128)S(1)} %pad_add_fusion.own_ref, ...), custom_call_target="tpu_custom_call" | custom-call | flops 88000004096 | tf_op jit(solution)/shard_map/ahead/pallas_call | solution.py:404
  44.0 0.4 collective-permute-start.3
  44.5 2.5 %reduce_kept.1 = (bf16[2,8,96,768]{3,2,1,0:T(8,128)(2,1)S(1)}, bf16[768,384]{1,0:T(8,128)(2,1)S(1)}, bf16[768,384]{1,0:T(8,128)(2,1)S(1)}) custom-call(s32[2]{0:T(128)S(1)} %pad_add_fusion.own_ref, bf16[768,384]{1,0:T(8,128)(2,1)S(1)} %get-tuple-element.167.gbt_ref, bf16[4,384,768]{2,1,0:T(8,128)(2,1)S(1)} %get-tuple-element.168.act_ref, ...), custom_call_target="tpu_custom_call" | custom-call | flops 22000001024 | tf_op jit(solution)/shard_map/reduce_kept/pallas_call | solution.py:293
  46.9 1.7 collective-permute-done.3
  48.6 1.1 gather.10
  49.7 1.8 %collective-permute-start.5 = (bf16[2,192,768]{2,1,0:T(8,128)(2,1)S(1)}, bf16[2,192,768]{2,1,0:T(8,128)(2,1)S(1)}, u32[]{:S(2)}, u32[]{:S(2)}) collective-permute-start(bf16[2,192,768]{2,1,0:T(8,128)(2,1)S(1)} %get-tuple-element.178), channel_id=1, source_target_pairs={{0,2},{1,3},{2,0},{3,1},{4,6},{5,7},{6,4},{7,5},{8,10},{9,11},{10,... | collective-permute-start | bytes 1769480 | tf_op jit(solution)/shard_map/ppermute | solution.py:933
  51.6 1.5 collective-permute-start.6
  53.0 11.7 %behind.1 = (f32[384,768]{1,0:T(8,128)S(1)}, bf16[384,768]{1,0:T(8,128)(2,1)S(1)}, bf16[2,2,4,240,384]{4,3,2,1,0:T(8,128)(2,1)S(1)}, bf16[2,2,4,240,384]{4,3,2,1,0:T(8,128)(2,1)S(1)}, f32[16,768]{1,0:T(8,128)S(1)}) custom-call(s32[2]{0:T(128)S(1)} %pad_add_fusion.own_ref, f32[4,384,768]{2,1,0:T(8,128)S(1)} %get-tuple-element.162.slope_ref, ...), custom_call_target="tpu_custom_call" | custom-call | flops 79200002048 | tf_op jit(solution)/shard_map/behind/pallas_call | solution.py:514
  64.8 0.6 collective-permute-done.5.refs_1_
  65.4 1.5 collective-permute-done.6.refs_3_
  66.9 0.5 gather.11
  67.4 1.6 collective-permute-start.9
  68.9 0.5 collective-permute-start.10
  69.4 0.7 collective-permute-done.4
  70.2 1.7 gather.12
  71.9 0.9 collective-permute-start.7
  72.8 0.5 collective-permute-start.8
  74.2 9.3 %attend_back.3 = (bf16[384,256]{1,0:T(8,128)(2,1)S(1)}, bf16[512,1536]{1,0:T(8,128)(2,1)S(1)}, f32[8,256]{1,0:T(8,128)S(1)}, bf16[4,8,96,384]{3,2,1,0:T(8,128)(2,1)S(1)}) custom-call(s32[2]{0:T(128)S(1)} %pad_add_fusion.own_ref, bf16[384,768]{1,0:T(8,128)(2,1)S(1)} %copy-done.9, bf16[384,768]{1,0:T(8,128)(2,1)S(1)} %get-tuple-element.187.gm_ref, ...), custom_call_target="tpu_custom_call" | custom-call | flops 52800000000 | tf_op jit(solution)/shard_map/attend_back/pallas_call | solution.py:679
  83.7 2.7 %collective-permute-start.14 = (bf16[1,192,768]{2,1,0:T(8,128)(2,1)S(1)}, bf16[1,192,768]{2,1,0:T(8,128)(2,1)S(1)}, u32[]{:S(2)}, u32[]{:S(2)}) collective-permute-start(bf16[1,192,768]{2,1,0:T(8,128)(2,1)S(1)} %get-tuple-element.216), channel_id=1, source_target_pairs={{0,16},{1,17},{2,18},{3,19},{4,20},{5,21},{6,22},{7,23},{8,24},{9,... | collective-permute-start | bytes 884744 | tf_op jit(solution)/shard_map/ppermute | solution.py:933
  86.3 9.7 %attend_back.4 = (bf16[384,256]{1,0:T(8,128)(2,1)S(1)}, bf16[512,1536]{1,0:T(8,128)(2,1)S(1)}, f32[8,256]{1,0:T(8,128)S(1)}, bf16[2,8,96,384]{3,2,1,0:T(8,128)(2,1)S(1)}, bf16[2,8,96,384]{3,2,1,0:T(8,128)(2,1)S(1)}) custom-call(s32[2]{0:T(128)S(1)} %pad_add_fusion.own_ref, bf16[384,768]{1,0:T(8,128)(2,1)S(1)} %copy-done.9, ...), custom_call_target="tpu_custom_call" | custom-call | flops 4400000000 | tf_op jit(solution)/shard_map/attend_back/pallas_call | solution.py:679
  96.2 1.0 gather.14
  97.1 0.8 collective-permute-start.11
  97.9 1.2 collective-permute-start.12
  99.1 5.3 %frames_back.2 = (f32[384,768]{1,0:T(8,128)S(1)}, f32[4,768,384]{2,1,0:T(8,128)S(1)}) custom-call(bf16[768,2304]{1,0:T(8,128)(2,1)S(1)} %copy-done.12, f32[384,768]{1,0:T(8,128)S(1)} %get-tuple-element.175.gx_in_ref, bf16[1,480,384]{2,1,0:T(8,128)(2,1)S(1)} %get-tuple-element.205.after_ref.refs_0_, bf16[384,256]{1,0:T(8,128)(2,1)S(1)} %get-tuple-element.206.refs_0_, ...), custom_call_target="tpu_custom_call" | custom-call | flops 35200000000 | tf_op jit(solution)/shard_map/frames_back/pallas_call | solution.py:738
  104.4 3.7 %collective-permute-done.11.refs_1_ = bf16[1,480,384]{2,1,0:T(8,128)(2,1)S(1)} collective-permute-done((bf16[1,480,384]{2,1,0:T(8,128)(2,1)S(1)}, bf16[1,480,384]{2,1,0:T(8,128)(2,1)S(1)}, u32[]{:S(2)}, u32[]{:S(2)}) %collective-permute-start.11) | collective-permute-done | bytes 368672 | tf_op jit(solution)/shard_map/ppermute | solution.py:933
  108.6 0.9 gather.15
  109.5 1.6 collective-permute-start.26
  111.1 1.3 collective-permute-start.16
  112.4 0.8 collective-permute-start.17
  113.2 1.4 collective-permute-start.18
  115.0 9.5 %attend_back.5 = (bf16[384,256]{1,0:T(8,128)(2,1)S(1)}, bf16[512,1536]{1,0:T(8,128)(2,1)S(1)}, f32[8,256]{1,0:T(8,128)S(1)}, bf16[2,8,112,256]{3,2,1,0:T(8,128)(2,1)S(1)}, bf16[2,8,112,256]{3,2,1,0:T(8,128)(2,1)S(1)}) custom-call(s32[2]{0:T(128)S(1)} %pad_add_fusion.own_ref, bf16[384,768]{1,0:T(8,128)(2,1)S(1)} %copy-done.9, ...), custom_call_target="tpu_custom_call" | custom-call | flops 52800000000 | tf_op jit(solution)/shard_map/attend_back/pallas_call | solution.py:679
  124.6 1.9 %collective-permute-done.17 = bf16[1,384,384]{2,1,0:T(8,128)(2,1)S(1)} collective-permute-done((bf16[1,384,384]{2,1,0:T(8,128)(2,1)S(1)}, bf16[1,384,384]{2,1,0:T(8,128)(2,1)S(1)}, u32[]{:S(2)}, u32[]{:S(2)}) %collective-permute-start.17) | collective-permute-done | bytes 294944 | tf_op jit(solution)/shard_map/ppermute | solution.py:933
  126.6 0.8 collective-permute-start.24
  127.7 1.4 collective-permute-start.20
  129.0 0.8 collective-permute-start.21
  129.8 3.3 %frames_back.3 = (f32[384,768]{1,0:T(8,128)S(1)}, bf16[2,768,384]{2,1,0:T(8,128)(2,1)S(1)}, f32[2,768,384]{2,1,0:T(8,128)S(1)}) custom-call(bf16[768,2304]{1,0:T(8,128)(2,1)S(1)} %copy-done.12, f32[384,768]{1,0:T(8,128)S(1)} %get-tuple-element.210.refs_8_.gx_in_ref, bf16[1,448,256]{2,1,0:T(8,128)(2,1)S(1)} %get-tuple-element.227.after_ref, ...), custom_call_target="tpu_custom_call" | custom-call | flops 17600000000 | tf_op jit(solution)/shard_map/frames_back/pallas_call | solution.py:738
  133.2 2.1 %collective-permute-done.23 = bf16[1,480,384]{2,1,0:T(8,128)(2,1)S(1)} collective-permute-done((bf16[1,480,384]{2,1,0:T(8,128)(2,1)S(1)}, bf16[1,480,384]{2,1,0:T(8,128)(2,1)S(1)}, u32[]{:S(2)}, u32[]{:S(2)}) %collective-permute-start.23) | collective-permute-done | bytes 368672 | tf_op jit(solution)/shard_map/ppermute | solution.py:933
  135.3 1.5 collective-permute-start.22
  136.8 1.5 collective-permute-done.24.b_came_ref
  138.7 5.0 %collective-permute-done.22 = bf16[1,448,256]{2,1,0:T(8,128)(2,1)S(1)} collective-permute-done((bf16[1,448,256]{2,1,0:T(8,128)(2,1)S(1)}, bf16[1,448,256]{2,1,0:T(8,128)(2,1)S(1)}, u32[]{:S(2)}, u32[]{:S(2)}) %collective-permute-start.22) | collective-permute-done | bytes 229408 | tf_op jit(solution)/shard_map/ppermute | solution.py:933
  144.2 3.9 %collective-permute-start.30 = (bf16[1,112,256]{2,1,0:T(8,128)(2,1)S(1)}, bf16[1,112,256]{2,1,0:T(8,128)(2,1)S(1)}, u32[]{:S(2)}, u32[]{:S(2)}) collective-permute-start(bf16[1,112,256]{2,1,0:T(8,128)(2,1)S(1)} %get-tuple-element.250), channel_id=1, source_target_pairs={{0,24},{1,25},{2,26},{3,27},{4,28},{5,29},{6,30},{7,31},{8,16},{9,... | collective-permute-start | bytes 172040 | tf_op jit(solution)/shard_map/ppermute | solution.py:933
  148.2 0.5 gather.19
  148.7 1.3 collective-permute-start.25
  150.1 1.0 collective-permute-done.30.refs_8_
  151.1 0.8 finish.1
  151.9 1.2 collective-permute-done.31
  153.1 3.1 %collective-permute-start.34 = (f32[8,128]{1,0:T(8,128)S(1)}, f32[8,128]{1,0:T(8,128)S(1)}, u32[]{:S(2)}, u32[]{:S(2)}) collective-permute-start(f32[8,128]{1,0:T(8,128)S(1)} %add.24), channel_id=1, source_target_pairs={{0,24},{1,25},{2,26},{3,27},{4,28},{5,29},{6,30},{7,31},{8,16},{9,... | collective-permute-start | bytes 12296 | tf_op jit(solution)/shard_map/ppermute | solution.py:933
  156.2 1.3 collective-permute-start.32
  157.5 1.0 collective-permute-done.34
  158.5 2.2 %collective-permute-done.33 = f32[8,128]{1,0:T(8,128)S(1)} collective-permute-done((f32[8,128]{1,0:T(8,128)S(1)}, f32[8,128]{1,0:T(8,128)S(1)}, u32[]{:S(2)}, u32[]{:S(2)}) %collective-permute-start.33) | collective-permute-done | bytes 4128 | tf_op jit(solution)/shard_map/ppermute | solution.py:933
  160.9 1.6 collective-permute-start.37
  162.5 1.2 collective-permute-start.36
  163.7 0.8 collective-permute-start.35
  164.5 1.4 frames_end.1
  166.1 1.2 collective-permute-done.35
  167.4 2.4 %adam.1 = (f32[1,1]{1,0:T(1,128)}, f32[96,576]{1,0:T(8,128)}, f32[96,576]{1,0:T(8,128)}, f32[96,576]{1,0:T(8,128)}, bf16[96,576]{1,0:T(8,128)(2,1)}, /*index=5*/...) custom-call(f32[8,128]{1,0:T(8,128)S(1)} %add_add_fusion.squares_ref, ...), custom_call_target="tpu_custom_call" | custom-call | flops 22000001024 | tf_op jit(solution)/shard_map/adam/pallas_call | solution.py:923
  (122 shorter events, 4.0 us)
Async XLA Ops:
  0.7 3.2 %collective-permute-start.1 = (bf16[384,768]{1,0:T(8,128)(2,1)}, bf16[384,768]{1,0:T(8,128)(2,1)S(1)}, u32[]{:S(2)}, u32[]{:S(2)}) collective-permute-start(bf16[384,768]{1,0:T(8,128)(2,1)} %x_ref.1), channel_id=1, source_target_pairs={{0,1},{1,0},{2,3},{3,2},{4,5},{5,4},{6,7},{7,6},{8,9},{9,8},{10,11... | collective-permute-start | bytes 1769480 | tf_op jit(solution)/shard_map/ppermute | solution.py:933
  1.2 16.7 %collective-permute-start = (bf16[384,768]{1,0:T(8,128)(2,1)}, bf16[384,768]{1,0:T(8,128)(2,1)S(1)}, u32[]{:S(2)}, u32[]{:S(2)}) collective-permute-start(bf16[384,768]{1,0:T(8,128)(2,1)} %x_ref.1), channel_id=1, source_target_pairs={{0,2},{1,3},{2,0},{3,1},{4,6},{5,7},{6,4},{7,5},{8,10},{9,11},{10,... | collective-permute-start | bytes 1769480 | tf_op jit(solution)/shard_map/ppermute | solution.py:933
  17.0 4.2 %copy-start.8 = (bf16[384,768]{1,0:T(8,128)(2,1)}, bf16[384,768]{1,0:T(8,128)(2,1)S(1)}, u32[]{:S(2)}) copy-start(bf16[384,768]{1,0:T(8,128)(2,1)S(1)} %get-tuple-element.154.q_ref) | copy-start | bytes 1769476
  17.9 3.3 %collective-permute-start.2 = (bf16[384,768]{1,0:T(8,128)(2,1)S(1)}, bf16[384,768]{1,0:T(8,128)(2,1)S(1)}, u32[]{:S(2)}, u32[]{:S(2)}) collective-permute-start(bf16[384,768]{1,0:T(8,128)(2,1)S(1)} %pass_on.1.x_ref.xp_ref), channel_id=1, source_target_pairs={{0,1},{1,0},{2,3},{3,2},{4,5},{5,4},{6,7},{7,6},{8,9},{9,8},{10,11... | collective-permute-start | bytes 1769480 | tf_op jit(solution)/shard_map/ppermute | solution.py:933
  18.0 13.7 %slice-start = ((s8[4718592]{0:T(1024)(128)(4,1)}), s8[4194304]{0:T(1024)(128)(4,1)S(1)}, s32[]{:S(2)}) async-start(s8[4718592]{0:T(1024)(128)(4,1)} %bitcast.31), calls=%async_computation | async-start | bytes 8388608
  18.0 13.7 %slice-start.2 = ((s8[4718592]{0:T(1024)(128)(4,1)}), s8[4194304]{0:T(1024)(128)(4,1)S(1)}, s32[]{:S(2)}) async-start(s8[4718592]{0:T(1024)(128)(4,1)} %bitcast.33), calls=%async_computation.2 | async-start | bytes 8388608
  21.2 10.5 %slice-start.1 = ((s8[4718592]{0:T(1024)(128)(4,1)}), s8[524288]{0:T(1024)(128)(4,1)S(1)}, s32[]{:S(2)}) async-start(s8[4718592]{0:T(1024)(128)(4,1)} %bitcast.31), calls=%async_computation.1 | async-start | bytes 1048576
  21.3 10.5 %slice-start.3 = ((s8[4718592]{0:T(1024)(128)(4,1)}), s8[524288]{0:T(1024)(128)(4,1)S(1)}, s32[]{:S(2)}) async-start(s8[4718592]{0:T(1024)(128)(4,1)} %bitcast.33), calls=%async_computation.3 | async-start | bytes 1048576
  21.3 10.5 %copy-start.13 = (bf16[768,768]{1,0:T(8,128)(2,1)S(1)}, bf16[768,768]{1,0:T(8,128)(2,1)}, u32[]{:S(2)}) copy-start(bf16[768,768]{1,0:T(8,128)(2,1)} %wo_ref.3) | copy-start | bytes 3538948
  21.3 10.5 %copy-start.14 = (bf16[384,768]{1,0:T(8,128)(2,1)S(1)}, bf16[384,768]{1,0:T(8,128)(2,1)}, u32[]{:S(2)}) copy-start(bf16[384,768]{1,0:T(8,128)(2,1)} %x_ref.1) | copy-start | bytes 1769476
  21.3 10.5 %copy-start.15 = (bf16[384,768]{1,0:T(8,128)(2,1)S(1)}, bf16[384,768]{1,0:T(8,128)(2,1)}, u32[]{:S(2)}) copy-start(bf16[384,768]{1,0:T(8,128)(2,1)} %cot_ref.1) | copy-start | bytes 1769476
  31.8 12.7 %copy-start.10 = (bf16[384,768]{1,0:T(8,128)(2,1)}, bf16[384,768]{1,0:T(8,128)(2,1)S(1)}, u32[]{:S(2)}) copy-start(bf16[384,768]{1,0:T(8,128)(2,1)S(1)} %get-tuple-element.160.mixed_ref) | copy-start | bytes 1769476
  44.0 4.6 %collective-permute-start.3 = (bf16[2,8,96,768]{3,2,1,0:T(8,128)(2,1)S(1)}, bf16[2,8,96,768]{3,2,1,0:T(8,128)(2,1)S(1)}, u32[]{:S(2)}, u32[]{:S(2)}) collective-permute-start(bf16[2,8,96,768]{3,2,1,0:T(8,128)(2,1)S(1)} %get-tuple-element.173), channel_id=1, source_target_pairs={{0,1},{1,0},{2,3},{3,2},{4,5},{5,4},{6,7},{7,6},{8,9},{9,8},{10,11... | collective-permute-start | bytes 7077896 | tf_op jit(solution)/shard_map/ppermute | solution.py:933
  49.7 15.7 %collective-permute-start.5 = (bf16[2,192,768]{2,1,0:T(8,128)(2,1)S(1)}, bf16[2,192,768]{2,1,0:T(8,128)(2,1)S(1)}, u32[]{:S(2)}, u32[]{:S(2)}) collective-permute-start(bf16[2,192,768]{2,1,0:T(8,128)(2,1)S(1)} %get-tuple-element.178), channel_id=1, source_target_pairs={{0,2},{1,3},{2,0},{3,1},{4,6},{5,7},{6,4},{7,5},{8,10},{9,11},{10,... | collective-permute-start | bytes 1769480 | tf_op jit(solution)/shard_map/ppermute | solution.py:933
  51.6 15.3 %collective-permute-start.6 = (bf16[2,192,768]{2,1,0:T(8,128)(2,1)S(1)}, bf16[2,192,768]{2,1,0:T(8,128)(2,1)S(1)}, u32[]{:S(2)}, u32[]{:S(2)}) collective-permute-start(bf16[2,192,768]{2,1,0:T(8,128)(2,1)S(1)} %get-tuple-element.180), channel_id=1, source_target_pairs={{0,4},{1,5},{2,6},{3,7},{4,0},{5,1},{6,2},{7,3},{8,12},{9,13},{10,... | collective-permute-start | bytes 1769480 | tf_op jit(solution)/shard_map/ppermute | solution.py:933
  64.7 5.4 %collective-permute-start.4 = (bf16[2,2,4,240,384]{4,3,2,1,0:T(8,128)(2,1)S(1)}, bf16[2,2,4,240,384]{4,3,2,1,0:T(8,128)(2,1)S(1)}, u32[]{:S(2)}, u32[]{:S(2)}) collective-permute-start(bf16[2,2,4,240,384]{4,3,2,1,0:T(8,128)(2,1)S(1)} %get-tuple-element.177), channel_id=1, source_target_pairs={{0,1},{1,0},{2,3},{3,2},{4,5},{5,4},{6,7},{7,6},{8,9},{9,8},{10,11... | collective-permute-start | bytes 8847368 | tf_op jit(solution)/shard_map/ppermute | solution.py:933
  67.4 16.1 %collective-permute-start.9 = (bf16[1,192,768]{2,1,0:T(8,128)(2,1)S(1)}, bf16[1,192,768]{2,1,0:T(8,128)(2,1)S(1)}, u32[]{:S(2)}, u32[]{:S(2)}) collective-permute-start(bf16[1,192,768]{2,1,0:T(8,128)(2,1)S(1)} %get-tuple-element.198), channel_id=1, source_target_pairs={{0,4},{1,5},{2,6},{3,7},{4,0},{5,1},{6,2},{7,3},{8,12},{9,13},{10,... | collective-permute-start | bytes 884744 | tf_op jit(solution)/shard_map/ppermute | solution.py:933
  68.9 14.5 %collective-permute-start.10 = (bf16[1,192,768]{2,1,0:T(8,128)(2,1)S(1)}, bf16[1,192,768]{2,1,0:T(8,128)(2,1)S(1)}, u32[]{:S(2)}, u32[]{:S(2)}) collective-permute-start(bf16[1,192,768]{2,1,0:T(8,128)(2,1)S(1)} %get-tuple-element.200), channel_id=1, source_target_pairs={{0,2},{1,3},{2,0},{3,1},{4,6},{5,7},{6,4},{7,5},{8,10},{9,11},{10,... | collective-permute-start | bytes 884744 | tf_op jit(solution)/shard_map/ppermute | solution.py:933
  70.2 4.0 %copy-start.11 = (bf16[384,768]{1,0:T(8,128)(2,1)S(1)}, bf16[384,768]{1,0:T(8,128)(2,1)}, u32[]{:S(2)}) copy-start(bf16[384,768]{1,0:T(8,128)(2,1)} %copy-done.10) | copy-start | bytes 1769476
  71.9 24.2 %collective-permute-start.7 = (bf16[2,480,384]{2,1,0:T(8,128)(2,1)S(1)}, bf16[2,480,384]{2,1,0:T(8,128)(2,1)S(1)}, u32[]{:S(2)}, u32[]{:S(2)}) collective-permute-start(bf16[2,480,384]{2,1,0:T(8,128)(2,1)S(1)} %get-tuple-element.184), channel_id=1, source_target_pairs={{0,2},{1,3},{2,0},{3,1},{4,6},{5,7},{6,4},{7,5},{8,10},{9,11},{10,... | collective-permute-start | bytes 2211848 | tf_op jit(solution)/shard_map/ppermute | solution.py:933
  72.8 23.4 %collective-permute-start.8 = (bf16[2,480,384]{2,1,0:T(8,128)(2,1)S(1)}, bf16[2,480,384]{2,1,0:T(8,128)(2,1)S(1)}, u32[]{:S(2)}, u32[]{:S(2)}) collective-permute-start(bf16[2,480,384]{2,1,0:T(8,128)(2,1)S(1)} %get-tuple-element.186), channel_id=1, source_target_pairs={{0,4},{1,5},{2,6},{3,7},{4,0},{5,1},{6,2},{7,3},{8,12},{9,13},{10,... | collective-permute-start | bytes 2211848 | tf_op jit(solution)/shard_map/ppermute | solution.py:933
  83.7 20.8 %collective-permute-start.14 = (bf16[1,192,768]{2,1,0:T(8,128)(2,1)S(1)}, bf16[1,192,768]{2,1,0:T(8,128)(2,1)S(1)}, u32[]{:S(2)}, u32[]{:S(2)}) collective-permute-start(bf16[1,192,768]{2,1,0:T(8,128)(2,1)S(1)} %get-tuple-element.216), channel_id=1, source_target_pairs={{0,16},{1,17},{2,18},{3,19},{4,20},{5,21},{6,22},{7,23},{8,24},{9,... | collective-permute-start | bytes 884744 | tf_op jit(solution)/shard_map/ppermute | solution.py:933
  96.0 12.5 %collective-permute-start.13 = (bf16[2,8,96,384]{3,2,1,0:T(8,128)(2,1)S(1)}, bf16[2,8,96,384]{3,2,1,0:T(8,128)(2,1)S(1)}, u32[]{:S(2)}, u32[]{:S(2)}) collective-permute-start(bf16[2,8,96,384]{3,2,1,0:T(8,128)(2,1)S(1)} %get-tuple-element.215), channel_id=1, source_target_pairs={{0,1},{1,0},{2,3},{3,2},{4,5},{5,4},{6,7},{7,6},{8,9},{9,8},{10,11... | collective-permute-start | bytes 3538952 | tf_op jit(solution)/shard_map/ppermute | solution.py:933
  97.1 11.0 %collective-permute-start.11 = (bf16[1,480,384]{2,1,0:T(8,128)(2,1)S(1)}, bf16[1,480,384]{2,1,0:T(8,128)(2,1)S(1)}, u32[]{:S(2)}, u32[]{:S(2)}) collective-permute-start(bf16[1,480,384]{2,1,0:T(8,128)(2,1)S(1)} %get-tuple-element.211), channel_id=1, source_target_pairs={{0,4},{1,5},{2,6},{3,7},{4,0},{5,1},{6,2},{7,3},{8,12},{9,13},{10,... | collective-permute-start | bytes 1105928 | tf_op jit(solution)/shard_map/ppermute | solution.py:933
  97.9 10.7 %collective-permute-start.12 = (bf16[1,480,384]{2,1,0:T(8,128)(2,1)S(1)}, bf16[1,480,384]{2,1,0:T(8,128)(2,1)S(1)}, u32[]{:S(2)}, u32[]{:S(2)}) collective-permute-start(bf16[1,480,384]{2,1,0:T(8,128)(2,1)S(1)} %get-tuple-element.213), channel_id=1, source_target_pairs={{0,2},{1,3},{2,0},{3,1},{4,6},{5,7},{6,4},{7,5},{8,10},{9,11},{10,... | collective-permute-start | bytes 1105928 | tf_op jit(solution)/shard_map/ppermute | solution.py:933
  108.6 6.4 %copy-start.34 = (f32[16,768]{1,0:T(8,128)S(1)}, f32[16,768]{1,0:T(8,128)}, u32[]{:S(2)}) copy-start(f32[16,768]{1,0:T(8,128)} %copy-done.33) | copy-start | bytes 147460
  109.5 39.3 %collective-permute-start.26 = (bf16[1,96,768]{2,1,0:T(8,128)(2,1)S(1)}, bf16[1,96,768]{2,1,0:T(8,128)(2,1)S(1)}, u32[]{:S(2)}, u32[]{:S(2)}) collective-permute-start(bf16[1,96,768]{2,1,0:T(8,128)(2,1)S(1)} %get-tuple-element.245), channel_id=1, source_target_pairs={{0,8},{1,9},{2,10},{3,11},{4,12},{5,13},{6,14},{7,15},{8,0},{9,1},... | collective-permute-start | bytes 442376 | tf_op jit(solution)/shard_map/ppermute | solution.py:933
  111.1 13.4 %collective-permute-start.16 = (bf16[1,384,384]{2,1,0:T(8,128)(2,1)S(1)}, bf16[1,384,384]{2,1,0:T(8,128)(2,1)S(1)}, u32[]{:S(2)}, u32[]{:S(2)}) collective-permute-start(bf16[1,384,384]{2,1,0:T(8,128)(2,1)S(1)} %get-tuple-element.222), channel_id=1, source_target_pairs={{0,4},{1,5},{2,6},{3,7},{4,0},{5,1},{6,2},{7,3},{8,12},{9,13},{10,... | collective-permute-start | bytes 884744 | tf_op jit(solution)/shard_map/ppermute | solution.py:933
  112.4 14.0 %collective-permute-start.17 = (bf16[1,384,384]{2,1,0:T(8,128)(2,1)S(1)}, bf16[1,384,384]{2,1,0:T(8,128)(2,1)S(1)}, u32[]{:S(2)}, u32[]{:S(2)}) collective-permute-start(bf16[1,384,384]{2,1,0:T(8,128)(2,1)S(1)} %get-tuple-element.223), channel_id=1, source_target_pairs={{0,2},{1,3},{2,0},{3,1},{4,6},{5,7},{6,4},{7,5},{8,10},{9,11},{10,... | collective-permute-start | bytes 884744 | tf_op jit(solution)/shard_map/ppermute | solution.py:933
  113.2 13.2 %collective-permute-start.18 = (bf16[1,384,384]{2,1,0:T(8,128)(2,1)S(1)}, bf16[1,384,384]{2,1,0:T(8,128)(2,1)S(1)}, u32[]{:S(2)}, u32[]{:S(2)}) collective-permute-start(bf16[1,384,384]{2,1,0:T(8,128)(2,1)S(1)} %get-tuple-element.224), channel_id=1, source_target_pairs={{0,6},{1,7},{2,4},{3,5},{4,2},{5,3},{6,0},{7,1},{8,14},{9,15},{10,... | collective-permute-start | bytes 884744 | tf_op jit(solution)/shard_map/ppermute | solution.py:933
  114.6 20.7 %collective-permute-start.23 = (bf16[1,480,384]{2,1,0:T(8,128)(2,1)S(1)}, bf16[1,480,384]{2,1,0:T(8,128)(2,1)S(1)}, u32[]{:S(2)}, u32[]{:S(2)}) collective-permute-start(bf16[1,480,384]{2,1,0:T(8,128)(2,1)S(1)} %get-tuple-element.237), channel_id=1, source_target_pairs={{0,16},{1,17},{2,18},{3,19},{4,20},{5,21},{6,22},{7,23},{8,24},{9,... | collective-permute-start | bytes 1105928 | tf_op jit(solution)/shard_map/ppermute | solution.py:933
  124.5 2.9 %collective-permute-start.15 = (bf16[2,8,112,256]{3,2,1,0:T(8,128)(2,1)S(1)}, bf16[2,8,112,256]{3,2,1,0:T(8,128)(2,1)S(1)}, u32[]{:S(2)}, u32[]{:S(2)}) collective-permute-start(bf16[2,8,112,256]{3,2,1,0:T(8,128)(2,1)S(1)} %get-tuple-element.220), channel_id=1, source_target_pairs={{0,1},{1,0},{2,3},{3,2},{4,5},{5,4},{6,7},{7,6},{8,9},{9,8},{10,11... | collective-permute-start | bytes 2752520 | tf_op jit(solution)/shard_map/ppermute | solution.py:933
  126.6 11.7 %collective-permute-start.24 = (bf16[2,96,384]{2,1,0:T(8,128)(2,1)S(1)}, bf16[2,96,384]{2,1,0:T(8,128)(2,1)S(1)}, u32[]{:S(2)}, u32[]{:S(2)}) collective-permute-start(bf16[2,96,384]{2,1,0:T(8,128)(2,1)S(1)} %get-tuple-element.238), channel_id=1, source_target_pairs={{0,16},{1,17},{2,18},{3,19},{4,20},{5,21},{6,22},{7,23},{8,24},{9,... | collective-permute-start | bytes 442376 | tf_op jit(solution)/shard_map/ppermute | solution.py:933
  127.7 10.9 %collective-permute-start.20 = (bf16[1,448,256]{2,1,0:T(8,128)(2,1)S(1)}, bf16[1,448,256]{2,1,0:T(8,128)(2,1)S(1)}, u32[]{:S(2)}, u32[]{:S(2)}) collective-permute-start(bf16[1,448,256]{2,1,0:T(8,128)(2,1)S(1)} %get-tuple-element.234), channel_id=1, source_target_pairs={{0,4},{1,5},{2,6},{3,7},{4,0},{5,1},{6,2},{7,3},{8,12},{9,13},{10,... | collective-permute-start | bytes 688136 | tf_op jit(solution)/shard_map/ppermute | solution.py:933
  129.0 9.6 %collective-permute-start.21 = (bf16[1,448,256]{2,1,0:T(8,128)(2,1)S(1)}, bf16[1,448,256]{2,1,0:T(8,128)(2,1)S(1)}, u32[]{:S(2)}, u32[]{:S(2)}) collective-permute-start(bf16[1,448,256]{2,1,0:T(8,128)(2,1)S(1)} %get-tuple-element.235), channel_id=1, source_target_pairs={{0,2},{1,3},{2,0},{3,1},{4,6},{5,7},{6,4},{7,5},{8,10},{9,11},{10,... | collective-permute-start | bytes 688136 | tf_op jit(solution)/shard_map/ppermute | solution.py:933
  135.3 8.3 %collective-permute-start.22 = (bf16[1,448,256]{2,1,0:T(8,128)(2,1)S(1)}, bf16[1,448,256]{2,1,0:T(8,128)(2,1)S(1)}, u32[]{:S(2)}, u32[]{:S(2)}) collective-permute-start(bf16[1,448,256]{2,1,0:T(8,128)(2,1)S(1)} %get-tuple-element.236), channel_id=1, source_target_pairs={{0,6},{1,7},{2,4},{3,5},{4,2},{5,3},{6,0},{7,1},{8,14},{9,15},{10,... | collective-permute-start | bytes 688136 | tf_op jit(solution)/shard_map/ppermute | solution.py:933
  138.5 11.6 %collective-permute-start.27 = (bf16[336,384]{1,0:T(8,128)(2,1)S(1)}, bf16[336,384]{1,0:T(8,128)(2,1)S(1)}, u32[]{:S(2)}, u32[]{:S(2)}) collective-permute-start(bf16[336,384]{1,0:T(8,128)(2,1)S(1)} %get-tuple-element.247), channel_id=1, source_target_pairs={{0,8},{1,9},{2,10},{3,11},{4,12},{5,13},{6,14},{7,15},{8,0},{9,1},... | collective-permute-start | bytes 774152 | tf_op jit(solution)/shard_map/ppermute | solution.py:933
  138.6 5.7 %collective-permute-start.19 = (bf16[2,768,384]{2,1,0:T(8,128)(2,1)S(1)}, bf16[2,768,384]{2,1,0:T(8,128)(2,1)S(1)}, u32[]{:S(2)}, u32[]{:S(2)}) collective-permute-start(bf16[2,768,384]{2,1,0:T(8,128)(2,1)S(1)} %get-tuple-element.233), channel_id=1, source_target_pairs={{0,1},{1,0},{2,3},{3,2},{4,5},{5,4},{6,7},{7,6},{8,9},{9,8},{10,11... | collective-permute-start | bytes 3538952 | tf_op jit(solution)/shard_map/ppermute | solution.py:933
  143.7 6.3 %collective-permute-start.28 = (bf16[1,112,256]{2,1,0:T(8,128)(2,1)S(1)}, bf16[1,112,256]{2,1,0:T(8,128)(2,1)S(1)}, u32[]{:S(2)}, u32[]{:S(2)}) collective-permute-start(bf16[1,112,256]{2,1,0:T(8,128)(2,1)S(1)} %get-tuple-element.248), channel_id=1, source_target_pairs={{0,8},{1,9},{2,10},{3,11},{4,12},{5,13},{6,14},{7,15},{8,0},{9,1},... | collective-permute-start | bytes 172040 | tf_op jit(solution)/shard_map/ppermute | solution.py:933
  143.8 6.2 %collective-permute-start.29 = (bf16[1,112,256]{2,1,0:T(8,128)(2,1)S(1)}, bf16[1,112,256]{2,1,0:T(8,128)(2,1)S(1)}, u32[]{:S(2)}, u32[]{:S(2)}) collective-permute-start(bf16[1,112,256]{2,1,0:T(8,128)(2,1)S(1)} %get-tuple-element.249), channel_id=1, source_target_pairs={{0,16},{1,17},{2,18},{3,19},{4,20},{5,21},{6,22},{7,23},{8,24},{9,... | collective-permute-start | bytes 172040 | tf_op jit(solution)/shard_map/ppermute | solution.py:933
  144.2 6.8 %collective-permute-start.30 = (bf16[1,112,256]{2,1,0:T(8,128)(2,1)S(1)}, bf16[1,112,256]{2,1,0:T(8,128)(2,1)S(1)}, u32[]{:S(2)}, u32[]{:S(2)}) collective-permute-start(bf16[1,112,256]{2,1,0:T(8,128)(2,1)S(1)} %get-tuple-element.250), channel_id=1, source_target_pairs={{0,24},{1,25},{2,26},{3,27},{4,28},{5,29},{6,30},{7,31},{8,16},{9,... | collective-permute-start | bytes 172040 | tf_op jit(solution)/shard_map/ppermute | solution.py:933
  148.7 15.7 %collective-permute-start.25 = (bf16[1,768,384]{2,1,0:T(8,128)(2,1)S(1)}, bf16[1,768,384]{2,1,0:T(8,128)(2,1)S(1)}, u32[]{:S(2)}, u32[]{:S(2)}) collective-permute-start(bf16[1,768,384]{2,1,0:T(8,128)(2,1)S(1)} %get-tuple-element.242), channel_id=1, source_target_pairs={{0,2},{1,3},{2,0},{3,1},{4,6},{5,7},{6,4},{7,5},{8,10},{9,11},{10,... | collective-permute-start | bytes 1769480 | tf_op jit(solution)/shard_map/ppermute | solution.py:933
  151.9 1.2 collective-permute-start.31
  153.1 5.4 %collective-permute-start.34 = (f32[8,128]{1,0:T(8,128)S(1)}, f32[8,128]{1,0:T(8,128)S(1)}, u32[]{:S(2)}, u32[]{:S(2)}) collective-permute-start(f32[8,128]{1,0:T(8,128)S(1)} %add.24), channel_id=1, source_target_pairs={{0,24},{1,25},{2,26},{3,27},{4,28},{5,29},{6,30},{7,31},{8,16},{9,... | collective-permute-start | bytes 12296 | tf_op jit(solution)/shard_map/ppermute | solution.py:933
  156.2 4.5 %collective-permute-start.33 = (f32[8,128]{1,0:T(8,128)S(1)}, f32[8,128]{1,0:T(8,128)S(1)}, u32[]{:S(2)}, u32[]{:S(2)}) collective-permute-start(f32[8,128]{1,0:T(8,128)S(1)} %add.24), channel_id=1, source_target_pairs={{0,16},{1,17},{2,18},{3,19},{4,20},{5,21},{6,22},{7,23},{8,24},{9,... | collective-permute-start | bytes 12296 | tf_op jit(solution)/shard_map/ppermute | solution.py:933
  156.2 4.5 %collective-permute-start.32 = (f32[8,128]{1,0:T(8,128)S(1)}, f32[8,128]{1,0:T(8,128)S(1)}, u32[]{:S(2)}, u32[]{:S(2)}) collective-permute-start(f32[8,128]{1,0:T(8,128)S(1)} %add.24), channel_id=1, source_target_pairs={{0,8},{1,9},{2,10},{3,11},{4,12},{5,13},{6,14},{7,15},{8,0},{9,1},... | collective-permute-start | bytes 12296 | tf_op jit(solution)/shard_map/ppermute | solution.py:933
  160.7 6.6 %copy-start.16 = (f32[192,384]{1,0:T(8,128)S(1)}, f32[192,384]{1,0:T(8,128)}, u32[]{:S(2)}) copy-start(f32[192,384]{1,0:T(8,128)} %refs_8_.1) | copy-start | bytes 884740
  160.7 6.6 %copy-start.17 = (f32[192,384]{1,0:T(8,128)S(1)}, f32[192,384]{1,0:T(8,128)}, u32[]{:S(2)}) copy-start(f32[192,384]{1,0:T(8,128)} %refs_9_.1) | copy-start | bytes 884740
  160.8 6.6 %copy-start.18 = (f32[192,384]{1,0:T(8,128)S(1)}, f32[192,384]{1,0:T(8,128)}, u32[]{:S(2)}) copy-start(f32[192,384]{1,0:T(8,128)} %refs_10_.1) | copy-start | bytes 884740
  160.8 6.6 %copy-start.19 = (f32[768,96]{0,1:T(8,128)S(1)}, f32[768,96]{0,1:T(8,128)}, u32[]{:S(2)}) copy-start(f32[768,96]{0,1:T(8,128)} %param.34) | copy-start | bytes 884740
  160.8 6.6 %copy-start.20 = (f32[768,96]{0,1:T(8,128)S(1)}, f32[768,96]{0,1:T(8,128)}, u32[]{:S(2)}) copy-start(f32[768,96]{0,1:T(8,128)} %param.39) | copy-start | bytes 884740
  160.8 6.6 %copy-start.21 = (f32[768,96]{0,1:T(8,128)S(1)}, f32[768,96]{0,1:T(8,128)}, u32[]{:S(2)}) copy-start(f32[768,96]{0,1:T(8,128)} %param.44) | copy-start | bytes 884740
  160.8 6.5 %copy-start.22 = (f32[96,576]{1,0:T(8,128)S(1)}, f32[96,576]{1,0:T(8,128)}, u32[]{:S(2)}) copy-start(f32[96,576]{1,0:T(8,128)} %refs_0_.1) | copy-start | bytes 663556
  160.8 6.5 %copy-start.23 = (f32[96,576]{1,0:T(8,128)S(1)}, f32[96,576]{1,0:T(8,128)}, u32[]{:S(2)}) copy-start(f32[96,576]{1,0:T(8,128)} %refs_1_.1) | copy-start | bytes 663556
  160.8 6.5 %copy-start.24 = (f32[96,576]{1,0:T(8,128)S(1)}, f32[96,576]{1,0:T(8,128)}, u32[]{:S(2)}) copy-start(f32[96,576]{1,0:T(8,128)} %refs_2_.1) | copy-start | bytes 663556
  160.8 6.5 %copy-start.25 = (f32[192,96]{1,0:T(8,128)S(1)}, f32[192,96]{1,0:T(8,128)}, u32[]{:S(2)}) copy-start(f32[192,96]{1,0:T(8,128)} %refs_4_.1) | copy-start | bytes 221188
  160.8 6.5 %copy-start.26 = (f32[192,96]{1,0:T(8,128)S(1)}, f32[192,96]{1,0:T(8,128)}, u32[]{:S(2)}) copy-start(f32[192,96]{1,0:T(8,128)} %refs_5_.1) | copy-start | bytes 221188
  160.9 6.5 %copy-start.27 = (f32[192,96]{1,0:T(8,128)S(1)}, f32[192,96]{1,0:T(8,128)}, u32[]{:S(2)}) copy-start(f32[192,96]{1,0:T(8,128)} %refs_6_.1) | copy-start | bytes 221188
  160.9 6.5 %copy-start.29 = (f32[3,96]{1,0:T(4,128)S(1)}, f32[3,96]{1,0:T(4,128)}, u32[]{:S(2)}) copy-start(f32[3,96]{1,0:T(4,128)} %refs_16_.1) | copy-start | bytes 3460
  160.9 6.5 %copy-start.30 = (f32[3,96]{1,0:T(4,128)S(1)}, f32[3,96]{1,0:T(4,128)}, u32[]{:S(2)}) copy-start(f32[3,96]{1,0:T(4,128)} %refs_17_.1) | copy-start | bytes 3460
  160.9 6.5 %copy-start.31 = (f32[3,96]{1,0:T(4,128)S(1)}, f32[3,96]{1,0:T(4,128)}, u32[]{:S(2)}) copy-start(f32[3,96]{1,0:T(4,128)} %refs_18_.1) | copy-start | bytes 3460
  160.9 5.0 %collective-permute-start.37 = (f32[8,128]{1,0:T(8,128)S(1)}, f32[8,128]{1,0:T(8,128)S(1)}, u32[]{:S(2)}, u32[]{:S(2)}) collective-permute-start(f32[8,128]{1,0:T(8,128)S(1)} %add_add_fusion.1), channel_id=1, source_target_pairs={{0,6},{1,7},{2,4},{3,5},{4,2},{5,3},{6,0},{7,1},{8,14},{9,15},{10,... | collective-permute-start | bytes 12296 | tf_op jit(solution)/shard_map/ppermute | solution.py:933
  162.5 3.6 %collective-permute-start.36 = (f32[8,128]{1,0:T(8,128)S(1)}, f32[8,128]{1,0:T(8,128)S(1)}, u32[]{:S(2)}, u32[]{:S(2)}) collective-permute-start(f32[8,128]{1,0:T(8,128)S(1)} %add_add_fusion.1), channel_id=1, source_target_pairs={{0,4},{1,5},{2,6},{3,7},{4,0},{5,1},{6,2},{7,3},{8,12},{9,13},{10,... | collective-permute-start | bytes 12296 | tf_op jit(solution)/shard_map/ppermute | solution.py:933
  163.7 3.6 %collective-permute-start.35 = (f32[8,128]{1,0:T(8,128)S(1)}, f32[8,128]{1,0:T(8,128)S(1)}, u32[]{:S(2)}, u32[]{:S(2)}) collective-permute-start(f32[8,128]{1,0:T(8,128)S(1)} %add_add_fusion.1), channel_id=1, source_target_pairs={{0,2},{1,3},{2,0},{3,1},{4,6},{5,7},{6,4},{7,5},{8,10},{9,11},{10,... | collective-permute-start | bytes 12296 | tf_op jit(solution)/shard_map/ppermute | solution.py:933
  (13 other events, 36.8 us)
